TPU v7x, 32 devices: a whole 2x2x4 slice. The times are simulated.
32 devices in a mesh: row: 8 (over y, x, core), col: 4 (over z).
Axes of the slice: x: 2, y: 2, z: 4, core: 2. Of those that a mesh axis runs over, the one named last changes fastest.
Arguments:
- sqrt_iterate: float32 [64, 128, 1024], P(('row', 'col'))
- inverse_iterate: float32 [64, 128, 1024], P(('row', 'col'))
- pattern: int32 [64, 8], replicated, may hold values from 0 to 63, as said below
- keep_mask: int32 [64, 8], replicated, may hold values 0 or 1
- row_order: int32 [64], replicated, may hold values from 0 to 63, as said below
Outputs:
- sqrt_next: float32 [64, 128, 1024], P(('row', 'col'))
- inverse_next: float32 [64, 128, 1024], P(('row', 'col'))
Inputs may be any that keep to these rules, and one draw needn't show every extreme that they name: row_order holds each of 0 to 63 once. pattern[s, 0] = row_order[s]; the labels of one row are distinct; each label in row s is that of a block row stored on the same device as s, on one of the two devices one step away along row (wrapping), or on the next device along col (wrapping). Stored position s lies on device index (s // 2) in the order of the mesh with row slowest.
All inputs are finite; a program needn't handle non-finite values.
Results may differ from a plain program's by a relative error of at most 0.00011.
Values sent between devices are 32-bit elements; how exact they have to be, the bound alone decides.
No kernel may reach another device: no remote copies, remote signals or barrier semaphores. Data moves between devices by JAX's collectives and lax.ppermute only.
A program may use at most 128 MiB of HBM per device.

v0:
```python
import jax
import jax.numpy as jnp
from jax import lax
from jax.sharding import PartitionSpec as P

PRECISE = lax.Precision.HIGHEST


def with_halo(block, sides, width):
    for axis, dim in sides:
        count = lax.axis_size(axis)
        forward = [(i, i + 1) for i in range(count - 1)]
        forward.append((count - 1, 0))
        backward = [(target, source) for source, target in forward]
        low = lax.ppermute(
            lax.slice_in_dim(block, block.shape[dim] - width, None, axis=dim), axis, forward
        )
        high = lax.ppermute(lax.slice_in_dim(block, 0, width, axis=dim), axis, backward)
        block = jnp.concatenate([low, block, high], axis=dim)
    return block


def shifted(block, axis, distance):
    devices = range(lax.axis_size(axis))
    route = [((i - distance) % len(devices), i) for i in devices]
    return lax.ppermute(block, axis, route)


def extended_index(position, rows_dev, row_devices, col_devices, row_here, col_here):
    device = position // rows_dev
    offset = position % rows_dev
    row_of = device // col_devices
    col_of = device % col_devices
    same_col = col_of == col_here
    region = jnp.where(
        same_col & (row_of == row_here),
        1,
        jnp.where(
            same_col & (row_of == (row_here + row_devices - 1) % row_devices),
            0,
            jnp.where(same_col, 2, 3),
        ),
    )
    return region * rows_dev + offset


def filtered_product(left_factor, extended, ext_index, selector, kept_cols):
    rows_dev, block_size, row_width = left_factor.shape
    slot_count = row_width // block_size
    picked = extended[ext_index].reshape(rows_dev, slot_count, block_size, slot_count, block_size)
    chosen = jnp.einsum("skimj,skpm->skipj", picked, selector, precision=PRECISE)
    chosen = chosen.reshape(rows_dev, row_width, row_width)
    result = jnp.einsum(
        "sik,skn->sin", left_factor, chosen, precision=PRECISE, preferred_element_type=jnp.float32
    )
    return result * kept_cols


def local(sqrt_iterate, inverse_iterate, pattern, keep_mask, row_order):
    rows_dev, block_size, row_width = sqrt_iterate.shape
    slot_count = row_width // block_size
    row_devices = lax.axis_size("row")
    col_devices = lax.axis_size("col")
    row_here = lax.axis_index("row")
    col_here = lax.axis_index("col")
    block_rows = row_order.shape[0]
    inverse_order = (
        jnp.zeros((block_rows,), jnp.int32)
        .at[row_order]
        .set(jnp.arange(block_rows, dtype=jnp.int32))
    )
    first_row = (row_here * col_devices + col_here) * rows_dev
    local_pattern = lax.dynamic_slice_in_dim(pattern, first_row, rows_dev, 0)
    local_keep = lax.dynamic_slice_in_dim(keep_mask, first_row, rows_dev, 0)
    position = inverse_order[local_pattern]
    ext_index = extended_index(position, rows_dev, row_devices, col_devices, row_here, col_here)
    selector = (pattern[position][:, :, None, :] == local_pattern[:, None, :, None]).astype(
        jnp.float32
    )
    slot_ids = jnp.arange(slot_count, dtype=jnp.int32)
    kept = jnp.maximum(local_keep, (slot_ids == 0).astype(jnp.int32)[None, :])
    kept_cols = jnp.repeat(kept.astype(jnp.float32), block_size, axis=1)[:, None, :]
    identity = (jnp.arange(row_width)[None, :] == jnp.arange(block_size)[:, None]).astype(
        jnp.float32
    )
    stacked = jnp.stack((sqrt_iterate, inverse_iterate))
    cycle_parts = with_halo(stacked, (("row", 1),), rows_dev)
    side_parts = shifted(stacked, "col", -1)
    around_pair = jnp.concatenate([cycle_parts, side_parts], axis=1)
    product = filtered_product(inverse_iterate, around_pair[0], ext_index, selector, kept_cols)
    factor = 1.5 * identity[None] - 0.5 * product
    cycle_factor = with_halo(factor, (("row", 0),), rows_dev)
    side_factor = shifted(factor, "col", -1)
    around_factor = jnp.concatenate([cycle_factor, side_factor], axis=0)
    around_inverse = around_pair[1]
    sqrt_next = filtered_product(sqrt_iterate, around_factor, ext_index, selector, kept_cols)
    inverse_next = filtered_product(factor, around_inverse, ext_index, selector, kept_cols)
    return (sqrt_next, inverse_next)


def solution(mesh):
    in_specs = (P(("row", "col"), None, None), P(("row", "col"), None, None), P(), P(), P())
    out_specs = (P(("row", "col"), None, None), P(("row", "col"), None, None))
    return jax.shard_map(local, mesh=mesh, in_specs=in_specs, out_specs=out_specs, check_vma=False)
```

profile of v0, /device:TPU:0, one launch (start us, length us, event | category | flops | bytes accessed | tf_op | source)
XLA Modules:
  0.0 204.7 jit_solution(17631524899099636340)
XLA Ops:
  0.6 3.1 %pad_maximum_fusion.2 = f32[2,2,128,1024]{3,2,1,0:T(8,128)} fusion(f32[1,2,128,1024]{3,2,1,0:T(8,128)} %bitcast.66, f32[1,2,128,1024]{3,2,1,0:T(8,128)} %bitcast.68), kind=kLoop, calls=%fused_computation.13 | loop fusion | flops 524288 | bytes 4194304 | tf_op jit(solution)/shard_map/stack | solution.py:86
  4.2 2.9 %collective-permute-start.1 = (f32[2,2,128,1024]{3,2,1,0:T(8,128)}, f32[2,2,128,1024]{3,2,1,0:T(8,128)}, u32[]{:S(2)}, u32[]{:S(2)}) collective-permute-start(f32[2,2,128,1024]{3,2,1,0:T(8,128)} %pad_maximum_fusion.2), channel_id=1, source_target_pairs={{4,0},{8,4},{12,8},{16,12},{20,16},{24,20},{28,24},{0,28},{5,1},{9... | collective-permute-start | bytes 6291464 | tf_op jit(solution)/shard_map/ppermute | solution.py:18
  7.1 4.4 %collective-permute-start.2 = (f32[2,2,128,1024]{3,2,1,0:T(8,128)}, f32[2,2,128,1024]{3,2,1,0:T(8,128)}, u32[]{:S(2)}, u32[]{:S(2)}) collective-permute-start(f32[2,2,128,1024]{3,2,1,0:T(8,128)} %pad_maximum_fusion.2), channel_id=1, source_target_pairs={{1,0},{2,1},{3,2},{0,3},{5,4},{6,5},{7,6},{4,7},{9,8},{10,9},{11,1... | collective-permute-start | bytes 6291464 | tf_op jit(solution)/shard_map/ppermute | solution.py:26
  16.5 34.5 %collective-permute-done = f32[2,2,128,1024]{3,2,1,0:T(8,128)} collective-permute-done((f32[2,2,128,1024]{3,2,1,0:T(8,128)}, f32[2,2,128,1024]{3,2,1,0:T(8,128)}, u32[]{:S(2)}, u32[]{:S(2)}) %collective-permute-start) | collective-permute-done | bytes 2097184 | tf_op jit(solution)/shard_map/ppermute | solution.py:15
  52.5 3.3 %collective-permute-done.2 = f32[2,2,128,1024]{3,2,1,0:T(8,128)} collective-permute-done((f32[2,2,128,1024]{3,2,1,0:T(8,128)}, f32[2,2,128,1024]{3,2,1,0:T(8,128)}, u32[]{:S(2)}, u32[]{:S(2)}) %collective-permute-start.2) | collective-permute-done | bytes 2097184 | tf_op jit(solution)/shard_map/ppermute | solution.py:26
  55.8 3.7 %pad_maximum_fusion = f32[2,8,128,1024]{3,2,1,0:T(8,128)S(1)} fusion(f32[2,2,128,1024]{3,2,1,0:T(8,128)} %collective-permute-done.2, f32[2,2,128,1024]{3,2,1,0:T(8,128)} %collective-permute-done.1, f32[1,2,128,1024]{3,2,1,0:T(8,128)} %bitcast.67, f32[1,2,128,1024]{3,2,1,0:T(8,128)} %bitcast.69, f32[2,2,128,1024]{3,2,1,0:T(8,128)} %collective-permute-done), kind=kLoop, calls=%fused_computation.6 | loop fusion | flops 8388608 | bytes 16777216 | tf_op jit(solution)/shard_map/concatenate | solution.py:89
  59.5 4.1 %slice_bitcast_fusion = (f32[8,128,1024]{2,1,0:T(8,128)}, f32[8,128,1024]{2,1,0:T(8,128)}) fusion(f32[2,8,128,1024]{3,2,1,0:T(8,128)S(1)} %pad_maximum_fusion), kind=kLoop, calls=%fused_computation.7 | loop fusion | bytes 16777216 | tf_op jit(solution)/shard_map/squeeze | solution.py:95
  63.6 6.5 %gather_fusion.2 = f32[16,128,1024]{2,1,0:T(8,128)} fusion(f32[8,128,1024]{2,1,0:T(8,128)} %get-tuple-element.9, s32[1024]{0:T(1024)S(1)} %pad_clamp_fusion), kind=kCustom, calls=%fused_computation.2 | custom fusion | bytes 16777280 | tf_op jit(solution)/shard_map/gather | solution.py:50
  70.1 5.5 %copy.34 = f32[256,8,8,128]{3,2,1,0:T(8,128)S(1)} copy(f32[256,8,8,128]{3,1,2,0:T(8,128)} %bitcast.62) | data formatting | bytes 16777216
  75.6 6.1 %convolution_bitcast_fusion.2 = f32[2,8,128,8,128]{4,3,2,1,0:T(8,128)} fusion(f32[2,8,128,8,128]{4,3,2,1,0:T(8,128)S(1)} %bitcast.63, s32[2,8]{1,0:T(2,128)S(1)} %copy.22, s32[2,8,8]{2,1,0:T(8,128)S(1)} %bitcast.70), kind=kOutput, calls=%fused_computation.12 | convolution fusion | flops 201327616 | bytes 16777792 | tf_op jit(solution)/shard_map/skimj,skpm->skipj/dot_general | solution.py:51
  81.7 9.3 %reshape.226 = f32[2,1024,1024]{2,1,0:T(8,128)} reshape(f32[2,8,128,8,128]{4,3,2,1,0:T(8,128)} %convolution_bitcast_fusion.2) | data formatting | bytes 16777216 | tf_op jit(solution)/shard_map/reshape | solution.py:52
  91.0 15.6 %fusion.3 = f32[2,128,1024]{1,2,0:T(8,128)S(1)} fusion(f32[2,1024,1024]{2,1,0:T(8,128)} %reshape.226, f32[2,128,1024]{2,1,0:T(8,128)S(1)} %copy-done, f32[2,1024]{1,0:T(2,128)S(1)} %bitcast.73, f32[128,1024]{0,1:T(8,128)S(1)} %fusion.4), kind=kOutput, calls=%fused_computation.20 | convolution fusion | flops 3222011904 | bytes 11018240 | tf_op jit(solution)/shard_map/sik,skn->sin/dot_general | solution.py:53
  109.3 4.3 %collective-permute-start.5 = (f32[2,128,1024]{1,2,0:T(8,128)S(1)}, f32[2,128,1024]{1,2,0:T(8,128)}, u32[]{:S(2)}, u32[]{:S(2)}) collective-permute-start(f32[2,128,1024]{1,2,0:T(8,128)S(1)} %fusion.3), channel_id=1, source_target_pairs={{1,0},{2,1},{3,2},{0,3},{5,4},{6,5},{7,6},{4,7},{9,8},{10,9},{11,1... | collective-permute-start | bytes 3145736 | tf_op jit(solution)/shard_map/ppermute | solution.py:26
  113.6 6.5 %gather_fusion.4 = f32[16,128,1024]{2,1,0:T(8,128)} fusion(f32[8,128,1024]{2,1,0:T(8,128)} %get-tuple-element.8, s32[1024]{0:T(1024)S(1)} %pad_clamp_fusion), kind=kCustom, calls=%fused_computation.4 | custom fusion | bytes 16777280 | tf_op jit(solution)/shard_map/gather | solution.py:50
  120.1 5.5 %copy.36 = f32[256,8,8,128]{3,2,1,0:T(8,128)S(1)} copy(f32[256,8,8,128]{3,1,2,0:T(8,128)} %bitcast.64) | data formatting | bytes 16777216
  125.6 6.3 %convolution_bitcast_fusion = f32[2,8,128,8,128]{4,3,2,1,0:T(8,128)} fusion(f32[2,8,128,8,128]{4,3,2,1,0:T(8,128)S(1)} %bitcast.65, s32[2,8]{1,0:T(2,128)S(1)} %copy.22, s32[2,8,8]{2,1,0:T(8,128)S(1)} %bitcast.71), kind=kOutput, calls=%fused_computation.10 | convolution fusion | flops 201327616 | bytes 16777792 | tf_op jit(solution)/shard_map/skimj,skpm->skipj/dot_general | solution.py:51
  131.9 9.2 %reshape.230 = f32[2,1024,1024]{2,1,0:T(8,128)} reshape(f32[2,8,128,8,128]{4,3,2,1,0:T(8,128)} %convolution_bitcast_fusion) | data formatting | bytes 16777216 | tf_op jit(solution)/shard_map/reshape | solution.py:52
  141.2 8.1 %convolution_multiply_fusion = f32[2,128,1024]{2,1,0:T(8,128)} fusion(f32[2,128,1024]{1,2,0:T(8,128)S(1)} %fusion.3, f32[2,1024,1024]{2,1,0:T(8,128)} %reshape.230, f32[2,1024]{1,0:T(2,128)S(1)} %bitcast.74), kind=kOutput, calls=%fused_computation.14 | convolution fusion | flops 3221487616 | bytes 10493952 | tf_op jit(solution)/shard_map/sik,skn->sin/dot_general | solution.py:53
  149.2 3.5 %pad_maximum_fusion.1 = f32[8,128,1024]{1,2,0:T(8,128)} fusion(f32[2,128,1024]{1,2,0:T(8,128)} %collective-permute-done.5, f32[2,128,1024]{1,2,0:T(8,128)S(1)} %collective-permute-done.4, f32[2,128,1024]{1,2,0:T(8,128)S(1)} %fusion.3, f32[2,128,1024]{1,2,0:T(8,128)S(1)} %collective-permute-done.3), kind=kLoop, calls=%fused_computation.9 | loop fusion | flops 3145728 | bytes 8388608 | tf_op jit(solution)/shard_map/concatenate | solution.py:94
  152.7 6.5 %gather_fusion.3 = f32[16,128,1024]{1,2,0:T(8,128)} fusion(f32[8,128,1024]{1,2,0:T(8,128)} %pad_maximum_fusion.1, s32[1024]{0:T(1024)S(1)} %pad_clamp_fusion), kind=kCustom, calls=%fused_computation.3 | custom fusion | bytes 16777280 | tf_op jit(solution)/shard_map/gather | solution.py:50
  159.2 8.7 %copy.25 = f32[2,8,128,8,128]{4,3,2,1,0:T(8,128)} copy(f32[2,8,128,8,128]{2,4,3,1,0:T(8,128)} %bitcast.61) | data formatting | bytes 16777216 | tf_op jit(solution)/shard_map/reshape | solution.py:50
  167.9 10.5 %convolution_bitcast_fusion.1 = f32[2,8,128,8,128]{4,3,2,1,0:T(8,128)} fusion(f32[2,8,128,8,128]{4,3,2,1,0:T(8,128)} %copy.25, s32[2,8]{1,0:T(2,128)S(1)} %copy.22, s32[2,8,8]{2,1,0:T(8,128)S(1)} %bitcast.72), kind=kOutput, calls=%fused_computation.11 | convolution fusion | flops 201327616 | bytes 16777792 | tf_op jit(solution)/shard_map/skimj,skpm->skipj/dot_general | solution.py:51
  178.4 9.3 %reshape.228 = f32[2,1024,1024]{2,1,0:T(8,128)} reshape(f32[2,8,128,8,128]{4,3,2,1,0:T(8,128)} %convolution_bitcast_fusion.1) | data formatting | bytes 16777216 | tf_op jit(solution)/shard_map/reshape | solution.py:52
  187.8 15.6 %fusion = f32[2,128,1024]{1,2,0:T(8,128)S(1)} fusion(f32[2,1024,1024]{2,1,0:T(8,128)} %reshape.228, f32[2,128,1024]{2,1,0:T(8,128)S(1)} %copy-done.1, f32[2,1024]{1,0:T(2,128)S(1)} %bitcast.75), kind=kOutput, calls=%fused_computation.16 | convolution fusion | flops 3221487616 | bytes 10493952 | tf_op jit(solution)/shard_map/sik,skn->sin/dot_general | solution.py:53
  (34 shorter events, 10.9 us)
Async XLA Ops:
  3.8 47.2 %collective-permute-start = (f32[2,2,128,1024]{3,2,1,0:T(8,128)}, f32[2,2,128,1024]{3,2,1,0:T(8,128)}, u32[]{:S(2)}, u32[]{:S(2)}) collective-permute-start(f32[2,2,128,1024]{3,2,1,0:T(8,128)} %pad_maximum_fusion.2), channel_id=1, source_target_pairs={{0,4},{4,8},{8,12},{12,16},{16,20},{20,24},{24,28},{28,0},{1,5},{5... | collective-permute-start | bytes 6291464 | tf_op jit(solution)/shard_map/ppermute | solution.py:15
  4.2 48.2 %collective-permute-start.1 = (f32[2,2,128,1024]{3,2,1,0:T(8,128)}, f32[2,2,128,1024]{3,2,1,0:T(8,128)}, u32[]{:S(2)}, u32[]{:S(2)}) collective-permute-start(f32[2,2,128,1024]{3,2,1,0:T(8,128)} %pad_maximum_fusion.2), channel_id=1, source_target_pairs={{4,0},{8,4},{12,8},{16,12},{20,16},{24,20},{28,24},{0,28},{5,1},{9... | collective-permute-start | bytes 6291464 | tf_op jit(solution)/shard_map/ppermute | solution.py:18
  7.1 48.7 %collective-permute-start.2 = (f32[2,2,128,1024]{3,2,1,0:T(8,128)}, f32[2,2,128,1024]{3,2,1,0:T(8,128)}, u32[]{:S(2)}, u32[]{:S(2)}) collective-permute-start(f32[2,2,128,1024]{3,2,1,0:T(8,128)} %pad_maximum_fusion.2), channel_id=1, source_target_pairs={{1,0},{2,1},{3,2},{0,3},{5,4},{6,5},{7,6},{4,7},{9,8},{10,9},{11,1... | collective-permute-start | bytes 6291464 | tf_op jit(solution)/shard_map/ppermute | solution.py:26
  81.7 9.3 %copy-start = (f32[2,128,1024]{2,1,0:T(8,128)S(1)}, f32[2,128,1024]{2,1,0:T(8,128)}, u32[]{:S(2)}) copy-start(f32[2,128,1024]{2,1,0:T(8,128)} %param.6) | copy-start | bytes 3145732
  106.6 42.6 %collective-permute-start.3 = (f32[2,128,1024]{1,2,0:T(8,128)S(1)}, f32[2,128,1024]{1,2,0:T(8,128)S(1)}, u32[]{:S(2)}, u32[]{:S(2)}) collective-permute-start(f32[2,128,1024]{1,2,0:T(8,128)S(1)} %fusion.3), channel_id=1, source_target_pairs={{0,4},{4,8},{8,12},{12,16},{16,20},{20,24},{24,28},{28,0},{1,5},{5... | collective-permute-start | bytes 3145736 | tf_op jit(solution)/shard_map/ppermute | solution.py:15
  106.7 42.5 %collective-permute-start.4 = (f32[2,128,1024]{1,2,0:T(8,128)S(1)}, f32[2,128,1024]{1,2,0:T(8,128)S(1)}, u32[]{:S(2)}, u32[]{:S(2)}) collective-permute-start(f32[2,128,1024]{1,2,0:T(8,128)S(1)} %fusion.3), channel_id=1, source_target_pairs={{4,0},{8,4},{12,8},{16,12},{20,16},{24,20},{28,24},{0,28},{5,1},{9... | collective-permute-start | bytes 3145736 | tf_op jit(solution)/shard_map/ppermute | solution.py:18
  109.3 39.9 %collective-permute-start.5 = (f32[2,128,1024]{1,2,0:T(8,128)S(1)}, f32[2,128,1024]{1,2,0:T(8,128)}, u32[]{:S(2)}, u32[]{:S(2)}) collective-permute-start(f32[2,128,1024]{1,2,0:T(8,128)S(1)} %fusion.3), channel_id=1, source_target_pairs={{1,0},{2,1},{3,2},{0,3},{5,4},{6,5},{7,6},{4,7},{9,8},{10,9},{11,1... | collective-permute-start | bytes 3145736 | tf_op jit(solution)/shard_map/ppermute | solution.py:26
  178.4 9.3 %copy-start.1 = (f32[2,128,1024]{2,1,0:T(8,128)S(1)}, f32[2,128,1024]{2,1,0:T(8,128)}, u32[]{:S(2)}) copy-start(f32[2,128,1024]{2,1,0:T(8,128)} %param.5) | copy-start | bytes 3145732
where the time goes:
time: 206 us; the launch traced here: 205 us
  local copies, waits for them, and re-layouts  75.8 us (37%)
  matrix products  62.2 us (30%)
  waiting for transfers between devices  39.3 us (19%)
  starting transfers between devices  14.7 us (7%)
  other arithmetic  11.9 us (6%)
    dot_general x3, matrix products, filtered_product(): jnp.einsum('sik,skn->sin', left_factor, chosen, precision=PRECISE, prefer...  39.3 us
    ppermute x2, waiting for transfers between devices, with_halo(): lax.ppermute(lax.slice_in_dim(block, block.shape[dim] - width, None, axis...  34.5 us
    reshape x3, local copies, waits for them, and re-layouts, filtered_product(): chosen = chosen.reshape(rows_dev, row_width, row_width)  27.9 us
    dot_general x3, matrix products, filtered_product(): jnp.einsum('skimj,skpm->skipj', picked, selector, precision=PRECISE)  22.9 us
    gather x3, local copies, waits for them, and re-layouts, filtered_product(): extended[ext_index]  19.5 us
    unnamed x10, local copies, waits for them, and re-layouts  13.1 us
    reshape x1, local copies, waits for them, and re-layouts, filtered_product(): extended[ext_index]  8.66 us
    ppermute x2, starting transfers between devices, shifted(): return lax.ppermute(block, axis, route)  8.64 us
  transfers between devices with their start and end apart: 6, of which 3 were waited for; matrix products, arithmetic and copies ran while one was open for 20% of the time, Pallas kernels for 0%

commit v1 on v0

v1 whole, which is shorter than its diff:
```python
import functools

import jax
import jax.numpy as jnp
from jax import lax
from jax.experimental import pallas as pl
from jax.experimental.pallas import tpu as pltpu
from jax.sharding import PartitionSpec as P

PREV, OWN, NEXT, SIDE = range(4)
ROWS = 2
SLOTS = 8
SLOT_AT, KEPT_AT, KEPT_PREV_AT, KEPT_NEXT_AT, TABLE = 0, 16, 32, 36, 40
LARGEST = float(jnp.finfo(jnp.bfloat16).max)
VMEM_LIMIT = 24 * 2**20


def split(value):
    clipped = jnp.clip(value, -LARGEST, LARGEST)
    high = clipped.astype(jnp.bfloat16)
    low = (value - high.astype(jnp.float32)).astype(jnp.bfloat16)
    return high, low


def products(*pairs):
    left = [part for (high, low), _ in pairs for part in (high, low, high)]
    right = [part for _, (high, low) in pairs for part in (high, high, low)]
    return jnp.dot(
        jnp.concatenate(left, axis=1),
        jnp.concatenate(right, axis=0),
        preferred_element_type=jnp.float32,
    )


def filtered(table, value, region, scale=None, base=KEPT_AT, width=SLOTS):
    size = value.shape[0] // ROWS
    rows = []
    for i in range(ROWS):
        row = []
        for j in range(ROWS):
            kept = table[base + i * width + region * ROWS + j].astype(jnp.float32)
            if scale is not None:
                kept = kept * scale
            row.append(value[i * size:(i + 1) * size, j * size:(j + 1) * size] * kept)
        rows.append(jnp.concatenate(row, axis=1))
    return jnp.concatenate(rows, axis=0)


def store_slots(table, out, value, region):
    size = out.shape[1]
    for i in range(ROWS):
        for j in range(ROWS):
            slot = table[SLOT_AT + i * SLOTS + region * ROWS + j]
            out[i, :, pl.ds(pl.multiple_of(slot * size, size), size)] = value[
                i * size:(i + 1) * size, j * size:(j + 1) * size
            ]


def fill_table(row_devices, col_devices, pattern, keep, order, table):
    row = lax.axis_index("row")
    col = lax.axis_index("col")

    def first(row_of, col_of):
        return (lax.rem(row_of, row_devices) * col_devices + lax.rem(col_of, col_devices)) * ROWS

    prev = first(row + row_devices - 1, col)
    own = first(row, col)
    nxt = first(row + 1, col)
    side = first(row, col + 1)
    labels = [order[start + j] for start in (prev, own, nxt, side) for j in range(ROWS)]
    own_labels = labels[OWN * ROWS:(OWN + 1) * ROWS]

    def look_up(stored, wanted, slot_at, kept_at):
        slots = [jnp.int32(0)] * len(wanted)
        kepts = [jnp.int32(0)] * len(wanted)
        for k in range(SLOTS):
            label = pattern[k, stored]
            flag = jnp.int32(1) if k == 0 else (keep[k, stored] == 1).astype(jnp.int32)
            for j, want in enumerate(wanted):
                same = label == want
                slots[j] = jnp.where(same, k, slots[j])
                kepts[j] = jnp.where(same, flag, kepts[j])
        for j in range(len(wanted)):
            if slot_at is not None:
                table[slot_at + j] = slots[j]
            table[kept_at + j] = kepts[j]

    for i in range(ROWS):
        look_up(own + i, labels, SLOT_AT + i * SLOTS, KEPT_AT + i * SLOTS)
        look_up(prev + i, own_labels, None, KEPT_PREV_AT + i * ROWS)
        look_up(nxt + i, own_labels, None, KEPT_NEXT_AT + i * ROWS)


def gather(table, source, i, j):
    size = source.shape[1]
    slot = table[SLOT_AT + i * SLOTS + j]
    return source[i, :, pl.ds(pl.multiple_of(slot * size, size), size)]


def pack(table, source, to_prev, to_next, side_own, side):
    size = source.shape[1]
    for i in range(ROWS):
        rows = slice(i * size, (i + 1) * size)
        for j in range(SLOTS):
            region, offset = divmod(j, ROWS)
            cols = slice(offset * size, (offset + 1) * size)
            block = gather(table, source, i, j)
            if region == PREV:
                to_prev[0, rows, cols] = block
            elif region == OWN:
                to_prev[1, rows, cols] = block
                to_next[0, rows, cols] = block
                side_own[rows, cols] = block
            elif region == NEXT:
                to_next[1, rows, cols] = block
            else:
                side[rows, cols] = block


def pack_kernel(
    row_devices, col_devices, pattern, keep, order, sqrt_ref, inv_ref,
    table, y_to_prev, y_to_next, y_side, z_to_prev, z_to_next, z_side, to_side,
):
    fill_table(row_devices, col_devices, pattern, keep, order, table)
    pack(table, sqrt_ref, y_to_prev, y_to_next, to_side.at[0], y_side)
    pack(table, inv_ref, z_to_prev, z_to_next, to_side.at[1], z_side)


def factor_own_kernel(table, y_to_prev, z_to_prev, z_to_next, y_prev, y_next, factor):
    total = products(
        (split(z_to_prev[0]), split(y_prev[1])),
        (split(z_to_prev[1]), split(y_to_prev[1])),
        (split(z_to_next[1]), split(y_next[0])),
    )
    rows = lax.broadcasted_iota(jnp.int32, total.shape, 0)
    cols = lax.broadcasted_iota(jnp.int32, total.shape, 1)
    identity = jnp.where(rows == cols, 1.5, 0.0)
    factor[...] = identity + filtered(table, total, OWN, -0.5)


def factor_rest_kernel(
    table, y_to_prev, y_to_next, y_side, z_to_prev, z_to_next, z_side,
    y_prev, y_next, from_side, factors, partial,
):
    y_own = split(y_to_prev[1])
    z_own = split(z_to_prev[1])
    parts = (
        (PREV, z_to_prev[0], y_prev[0], y_to_prev[0]),
        (NEXT, z_to_next[1], y_next[1], y_to_next[1]),
        (SIDE, z_side[...], from_side[0], y_side[...]),
    )
    for at, (region, z_here, y_there, y_here) in enumerate(parts):
        total = products((split(z_here), split(y_there)), (z_own, split(y_here)))
        factor = filtered(table, total, region, -0.5)
        factors[at] = factor
        partial[at] = products((y_own, split(factor)))


def inverse_kernel(
    table, y_to_prev, y_to_next, z_to_prev, z_to_next, z_side,
    y_prev, y_next, z_prev, z_next, from_side, factor_own, factors,
    inverse_next, sqrt_own,
):
    y_own = split(y_to_prev[1])
    zp_own, zp_next = split(z_prev[0]), split(z_prev[1])
    zn_prev, zn_own = split(z_next[0]), split(z_next[1])
    prev_total = products((zp_own, split(y_prev[1])), (zp_next, y_own))
    prev_next = split(filtered(table, prev_total, 0, -0.5, KEPT_PREV_AT, ROWS))
    next_total = products((zn_own, split(y_next[0])), (zn_prev, y_own))
    next_prev = split(filtered(table, next_total, 0, -0.5, KEPT_NEXT_AT, ROWS))
    f_own = split(factor_own[...])
    f_prev, f_next, f_side = (split(factors[at]) for at in range(3))
    value = products(
        (split(y_to_prev[0]), prev_next), (y_own, f_own), (split(y_to_next[1]), next_prev)
    )
    sqrt_own[...] = filtered(table, value, OWN)
    results = (
        (PREV, ((f_prev, zp_own), (f_own, split(z_to_prev[0])))),
        (OWN, ((f_prev, zp_next), (f_own, split(z_to_prev[1])), (f_next, zn_prev))),
        (NEXT, ((f_own, split(z_to_next[1])), (f_next, zn_own))),
        (SIDE, ((f_own, split(z_side[...])), (f_side, split(from_side[1])))),
    )
    for region, pairs in results:
        store_slots(table, inverse_next, filtered(table, products(*pairs), region), region)


def sqrt_kernel(
    table, y_to_prev, y_to_next, y_side, partial, sqrt_own, f_prev, f_next, f_side, sqrt_next
):
    parts = (
        (PREV, y_to_prev[0], f_prev),
        (NEXT, y_to_next[1], f_next),
        (SIDE, y_side[...], f_side),
    )
    store_slots(table, sqrt_next, sqrt_own[...], OWN)
    for at, (region, y_here, f_there) in enumerate(parts):
        value = partial[at] + products((split(y_here), split(f_there[...])))
        store_slots(table, sqrt_next, filtered(table, value, region), region)


def call(kernel, outs, operands, terms):
    def spec(array):
        small = array.dtype == jnp.int32
        return pl.BlockSpec(memory_space=pltpu.SMEM if small else pltpu.VMEM)

    moved = sum(array.size * 4 for array in (*outs, *operands))
    return pl.pallas_call(
        kernel,
        out_shape=outs,
        in_specs=[spec(array) for array in operands],
        out_specs=jax.tree.map(spec, outs),
        compiler_params=pltpu.CompilerParams(vmem_limit_bytes=VMEM_LIMIT),
        cost_estimate=pl.CostEstimate(
            flops=terms * 6 * 256**3, bytes_accessed=moved, transcendentals=0
        ),
    )(*operands)


def shifted(value, axis, distance):
    count = lax.axis_size(axis)
    return lax.ppermute(value, axis, [((i + distance) % count, i) for i in range(count)])


def local(sqrt_iterate, inverse_iterate, pattern, keep_mask, row_order):
    rows_dev, block, width = sqrt_iterate.shape
    row_devices, col_devices = lax.axis_size("row"), lax.axis_size("col")
    assert rows_dev == ROWS and width == SLOTS * block and pattern.shape[1] == SLOTS
    assert row_devices > 3 and col_devices > 2
    size = ROWS * block

    def shape(*dims):
        return jax.ShapeDtypeStruct(dims, jnp.float32)

    pair, one = shape(2, size, size), shape(size, size)
    table, y_to_prev, y_to_next, y_side, z_to_prev, z_to_next, z_side, to_side = call(
        functools.partial(pack_kernel, row_devices, col_devices),
        (jax.ShapeDtypeStruct((TABLE,), jnp.int32), pair, pair, one, pair, pair, one, pair),
        (pattern.T, keep_mask.T, row_order, sqrt_iterate, inverse_iterate),
        0,
    )
    y_next = shifted(y_to_prev, "row", 1)
    y_prev = shifted(y_to_next, "row", -1)
    from_side = shifted(to_side, "col", 1)
    z_next = shifted(z_to_prev, "row", 1)
    z_prev = shifted(z_to_next, "row", -1)
    (factor_own,) = call(
        factor_own_kernel,
        (one,),
        (table, y_to_prev, z_to_prev, z_to_next, y_prev, y_next),
        3,
    )
    f_side = shifted(factor_own, "col", 1)
    f_next = shifted(factor_own, "row", 1)
    f_prev = shifted(factor_own, "row", -1)
    factors, partial = call(
        factor_rest_kernel,
        (shape(3, size, size), shape(3, size, size)),
        (
            table, y_to_prev, y_to_next, y_side, z_to_prev, z_to_next, z_side,
            y_prev, y_next, from_side,
        ),
        9,
    )
    inverse_next, sqrt_own = call(
        inverse_kernel,
        (shape(rows_dev, block, width), one),
        (
            table, y_to_prev, y_to_next, z_to_prev, z_to_next, z_side,
            y_prev, y_next, z_prev, z_next, from_side, factor_own, factors,
        ),
        16,
    )
    (sqrt_next,) = call(
        sqrt_kernel,
        (shape(rows_dev, block, width),),
        (table, y_to_prev, y_to_next, y_side, partial, sqrt_own, f_prev, f_next, f_side),
        3,
    )
    return sqrt_next, inverse_next


def solution(mesh):
    rows = P(("row", "col"), None, None)
    return jax.shard_map(
        local,
        mesh=mesh,
        in_specs=(rows, rows, P(), P(), P()),
        out_specs=(rows, rows),
        check_vma=False,
    )
```

time: 206 us -> 42.1 us (0.20)
  the two profiles are of different devices: /device:TPU:0 before, /device:TPU:1 now
where the time goes in v1:
time: 42.1 us; the launch traced here: 41.8 us
  waiting for transfers between devices  13.6 us (32%)
  starting transfers between devices  11.9 us (28%)
  Pallas kernels  11.2 us (27%)
  local copies, waits for them, and re-layouts  4.47 us (11%)
  between operations  0.69 us (2%)
    ppermute x8, waiting for transfers between devices, shifted(): lax.ppermute(value, axis, [((i + distance) % count, i) for i in range(cou...  13.6 us
    ppermute x8, starting transfers between devices, shifted(): lax.ppermute(value, axis, [((i + distance) % count, i) for i in range(cou...  11.9 us
    pallas_call x5, Pallas kernels, call(): pl.pallas_call(kernel, out_shape=outs, in_specs=[spec(array) for array in...  11.2 us
    unnamed x10, local copies, waits for them, and re-layouts  4.47 us
  transfers between devices with their start and end apart: 8, of which 4 were waited for; matrix products, arithmetic and copies ran while one was open for 0% of the time, Pallas kernels for 18%

profile of v1, /device:TPU:1, one launch (start us, length us, event | category | flops | bytes accessed | tf_op | source)
XLA Modules:
  0.0 41.8 jit_solution(13390179339037599154)
XLA Ops:
  0.6 0.6 %copy-done.4 = s32[64]{0:T(128)S(1)} copy-done((s32[64]{0:T(128)S(1)}, s32[64]{0:T(128)}, u32[]{:S(2)}) %copy-start.4) | copy-done | bytes 280
  1.3 1.2 %copy-done = f32[2,128,1024]{2,1,0:T(8,128)S(1)} copy-done((f32[2,128,1024]{2,1,0:T(8,128)S(1)}, f32[2,128,1024]{2,1,0:T(8,128)}, u32[]{:S(2)}) %copy-start) | copy-done | bytes 1048600
  2.5 1.2 %copy-done.1 = f32[2,128,1024]{2,1,0:T(8,128)S(1)} copy-done((f32[2,128,1024]{2,1,0:T(8,128)S(1)}, f32[2,128,1024]{2,1,0:T(8,128)}, u32[]{:S(2)}) %copy-start.1) | copy-done | bytes 1048600
  3.7 0.7 %copy-done.2 = s32[64,8]{0,1:T(8,128)S(1)} copy-done((s32[64,8]{0,1:T(8,128)S(1)}, s32[64,8]{0,1:T(8,128)}, u32[]{:S(2)}) %copy-start.2) | copy-done | bytes 2072
  4.4 0.7 %copy-done.3 = s32[64,8]{0,1:T(8,128)S(1)} copy-done((s32[64,8]{0,1:T(8,128)S(1)}, s32[64,8]{0,1:T(8,128)}, u32[]{:S(2)}) %copy-start.3) | copy-done | bytes 2072
  5.1 1.6 %shard_map.68 = (s32[40]{0:T(128)S(1)}, f32[2,256,256]{2,1,0:T(8,128)S(1)}, f32[2,256,256]{2,1,0:T(8,128)S(1)}, f32[256,256]{1,0:T(8,128)S(1)}, f32[2,256,256]{2...) custom-call(s32[8,64]{1,0:T(8,128)S(1)} %bitcast.2, ...), custom_call_target="tpu_custom_call" | custom-call | bytes 5247392 | tf_op jit(solution)/shard_map/pallas_call | solution.py:207
  6.8 2.7 %collective-permute-start = (f32[2,256,256]{2,1,0:T(8,128)S(1)}, f32[2,256,256]{2,1,0:T(8,128)S(1)}, u32[]{:S(2)}, u32[]{:S(2)}) collective-permute-start(f32[2,256,256]{2,1,0:T(8,128)S(1)} %get-tuple-element.16.y_to_next), channel_id=1, source_target_pairs={{28,0},{0,4},{4,8},{8,12},{12,16},{16,20},{20,24},{24,28},{29,1},{... | collective-permute-start | bytes 1572872 | tf_op jit(solution)/shard_map/ppermute | solution.py:221
  9.4 0.0 collective-permute-start.1
  9.4 3.3 %collective-permute-start.2 = (f32[2,256,256]{2,1,0:T(8,128)S(1)}, f32[2,256,256]{2,1,0:T(8,128)S(1)}, u32[]{:S(2)}, u32[]{:S(2)}) collective-permute-start(f32[2,256,256]{2,1,0:T(8,128)S(1)} %get-tuple-element.21), channel_id=1, source_target_pairs={{1,0},{2,1},{3,2},{0,3},{5,4},{6,5},{7,6},{4,7},{9,8},{10,9},{11,1... | collective-permute-start | bytes 1572872 | tf_op jit(solution)/shard_map/ppermute | solution.py:221
  12.7 2.0 %collective-permute-start.3 = (f32[2,256,256]{2,1,0:T(8,128)S(1)}, f32[2,256,256]{2,1,0:T(8,128)S(1)}, u32[]{:S(2)}, u32[]{:S(2)}) collective-permute-start(f32[2,256,256]{2,1,0:T(8,128)S(1)} %get-tuple-element.19.z_to_next), channel_id=1, source_target_pairs={{28,0},{0,4},{4,8},{8,12},{12,16},{16,20},{20,24},{24,28},{29,1},{... | collective-permute-start | bytes 1572872 | tf_op jit(solution)/shard_map/ppermute | solution.py:221
  14.8 0.0 collective-permute-start.4
  14.8 5.4 %collective-permute-done.y_prev = f32[2,256,256]{2,1,0:T(8,128)S(1)} collective-permute-done((f32[2,256,256]{2,1,0:T(8,128)S(1)}, f32[2,256,256]{2,1,0:T(8,128)S(1)}, u32[]{:S(2)}, u32[]{:S(2)}) %collective-permute-start) | collective-permute-done | bytes 524320 | tf_op jit(solution)/shard_map/ppermute | solution.py:221
  20.1 3.8 %collective-permute-done.1.y_next = f32[2,256,256]{2,1,0:T(8,128)S(1)} collective-permute-done((f32[2,256,256]{2,1,0:T(8,128)S(1)}, f32[2,256,256]{2,1,0:T(8,128)S(1)}, u32[]{:S(2)}, u32[]{:S(2)}) %collective-permute-start.1) | collective-permute-done | bytes 524320 | tf_op jit(solution)/shard_map/ppermute | solution.py:221
  23.9 1.0 %shard_map.70.factor_own = f32[256,256]{1,0:T(8,128)S(1)} custom-call(s32[40]{0:T(128)S(1)} %get-tuple-element.14.table, f32[2,256,256]{2,1,0:T(8,128)S(1)} %get-tuple-element.15.y_to_prev, f32[2,256,256]{2,1,0:T(8,128)S(1)} %get-tuple-element.18.z_to_prev, f32[2,256,256]{2,1,0:T(8,128)S(1)} %get-tuple-element.19.z_to_next, ...), custom_call_target="tpu_custom_call" | custom-call | flops 301989888 | bytes 2883744 | tf_op jit(solution)/shard_map/pallas_call | solution.py:207
  24.9 0.1 collective-permute-start.5
  25.0 0.5 %collective-permute-start.6 = (f32[256,256]{1,0:T(8,128)S(1)}, f32[256,256]{1,0:T(8,128)S(1)}, u32[]{:S(2)}, u32[]{:S(2)}) collective-permute-start(f32[256,256]{1,0:T(8,128)S(1)} %shard_map.70.factor_own), channel_id=1, source_target_pairs={{4,0},{8,4},{12,8},{16,12},{20,16},{24,20},{28,24},{0,28},{5,1},{9... | collective-permute-start | bytes 786440 | tf_op jit(solution)/shard_map/ppermute | solution.py:221
  25.5 3.3 %collective-permute-start.7 = (f32[256,256]{1,0:T(8,128)S(1)}, f32[256,256]{1,0:T(8,128)S(1)}, u32[]{:S(2)}, u32[]{:S(2)}) collective-permute-start(f32[256,256]{1,0:T(8,128)S(1)} %shard_map.70.factor_own), channel_id=1, source_target_pairs={{1,0},{2,1},{3,2},{0,3},{5,4},{6,5},{7,6},{4,7},{9,8},{10,9},{11,1... | collective-permute-start | bytes 786440 | tf_op jit(solution)/shard_map/ppermute | solution.py:221
  28.8 2.8 %shard_map.69 = (f32[3,256,256]{2,1,0:T(8,128)S(1)}, f32[3,256,256]{2,1,0:T(8,128)S(1)}) custom-call(s32[40]{0:T(128)S(1)} %get-tuple-element.14.table, f32[2,256,256]{2,1,0:T(8,128)S(1)} %get-tuple-element.15.y_to_prev, f32[2,256,256]{2,1,0:T(8,128)S(1)} %get-tuple-element.16.y_to_next, f32[256,256]{1,0:T(8,128)S(1)} %get-tuple-element.17.y_side, ...), custom_call_target="tpu_custom_call" | custom-call | flops 905969664 | bytes 5767328 | tf_op jit(solution)/shard_map/pallas_call | solution.py:207
  31.7 0.0 collective-permute-done.3.z_prev
  31.7 3.5 %collective-permute-done.4.z_next = f32[2,256,256]{2,1,0:T(8,128)S(1)} collective-permute-done((f32[2,256,256]{2,1,0:T(8,128)S(1)}, f32[2,256,256]{2,1,0:T(8,128)S(1)}, u32[]{:S(2)}, u32[]{:S(2)}) %collective-permute-start.4) | collective-permute-done | bytes 524320 | tf_op jit(solution)/shard_map/ppermute | solution.py:221
  35.1 3.6 %shard_map.71 = (f32[2,128,1024]{2,1,0:T(8,128)}, f32[256,256]{1,0:T(8,128)S(1)}) custom-call(s32[40]{0:T(128)S(1)} %get-tuple-element.14.table, f32[2,256,256]{2,1,0:T(8,128)S(1)} %get-tuple-element.15.y_to_prev, f32[2,256,256]{2,1,0:T(8,128)S(1)} %get-tuple-element.16.y_to_next, f32[2,256,256]{2,1,0:T(8,128)S(1)} %get-tuple-element.18.z_to_prev, ...), custom_call_target="tpu_custom_call" | custom-call | flops 1610612736 | bytes 7340192 | tf_op jit(solution)/shard_map/pallas_call | solution.py:207
  38.7 0.0 collective-permute-done.5.f_prev
  38.7 1.0 %collective-permute-done.6.f_next = f32[256,256]{1,0:T(8,128)S(1)} collective-permute-done((f32[256,256]{1,0:T(8,128)S(1)}, f32[256,256]{1,0:T(8,128)S(1)}, u32[]{:S(2)}, u32[]{:S(2)}) %collective-permute-start.6) | collective-permute-done | bytes 262176 | tf_op jit(solution)/shard_map/ppermute | solution.py:221
  39.7 2.1 %shard_map.72 = f32[2,128,1024]{2,1,0:T(8,128)} custom-call(s32[40]{0:T(128)S(1)} %get-tuple-element.14.table, f32[2,256,256]{2,1,0:T(8,128)S(1)} %get-tuple-element.15.y_to_prev, f32[2,256,256]{2,1,0:T(8,128)S(1)} %get-tuple-element.16.y_to_next, f32[256,256]{1,0:T(8,128)S(1)} %get-tuple-element.17.y_side, f32[3,256,256]{2,1,0:T(8,128)S(1)} %get-tuple-element.22.partial, ...), custom_call_target="tpu_custom_call" | custom-call | flops 301989888 | bytes 4194464 | tf_op jit(solution)/shard_map/pallas_call | solution.py:207
  (7 shorter events, 0.0 us)
Async XLA Ops:
  0.6 0.7 %copy-start.4 = (s32[64]{0:T(128)S(1)}, s32[64]{0:T(128)}, u32[]{:S(2)}) copy-start(s32[64]{0:T(128)} %order.1) | copy-start | bytes 772
  1.3 1.2 %copy-start = (f32[2,128,1024]{2,1,0:T(8,128)S(1)}, f32[2,128,1024]{2,1,0:T(8,128)}, u32[]{:S(2)}) copy-start(f32[2,128,1024]{2,1,0:T(8,128)} %sqrt_ref.1) | copy-start | bytes 3145732
  2.5 1.2 %copy-start.1 = (f32[2,128,1024]{2,1,0:T(8,128)S(1)}, f32[2,128,1024]{2,1,0:T(8,128)}, u32[]{:S(2)}) copy-start(f32[2,128,1024]{2,1,0:T(8,128)} %inv_ref.1) | copy-start | bytes 3145732
  3.7 0.7 %copy-start.2 = (s32[64,8]{0,1:T(8,128)S(1)}, s32[64,8]{0,1:T(8,128)}, u32[]{:S(2)}) copy-start(s32[64,8]{0,1:T(8,128)} %param.7) | copy-start | bytes 6148
  4.4 0.7 %copy-start.3 = (s32[64,8]{0,1:T(8,128)S(1)}, s32[64,8]{0,1:T(8,128)}, u32[]{:S(2)}) copy-start(s32[64,8]{0,1:T(8,128)} %param.8) | copy-start | bytes 6148
  6.8 13.4 %collective-permute-start = (f32[2,256,256]{2,1,0:T(8,128)S(1)}, f32[2,256,256]{2,1,0:T(8,128)S(1)}, u32[]{:S(2)}, u32[]{:S(2)}) collective-permute-start(f32[2,256,256]{2,1,0:T(8,128)S(1)} %get-tuple-element.16.y_to_next), channel_id=1, source_target_pairs={{28,0},{0,4},{4,8},{8,12},{12,16},{16,20},{20,24},{24,28},{29,1},{... | collective-permute-start | bytes 1572872 | tf_op jit(solution)/shard_map/ppermute | solution.py:221
  9.4 14.5 %collective-permute-start.1 = (f32[2,256,256]{2,1,0:T(8,128)S(1)}, f32[2,256,256]{2,1,0:T(8,128)S(1)}, u32[]{:S(2)}, u32[]{:S(2)}) collective-permute-start(f32[2,256,256]{2,1,0:T(8,128)S(1)} %get-tuple-element.15.y_to_prev), channel_id=1, source_target_pairs={{4,0},{8,4},{12,8},{16,12},{20,16},{24,20},{28,24},{0,28},{5,1},{9... | collective-permute-start | bytes 1572872 | tf_op jit(solution)/shard_map/ppermute | solution.py:221
  9.4 16.1 %collective-permute-start.2 = (f32[2,256,256]{2,1,0:T(8,128)S(1)}, f32[2,256,256]{2,1,0:T(8,128)S(1)}, u32[]{:S(2)}, u32[]{:S(2)}) collective-permute-start(f32[2,256,256]{2,1,0:T(8,128)S(1)} %get-tuple-element.21), channel_id=1, source_target_pairs={{1,0},{2,1},{3,2},{0,3},{5,4},{6,5},{7,6},{4,7},{9,8},{10,9},{11,1... | collective-permute-start | bytes 1572872 | tf_op jit(solution)/shard_map/ppermute | solution.py:221
  12.7 18.9 %collective-permute-start.3 = (f32[2,256,256]{2,1,0:T(8,128)S(1)}, f32[2,256,256]{2,1,0:T(8,128)S(1)}, u32[]{:S(2)}, u32[]{:S(2)}) collective-permute-start(f32[2,256,256]{2,1,0:T(8,128)S(1)} %get-tuple-element.19.z_to_next), channel_id=1, source_target_pairs={{28,0},{0,4},{4,8},{8,12},{12,16},{16,20},{20,24},{24,28},{29,1},{... | collective-permute-start | bytes 1572872 | tf_op jit(solution)/shard_map/ppermute | solution.py:221
  14.8 20.4 %collective-permute-start.4 = (f32[2,256,256]{2,1,0:T(8,128)S(1)}, f32[2,256,256]{2,1,0:T(8,128)S(1)}, u32[]{:S(2)}, u32[]{:S(2)}) collective-permute-start(f32[2,256,256]{2,1,0:T(8,128)S(1)} %get-tuple-element.18.z_to_prev), channel_id=1, source_target_pairs={{4,0},{8,4},{12,8},{16,12},{20,16},{24,20},{28,24},{0,28},{5,1},{9... | collective-permute-start | bytes 1572872 | tf_op jit(solution)/shard_map/ppermute | solution.py:221
  24.9 13.8 %collective-permute-start.5 = (f32[256,256]{1,0:T(8,128)S(1)}, f32[256,256]{1,0:T(8,128)S(1)}, u32[]{:S(2)}, u32[]{:S(2)}) collective-permute-start(f32[256,256]{1,0:T(8,128)S(1)} %shard_map.70.factor_own), channel_id=1, source_target_pairs={{28,0},{0,4},{4,8},{8,12},{12,16},{16,20},{20,24},{24,28},{29,1},{... | collective-permute-start | bytes 786440 | tf_op jit(solution)/shard_map/ppermute | solution.py:221
  25.0 14.7 %collective-permute-start.6 = (f32[256,256]{1,0:T(8,128)S(1)}, f32[256,256]{1,0:T(8,128)S(1)}, u32[]{:S(2)}, u32[]{:S(2)}) collective-permute-start(f32[256,256]{1,0:T(8,128)S(1)} %shard_map.70.factor_own), channel_id=1, source_target_pairs={{4,0},{8,4},{12,8},{16,12},{20,16},{24,20},{28,24},{0,28},{5,1},{9... | collective-permute-start | bytes 786440 | tf_op jit(solution)/shard_map/ppermute | solution.py:221
  25.5 14.2 %collective-permute-start.7 = (f32[256,256]{1,0:T(8,128)S(1)}, f32[256,256]{1,0:T(8,128)S(1)}, u32[]{:S(2)}, u32[]{:S(2)}) collective-permute-start(f32[256,256]{1,0:T(8,128)S(1)} %shard_map.70.factor_own), channel_id=1, source_target_pairs={{1,0},{2,1},{3,2},{0,3},{5,4},{6,5},{7,6},{4,7},{9,8},{10,9},{11,1... | collective-permute-start | bytes 786440 | tf_op jit(solution)/shard_map/ppermute | solution.py:221

commit v2 on v1

v2 whole, which is shorter than its diff:
```python
import functools

import jax
import jax.numpy as jnp
from jax import lax
from jax.experimental import pallas as pl
from jax.experimental.pallas import tpu as pltpu
from jax.sharding import PartitionSpec as P

PEER, OWN, MATE, SIDE = range(4)
ROWS = 2
SLOTS = 8
SLOT_AT, KEPT_AT, KEPT_PEER_AT, KEPT_MATE_AT, TABLE = 0, 16, 32, 36, 40
LARGEST = float(jnp.finfo(jnp.bfloat16).max)
VMEM_LIMIT = 24 * 2**20


def split(value):
    clipped = jnp.clip(value, -LARGEST, LARGEST)
    high = clipped.astype(jnp.bfloat16)
    low = (value - high.astype(jnp.float32)).astype(jnp.bfloat16)
    return high, low


def products(*pairs):
    left = [part for (high, low), _ in pairs for part in (high, low, high)]
    right = [part for _, (high, low) in pairs for part in (high, high, low)]
    return jnp.dot(
        jnp.concatenate(left, axis=1),
        jnp.concatenate(right, axis=0),
        preferred_element_type=jnp.float32,
    )


def filtered(table, value, region, scale=None, base=KEPT_AT, width=SLOTS):
    size = value.shape[0] // ROWS
    rows = []
    for i in range(ROWS):
        row = []
        for j in range(ROWS):
            kept = table[base + i * width + region * ROWS + j].astype(jnp.float32)
            if scale is not None:
                kept = kept * scale
            row.append(value[i * size:(i + 1) * size, j * size:(j + 1) * size] * kept)
        rows.append(jnp.concatenate(row, axis=1))
    return jnp.concatenate(rows, axis=0)


def fill_table(row_devices, col_devices, pattern, keep, order, table):
    row = lax.axis_index("row")
    col = lax.axis_index("col")
    odd = lax.rem(row, 2)

    def first(row_of, col_of):
        return (lax.rem(row_of, row_devices) * col_devices + lax.rem(col_of, col_devices)) * ROWS

    peer = first(row + row_devices - 1 + 2 * odd, col)
    own = first(row, col)
    mate = first(row + 1 - 2 * odd, col)
    side = first(row, col + 1)
    labels = [order[start + j] for start in (peer, own, mate, side) for j in range(ROWS)]
    own_labels = labels[OWN * ROWS:(OWN + 1) * ROWS]

    def look_up(stored, wanted, slot_at, kept_at):
        slots = [jnp.int32(0)] * len(wanted)
        kepts = [jnp.int32(0)] * len(wanted)
        for k in range(SLOTS):
            label = pattern[k, stored]
            flag = jnp.int32(1) if k == 0 else (keep[k, stored] == 1).astype(jnp.int32)
            for j, want in enumerate(wanted):
                same = label == want
                slots[j] = jnp.where(same, k, slots[j])
                kepts[j] = jnp.where(same, flag, kepts[j])
        for j in range(len(wanted)):
            if slot_at is not None:
                table[slot_at + j] = slots[j]
            table[kept_at + j] = kepts[j]

    for i in range(ROWS):
        look_up(own + i, labels, SLOT_AT + i * SLOTS, KEPT_AT + i * SLOTS)
        look_up(peer + i, own_labels, None, KEPT_PEER_AT + i * ROWS)
        look_up(mate + i, own_labels, None, KEPT_MATE_AT + i * ROWS)


def gather(table, source, places):
    size = source.shape[1]
    for i in range(ROWS):
        rows = slice(i * size, (i + 1) * size)
        for j in range(SLOTS):
            region, offset = divmod(j, ROWS)
            cols = slice(offset * size, (offset + 1) * size)
            slot = table[SLOT_AT + i * SLOTS + j]
            block = source[i, :, pl.ds(pl.multiple_of(slot * size, size), size)]
            for place in places[region]:
                place[rows, cols] = block


def pack_sqrt_kernel(
    row_devices, col_devices, pattern, keep, order, sqrt_iterate,
    table, y_peer, y_mate, y_side,
    pattern_here, keep_here, order_here, sqrt_here, sems,
):
    copies = [
        pltpu.make_async_copy(source, here, sems.at[at])
        for at, (source, here) in enumerate((
            (order, order_here), (pattern, pattern_here), (keep, keep_here),
            (sqrt_iterate, sqrt_here),
        ))
    ]
    for copy in copies:
        copy.start()
    for copy in copies[:3]:
        copy.wait()
    fill_table(row_devices, col_devices, pattern_here, keep_here, order_here, table)
    copies[3].wait()
    places = ((y_peer.at[0],), (y_peer.at[1], y_mate.at[1]), (y_mate.at[0],), (y_side,))
    gather(table, sqrt_here, places)


def pack_inverse_kernel(table, y_peer, inverse_iterate, z_peer, z_mate, z_side, to_side):
    to_side[0] = y_peer[1]
    places = ((z_peer,), (z_mate.at[1], to_side.at[1]), (z_mate.at[0],), (z_side,))
    gather(table, inverse_iterate, places)


def mate_kernel(
    table, y_peer, y_mate, z_peer, z_mate, mate_y,
    z_to_peer, factor_mate, own_partial, peer_partial,
):
    z_to_peer[0] = z_peer[...]
    z_to_peer[1] = z_mate[1]
    z_own, z_to_mate = split(z_mate[1]), split(z_mate[0])
    own_partial[...] = products((z_own, split(y_mate[1])), (z_to_mate, split(mate_y[0])))
    total = products((z_own, split(y_mate[0])), (z_to_mate, split(mate_y[1])))
    factor_mate[...] = filtered(table, total, MATE, -0.5)
    peer_partial[...] = products((z_own, split(y_peer[0])))


def factor_own_kernel(table, own_partial, z_peer, peer_y, factor_own):
    total = own_partial[...] + products((split(z_peer[...]), split(peer_y[0])))
    rows = lax.broadcasted_iota(jnp.int32, total.shape, 0)
    cols = lax.broadcasted_iota(jnp.int32, total.shape, 1)
    factor_own[...] = jnp.where(rows == cols, 1.5, 0.0) + filtered(table, total, OWN, -0.5)


Y_MATE, Z_MATE, Z_SIDE = range(3)
Y_OWN_PART, Y_PEER_PART, Y_SIDE_PART, Z_OWN_PART, Z_PEER_PART = range(5)
Y_PEER, Y_OWN, Y_SIDE, F_PEER, PEER_Y = range(5)


def middle_kernel(
    table, y_peer, y_mate, y_side, z_peer, z_mate, z_side, mate_y, mate_z, peer_y, from_side,
    factor_mate, peer_partial, factor_own, mate_factor,
    finished, partial, ready,
):
    def keep(at, parts):
        ready[at, 0], ready[at, 1] = parts

    y_own, z_own = split(y_peer[1]), split(z_mate[1])
    y_to_mate, z_to_mate = split(y_mate[0]), split(z_mate[0])
    y_to_side, z_to_side = split(y_side[...]), split(z_side[...])
    z_to_peer = split(z_peer[...])
    f_own, f_mate = split(factor_own[...]), split(factor_mate[...])
    mate_z_mate, mate_z_own = split(mate_z[0]), split(mate_z[1])
    keep(Y_OWN, y_own)
    keep(Y_SIDE, y_to_side)
    keep(Y_PEER, split(y_peer[0]))
    keep(PEER_Y, split(peer_y[0]))

    total = peer_partial[...] + products((z_to_peer, split(peer_y[1])))
    f_peer = split(filtered(table, total, PEER, -0.5))
    keep(F_PEER, f_peer)
    total = products((z_own, y_to_side), (z_to_side, split(from_side[0])))
    f_side = split(filtered(table, total, SIDE, -0.5))
    total = products((mate_z_own, split(mate_y[0])), (mate_z_mate, y_own))
    mate_f_mate = split(filtered(table, total, 0, -0.5, KEPT_MATE_AT, ROWS))

    partial[Y_PEER_PART] = products((y_own, f_peer))
    partial[Y_SIDE_PART] = products((y_own, f_side))
    partial[Y_OWN_PART] = products((y_to_mate, mate_f_mate), (y_own, f_own))
    partial[Z_PEER_PART] = products((f_own, z_to_peer))
    partial[Z_OWN_PART] = products((f_mate, mate_z_mate), (f_own, z_own))
    value = products((y_own, f_mate), (y_to_mate, split(mate_factor[...])))
    finished[Y_MATE] = filtered(table, value, MATE)
    value = products((f_mate, mate_z_own), (f_own, z_to_mate))
    finished[Z_MATE] = filtered(table, value, MATE)
    value = products((f_own, z_to_side), (f_side, split(from_side[1])))
    finished[Z_SIDE] = filtered(table, value, SIDE)


def last_kernel(
    table, finished, partial, ready, peer_z, peer_factor, side_factor,
    sqrt_next, inverse_next, result, sems,
):
    size = sqrt_next.shape[1]
    started = []

    def write(source, out, region):
        for i in range(ROWS):
            for j in range(ROWS):
                slot = table[SLOT_AT + i * SLOTS + region * ROWS + j]
                copy = pltpu.make_async_copy(
                    source.at[pl.ds(i * size, size), pl.ds(j * size, size)],
                    out.at[i, :, pl.ds(pl.multiple_of(slot * size, size), size)],
                    sems.at[len(started)],
                )
                copy.start()
                started.append(copy)

    def finish(at, value, out, region):
        result[at] = filtered(table, value, region)
        write(result.at[at], out, region)

    def held(at):
        return ready[at, 0], ready[at, 1]

    write(finished.at[Y_MATE], sqrt_next, MATE)
    write(finished.at[Z_MATE], inverse_next, MATE)
    write(finished.at[Z_SIDE], inverse_next, SIDE)
    peer_z_peer, peer_z_own = split(peer_z[0]), split(peer_z[1])
    f_peer, y_peer = held(F_PEER), held(Y_PEER)
    value = partial[Z_PEER_PART] + products((f_peer, peer_z_own))
    finish(0, value, inverse_next, PEER)
    value = partial[Z_OWN_PART] + products((f_peer, peer_z_peer))
    finish(1, value, inverse_next, OWN)
    total = products((peer_z_own, held(PEER_Y)), (peer_z_peer, held(Y_OWN)))
    peer_f_peer = split(filtered(table, total, 0, -0.5, KEPT_PEER_AT, ROWS))
    value = partial[Y_SIDE_PART] + products((held(Y_SIDE), split(side_factor[...])))
    finish(2, value, sqrt_next, SIDE)
    value = partial[Y_PEER_PART] + products((y_peer, split(peer_factor[...])))
    finish(3, value, sqrt_next, PEER)
    value = partial[Y_OWN_PART] + products((y_peer, peer_f_peer))
    finish(4, value, sqrt_next, OWN)
    for copy in started:
        copy.wait()


def call(kernel, outs, operands, terms, scratch=(), hbm_in=(), hbm_out=False):
    def spec(array, outside=False):
        if outside:
            return pl.BlockSpec(memory_space=pltpu.HBM)
        small = array.dtype == jnp.int32
        return pl.BlockSpec(memory_space=pltpu.SMEM if small else pltpu.VMEM)

    moved = sum(array.size * array.dtype.itemsize for array in (*outs, *operands))
    operands = [
        pltpu.with_memory_space_constraint(array, pltpu.HBM) if at in hbm_in else array
        for at, array in enumerate(operands)
    ]
    return pl.pallas_call(
        kernel,
        out_shape=outs,
        in_specs=[spec(array, at in hbm_in) for at, array in enumerate(operands)],
        out_specs=tuple(spec(array, hbm_out) for array in outs),
        scratch_shapes=scratch,
        compiler_params=pltpu.CompilerParams(vmem_limit_bytes=VMEM_LIMIT),
        cost_estimate=pl.CostEstimate(
            flops=terms * 6 * 256**3, bytes_accessed=moved, transcendentals=0
        ),
    )(*operands)


def local(sqrt_iterate, inverse_iterate, pattern, keep_mask, row_order):
    rows_dev, block, width = sqrt_iterate.shape
    row_devices, col_devices = lax.axis_size("row"), lax.axis_size("col")
    assert rows_dev == ROWS and width == SLOTS * block and pattern.shape[1] == SLOTS
    assert row_devices > 3 and row_devices % 2 == 0 and col_devices > 2
    size = ROWS * block

    def to_mate(value):
        return lax.ppermute(value, "row", [(i, i ^ 1) for i in range(row_devices)])

    def to_peer(value):
        route = [(i, (i + (1 if i % 2 else -1)) % row_devices) for i in range(row_devices)]
        return lax.ppermute(value, "row", route)

    def to_side(value):
        route = [((i + 1) % col_devices, i) for i in range(col_devices)]
        return lax.ppermute(value, "col", route)

    def shape(*dims, dtype=jnp.float32):
        return jax.ShapeDtypeStruct(dims, dtype)

    one, pair = shape(size, size), shape(2, size, size)
    table, y_peer, y_mate, y_side = call(
        functools.partial(pack_sqrt_kernel, row_devices, col_devices),
        (shape(TABLE, dtype=jnp.int32), pair, pair, one),
        (pattern.T, keep_mask.T, row_order, sqrt_iterate),
        0,
        scratch=[
            pltpu.SMEM(pattern.T.shape, jnp.int32),
            pltpu.SMEM(keep_mask.T.shape, jnp.int32),
            pltpu.SMEM(row_order.shape, jnp.int32),
            pltpu.VMEM(sqrt_iterate.shape, jnp.float32),
            pltpu.SemaphoreType.DMA((4,)),
        ],
        hbm_in=range(4),
    )
    mate_y = to_mate(y_mate)
    peer_y = to_peer(y_peer)
    z_peer, z_mate, z_side, own_pair = call(
        pack_inverse_kernel, (one, pair, one, pair), (table, y_peer, inverse_iterate), 0
    )
    from_side = to_side(own_pair)
    mate_z = to_mate(z_mate)
    z_to_peer, factor_mate, own_partial, peer_partial = call(
        mate_kernel, (pair, one, one, one), (table, y_peer, y_mate, z_peer, z_mate, mate_y), 5
    )
    peer_z = to_peer(z_to_peer)
    (factor_own,) = call(factor_own_kernel, (one,), (table, own_partial, z_peer, peer_y), 1)
    mate_factor = to_mate(factor_own)
    peer_factor = to_peer(factor_own)
    side_factor = to_side(factor_own)
    finished, partial, ready = call(
        middle_kernel,
        (
            shape(3, size, size), shape(5, size, size),
            shape(5, 2, size, size, dtype=jnp.bfloat16),
        ),
        (
            table, y_peer, y_mate, y_side, z_peer, z_mate, z_side, mate_y, mate_z, peer_y,
            from_side, factor_mate, peer_partial, factor_own, mate_factor,
        ),
        19,
    )
    sqrt_next, inverse_next = call(
        last_kernel,
        (shape(rows_dev, block, width), shape(rows_dev, block, width)),
        (table, finished, partial, ready, peer_z, peer_factor, side_factor),
        7,
        scratch=[pltpu.VMEM((5, size, size), jnp.float32), pltpu.SemaphoreType.DMA((32,))],
        hbm_out=True,
    )
    return sqrt_next, inverse_next


def solution(mesh):
    rows = P(("row", "col"), None, None)
    return jax.shard_map(
        local,
        mesh=mesh,
        in_specs=(rows, rows, P(), P(), P()),
        out_specs=(rows, rows),
        check_vma=False,
    )
```

time: 42.1 us -> 37.9 us (0.900)
  the two profiles are of different devices: /device:TPU:1 before, /device:TPU:0 now
where the time goes in v2:
time: 37.9 us; the launch traced here: 37.8 us
  starting transfers between devices  15 us (40%)
  waiting for transfers between devices  11.8 us (31%)
  Pallas kernels  10.3 us (27%)
  between operations  0.7 us (2%)
    ppermute x3, waiting for transfers between devices, to_peer(): return lax.ppermute(value, 'row', route)  11.8 us
    pallas_call x6, Pallas kernels, call(): pl.pallas_call(kernel, out_shape=outs, in_specs=[spec(array, at in hbm_in...  10.3 us
    ppermute x2, starting transfers between devices, to_side(): return lax.ppermute(value, 'col', route)  7.55 us
    ppermute x3, starting transfers between devices, to_peer(): return lax.ppermute(value, 'row', route)  6.79 us
  transfers between devices with their start and end apart: 8, of which 2 were waited for; matrix products, arithmetic and copies ran while one was open for 0% of the time, Pallas kernels for 15%

profile of v2, /device:TPU:0, one launch (start us, length us, event | category | flops | bytes accessed | tf_op | source)
XLA Modules:
  0.0 37.8 jit_solution(9541925615202101714)
XLA Ops:
  0.6 0.0 copy-start
  0.6 2.0 %shard_map.68 = (s32[40]{0:T(128)S(1)}, f32[2,256,256]{2,1,0:T(8,128)S(1)}, f32[2,256,256]{2,1,0:T(8,128)S(1)}, f32[256,256]{1,0:T(8,128)S(1)}) custom-call(s32[8,64]{1,0:T(8,128)} %bitcast.2, s32[8,64]{1,0:T(8,128)} %bitcast.3, s32[64]{0:T(128)} %order.1, f32[2,128,1024]{2,1,0:T(8,128)} %sqrt_iterate.1), custom_call_target="tpu_custom_call" | custom-call | bytes 2363808 | tf_op jit(solution)/shard_map/pallas_call | solution.py:250
  2.6 0.5 %collective-permute-start = (f32[2,256,256]{2,1,0:T(8,128)S(1)}, f32[2,256,256]{2,1,0:T(8,128)S(1)}, u32[]{:S(2)}, u32[]{:S(2)}) collective-permute-start(f32[2,256,256]{2,1,0:T(8,128)S(1)} %get-tuple-element.19.y_mate), channel_id=1, source_target_pairs={{0,4},{4,0},{8,12},{12,8},{16,20},{20,16},{24,28},{28,24},{1,5},{5... | collective-permute-start | bytes 1572872 | tf_op jit(solution)/shard_map/ppermute | solution.py:271
  3.1 3.6 %collective-permute-start.2 = (f32[2,256,256]{2,1,0:T(8,128)S(1)}, f32[2,256,256]{2,1,0:T(8,128)S(1)}, u32[]{:S(2)}, u32[]{:S(2)}) collective-permute-start(f32[2,256,256]{2,1,0:T(8,128)S(1)} %get-tuple-element.18.y_peer), channel_id=1, source_target_pairs={{0,28},{4,8},{8,4},{12,16},{16,12},{20,24},{24,20},{28,0},{1,29},{... | collective-permute-start | bytes 1572872 | tf_op jit(solution)/shard_map/ppermute | solution.py:275
  6.7 0.0 copy-done
  6.7 0.7 %shard_map.69 = (f32[256,256]{1,0:T(8,128)S(1)}, f32[2,256,256]{2,1,0:T(8,128)S(1)}, f32[256,256]{1,0:T(8,128)S(1)}, f32[2,256,256]{2,1,0:T(8,128)S(1)}) custom-call(s32[40]{0:T(128)S(1)} %get-tuple-element.17.table, f32[2,256,256]{2,1,0:T(8,128)S(1)} %get-tuple-element.18.y_peer, f32[2,128,1024]{2,1,0:T(8,128)S(1)} %copy-done), custom_call_target="tpu_custom_call" | custom-call | bytes 3145888 | tf_op jit(solution)/shard_map/pallas_call | solution.py:250
  7.4 0.1 collective-permute-start.1
  7.5 3.7 %collective-permute-start.3 = (f32[2,256,256]{2,1,0:T(8,128)S(1)}, f32[2,256,256]{2,1,0:T(8,128)S(1)}, u32[]{:S(2)}, u32[]{:S(2)}) collective-permute-start(f32[2,256,256]{2,1,0:T(8,128)S(1)} %get-tuple-element.24), channel_id=1, source_target_pairs={{1,0},{2,1},{3,2},{0,3},{5,4},{6,5},{7,6},{4,7},{9,8},{10,9},{11,1... | collective-permute-start | bytes 1572872 | tf_op jit(solution)/shard_map/ppermute | solution.py:279
  11.1 0.0 collective-permute-done.mate_y
  11.1 1.3 %shard_map.70 = (f32[2,256,256]{2,1,0:T(8,128)S(1)}, f32[256,256]{1,0:T(8,128)S(1)}, f32[256,256]{1,0:T(8,128)S(1)}, f32[256,256]{1,0:T(8,128)S(1)}) custom-call(s32[40]{0:T(128)S(1)} %get-tuple-element.17.table, f32[2,256,256]{2,1,0:T(8,128)S(1)} %get-tuple-element.18.y_peer, f32[2,256,256]{2,1,0:T(8,128)S(1)} %get-tuple-element.19.y_mate, ...), custom_call_target="tpu_custom_call" | custom-call | flops 503316480 | bytes 3670176 | tf_op jit(solution)/shard_map/pallas_call | solution.py:250
  12.4 0.4 collective-permute-start.5
  12.8 6.2 %collective-permute-done.2.peer_y = f32[2,256,256]{2,1,0:T(8,128)S(1)} collective-permute-done((f32[2,256,256]{2,1,0:T(8,128)S(1)}, f32[2,256,256]{2,1,0:T(8,128)S(1)}, u32[]{:S(2)}, u32[]{:S(2)}) %collective-permute-start.2) | collective-permute-done | bytes 524320 | tf_op jit(solution)/shard_map/ppermute | solution.py:275
  19.1 0.8 %shard_map.71.factor_own = f32[256,256]{1,0:T(8,128)S(1)} custom-call(s32[40]{0:T(128)S(1)} %get-tuple-element.17.table, f32[256,256]{1,0:T(8,128)S(1)} %get-tuple-element.27.own_partial, f32[256,256]{1,0:T(8,128)S(1)} %get-tuple-element.21.z_peer, f32[2,256,256]{2,1,0:T(8,128)S(1)} %collective-permute-done.2.peer_y), custom_call_target="tpu_custom_call" | custom-call | flops 100663296 | bytes 1310880 | tf_op jit(solution)/shard_map/pallas_call | solution.py:250
  19.9 0.1 collective-permute-start.4
  20.0 2.9 %collective-permute-start.6 = (f32[256,256]{1,0:T(8,128)S(1)}, f32[256,256]{1,0:T(8,128)S(1)}, u32[]{:S(2)}, u32[]{:S(2)}) collective-permute-start(f32[256,256]{1,0:T(8,128)S(1)} %shard_map.71.factor_own), channel_id=1, source_target_pairs={{0,28},{4,8},{8,4},{12,16},{16,12},{20,24},{24,20},{28,0},{1,29},{... | collective-permute-start | bytes 786440 | tf_op jit(solution)/shard_map/ppermute | solution.py:275
  22.8 0.0 collective-permute-done.1.mate_z
  22.8 3.9 %collective-permute-start.7 = (f32[256,256]{1,0:T(8,128)S(1)}, f32[256,256]{1,0:T(8,128)S(1)}, u32[]{:S(2)}, u32[]{:S(2)}) collective-permute-start(f32[256,256]{1,0:T(8,128)S(1)} %shard_map.71.factor_own), channel_id=1, source_target_pairs={{1,0},{2,1},{3,2},{0,3},{5,4},{6,5},{7,6},{4,7},{9,8},{10,9},{11,1... | collective-permute-start | bytes 786440 | tf_op jit(solution)/shard_map/ppermute | solution.py:279
  26.7 0.0 collective-permute-done.3.from_side
  26.7 0.0 collective-permute-done.4.mate_factor
  26.7 2.9 %shard_map.72 = (f32[3,256,256]{2,1,0:T(8,128)S(1)}, f32[5,256,256]{2,1,0:T(8,128)S(1)}, bf16[5,2,256,256]{3,2,1,0:T(8,128)(2,1)S(1)}) custom-call(s32[40]{0:T(128)S(1)} %get-tuple-element.17.table, f32[2,256,256]{2,1,0:T(8,128)S(1)} %get-tuple-element.18.y_peer, f32[2,256,256]{2,1,0:T(8,128)S(1)} %get-tuple-element.19.y_mate, ...), custom_call_target="tpu_custom_call" | custom-call | flops 1912602624 | bytes 8913056 | tf_op jit(solution)/shard_map/pallas_call | solution.py:250
  29.7 5.5 %collective-permute-done.6.peer_factor = f32[256,256]{1,0:T(8,128)S(1)} collective-permute-done((f32[256,256]{1,0:T(8,128)S(1)}, f32[256,256]{1,0:T(8,128)S(1)}, u32[]{:S(2)}, u32[]{:S(2)}) %collective-permute-start.6) | collective-permute-done | bytes 262176 | tf_op jit(solution)/shard_map/ppermute | solution.py:275
  35.2 0.0 collective-permute-done.7.side_factor
  35.2 0.0 collective-permute-done.5.peer_z
  35.2 2.6 %shard_map.73 = (f32[2,128,1024]{2,1,0:T(8,128)}, f32[2,128,1024]{2,1,0:T(8,128)}) custom-call(s32[40]{0:T(128)S(1)} %get-tuple-element.17.table, f32[3,256,256]{2,1,0:T(8,128)S(1)} %get-tuple-element.28.finished, f32[5,256,256]{2,1,0:T(8,128)S(1)} %get-tuple-element.29.partial, bf16[5,2,256,256]{3,2,1,0:T(8,128)(2,1)S(1)} %get-tuple-element.30.ready, ...), custom_call_target="tpu_custom_call" | custom-call | flops 704643072 | bytes 6553760 | tf_op jit(solution)/shard_map/pallas_call | solution.py:250
Async XLA Ops:
  0.6 6.0 %copy-start = (f32[2,128,1024]{2,1,0:T(8,128)S(1)}, f32[2,128,1024]{2,1,0:T(8,128)}, u32[]{:S(2)}) copy-start(f32[2,128,1024]{2,1,0:T(8,128)} %inverse_iterate.1) | copy-start | bytes 3145732
  2.6 8.5 %collective-permute-start = (f32[2,256,256]{2,1,0:T(8,128)S(1)}, f32[2,256,256]{2,1,0:T(8,128)S(1)}, u32[]{:S(2)}, u32[]{:S(2)}) collective-permute-start(f32[2,256,256]{2,1,0:T(8,128)S(1)} %get-tuple-element.19.y_mate), channel_id=1, source_target_pairs={{0,4},{4,0},{8,12},{12,8},{16,20},{20,16},{24,28},{28,24},{1,5},{5... | collective-permute-start | bytes 1572872 | tf_op jit(solution)/shard_map/ppermute | solution.py:271
  3.1 15.9 %collective-permute-start.2 = (f32[2,256,256]{2,1,0:T(8,128)S(1)}, f32[2,256,256]{2,1,0:T(8,128)S(1)}, u32[]{:S(2)}, u32[]{:S(2)}) collective-permute-start(f32[2,256,256]{2,1,0:T(8,128)S(1)} %get-tuple-element.18.y_peer), channel_id=1, source_target_pairs={{0,28},{4,8},{8,4},{12,16},{16,12},{20,24},{24,20},{28,0},{1,29},{... | collective-permute-start | bytes 1572872 | tf_op jit(solution)/shard_map/ppermute | solution.py:275
  7.4 15.5 %collective-permute-start.1 = (f32[2,256,256]{2,1,0:T(8,128)S(1)}, f32[2,256,256]{2,1,0:T(8,128)S(1)}, u32[]{:S(2)}, u32[]{:S(2)}) collective-permute-start(f32[2,256,256]{2,1,0:T(8,128)S(1)} %get-tuple-element.22.z_mate), channel_id=1, source_target_pairs={{0,4},{4,0},{8,12},{12,8},{16,20},{20,16},{24,28},{28,24},{1,5},{5... | collective-permute-start | bytes 1572872 | tf_op jit(solution)/shard_map/ppermute | solution.py:271
  7.5 19.3 %collective-permute-start.3 = (f32[2,256,256]{2,1,0:T(8,128)S(1)}, f32[2,256,256]{2,1,0:T(8,128)S(1)}, u32[]{:S(2)}, u32[]{:S(2)}) collective-permute-start(f32[2,256,256]{2,1,0:T(8,128)S(1)} %get-tuple-element.24), channel_id=1, source_target_pairs={{1,0},{2,1},{3,2},{0,3},{5,4},{6,5},{7,6},{4,7},{9,8},{10,9},{11,1... | collective-permute-start | bytes 1572872 | tf_op jit(solution)/shard_map/ppermute | solution.py:279
  12.4 22.8 %collective-permute-start.5 = (f32[2,256,256]{2,1,0:T(8,128)S(1)}, f32[2,256,256]{2,1,0:T(8,128)S(1)}, u32[]{:S(2)}, u32[]{:S(2)}) collective-permute-start(f32[2,256,256]{2,1,0:T(8,128)S(1)} %get-tuple-element.31), channel_id=1, source_target_pairs={{0,28},{4,8},{8,4},{12,16},{16,12},{20,24},{24,20},{28,0},{1,29},{... | collective-permute-start | bytes 1572872 | tf_op jit(solution)/shard_map/ppermute | solution.py:275
  19.9 6.9 %collective-permute-start.4 = (f32[256,256]{1,0:T(8,128)S(1)}, f32[256,256]{1,0:T(8,128)S(1)}, u32[]{:S(2)}, u32[]{:S(2)}) collective-permute-start(f32[256,256]{1,0:T(8,128)S(1)} %shard_map.71.factor_own), channel_id=1, source_target_pairs={{0,4},{4,0},{8,12},{12,8},{16,20},{20,16},{24,28},{28,24},{1,5},{5... | collective-permute-start | bytes 786440 | tf_op jit(solution)/shard_map/ppermute | solution.py:271
  20.0 15.2 %collective-permute-start.6 = (f32[256,256]{1,0:T(8,128)S(1)}, f32[256,256]{1,0:T(8,128)S(1)}, u32[]{:S(2)}, u32[]{:S(2)}) collective-permute-start(f32[256,256]{1,0:T(8,128)S(1)} %shard_map.71.factor_own), channel_id=1, source_target_pairs={{0,28},{4,8},{8,4},{12,16},{16,12},{20,24},{24,20},{28,0},{1,29},{... | collective-permute-start | bytes 786440 | tf_op jit(solution)/shard_map/ppermute | solution.py:275
  22.8 12.4 %collective-permute-start.7 = (f32[256,256]{1,0:T(8,128)S(1)}, f32[256,256]{1,0:T(8,128)S(1)}, u32[]{:S(2)}, u32[]{:S(2)}) collective-permute-start(f32[256,256]{1,0:T(8,128)S(1)} %shard_map.71.factor_own), channel_id=1, source_target_pairs={{1,0},{2,1},{3,2},{0,3},{5,4},{6,5},{7,6},{4,7},{9,8},{10,9},{11,1... | collective-permute-start | bytes 786440 | tf_op jit(solution)/shard_map/ppermute | solution.py:279

commit v3 on v2

--- a/solution.py
+++ b/solution.py
@@ -46,7 +46,7 @@
     return jnp.concatenate(rows, axis=0)
 
 
-def fill_table(row_devices, col_devices, pattern, keep, order, table):
+def neighbours(row_devices, col_devices, order):
     row = lax.axis_index("row")
     col = lax.axis_index("col")
     odd = lax.rem(row, 2)
@@ -54,73 +54,104 @@
     def first(row_of, col_of):
         return (lax.rem(row_of, row_devices) * col_devices + lax.rem(col_of, col_devices)) * ROWS
 
-    peer = first(row + row_devices - 1 + 2 * odd, col)
-    own = first(row, col)
-    mate = first(row + 1 - 2 * odd, col)
-    side = first(row, col + 1)
-    labels = [order[start + j] for start in (peer, own, mate, side) for j in range(ROWS)]
+    starts = (
+        first(row + row_devices - 1 + 2 * odd, col),
+        first(row, col),
+        first(row + 1 - 2 * odd, col),
+        first(row, col + 1),
+    )
+    return starts, [order[start + j] for start in starts for j in range(ROWS)]
+
+
+def find_slots(pattern, stored, wanted):
+    slots = [jnp.int32(0)] * len(wanted)
+    for k in range(SLOTS):
+        label = pattern[k, stored]
+        slots = [jnp.where(label == want, k, slot) for want, slot in zip(wanted, slots)]
+    return slots
+
+
+def fill_table(row_devices, col_devices, pattern, keep, order, table):
+    starts, labels = neighbours(row_devices, col_devices, order)
     own_labels = labels[OWN * ROWS:(OWN + 1) * ROWS]
 
     def look_up(stored, wanted, slot_at, kept_at):
-        slots = [jnp.int32(0)] * len(wanted)
-        kepts = [jnp.int32(0)] * len(wanted)
-        for k in range(SLOTS):
-            label = pattern[k, stored]
-            flag = jnp.int32(1) if k == 0 else (keep[k, stored] == 1).astype(jnp.int32)
-            for j, want in enumerate(wanted):
-                same = label == want
-                slots[j] = jnp.where(same, k, slots[j])
-                kepts[j] = jnp.where(same, flag, kepts[j])
-        for j in range(len(wanted)):
+        for j, slot in enumerate(find_slots(pattern, stored, wanted)):
             if slot_at is not None:
-                table[slot_at + j] = slots[j]
-            table[kept_at + j] = kepts[j]
+                table[slot_at + j] = slot
+            kept = (slot == 0) | (keep[slot, stored] == 1)
+            table[kept_at + j] = kept.astype(jnp.int32)
 
     for i in range(ROWS):
-        look_up(own + i, labels, SLOT_AT + i * SLOTS, KEPT_AT + i * SLOTS)
-        look_up(peer + i, own_labels, None, KEPT_PEER_AT + i * ROWS)
-        look_up(mate + i, own_labels, None, KEPT_MATE_AT + i * ROWS)
-
-
-def gather(table, source, places):
+        look_up(starts[OWN] + i, labels, SLOT_AT + i * SLOTS, KEPT_AT + i * SLOTS)
+        look_up(starts[PEER] + i, own_labels, None, KEPT_PEER_AT + i * ROWS)
+        look_up(starts[MATE] + i, own_labels, None, KEPT_MATE_AT + i * ROWS)
+
+
+def gather(slot_of, source, places):
     size = source.shape[1]
     for i in range(ROWS):
         rows = slice(i * size, (i + 1) * size)
-        for j in range(SLOTS):
-            region, offset = divmod(j, ROWS)
-            cols = slice(offset * size, (offset + 1) * size)
-            slot = table[SLOT_AT + i * SLOTS + j]
-            block = source[i, :, pl.ds(pl.multiple_of(slot * size, size), size)]
-            for place in places[region]:
-                place[rows, cols] = block
-
-
-def pack_sqrt_kernel(
-    row_devices, col_devices, pattern, keep, order, sqrt_iterate,
-    table, y_peer, y_mate, y_side,
-    pattern_here, keep_here, order_here, sqrt_here, sems,
+        for region, region_places in places.items():
+            for j in range(ROWS):
+                cols = slice(j * size, (j + 1) * size)
+                start = pl.multiple_of(slot_of(i, region * ROWS + j) * size, size)
+                block = source[i, :, pl.ds(start, size)]
+                for place in region_places:
+                    place[rows, cols] = block
+
+
+def pack_first_kernel(
+    row_devices, col_devices, pattern, order, sqrt_iterate,
+    y_peer, y_mate, pattern_here, order_here, sqrt_here, sems,
+):
+    copies = [
+        pltpu.make_async_copy(source, here, sems.at[at])
+        for at, (source, here) in enumerate(
+            ((order, order_here), (pattern, pattern_here), (sqrt_iterate, sqrt_here))
+        )
+    ]
+    for copy in copies:
+        copy.start()
+    copies[0].wait()
+    copies[1].wait()
+    starts, labels = neighbours(row_devices, col_devices, order_here)
+    wanted = labels[PEER * ROWS:(MATE + 1) * ROWS]
+    slots = [find_slots(pattern_here, starts[OWN] + i, wanted) for i in range(ROWS)]
+    copies[2].wait()
+    places = {PEER: (y_peer.at[0],), OWN: (y_peer.at[1], y_mate.at[1]), MATE: (y_mate.at[0],)}
+    gather(lambda i, j: slots[i][j], sqrt_here, places)
+
+
+def pack_rest_kernel(
+    row_devices, col_devices, pattern, keep, order, sqrt_iterate, inverse_iterate, y_peer,
+    table, y_side, z_peer, z_mate, z_side, to_side,
+    pattern_here, keep_here, order_here, sqrt_here, inverse_here, sems,
 ):
     copies = [
         pltpu.make_async_copy(source, here, sems.at[at])
         for at, (source, here) in enumerate((
             (order, order_here), (pattern, pattern_here), (keep, keep_here),
-            (sqrt_iterate, sqrt_here),
+            (inverse_iterate, inverse_here), (sqrt_iterate, sqrt_here),
         ))
     ]
     for copy in copies:
         copy.start()
+    to_side[0] = y_peer[1]
     for copy in copies[:3]:
         copy.wait()
     fill_table(row_devices, col_devices, pattern_here, keep_here, order_here, table)
+
+    def slot_of(i, j):
+        return table[SLOT_AT + i * SLOTS + j]
+
+    places = {
+        PEER: (z_peer,), OWN: (z_mate.at[1], to_side.at[1]), MATE: (z_mate.at[0],), SIDE: (z_side,)
+    }
     copies[3].wait()
-    places = ((y_peer.at[0],), (y_peer.at[1], y_mate.at[1]), (y_mate.at[0],), (y_side,))
-    gather(table, sqrt_here, places)
-
-
-def pack_inverse_kernel(table, y_peer, inverse_iterate, z_peer, z_mate, z_side, to_side):
-    to_side[0] = y_peer[1]
-    places = ((z_peer,), (z_mate.at[1], to_side.at[1]), (z_mate.at[0],), (z_side,))
-    gather(table, inverse_iterate, places)
+    gather(slot_of, inverse_here, places)
+    copies[4].wait()
+    gather(slot_of, sqrt_here, {SIDE: (y_side,)})
 
 
 def mate_kernel(
@@ -188,54 +219,73 @@
     finished[Z_SIDE] = filtered(table, value, SIDE)
 
 
-def last_kernel(
-    table, finished, partial, ready, peer_z, peer_factor, side_factor,
-    sqrt_next, inverse_next, result, sems,
-):
-    size = sqrt_next.shape[1]
-    started = []
-
-    def write(source, out, region):
+class Writer:
+    def __init__(self, table, result, sems):
+        self.table, self.result, self.sems = table, result, sems
+        self.started = []
+        self.held = 0
+
+    def write(self, source, out, region):
+        size = out.shape[1]
         for i in range(ROWS):
             for j in range(ROWS):
-                slot = table[SLOT_AT + i * SLOTS + region * ROWS + j]
+                slot = self.table[SLOT_AT + i * SLOTS + region * ROWS + j]
                 copy = pltpu.make_async_copy(
                     source.at[pl.ds(i * size, size), pl.ds(j * size, size)],
                     out.at[i, :, pl.ds(pl.multiple_of(slot * size, size), size)],
-                    sems.at[len(started)],
+                    self.sems.at[len(self.started)],
                 )
                 copy.start()
-                started.append(copy)
-
-    def finish(at, value, out, region):
-        result[at] = filtered(table, value, region)
-        write(result.at[at], out, region)
-
+                self.started.append(copy)
+
+    def finish(self, value, out, region):
+        place = self.result.at[self.held]
+        self.held += 1
+        place[...] = filtered(self.table, value, region)
+        self.write(place, out, region)
+
+    def wait(self):
+        for copy in self.started:
+            copy.wait()
+
+
+def peer_kernel(
+    table, finished, partial, ready, peer_z, sqrt_next, inverse_next, result, sems
+):
     def held(at):
         return ready[at, 0], ready[at, 1]
 
-    write(finished.at[Y_MATE], sqrt_next, MATE)
-    write(finished.at[Z_MATE], inverse_next, MATE)
-    write(finished.at[Z_SIDE], inverse_next, SIDE)
+    writer = Writer(table, result, sems)
+    writer.write(finished.at[Y_MATE], sqrt_next, MATE)
+    writer.write(finished.at[Z_MATE], inverse_next, MATE)
+    writer.write(finished.at[Z_SIDE], inverse_next, SIDE)
     peer_z_peer, peer_z_own = split(peer_z[0]), split(peer_z[1])
-    f_peer, y_peer = held(F_PEER), held(Y_PEER)
+    f_peer = held(F_PEER)
     value = partial[Z_PEER_PART] + products((f_peer, peer_z_own))
-    finish(0, value, inverse_next, PEER)
+    writer.finish(value, inverse_next, PEER)
     value = partial[Z_OWN_PART] + products((f_peer, peer_z_peer))
-    finish(1, value, inverse_next, OWN)
+    writer.finish(value, inverse_next, OWN)
     total = products((peer_z_own, held(PEER_Y)), (peer_z_peer, held(Y_OWN)))
     peer_f_peer = split(filtered(table, total, 0, -0.5, KEPT_PEER_AT, ROWS))
-    value = partial[Y_SIDE_PART] + products((held(Y_SIDE), split(side_factor[...])))
-    finish(2, value, sqrt_next, SIDE)
-    value = partial[Y_PEER_PART] + products((y_peer, split(peer_factor[...])))
-    finish(3, value, sqrt_next, PEER)
-    value = partial[Y_OWN_PART] + products((y_peer, peer_f_peer))
-    finish(4, value, sqrt_next, OWN)
-    for copy in started:
-        copy.wait()
-
-
-def call(kernel, outs, operands, terms, scratch=(), hbm_in=(), hbm_out=False):
+    value = partial[Y_OWN_PART] + products((held(Y_PEER), peer_f_peer))
+    writer.finish(value, sqrt_next, OWN)
+    writer.wait()
+
+
+def last_kernel(
+    table, partial, ready, peer_factor, side_factor, unfinished, sqrt_next, result, sems
+):
+    writer = Writer(table, result, sems)
+    for region, part, here, factor in (
+        (SIDE, Y_SIDE_PART, Y_SIDE, side_factor), (PEER, Y_PEER_PART, Y_PEER, peer_factor)
+    ):
+        left = (ready[here, 0], ready[here, 1])
+        value = partial[part] + products((left, split(factor[...])))
+        writer.finish(value, sqrt_next, region)
+    writer.wait()
+
+
+def call(kernel, outs, operands, terms, scratch=(), hbm_in=(), hbm_out=False, in_place=None):
     def spec(array, outside=False):
         if outside:
             return pl.BlockSpec(memory_space=pltpu.HBM)
@@ -253,6 +303,7 @@
         in_specs=[spec(array, at in hbm_in) for at, array in enumerate(operands)],
         out_specs=tuple(spec(array, hbm_out) for array in outs),
         scratch_shapes=scratch,
+        input_output_aliases={} if in_place is None else {in_place: 0},
         compiler_params=pltpu.CompilerParams(vmem_limit_bytes=VMEM_LIMIT),
         cost_estimate=pl.CostEstimate(
             flops=terms * 6 * 256**3, bytes_accessed=moved, transcendentals=0
@@ -282,27 +333,41 @@
         return jax.ShapeDtypeStruct(dims, dtype)
 
     one, pair = shape(size, size), shape(2, size, size)
-    table, y_peer, y_mate, y_side = call(
-        functools.partial(pack_sqrt_kernel, row_devices, col_devices),
-        (shape(TABLE, dtype=jnp.int32), pair, pair, one),
-        (pattern.T, keep_mask.T, row_order, sqrt_iterate),
+    labels = [
+        pltpu.SMEM(pattern.T.shape, jnp.int32),
+        pltpu.SMEM(keep_mask.T.shape, jnp.int32),
+        pltpu.SMEM(row_order.shape, jnp.int32),
+    ]
+    y_peer, y_mate = call(
+        functools.partial(pack_first_kernel, row_devices, col_devices),
+        (pair, pair),
+        (pattern.T, row_order, sqrt_iterate),
         0,
         scratch=[
-            pltpu.SMEM(pattern.T.shape, jnp.int32),
-            pltpu.SMEM(keep_mask.T.shape, jnp.int32),
-            pltpu.SMEM(row_order.shape, jnp.int32),
+            labels[0],
+            labels[2],
             pltpu.VMEM(sqrt_iterate.shape, jnp.float32),
-            pltpu.SemaphoreType.DMA((4,)),
+            pltpu.SemaphoreType.DMA((3,)),
         ],
-        hbm_in=range(4),
+        hbm_in=range(3),
     )
     mate_y = to_mate(y_mate)
     peer_y = to_peer(y_peer)
-    z_peer, z_mate, z_side, own_pair = call(
-        pack_inverse_kernel, (one, pair, one, pair), (table, y_peer, inverse_iterate), 0
-    )
+    table, y_side, z_peer, z_mate, z_side, own_pair = call(
+        functools.partial(pack_rest_kernel, row_devices, col_devices),
+        (shape(TABLE, dtype=jnp.int32), one, one, pair, one, pair),
+        (pattern.T, keep_mask.T, row_order, sqrt_iterate, inverse_iterate, y_peer),
+        0,
+        scratch=[
+            *labels,
+            pltpu.VMEM(sqrt_iterate.shape, jnp.float32),
+            pltpu.VMEM(inverse_iterate.shape, jnp.float32),
+            pltpu.SemaphoreType.DMA((5,)),
+        ],
+        hbm_in=range(5),
+    )
+    mate_z = to_mate(z_mate)
     from_side = to_side(own_pair)
-    mate_z = to_mate(z_mate)
     z_to_peer, factor_mate, own_partial, peer_partial = call(
         mate_kernel, (pair, one, one, one), (table, y_peer, y_mate, z_peer, z_mate, mate_y), 5
     )
@@ -323,13 +388,23 @@
         ),
         19,
     )
-    sqrt_next, inverse_next = call(
+    unfinished, inverse_next = call(
+        peer_kernel,
+        (shape(rows_dev, block, width), shape(rows_dev, block, width)),
+        (table, finished, partial, ready, peer_z),
+        5,
+        scratch=[pltpu.VMEM((3, size, size), jnp.float32), pltpu.SemaphoreType.DMA((24,))],
+        hbm_out=True,
+    )
+    (sqrt_next,) = call(
         last_kernel,
-        (shape(rows_dev, block, width), shape(rows_dev, block, width)),
-        (table, finished, partial, ready, peer_z, peer_factor, side_factor),
-        7,
-        scratch=[pltpu.VMEM((5, size, size), jnp.float32), pltpu.SemaphoreType.DMA((32,))],
+        (shape(rows_dev, block, width),),
+        (table, partial, ready, peer_factor, side_factor, unfinished),
+        2,
+        scratch=[pltpu.VMEM((2, size, size), jnp.float32), pltpu.SemaphoreType.DMA((8,))],
+        hbm_in=(5,),
         hbm_out=True,
+        in_place=5,
     )
     return sqrt_next, inverse_next
 

time: 37.9 us -> 36.6 us (0.966)
  waiting for transfers between devices: 11.8 us -> 7.81 us
  Pallas kernels: 10.3 us -> 12.9 us
    ppermute x3, waiting for transfers between devices: 11.8 us -> 7.79 us  [to_peer(): return lax.ppermute(value, 'row', route)]
    pallas_call x6 -> x7, Pallas kernels: 10.3 us -> 12.9 us  [call(): pl.pallas_call(kernel, out_shape=outs, in_specs=[spec(array, at in hbm_in...]
  transfers between devices with their start and end apart: 8 -> 8, of which waited for: 2 -> 3; matrix products, arithmetic and copies ran while one was open for 0% -> 0% of each run, Pallas kernels for 15% -> 27%
where the time goes in v3:
time: 36.6 us; the launch traced here: 36.4 us
  starting transfers between devices  15 us (41%)
  Pallas kernels  12.9 us (35%)
  waiting for transfers between devices  7.81 us (21%)
  between operations  0.7 us (2%)
    pallas_call x7, Pallas kernels, call(): pl.pallas_call(kernel, out_shape=outs, in_specs=[spec(array, at in hbm_in...  12.9 us
    ppermute x3, waiting for transfers between devices, to_peer(): return lax.ppermute(value, 'row', route)  7.79 us
    ppermute x2, starting transfers between devices, to_side(): return lax.ppermute(value, 'col', route)  7.55 us
    ppermute x3, starting transfers between devices, to_peer(): return lax.ppermute(value, 'row', route)  6.79 us
  transfers between devices with their start and end apart: 8, of which 3 were waited for; matrix products, arithmetic and copies ran while one was open for 0% of the time, Pallas kernels for 27%

profile of v3, /device:TPU:0, one launch (start us, length us, event | category | flops | bytes accessed | tf_op | source)
XLA Modules:
  0.0 36.4 jit_solution(6656437281738220771)
XLA Ops:
  0.6 1.4 %shard_map.68 = (f32[2,256,256]{2,1,0:T(8,128)S(1)}, f32[2,256,256]{2,1,0:T(8,128)S(1)}) custom-call(s32[8,64]{1,0:T(8,128)} %bitcast.2, s32[64]{0:T(128)} %order.3, f32[2,128,1024]{2,1,0:T(8,128)} %sqrt_iterate.3), custom_call_target="tpu_custom_call" | custom-call | bytes 2099456 | tf_op jit(solution)/shard_map/pallas_call | solution.py:300
  2.0 0.5 %collective-permute-start = (f32[2,256,256]{2,1,0:T(8,128)S(1)}, f32[2,256,256]{2,1,0:T(8,128)S(1)}, u32[]{:S(2)}, u32[]{:S(2)}) collective-permute-start(f32[2,256,256]{2,1,0:T(8,128)S(1)} %get-tuple-element.21.y_mate), channel_id=1, source_target_pairs={{0,4},{4,0},{8,12},{12,8},{16,20},{20,16},{24,28},{28,24},{1,5},{5... | collective-permute-start | bytes 1572872 | tf_op jit(solution)/shard_map/ppermute | solution.py:322
  2.5 3.6 %collective-permute-start.2 = (f32[2,256,256]{2,1,0:T(8,128)S(1)}, f32[2,256,256]{2,1,0:T(8,128)S(1)}, u32[]{:S(2)}, u32[]{:S(2)}) collective-permute-start(f32[2,256,256]{2,1,0:T(8,128)S(1)} %get-tuple-element.19.y_peer), channel_id=1, source_target_pairs={{0,28},{4,8},{8,4},{12,16},{16,12},{20,24},{24,20},{28,0},{1,29},{... | collective-permute-start | bytes 1572872 | tf_op jit(solution)/shard_map/ppermute | solution.py:326
  6.1 2.2 %shard_map.69 = (s32[40]{0:T(128)S(1)}, f32[256,256]{1,0:T(8,128)S(1)}, f32[256,256]{1,0:T(8,128)S(1)}, f32[2,256,256]{2,1,0:T(8,128)S(1)}, f32[256,256]{1,0:T(8,128)S(1)}, /*index=5*/f32[2,256,256]{2,1,0:T(8,128)S(1)}) custom-call(s32[8,64]{1,0:T(8,128)} %bitcast.3, s32[8,64]{1,0:T(8,128)} %bitcast.4, s32[64]{0:T(128)} %order.3, ...), custom_call_target="tpu_custom_call" | custom-call | bytes 4460960 | tf_op jit(solution)/shard_map/pallas_call | solution.py:300
  8.3 0.1 collective-permute-start.1
  8.3 3.7 %collective-permute-start.3 = (f32[2,256,256]{2,1,0:T(8,128)S(1)}, f32[2,256,256]{2,1,0:T(8,128)S(1)}, u32[]{:S(2)}, u32[]{:S(2)}) collective-permute-start(f32[2,256,256]{2,1,0:T(8,128)S(1)} %get-tuple-element.26), channel_id=1, source_target_pairs={{1,0},{2,1},{3,2},{0,3},{5,4},{6,5},{7,6},{4,7},{9,8},{10,9},{11,1... | collective-permute-start | bytes 1572872 | tf_op jit(solution)/shard_map/ppermute | solution.py:330
  12.0 0.0 collective-permute-done.mate_y
  12.0 1.3 %shard_map.70 = (f32[2,256,256]{2,1,0:T(8,128)S(1)}, f32[256,256]{1,0:T(8,128)S(1)}, f32[256,256]{1,0:T(8,128)S(1)}, f32[256,256]{1,0:T(8,128)S(1)}) custom-call(s32[40]{0:T(128)S(1)} %get-tuple-element.20.table, f32[2,256,256]{2,1,0:T(8,128)S(1)} %get-tuple-element.19.y_peer, f32[2,256,256]{2,1,0:T(8,128)S(1)} %get-tuple-element.21.y_mate, ...), custom_call_target="tpu_custom_call" | custom-call | flops 503316480 | bytes 3670176 | tf_op jit(solution)/shard_map/pallas_call | solution.py:300
  13.3 0.4 collective-permute-start.7
  13.7 4.8 %collective-permute-done.2.peer_y = f32[2,256,256]{2,1,0:T(8,128)S(1)} collective-permute-done((f32[2,256,256]{2,1,0:T(8,128)S(1)}, f32[2,256,256]{2,1,0:T(8,128)S(1)}, u32[]{:S(2)}, u32[]{:S(2)}) %collective-permute-start.2) | collective-permute-done | bytes 524320 | tf_op jit(solution)/shard_map/ppermute | solution.py:326
  18.5 0.8 %shard_map.71.factor_own = f32[256,256]{1,0:T(8,128)S(1)} custom-call(s32[40]{0:T(128)S(1)} %get-tuple-element.20.table, f32[256,256]{1,0:T(8,128)S(1)} %get-tuple-element.29.own_partial, f32[256,256]{1,0:T(8,128)S(1)} %get-tuple-element.23.z_peer, f32[2,256,256]{2,1,0:T(8,128)S(1)} %collective-permute-done.2.peer_y), custom_call_target="tpu_custom_call" | custom-call | flops 100663296 | bytes 1310880 | tf_op jit(solution)/shard_map/pallas_call | solution.py:300
  19.3 0.1 collective-permute-start.4
  19.4 2.9 %collective-permute-start.5 = (f32[256,256]{1,0:T(8,128)S(1)}, f32[256,256]{1,0:T(8,128)S(1)}, u32[]{:S(2)}, u32[]{:S(2)}) collective-permute-start(f32[256,256]{1,0:T(8,128)S(1)} %shard_map.71.factor_own), channel_id=1, source_target_pairs={{0,28},{4,8},{8,4},{12,16},{16,12},{20,24},{24,20},{28,0},{1,29},{... | collective-permute-start | bytes 786440 | tf_op jit(solution)/shard_map/ppermute | solution.py:326
  22.2 0.0 collective-permute-done.1.mate_z
  22.2 3.9 %collective-permute-start.6 = (f32[256,256]{1,0:T(8,128)S(1)}, f32[256,256]{1,0:T(8,128)S(1)}, u32[]{:S(2)}, u32[]{:S(2)}) collective-permute-start(f32[256,256]{1,0:T(8,128)S(1)} %shard_map.71.factor_own), channel_id=1, source_target_pairs={{1,0},{2,1},{3,2},{0,3},{5,4},{6,5},{7,6},{4,7},{9,8},{10,9},{11,1... | collective-permute-start | bytes 786440 | tf_op jit(solution)/shard_map/ppermute | solution.py:330
  26.1 0.0 collective-permute-done.3.from_side
  26.1 0.0 collective-permute-done.4.mate_factor
  26.1 3.0 %shard_map.72 = (f32[3,256,256]{2,1,0:T(8,128)S(1)}, f32[5,256,256]{2,1,0:T(8,128)S(1)}, bf16[5,2,256,256]{3,2,1,0:T(8,128)(2,1)S(1)}) custom-call(s32[40]{0:T(128)S(1)} %get-tuple-element.20.table, f32[2,256,256]{2,1,0:T(8,128)S(1)} %get-tuple-element.19.y_peer, f32[2,256,256]{2,1,0:T(8,128)S(1)} %get-tuple-element.21.y_mate, ...), custom_call_target="tpu_custom_call" | custom-call | flops 1912602624 | bytes 8913056 | tf_op jit(solution)/shard_map/pallas_call | solution.py:300
  29.1 0.6 %collective-permute-done.7.peer_z = f32[2,256,256]{2,1,0:T(8,128)S(1)} collective-permute-done((f32[2,256,256]{2,1,0:T(8,128)S(1)}, f32[2,256,256]{2,1,0:T(8,128)S(1)}, u32[]{:S(2)}, u32[]{:S(2)}) %collective-permute-start.7) | collective-permute-done | bytes 524320 | tf_op jit(solution)/shard_map/ppermute | solution.py:326
  29.7 2.5 %shard_map.73 = (f32[2,128,1024]{2,1,0:T(8,128)}, f32[2,128,1024]{2,1,0:T(8,128)}) custom-call(s32[40]{0:T(128)S(1)} %get-tuple-element.20.table, f32[3,256,256]{2,1,0:T(8,128)S(1)} %get-tuple-element.32.finished, f32[5,256,256]{2,1,0:T(8,128)S(1)} %get-tuple-element.30.partial, bf16[5,2,256,256]{3,2,1,0:T(8,128)(2,1)S(1)} %get-tuple-element.31.ready, ...), custom_call_target="tpu_custom_call" | custom-call | flops 503316480 | bytes 6029472 | tf_op jit(solution)/shard_map/pallas_call | solution.py:300
  32.2 2.4 %collective-permute-done.5.peer_factor = f32[256,256]{1,0:T(8,128)S(1)} collective-permute-done((f32[256,256]{1,0:T(8,128)S(1)}, f32[256,256]{1,0:T(8,128)S(1)}, u32[]{:S(2)}, u32[]{:S(2)}) %collective-permute-start.5) | collective-permute-done | bytes 262176 | tf_op jit(solution)/shard_map/ppermute | solution.py:326
  34.6 0.0 collective-permute-done.6.side_factor
  34.6 1.8 %shard_map.74 = f32[2,128,1024]{2,1,0:T(8,128)} custom-call(s32[40]{0:T(128)S(1)} %get-tuple-element.20.table, f32[5,256,256]{2,1,0:T(8,128)S(1)} %get-tuple-element.30.partial, bf16[5,2,256,256]{3,2,1,0:T(8,128)(2,1)S(1)} %get-tuple-element.31.ready, f32[256,256]{1,0:T(8,128)S(1)} %collective-permute-done.5.peer_factor, ...), custom_call_target="tpu_custom_call", output_to_operand_aliasing={{}: (5, {})} | custom-call | flops 201326592 | bytes 5243040 | tf_op jit(solution)/shard_map/pallas_call | solution.py:300
Async XLA Ops:
  2.0 10.0 %collective-permute-start = (f32[2,256,256]{2,1,0:T(8,128)S(1)}, f32[2,256,256]{2,1,0:T(8,128)S(1)}, u32[]{:S(2)}, u32[]{:S(2)}) collective-permute-start(f32[2,256,256]{2,1,0:T(8,128)S(1)} %get-tuple-element.21.y_mate), channel_id=1, source_target_pairs={{0,4},{4,0},{8,12},{12,8},{16,20},{20,16},{24,28},{28,24},{1,5},{5... | collective-permute-start | bytes 1572872 | tf_op jit(solution)/shard_map/ppermute | solution.py:322
  2.5 15.9 %collective-permute-start.2 = (f32[2,256,256]{2,1,0:T(8,128)S(1)}, f32[2,256,256]{2,1,0:T(8,128)S(1)}, u32[]{:S(2)}, u32[]{:S(2)}) collective-permute-start(f32[2,256,256]{2,1,0:T(8,128)S(1)} %get-tuple-element.19.y_peer), channel_id=1, source_target_pairs={{0,28},{4,8},{8,4},{12,16},{16,12},{20,24},{24,20},{28,0},{1,29},{... | collective-permute-start | bytes 1572872 | tf_op jit(solution)/shard_map/ppermute | solution.py:326
  8.3 14.0 %collective-permute-start.1 = (f32[2,256,256]{2,1,0:T(8,128)S(1)}, f32[2,256,256]{2,1,0:T(8,128)S(1)}, u32[]{:S(2)}, u32[]{:S(2)}) collective-permute-start(f32[2,256,256]{2,1,0:T(8,128)S(1)} %get-tuple-element.24.z_mate), channel_id=1, source_target_pairs={{0,4},{4,0},{8,12},{12,8},{16,20},{20,16},{24,28},{28,24},{1,5},{5... | collective-permute-start | bytes 1572872 | tf_op jit(solution)/shard_map/ppermute | solution.py:322
  8.3 17.8 %collective-permute-start.3 = (f32[2,256,256]{2,1,0:T(8,128)S(1)}, f32[2,256,256]{2,1,0:T(8,128)S(1)}, u32[]{:S(2)}, u32[]{:S(2)}) collective-permute-start(f32[2,256,256]{2,1,0:T(8,128)S(1)} %get-tuple-element.26), channel_id=1, source_target_pairs={{1,0},{2,1},{3,2},{0,3},{5,4},{6,5},{7,6},{4,7},{9,8},{10,9},{11,1... | collective-permute-start | bytes 1572872 | tf_op jit(solution)/shard_map/ppermute | solution.py:330
  13.3 16.4 %collective-permute-start.7 = (f32[2,256,256]{2,1,0:T(8,128)S(1)}, f32[2,256,256]{2,1,0:T(8,128)S(1)}, u32[]{:S(2)}, u32[]{:S(2)}) collective-permute-start(f32[2,256,256]{2,1,0:T(8,128)S(1)} %get-tuple-element.33), channel_id=1, source_target_pairs={{0,28},{4,8},{8,4},{12,16},{16,12},{20,24},{24,20},{28,0},{1,29},{... | collective-permute-start | bytes 1572872 | tf_op jit(solution)/shard_map/ppermute | solution.py:326
  19.3 6.9 %collective-permute-start.4 = (f32[256,256]{1,0:T(8,128)S(1)}, f32[256,256]{1,0:T(8,128)S(1)}, u32[]{:S(2)}, u32[]{:S(2)}) collective-permute-start(f32[256,256]{1,0:T(8,128)S(1)} %shard_map.71.factor_own), channel_id=1, source_target_pairs={{0,4},{4,0},{8,12},{12,8},{16,20},{20,16},{24,28},{28,24},{1,5},{5... | collective-permute-start | bytes 786440 | tf_op jit(solution)/shard_map/ppermute | solution.py:322
  19.4 15.2 %collective-permute-start.5 = (f32[256,256]{1,0:T(8,128)S(1)}, f32[256,256]{1,0:T(8,128)S(1)}, u32[]{:S(2)}, u32[]{:S(2)}) collective-permute-start(f32[256,256]{1,0:T(8,128)S(1)} %shard_map.71.factor_own), channel_id=1, source_target_pairs={{0,28},{4,8},{8,4},{12,16},{16,12},{20,24},{24,20},{28,0},{1,29},{... | collective-permute-start | bytes 786440 | tf_op jit(solution)/shard_map/ppermute | solution.py:326
  22.2 12.4 %collective-permute-start.6 = (f32[256,256]{1,0:T(8,128)S(1)}, f32[256,256]{1,0:T(8,128)S(1)}, u32[]{:S(2)}, u32[]{:S(2)}) collective-permute-start(f32[256,256]{1,0:T(8,128)S(1)} %shard_map.71.factor_own), channel_id=1, source_target_pairs={{1,0},{2,1},{3,2},{0,3},{5,4},{6,5},{7,6},{4,7},{9,8},{10,9},{11,1... | collective-permute-start | bytes 786440 | tf_op jit(solution)/shard_map/ppermute | solution.py:330

commit v4 on v3

--- a/solution.py
+++ b/solution.py
@@ -103,7 +103,7 @@
 
 def pack_first_kernel(
     row_devices, col_devices, pattern, order, sqrt_iterate,
-    y_peer, y_mate, pattern_here, order_here, sqrt_here, sems,
+    y_peer, pattern_here, order_here, sqrt_here, sems,
 ):
     copies = [
         pltpu.make_async_copy(source, here, sems.at[at])
@@ -116,16 +116,16 @@
     copies[0].wait()
     copies[1].wait()
     starts, labels = neighbours(row_devices, col_devices, order_here)
-    wanted = labels[PEER * ROWS:(MATE + 1) * ROWS]
+    wanted = labels[PEER * ROWS:(OWN + 1) * ROWS]
     slots = [find_slots(pattern_here, starts[OWN] + i, wanted) for i in range(ROWS)]
     copies[2].wait()
-    places = {PEER: (y_peer.at[0],), OWN: (y_peer.at[1], y_mate.at[1]), MATE: (y_mate.at[0],)}
+    places = {PEER: (y_peer.at[0],), OWN: (y_peer.at[1],)}
     gather(lambda i, j: slots[i][j], sqrt_here, places)
 
 
 def pack_rest_kernel(
     row_devices, col_devices, pattern, keep, order, sqrt_iterate, inverse_iterate, y_peer,
-    table, y_side, z_peer, z_mate, z_side, to_side,
+    table, z_peer, y_mate, z_mate, y_side, z_side, to_side,
     pattern_here, keep_here, order_here, sqrt_here, inverse_here, sems,
 ):
     copies = [
@@ -137,6 +137,7 @@
     ]
     for copy in copies:
         copy.start()
+    y_mate[1] = y_peer[1]
     to_side[0] = y_peer[1]
     for copy in copies[:3]:
         copy.wait()
@@ -145,30 +146,24 @@
     def slot_of(i, j):
         return table[SLOT_AT + i * SLOTS + j]
 
+    copies[3].wait()
     places = {
-        PEER: (z_peer,), OWN: (z_mate.at[1], to_side.at[1]), MATE: (z_mate.at[0],), SIDE: (z_side,)
+        PEER: (z_peer.at[0],), OWN: (z_peer.at[1], z_mate.at[1], to_side.at[1]),
+        MATE: (z_mate.at[0],), SIDE: (z_side,),
     }
-    copies[3].wait()
     gather(slot_of, inverse_here, places)
     copies[4].wait()
-    gather(slot_of, sqrt_here, {SIDE: (y_side,)})
-
-
-def mate_kernel(
-    table, y_peer, y_mate, z_peer, z_mate, mate_y,
-    z_to_peer, factor_mate, own_partial, peer_partial,
-):
-    z_to_peer[0] = z_peer[...]
-    z_to_peer[1] = z_mate[1]
-    z_own, z_to_mate = split(z_mate[1]), split(z_mate[0])
-    own_partial[...] = products((z_own, split(y_mate[1])), (z_to_mate, split(mate_y[0])))
-    total = products((z_own, split(y_mate[0])), (z_to_mate, split(mate_y[1])))
-    factor_mate[...] = filtered(table, total, MATE, -0.5)
-    peer_partial[...] = products((z_own, split(y_peer[0])))
-
-
-def factor_own_kernel(table, own_partial, z_peer, peer_y, factor_own):
-    total = own_partial[...] + products((split(z_peer[...]), split(peer_y[0])))
+    gather(slot_of, sqrt_here, {MATE: (y_mate.at[0],), SIDE: (y_side,)})
+
+
+def factor_part_kernel(y_peer, z_peer, peer_y, part):
+    part[...] = products(
+        (split(z_peer[0]), split(peer_y[0])), (split(z_peer[1]), split(y_peer[1]))
+    )
+
+
+def factor_own_kernel(table, part, z_mate, mate_y, factor_own):
+    total = part[...] + products((split(z_mate[0]), split(mate_y[0])))
     rows = lax.broadcasted_iota(jnp.int32, total.shape, 0)
     cols = lax.broadcasted_iota(jnp.int32, total.shape, 1)
     factor_own[...] = jnp.where(rows == cols, 1.5, 0.0) + filtered(table, total, OWN, -0.5)
@@ -180,30 +175,33 @@
 
 
 def middle_kernel(
-    table, y_peer, y_mate, y_side, z_peer, z_mate, z_side, mate_y, mate_z, peer_y, from_side,
-    factor_mate, peer_partial, factor_own, mate_factor,
+    table, y_peer, z_peer, y_mate, z_mate, y_side, z_side, mate_y, mate_z, peer_y, from_side,
+    factor_own, mate_factor,
     finished, partial, ready,
 ):
     def keep(at, parts):
         ready[at, 0], ready[at, 1] = parts
 
-    y_own, z_own = split(y_peer[1]), split(z_mate[1])
+    y_own, z_own = split(y_peer[1]), split(z_peer[1])
+    y_to_peer, z_to_peer = split(y_peer[0]), split(z_peer[0])
     y_to_mate, z_to_mate = split(y_mate[0]), split(z_mate[0])
     y_to_side, z_to_side = split(y_side[...]), split(z_side[...])
-    z_to_peer = split(z_peer[...])
-    f_own, f_mate = split(factor_own[...]), split(factor_mate[...])
+    mate_y_mate, mate_y_own = split(mate_y[0]), split(mate_y[1])
     mate_z_mate, mate_z_own = split(mate_z[0]), split(mate_z[1])
+    f_own = split(factor_own[...])
     keep(Y_OWN, y_own)
     keep(Y_SIDE, y_to_side)
-    keep(Y_PEER, split(y_peer[0]))
+    keep(Y_PEER, y_to_peer)
     keep(PEER_Y, split(peer_y[0]))
 
-    total = peer_partial[...] + products((z_to_peer, split(peer_y[1])))
+    total = products((z_own, y_to_mate), (z_to_mate, mate_y_own))
+    f_mate = split(filtered(table, total, MATE, -0.5))
+    total = products((z_own, y_to_peer), (z_to_peer, split(peer_y[1])))
     f_peer = split(filtered(table, total, PEER, -0.5))
     keep(F_PEER, f_peer)
     total = products((z_own, y_to_side), (z_to_side, split(from_side[0])))
     f_side = split(filtered(table, total, SIDE, -0.5))
-    total = products((mate_z_own, split(mate_y[0])), (mate_z_mate, y_own))
+    total = products((mate_z_own, mate_y_mate), (mate_z_mate, y_own))
     mate_f_mate = split(filtered(table, total, 0, -0.5, KEPT_MATE_AT, ROWS))
 
     partial[Y_PEER_PART] = products((y_own, f_peer))
@@ -273,22 +271,24 @@
 
 
 def last_kernel(
-    table, partial, ready, peer_factor, side_factor, unfinished, sqrt_next, result, sems
-):
-    writer = Writer(table, result, sems)
-    for region, part, here, factor in (
-        (SIDE, Y_SIDE_PART, Y_SIDE, side_factor), (PEER, Y_PEER_PART, Y_PEER, peer_factor)
-    ):
-        left = (ready[here, 0], ready[here, 1])
-        value = partial[part] + products((left, split(factor[...])))
-        writer.finish(value, sqrt_next, region)
+    region, part, here, table, partial, ready, factor, unfinished,
+    sqrt_next, table_here, result, sems,
+):
+    fetch = pltpu.make_async_copy(table, table_here, sems.at[4])
+    fetch.start()
+    value = partial[part] + products(((ready[here, 0], ready[here, 1]), split(factor[...])))
+    fetch.wait()
+    writer = Writer(table_here, result, sems)
+    writer.finish(value, sqrt_next, region)
     writer.wait()
 
 
-def call(kernel, outs, operands, terms, scratch=(), hbm_in=(), hbm_out=False, in_place=None):
-    def spec(array, outside=False):
-        if outside:
-            return pl.BlockSpec(memory_space=pltpu.HBM)
+def call(
+    kernel, outs, operands, terms, scratch=(), hbm_in=(), any_in=(), hbm_out=False, in_place=None
+):
+    def spec(array, outside=False, anywhere=False):
+        if outside or anywhere:
+            return pl.BlockSpec(memory_space=pltpu.HBM if outside else pl.ANY)
         small = array.dtype == jnp.int32
         return pl.BlockSpec(memory_space=pltpu.SMEM if small else pltpu.VMEM)
 
@@ -300,7 +300,7 @@
     return pl.pallas_call(
         kernel,
         out_shape=outs,
-        in_specs=[spec(array, at in hbm_in) for at, array in enumerate(operands)],
+        in_specs=[spec(array, at in hbm_in, at in any_in) for at, array in enumerate(operands)],
         out_specs=tuple(spec(array, hbm_out) for array in outs),
         scratch_shapes=scratch,
         input_output_aliases={} if in_place is None else {in_place: 0},
@@ -338,9 +338,9 @@
         pltpu.SMEM(keep_mask.T.shape, jnp.int32),
         pltpu.SMEM(row_order.shape, jnp.int32),
     ]
-    y_peer, y_mate = call(
+    (y_peer,) = call(
         functools.partial(pack_first_kernel, row_devices, col_devices),
-        (pair, pair),
+        (pair,),
         (pattern.T, row_order, sqrt_iterate),
         0,
         scratch=[
@@ -351,11 +351,10 @@
         ],
         hbm_in=range(3),
     )
-    mate_y = to_mate(y_mate)
     peer_y = to_peer(y_peer)
-    table, y_side, z_peer, z_mate, z_side, own_pair = call(
+    table, z_peer, y_mate, z_mate, y_side, z_side, own_pair = call(
         functools.partial(pack_rest_kernel, row_devices, col_devices),
-        (shape(TABLE, dtype=jnp.int32), one, one, pair, one, pair),
+        (shape(TABLE, dtype=jnp.int32), pair, pair, pair, one, one, pair),
         (pattern.T, keep_mask.T, row_order, sqrt_iterate, inverse_iterate, y_peer),
         0,
         scratch=[
@@ -366,13 +365,12 @@
         ],
         hbm_in=range(5),
     )
+    peer_z = to_peer(z_peer)
+    mate_y = to_mate(y_mate)
     mate_z = to_mate(z_mate)
     from_side = to_side(own_pair)
-    z_to_peer, factor_mate, own_partial, peer_partial = call(
-        mate_kernel, (pair, one, one, one), (table, y_peer, y_mate, z_peer, z_mate, mate_y), 5
-    )
-    peer_z = to_peer(z_to_peer)
-    (factor_own,) = call(factor_own_kernel, (one,), (table, own_partial, z_peer, peer_y), 1)
+    (part,) = call(factor_part_kernel, (one,), (y_peer, z_peer, peer_y), 2)
+    (factor_own,) = call(factor_own_kernel, (one,), (table, part, z_mate, mate_y), 1)
     mate_factor = to_mate(factor_own)
     peer_factor = to_peer(factor_own)
     side_factor = to_side(factor_own)
@@ -383,12 +381,12 @@
             shape(5, 2, size, size, dtype=jnp.bfloat16),
         ),
         (
-            table, y_peer, y_mate, y_side, z_peer, z_mate, z_side, mate_y, mate_z, peer_y,
-            from_side, factor_mate, peer_partial, factor_own, mate_factor,
+            table, y_peer, z_peer, y_mate, z_mate, y_side, z_side, mate_y, mate_z, peer_y, from_side,
+            factor_own, mate_factor,
         ),
-        19,
-    )
-    unfinished, inverse_next = call(
+        22,
+    )
+    sqrt_next, inverse_next = call(
         peer_kernel,
         (shape(rows_dev, block, width), shape(rows_dev, block, width)),
         (table, finished, partial, ready, peer_z),
@@ -396,16 +394,24 @@
         scratch=[pltpu.VMEM((3, size, size), jnp.float32), pltpu.SemaphoreType.DMA((24,))],
         hbm_out=True,
     )
-    (sqrt_next,) = call(
-        last_kernel,
-        (shape(rows_dev, block, width),),
-        (table, partial, ready, peer_factor, side_factor, unfinished),
-        2,
-        scratch=[pltpu.VMEM((2, size, size), jnp.float32), pltpu.SemaphoreType.DMA((8,))],
-        hbm_in=(5,),
-        hbm_out=True,
-        in_place=5,
-    )
+    for region, part, here, factor in (
+        (SIDE, Y_SIDE_PART, Y_SIDE, side_factor), (PEER, Y_PEER_PART, Y_PEER, peer_factor)
+    ):
+        (sqrt_next,) = call(
+            functools.partial(last_kernel, region, part, here),
+            (shape(rows_dev, block, width),),
+            (table, partial, ready, factor, sqrt_next),
+            1,
+            scratch=[
+                pltpu.SMEM((TABLE,), jnp.int32),
+                pltpu.VMEM((1, size, size), jnp.float32),
+                pltpu.SemaphoreType.DMA((5,)),
+            ],
+            hbm_in=(4,),
+            any_in=(0,),
+            hbm_out=True,
+            in_place=4,
+        )
     return sqrt_next, inverse_next
 
 

time: 36.6 us -> 35.4 us (0.967)
  waiting for transfers between devices: 7.81 us -> 6.81 us
  starting transfers between devices: 15 us -> 14.6 us
    ppermute x3, waiting for transfers between devices: 7.79 us -> 6.79 us  [to_peer(): return lax.ppermute(value, 'row', route)]
    ppermute x3, starting transfers between devices: 6.79 us -> 5.89 us  [to_peer(): return lax.ppermute(value, 'row', route)]
    ppermute x2, starting transfers between devices: 7.55 us -> 8.08 us  [to_side(): return lax.ppermute(value, 'col', route)]
    pallas_call x7 -> x8, Pallas kernels: 12.9 us -> 13 us  [call(): pl.pallas_call(kernel, out_shape=outs, in_specs=[spec(array, at in hbm_in...]
  transfers between devices with their start and end apart: 8 -> 8, of which waited for: 3 -> 3; matrix products, arithmetic and copies ran while one was open for 0% -> 0% of each run, Pallas kernels for 27% -> 30%
where the time goes in v4:
time: 35.4 us; the launch traced here: 35.2 us
  starting transfers between devices  14.6 us (41%)
  Pallas kernels  13 us (37%)
  waiting for transfers between devices  6.81 us (19%)
  between operations  0.72 us (2%)
    pallas_call x8, Pallas kernels, call(): pl.pallas_call(kernel, out_shape=outs, in_specs=[spec(array, at in hbm_in...  13 us
    ppermute x2, starting transfers between devices, to_side(): return lax.ppermute(value, 'col', route)  8.08 us
    ppermute x3, waiting for transfers between devices, to_peer(): return lax.ppermute(value, 'row', route)  6.79 us
    ppermute x3, starting transfers between devices, to_peer(): return lax.ppermute(value, 'row', route)  5.89 us
  transfers between devices with their start and end apart: 8, of which 3 were waited for; matrix products, arithmetic and copies ran while one was open for 0% of the time, Pallas kernels for 30%

profile of v4, /device:TPU:0, one launch (start us, length us, event | category | flops | bytes accessed | tf_op | source)
XLA Modules:
  0.0 35.2 jit_solution(9630586715487116039)
XLA Ops:
  0.6 1.3 %shard_map.68.y_peer = f32[2,256,256]{2,1,0:T(8,128)S(1)} custom-call(s32[8,64]{1,0:T(8,128)} %bitcast.2, s32[64]{0:T(128)} %order.3, f32[2,128,1024]{2,1,0:T(8,128)} %sqrt_iterate.3), custom_call_target="tpu_custom_call" | custom-call | bytes 1575168 | tf_op jit(solution)/shard_map/pallas_call | solution.py:300
  2.0 3.4 %collective-permute-start.2 = (f32[2,256,256]{2,1,0:T(8,128)S(1)}, f32[2,256,256]{2,1,0:T(8,128)S(1)}, u32[]{:S(2)}, u32[]{:S(2)}) collective-permute-start(f32[2,256,256]{2,1,0:T(8,128)S(1)} %shard_map.68.y_peer), channel_id=1, source_target_pairs={{0,28},{4,8},{8,4},{12,16},{16,12},{20,24},{24,20},{28,0},{1,29},{... | collective-permute-start | bytes 1572872 | tf_op jit(solution)/shard_map/ppermute | solution.py:326
  5.4 2.2 %shard_map.69 = (s32[40]{0:T(128)S(1)}, f32[2,256,256]{2,1,0:T(8,128)S(1)}, f32[2,256,256]{2,1,0:T(8,128)S(1)}, f32[2,256,256]{2,1,0:T(8,128)S(1)}, f32[256,256]...) custom-call(s32[8,64]{1,0:T(8,128)} %bitcast.3, s32[8,64]{1,0:T(8,128)} %bitcast.4, s32[64]{0:T(128)} %order.3, ...), custom_call_target="tpu_custom_call" | custom-call | bytes 5247392 | tf_op jit(solution)/shard_map/pallas_call | solution.py:300
  7.5 0.1 collective-permute-start
  7.6 0.5 %collective-permute-start.1 = (f32[2,256,256]{2,1,0:T(8,128)S(1)}, f32[2,256,256]{2,1,0:T(8,128)S(1)}, u32[]{:S(2)}, u32[]{:S(2)}) collective-permute-start(f32[2,256,256]{2,1,0:T(8,128)S(1)} %get-tuple-element.17.z_mate), channel_id=1, source_target_pairs={{0,4},{4,0},{8,12},{12,8},{16,20},{20,16},{24,28},{28,24},{1,5},{5... | collective-permute-start | bytes 1572872 | tf_op jit(solution)/shard_map/ppermute | solution.py:322
  8.1 3.6 %collective-permute-start.3 = (f32[2,256,256]{2,1,0:T(8,128)S(1)}, f32[2,256,256]{2,1,0:T(8,128)S(1)}, u32[]{:S(2)}, u32[]{:S(2)}) collective-permute-start(f32[2,256,256]{2,1,0:T(8,128)S(1)} %get-tuple-element.20), channel_id=1, source_target_pairs={{1,0},{2,1},{3,2},{0,3},{5,4},{6,5},{7,6},{4,7},{9,8},{10,9},{11,1... | collective-permute-start | bytes 1572872 | tf_op jit(solution)/shard_map/ppermute | solution.py:330
  11.7 0.5 %collective-permute-start.7 = (f32[2,256,256]{2,1,0:T(8,128)S(1)}, f32[2,256,256]{2,1,0:T(8,128)S(1)}, u32[]{:S(2)}, u32[]{:S(2)}) collective-permute-start(f32[2,256,256]{2,1,0:T(8,128)S(1)} %get-tuple-element.15.z_peer), channel_id=1, source_target_pairs={{0,28},{4,8},{8,4},{12,16},{16,12},{20,24},{24,20},{28,0},{1,29},{... | collective-permute-start | bytes 1572872 | tf_op jit(solution)/shard_map/ppermute | solution.py:326
  12.2 5.4 %collective-permute-done.2.peer_y = f32[2,256,256]{2,1,0:T(8,128)S(1)} collective-permute-done((f32[2,256,256]{2,1,0:T(8,128)S(1)}, f32[2,256,256]{2,1,0:T(8,128)S(1)}, u32[]{:S(2)}, u32[]{:S(2)}) %collective-permute-start.2) | collective-permute-done | bytes 524320 | tf_op jit(solution)/shard_map/ppermute | solution.py:326
  17.7 0.4 %shard_map.70.part = f32[256,256]{1,0:T(8,128)S(1)} custom-call(f32[2,256,256]{2,1,0:T(8,128)S(1)} %shard_map.68.y_peer, f32[2,256,256]{2,1,0:T(8,128)S(1)} %get-tuple-element.15.z_peer, f32[2,256,256]{2,1,0:T(8,128)S(1)} %collective-permute-done.2.peer_y), custom_call_target="tpu_custom_call" | custom-call | flops 201326592 | bytes 1835008 | tf_op jit(solution)/shard_map/pallas_call | solution.py:300
  18.1 0.0 collective-permute-done.mate_y
  18.1 0.8 %shard_map.71.factor_own = f32[256,256]{1,0:T(8,128)S(1)} custom-call(s32[40]{0:T(128)S(1)} %get-tuple-element.14.table, f32[256,256]{1,0:T(8,128)S(1)} %shard_map.70.part, f32[2,256,256]{2,1,0:T(8,128)S(1)} %get-tuple-element.17.z_mate, f32[2,256,256]{2,1,0:T(8,128)S(1)} %collective-permute-done.mate_y), custom_call_target="tpu_custom_call" | custom-call | flops 100663296 | bytes 1573024 | tf_op jit(solution)/shard_map/pallas_call | solution.py:300
  18.9 0.1 collective-permute-start.4
  19.0 4.5 %collective-permute-start.6 = (f32[256,256]{1,0:T(8,128)S(1)}, f32[256,256]{1,0:T(8,128)S(1)}, u32[]{:S(2)}, u32[]{:S(2)}) collective-permute-start(f32[256,256]{1,0:T(8,128)S(1)} %shard_map.71.factor_own), channel_id=1, source_target_pairs={{1,0},{2,1},{3,2},{0,3},{5,4},{6,5},{7,6},{4,7},{9,8},{10,9},{11,1... | collective-permute-start | bytes 786440 | tf_op jit(solution)/shard_map/ppermute | solution.py:330
  23.5 0.0 collective-permute-done.1.mate_z
  23.5 2.0 %collective-permute-start.5 = (f32[256,256]{1,0:T(8,128)S(1)}, f32[256,256]{1,0:T(8,128)S(1)}, u32[]{:S(2)}, u32[]{:S(2)}) collective-permute-start(f32[256,256]{1,0:T(8,128)S(1)} %shard_map.71.factor_own), channel_id=1, source_target_pairs={{0,28},{4,8},{8,4},{12,16},{16,12},{20,24},{24,20},{28,0},{1,29},{... | collective-permute-start | bytes 786440 | tf_op jit(solution)/shard_map/ppermute | solution.py:326
  25.5 0.0 collective-permute-done.3.from_side
  25.5 0.0 collective-permute-done.4.mate_factor
  25.5 3.2 %shard_map.72 = (f32[3,256,256]{2,1,0:T(8,128)S(1)}, f32[5,256,256]{2,1,0:T(8,128)S(1)}, bf16[5,2,256,256]{3,2,1,0:T(8,128)(2,1)S(1)}) custom-call(s32[40]{0:T(128)S(1)} %get-tuple-element.14.table, f32[2,256,256]{2,1,0:T(8,128)S(1)} %shard_map.68.y_peer, f32[2,256,256]{2,1,0:T(8,128)S(1)} %get-tuple-element.15.z_peer, ...), custom_call_target="tpu_custom_call" | custom-call | flops 2214592512 | bytes 8650912 | tf_op jit(solution)/shard_map/pallas_call | solution.py:300
  28.7 0.2 collective-permute-done.7.peer_z
  28.9 2.5 %shard_map.73 = (f32[2,128,1024]{2,1,0:T(8,128)}, f32[2,128,1024]{2,1,0:T(8,128)}) custom-call(s32[40]{0:T(128)S(1)} %get-tuple-element.14.table, f32[3,256,256]{2,1,0:T(8,128)S(1)} %get-tuple-element.23.finished, f32[5,256,256]{2,1,0:T(8,128)S(1)} %get-tuple-element.21.partial, bf16[5,2,256,256]{3,2,1,0:T(8,128)(2,1)S(1)} %get-tuple-element.22.ready, ...), custom_call_target="tpu_custom_call" | custom-call | flops 503316480 | bytes 6029472 | tf_op jit(solution)/shard_map/pallas_call | solution.py:300
  31.4 0.0 collective-permute-done.6.factor
  31.4 1.3 %shard_map.74.unfinished = f32[2,128,1024]{2,1,0:T(8,128)} custom-call(s32[40]{0:T(128)S(1)} %get-tuple-element.14.table, f32[5,256,256]{2,1,0:T(8,128)S(1)} %get-tuple-element.21.partial, bf16[5,2,256,256]{3,2,1,0:T(8,128)(2,1)S(1)} %get-tuple-element.22.ready, f32[256,256]{1,0:T(8,128)S(1)} %collective-permute-done.6.factor, ...), custom_call_target="tpu_custom_call", output_to_operand_aliasing={{}: (4, {})} | custom-call | flops 100663296 | bytes 4980896 | tf_op jit(solution)/shard_map/pallas_call | solution.py:300
  32.7 1.2 %collective-permute-done.5.factor = f32[256,256]{1,0:T(8,128)S(1)} collective-permute-done((f32[256,256]{1,0:T(8,128)S(1)}, f32[256,256]{1,0:T(8,128)S(1)}, u32[]{:S(2)}, u32[]{:S(2)}) %collective-permute-start.5) | collective-permute-done | bytes 262176 | tf_op jit(solution)/shard_map/ppermute | solution.py:326
  33.9 1.3 %shard_map.75 = f32[2,128,1024]{2,1,0:T(8,128)} custom-call(s32[40]{0:T(128)S(1)} %get-tuple-element.14.table, f32[5,256,256]{2,1,0:T(8,128)S(1)} %get-tuple-element.21.partial, bf16[5,2,256,256]{3,2,1,0:T(8,128)(2,1)S(1)} %get-tuple-element.22.ready, f32[256,256]{1,0:T(8,128)S(1)} %collective-permute-done.5.factor, ...), custom_call_target="tpu_custom_call", output_to_operand_aliasing={{}: (4, {})} | custom-call | flops 100663296 | bytes 4980896 | tf_op jit(solution)/shard_map/pallas_call | solution.py:300
Async XLA Ops:
  2.0 15.7 %collective-permute-start.2 = (f32[2,256,256]{2,1,0:T(8,128)S(1)}, f32[2,256,256]{2,1,0:T(8,128)S(1)}, u32[]{:S(2)}, u32[]{:S(2)}) collective-permute-start(f32[2,256,256]{2,1,0:T(8,128)S(1)} %shard_map.68.y_peer), channel_id=1, source_target_pairs={{0,28},{4,8},{8,4},{12,16},{16,12},{20,24},{24,20},{28,0},{1,29},{... | collective-permute-start | bytes 1572872 | tf_op jit(solution)/shard_map/ppermute | solution.py:326
  7.5 10.5 %collective-permute-start = (f32[2,256,256]{2,1,0:T(8,128)S(1)}, f32[2,256,256]{2,1,0:T(8,128)S(1)}, u32[]{:S(2)}, u32[]{:S(2)}) collective-permute-start(f32[2,256,256]{2,1,0:T(8,128)S(1)} %get-tuple-element.16.y_mate), channel_id=1, source_target_pairs={{0,4},{4,0},{8,12},{12,8},{16,20},{20,16},{24,28},{28,24},{1,5},{5... | collective-permute-start | bytes 1572872 | tf_op jit(solution)/shard_map/ppermute | solution.py:322
  7.6 15.9 %collective-permute-start.1 = (f32[2,256,256]{2,1,0:T(8,128)S(1)}, f32[2,256,256]{2,1,0:T(8,128)S(1)}, u32[]{:S(2)}, u32[]{:S(2)}) collective-permute-start(f32[2,256,256]{2,1,0:T(8,128)S(1)} %get-tuple-element.17.z_mate), channel_id=1, source_target_pairs={{0,4},{4,0},{8,12},{12,8},{16,20},{20,16},{24,28},{28,24},{1,5},{5... | collective-permute-start | bytes 1572872 | tf_op jit(solution)/shard_map/ppermute | solution.py:322
  8.1 17.4 %collective-permute-start.3 = (f32[2,256,256]{2,1,0:T(8,128)S(1)}, f32[2,256,256]{2,1,0:T(8,128)S(1)}, u32[]{:S(2)}, u32[]{:S(2)}) collective-permute-start(f32[2,256,256]{2,1,0:T(8,128)S(1)} %get-tuple-element.20), channel_id=1, source_target_pairs={{1,0},{2,1},{3,2},{0,3},{5,4},{6,5},{7,6},{4,7},{9,8},{10,9},{11,1... | collective-permute-start | bytes 1572872 | tf_op jit(solution)/shard_map/ppermute | solution.py:330
  11.7 17.2 %collective-permute-start.7 = (f32[2,256,256]{2,1,0:T(8,128)S(1)}, f32[2,256,256]{2,1,0:T(8,128)S(1)}, u32[]{:S(2)}, u32[]{:S(2)}) collective-permute-start(f32[2,256,256]{2,1,0:T(8,128)S(1)} %get-tuple-element.15.z_peer), channel_id=1, source_target_pairs={{0,28},{4,8},{8,4},{12,16},{16,12},{20,24},{24,20},{28,0},{1,29},{... | collective-permute-start | bytes 1572872 | tf_op jit(solution)/shard_map/ppermute | solution.py:326
  18.9 6.6 %collective-permute-start.4 = (f32[256,256]{1,0:T(8,128)S(1)}, f32[256,256]{1,0:T(8,128)S(1)}, u32[]{:S(2)}, u32[]{:S(2)}) collective-permute-start(f32[256,256]{1,0:T(8,128)S(1)} %shard_map.71.factor_own), channel_id=1, source_target_pairs={{0,4},{4,0},{8,12},{12,8},{16,20},{20,16},{24,28},{28,24},{1,5},{5... | collective-permute-start | bytes 786440 | tf_op jit(solution)/shard_map/ppermute | solution.py:322
  19.0 12.4 %collective-permute-start.6 = (f32[256,256]{1,0:T(8,128)S(1)}, f32[256,256]{1,0:T(8,128)S(1)}, u32[]{:S(2)}, u32[]{:S(2)}) collective-permute-start(f32[256,256]{1,0:T(8,128)S(1)} %shard_map.71.factor_own), channel_id=1, source_target_pairs={{1,0},{2,1},{3,2},{0,3},{5,4},{6,5},{7,6},{4,7},{9,8},{10,9},{11,1... | collective-permute-start | bytes 786440 | tf_op jit(solution)/shard_map/ppermute | solution.py:330
  23.5 10.4 %collective-permute-start.5 = (f32[256,256]{1,0:T(8,128)S(1)}, f32[256,256]{1,0:T(8,128)S(1)}, u32[]{:S(2)}, u32[]{:S(2)}) collective-permute-start(f32[256,256]{1,0:T(8,128)S(1)} %shard_map.71.factor_own), channel_id=1, source_target_pairs={{0,28},{4,8},{8,4},{12,16},{16,12},{20,24},{24,20},{28,0},{1,29},{... | collective-permute-start | bytes 786440 | tf_op jit(solution)/shard_map/ppermute | solution.py:326

commit v5 on v4

--- a/solution.py
+++ b/solution.py
@@ -10,6 +10,7 @@
 PEER, OWN, MATE, SIDE = range(4)
 ROWS = 2
 SLOTS = 8
+PIECES = 4
 SLOT_AT, KEPT_AT, KEPT_PEER_AT, KEPT_MATE_AT, TABLE = 0, 16, 32, 36, 40
 LARGEST = float(jnp.finfo(jnp.bfloat16).max)
 VMEM_LIMIT = 24 * 2**20
@@ -105,11 +106,15 @@
     row_devices, col_devices, pattern, order, sqrt_iterate,
     y_peer, pattern_here, order_here, sqrt_here, sems,
 ):
+    pieces = [(order, order_here), (pattern, pattern_here)]
+    height = sqrt_iterate.shape[1] // PIECES
+    for i in range(ROWS):
+        for piece in range(PIECES):
+            rows = pl.ds(piece * height, height)
+            pieces.append((sqrt_iterate.at[i, rows], sqrt_here.at[i, rows]))
     copies = [
         pltpu.make_async_copy(source, here, sems.at[at])
-        for at, (source, here) in enumerate(
-            ((order, order_here), (pattern, pattern_here), (sqrt_iterate, sqrt_here))
-        )
+        for at, (source, here) in enumerate(pieces)
     ]
     for copy in copies:
         copy.start()
@@ -118,7 +123,8 @@
     starts, labels = neighbours(row_devices, col_devices, order_here)
     wanted = labels[PEER * ROWS:(OWN + 1) * ROWS]
     slots = [find_slots(pattern_here, starts[OWN] + i, wanted) for i in range(ROWS)]
-    copies[2].wait()
+    for copy in copies[2:]:
+        copy.wait()
     places = {PEER: (y_peer.at[0],), OWN: (y_peer.at[1],)}
     gather(lambda i, j: slots[i][j], sqrt_here, places)
 
@@ -162,11 +168,14 @@
     )
 
 
-def factor_own_kernel(table, part, z_mate, mate_y, factor_own):
+def factor_own_kernel(table, part, z_mate, mate_y, peer_y, factor_own, peer_term):
     total = part[...] + products((split(z_mate[0]), split(mate_y[0])))
     rows = lax.broadcasted_iota(jnp.int32, total.shape, 0)
     cols = lax.broadcasted_iota(jnp.int32, total.shape, 1)
-    factor_own[...] = jnp.where(rows == cols, 1.5, 0.0) + filtered(table, total, OWN, -0.5)
+    factor = jnp.where(rows == cols, 1.5, 0.0) + filtered(table, total, OWN, -0.5)
+    factor_own[...] = factor
+    term = products((split(peer_y[0]), split(factor)))
+    peer_term[...] = filtered(table, term, 0, None, KEPT_PEER_AT, ROWS)
 
 
 Y_MATE, Z_MATE, Z_SIDE = range(3)
@@ -204,7 +213,7 @@
     total = products((mate_z_own, mate_y_mate), (mate_z_mate, y_own))
     mate_f_mate = split(filtered(table, total, 0, -0.5, KEPT_MATE_AT, ROWS))
 
-    partial[Y_PEER_PART] = products((y_own, f_peer))
+    partial[Y_PEER_PART] = filtered(table, products((y_own, f_peer)), PEER)
     partial[Y_SIDE_PART] = products((y_own, f_side))
     partial[Y_OWN_PART] = products((y_to_mate, mate_f_mate), (y_own, f_own))
     partial[Z_PEER_PART] = products((f_own, z_to_peer))
@@ -270,16 +279,26 @@
     writer.wait()
 
 
-def last_kernel(
-    region, part, here, table, partial, ready, factor, unfinished,
-    sqrt_next, table_here, result, sems,
+def side_kernel(
+    table, partial, ready, factor, unfinished, sqrt_next, table_here, result, sems
 ):
     fetch = pltpu.make_async_copy(table, table_here, sems.at[4])
     fetch.start()
-    value = partial[part] + products(((ready[here, 0], ready[here, 1]), split(factor[...])))
+    left = (ready[Y_SIDE, 0], ready[Y_SIDE, 1])
+    value = partial[Y_SIDE_PART] + products((left, split(factor[...])))
     fetch.wait()
     writer = Writer(table_here, result, sems)
-    writer.finish(value, sqrt_next, region)
+    writer.finish(value, sqrt_next, SIDE)
+    writer.wait()
+
+
+def last_kernel(table, partial, term, unfinished, sqrt_next, table_here, result, sems):
+    fetch = pltpu.make_async_copy(table, table_here, sems.at[4])
+    fetch.start()
+    result[0] = partial[Y_PEER_PART] + term[...]
+    fetch.wait()
+    writer = Writer(table_here, result, sems)
+    writer.write(result.at[0], sqrt_next, PEER)
     writer.wait()
 
 
@@ -347,7 +366,7 @@
             labels[0],
             labels[2],
             pltpu.VMEM(sqrt_iterate.shape, jnp.float32),
-            pltpu.SemaphoreType.DMA((3,)),
+            pltpu.SemaphoreType.DMA((2 + ROWS * PIECES,)),
         ],
         hbm_in=range(3),
     )
@@ -370,9 +389,11 @@
     mate_z = to_mate(z_mate)
     from_side = to_side(own_pair)
     (part,) = call(factor_part_kernel, (one,), (y_peer, z_peer, peer_y), 2)
-    (factor_own,) = call(factor_own_kernel, (one,), (table, part, z_mate, mate_y), 1)
+    factor_own, peer_term = call(
+        factor_own_kernel, (one, one), (table, part, z_mate, mate_y, peer_y), 2
+    )
     mate_factor = to_mate(factor_own)
-    peer_factor = to_peer(factor_own)
+    term = to_peer(peer_term)
     side_factor = to_side(factor_own)
     finished, partial, ready = call(
         middle_kernel,
@@ -394,23 +415,24 @@
         scratch=[pltpu.VMEM((3, size, size), jnp.float32), pltpu.SemaphoreType.DMA((24,))],
         hbm_out=True,
     )
-    for region, part, here, factor in (
-        (SIDE, Y_SIDE_PART, Y_SIDE, side_factor), (PEER, Y_PEER_PART, Y_PEER, peer_factor)
+    for kernel, operands in (
+        (side_kernel, (table, partial, ready, side_factor)),
+        (last_kernel, (table, partial, term)),
     ):
         (sqrt_next,) = call(
-            functools.partial(last_kernel, region, part, here),
+            kernel,
             (shape(rows_dev, block, width),),
-            (table, partial, ready, factor, sqrt_next),
+            (*operands, sqrt_next),
             1,
             scratch=[
                 pltpu.SMEM((TABLE,), jnp.int32),
                 pltpu.VMEM((1, size, size), jnp.float32),
                 pltpu.SemaphoreType.DMA((5,)),
             ],
-            hbm_in=(4,),
+            hbm_in=(len(operands),),
             any_in=(0,),
             hbm_out=True,
-            in_place=4,
+            in_place=len(operands),
         )
     return sqrt_next, inverse_next
 

time: 35.4 us -> 35.5 us (level)
  Pallas kernels: 13 us -> 13.5 us
  waiting for transfers between devices: 6.81 us -> 6.41 us
    pallas_call x8, Pallas kernels: 13 us -> 13.5 us  [call(): pl.pallas_call(kernel, out_shape=outs, in_specs=[spec(array, at in hbm_in...]
    ppermute x3, waiting for transfers between devices: 6.79 us -> 6.4 us  [to_peer(): return lax.ppermute(value, 'row', route)]
  transfers between devices with their start and end apart: 8 -> 8, of which waited for: 3 -> 2; matrix products, arithmetic and copies ran while one was open for 0% -> 0% of each run, Pallas kernels for 30% -> 31%
where the time goes in v5:
time: 35.5 us; the launch traced here: 35.3 us
  starting transfers between devices  14.6 us (41%)
  Pallas kernels  13.5 us (38%)
  waiting for transfers between devices  6.41 us (18%)
  between operations  0.73 us (2%)
    pallas_call x8, Pallas kernels, call(): pl.pallas_call(kernel, out_shape=outs, in_specs=[spec(array, at in hbm_in...  13.5 us
    ppermute x2, starting transfers between devices, to_side(): return lax.ppermute(value, 'col', route)  8.08 us
    ppermute x3, waiting for transfers between devices, to_peer(): return lax.ppermute(value, 'row', route)  6.4 us
    ppermute x3, starting transfers between devices, to_peer(): return lax.ppermute(value, 'row', route)  5.89 us
  transfers between devices with their start and end apart: 8, of which 2 were waited for; matrix products, arithmetic and copies ran while one was open for 0% of the time, Pallas kernels for 31%

profile of v5, /device:TPU:0, one launch (start us, length us, event | category | flops | bytes accessed | tf_op | source)
XLA Modules:
  0.0 35.3 jit_solution(17331357671527222316)
XLA Ops:
  0.6 1.4 %shard_map.68.y_peer = f32[2,256,256]{2,1,0:T(8,128)S(1)} custom-call(s32[8,64]{1,0:T(8,128)} %bitcast.2, s32[64]{0:T(128)} %order.3, f32[2,128,1024]{2,1,0:T(8,128)} %sqrt_iterate.3), custom_call_target="tpu_custom_call" | custom-call | bytes 1575168 | tf_op jit(solution)/shard_map/pallas_call | solution.py:319
  2.1 3.4 %collective-permute-start.2 = (f32[2,256,256]{2,1,0:T(8,128)S(1)}, f32[2,256,256]{2,1,0:T(8,128)S(1)}, u32[]{:S(2)}, u32[]{:S(2)}) collective-permute-start(f32[2,256,256]{2,1,0:T(8,128)S(1)} %shard_map.68.y_peer), channel_id=1, source_target_pairs={{0,28},{4,8},{8,4},{12,16},{16,12},{20,24},{24,20},{28,0},{1,29},{... | collective-permute-start | bytes 1572872 | tf_op jit(solution)/shard_map/ppermute | solution.py:345
  5.5 2.2 %shard_map.69 = (s32[40]{0:T(128)S(1)}, f32[2,256,256]{2,1,0:T(8,128)S(1)}, f32[2,256,256]{2,1,0:T(8,128)S(1)}, f32[2,256,256]{2,1,0:T(8,128)S(1)}, f32[256,256]...) custom-call(s32[8,64]{1,0:T(8,128)} %bitcast.3, s32[8,64]{1,0:T(8,128)} %bitcast.4, s32[64]{0:T(128)} %order.3, ...), custom_call_target="tpu_custom_call" | custom-call | bytes 5247392 | tf_op jit(solution)/shard_map/pallas_call | solution.py:319
  7.7 0.1 collective-permute-start
  7.7 0.5 %collective-permute-start.1 = (f32[2,256,256]{2,1,0:T(8,128)S(1)}, f32[2,256,256]{2,1,0:T(8,128)S(1)}, u32[]{:S(2)}, u32[]{:S(2)}) collective-permute-start(f32[2,256,256]{2,1,0:T(8,128)S(1)} %get-tuple-element.19.z_mate), channel_id=1, source_target_pairs={{0,4},{4,0},{8,12},{12,8},{16,20},{20,16},{24,28},{28,24},{1,5},{5... | collective-permute-start | bytes 1572872 | tf_op jit(solution)/shard_map/ppermute | solution.py:341
  8.2 3.6 %collective-permute-start.3 = (f32[2,256,256]{2,1,0:T(8,128)S(1)}, f32[2,256,256]{2,1,0:T(8,128)S(1)}, u32[]{:S(2)}, u32[]{:S(2)}) collective-permute-start(f32[2,256,256]{2,1,0:T(8,128)S(1)} %get-tuple-element.22), channel_id=1, source_target_pairs={{1,0},{2,1},{3,2},{0,3},{5,4},{6,5},{7,6},{4,7},{9,8},{10,9},{11,1... | collective-permute-start | bytes 1572872 | tf_op jit(solution)/shard_map/ppermute | solution.py:349
  11.8 0.5 %collective-permute-start.7 = (f32[2,256,256]{2,1,0:T(8,128)S(1)}, f32[2,256,256]{2,1,0:T(8,128)S(1)}, u32[]{:S(2)}, u32[]{:S(2)}) collective-permute-start(f32[2,256,256]{2,1,0:T(8,128)S(1)} %get-tuple-element.17.z_peer), channel_id=1, source_target_pairs={{0,28},{4,8},{8,4},{12,16},{16,12},{20,24},{24,20},{28,0},{1,29},{... | collective-permute-start | bytes 1572872 | tf_op jit(solution)/shard_map/ppermute | solution.py:345
  12.3 5.4 %collective-permute-done.2.peer_y = f32[2,256,256]{2,1,0:T(8,128)S(1)} collective-permute-done((f32[2,256,256]{2,1,0:T(8,128)S(1)}, f32[2,256,256]{2,1,0:T(8,128)S(1)}, u32[]{:S(2)}, u32[]{:S(2)}) %collective-permute-start.2) | collective-permute-done | bytes 524320 | tf_op jit(solution)/shard_map/ppermute | solution.py:345
  17.8 0.4 %shard_map.70.part = f32[256,256]{1,0:T(8,128)S(1)} custom-call(f32[2,256,256]{2,1,0:T(8,128)S(1)} %shard_map.68.y_peer, f32[2,256,256]{2,1,0:T(8,128)S(1)} %get-tuple-element.17.z_peer, f32[2,256,256]{2,1,0:T(8,128)S(1)} %collective-permute-done.2.peer_y), custom_call_target="tpu_custom_call" | custom-call | flops 201326592 | bytes 1835008 | tf_op jit(solution)/shard_map/pallas_call | solution.py:319
  18.2 0.0 collective-permute-done.mate_y
  18.2 1.2 %shard_map.71 = (f32[256,256]{1,0:T(8,128)S(1)}, f32[256,256]{1,0:T(8,128)S(1)}) custom-call(s32[40]{0:T(128)S(1)} %get-tuple-element.16.table, f32[256,256]{1,0:T(8,128)S(1)} %shard_map.70.part, f32[2,256,256]{2,1,0:T(8,128)S(1)} %get-tuple-element.19.z_mate, f32[2,256,256]{2,1,0:T(8,128)S(1)} %collective-permute-done.mate_y, ...), custom_call_target="tpu_custom_call" | custom-call | flops 201326592 | bytes 2359456 | tf_op jit(solution)/shard_map/pallas_call | solution.py:319
  19.4 0.1 collective-permute-start.4
  19.5 4.5 %collective-permute-start.6 = (f32[256,256]{1,0:T(8,128)S(1)}, f32[256,256]{1,0:T(8,128)S(1)}, u32[]{:S(2)}, u32[]{:S(2)}) collective-permute-start(f32[256,256]{1,0:T(8,128)S(1)} %get-tuple-element.23.factor_own), channel_id=1, source_target_pairs={{1,0},{2,1},{3,2},{0,3},{5,4},{6,5},{7,6},{4,7},{9,8},{10,9},{11,1... | collective-permute-start | bytes 786440 | tf_op jit(solution)/shard_map/ppermute | solution.py:349
  24.0 0.0 collective-permute-done.1.mate_z
  24.0 2.0 %collective-permute-start.5 = (f32[256,256]{1,0:T(8,128)S(1)}, f32[256,256]{1,0:T(8,128)S(1)}, u32[]{:S(2)}, u32[]{:S(2)}) collective-permute-start(f32[256,256]{1,0:T(8,128)S(1)} %get-tuple-element.25), channel_id=1, source_target_pairs={{0,28},{4,8},{8,4},{12,16},{16,12},{20,24},{24,20},{28,0},{1,29},{... | collective-permute-start | bytes 786440 | tf_op jit(solution)/shard_map/ppermute | solution.py:345
  26.0 0.0 collective-permute-done.3.from_side
  26.0 0.0 collective-permute-done.4.mate_factor
  26.0 3.2 %shard_map.72 = (f32[3,256,256]{2,1,0:T(8,128)S(1)}, f32[5,256,256]{2,1,0:T(8,128)S(1)}, bf16[5,2,256,256]{3,2,1,0:T(8,128)(2,1)S(1)}) custom-call(s32[40]{0:T(128)S(1)} %get-tuple-element.16.table, f32[2,256,256]{2,1,0:T(8,128)S(1)} %shard_map.68.y_peer, f32[2,256,256]{2,1,0:T(8,128)S(1)} %get-tuple-element.17.z_peer, ...), custom_call_target="tpu_custom_call" | custom-call | flops 2214592512 | bytes 8650912 | tf_op jit(solution)/shard_map/pallas_call | solution.py:319
  29.2 0.0 collective-permute-done.7.peer_z
  29.2 2.5 %shard_map.73 = (f32[2,128,1024]{2,1,0:T(8,128)}, f32[2,128,1024]{2,1,0:T(8,128)}) custom-call(s32[40]{0:T(128)S(1)} %get-tuple-element.16.table, f32[3,256,256]{2,1,0:T(8,128)S(1)} %get-tuple-element.27.finished, f32[5,256,256]{2,1,0:T(8,128)S(1)} %get-tuple-element.24.partial, bf16[5,2,256,256]{3,2,1,0:T(8,128)(2,1)S(1)} %get-tuple-element.26.ready, ...), custom_call_target="tpu_custom_call" | custom-call | flops 503316480 | bytes 6029472 | tf_op jit(solution)/shard_map/pallas_call | solution.py:319
  31.7 0.0 collective-permute-done.6.factor
  31.7 1.3 %shard_map.74.unfinished = f32[2,128,1024]{2,1,0:T(8,128)} custom-call(s32[40]{0:T(128)S(1)} %get-tuple-element.16.table, f32[5,256,256]{2,1,0:T(8,128)S(1)} %get-tuple-element.24.partial, bf16[5,2,256,256]{3,2,1,0:T(8,128)(2,1)S(1)} %get-tuple-element.26.ready, f32[256,256]{1,0:T(8,128)S(1)} %collective-permute-done.6.factor, ...), custom_call_target="tpu_custom_call", output_to_operand_aliasing={{}: (4, {})} | custom-call | flops 100663296 | bytes 4980896 | tf_op jit(solution)/shard_map/pallas_call | solution.py:319
  33.0 0.9 %collective-permute-done.5.term = f32[256,256]{1,0:T(8,128)S(1)} collective-permute-done((f32[256,256]{1,0:T(8,128)S(1)}, f32[256,256]{1,0:T(8,128)S(1)}, u32[]{:S(2)}, u32[]{:S(2)}) %collective-permute-start.5) | collective-permute-done | bytes 262176 | tf_op jit(solution)/shard_map/ppermute | solution.py:345
  34.0 1.3 %shard_map.75 = f32[2,128,1024]{2,1,0:T(8,128)} custom-call(s32[40]{0:T(128)S(1)} %get-tuple-element.16.table, f32[5,256,256]{2,1,0:T(8,128)S(1)} %get-tuple-element.24.partial, f32[256,256]{1,0:T(8,128)S(1)} %collective-permute-done.5.term, f32[2,128,1024]{2,1,0:T(8,128)} %shard_map.74.unfinished), custom_call_target="tpu_custom_call", output_to_operand_aliasing={{}: (3, {})} | custom-call | flops 100663296 | bytes 3670176 | tf_op jit(solution)/shard_map/pallas_call | solution.py:319
Async XLA Ops:
  2.1 15.7 %collective-permute-start.2 = (f32[2,256,256]{2,1,0:T(8,128)S(1)}, f32[2,256,256]{2,1,0:T(8,128)S(1)}, u32[]{:S(2)}, u32[]{:S(2)}) collective-permute-start(f32[2,256,256]{2,1,0:T(8,128)S(1)} %shard_map.68.y_peer), channel_id=1, source_target_pairs={{0,28},{4,8},{8,4},{12,16},{16,12},{20,24},{24,20},{28,0},{1,29},{... | collective-permute-start | bytes 1572872 | tf_op jit(solution)/shard_map/ppermute | solution.py:345
  7.7 10.5 %collective-permute-start = (f32[2,256,256]{2,1,0:T(8,128)S(1)}, f32[2,256,256]{2,1,0:T(8,128)S(1)}, u32[]{:S(2)}, u32[]{:S(2)}) collective-permute-start(f32[2,256,256]{2,1,0:T(8,128)S(1)} %get-tuple-element.18.y_mate), channel_id=1, source_target_pairs={{0,4},{4,0},{8,12},{12,8},{16,20},{20,16},{24,28},{28,24},{1,5},{5... | collective-permute-start | bytes 1572872 | tf_op jit(solution)/shard_map/ppermute | solution.py:341
  7.7 16.3 %collective-permute-start.1 = (f32[2,256,256]{2,1,0:T(8,128)S(1)}, f32[2,256,256]{2,1,0:T(8,128)S(1)}, u32[]{:S(2)}, u32[]{:S(2)}) collective-permute-start(f32[2,256,256]{2,1,0:T(8,128)S(1)} %get-tuple-element.19.z_mate), channel_id=1, source_target_pairs={{0,4},{4,0},{8,12},{12,8},{16,20},{20,16},{24,28},{28,24},{1,5},{5... | collective-permute-start | bytes 1572872 | tf_op jit(solution)/shard_map/ppermute | solution.py:341
  8.2 17.8 %collective-permute-start.3 = (f32[2,256,256]{2,1,0:T(8,128)S(1)}, f32[2,256,256]{2,1,0:T(8,128)S(1)}, u32[]{:S(2)}, u32[]{:S(2)}) collective-permute-start(f32[2,256,256]{2,1,0:T(8,128)S(1)} %get-tuple-element.22), channel_id=1, source_target_pairs={{1,0},{2,1},{3,2},{0,3},{5,4},{6,5},{7,6},{4,7},{9,8},{10,9},{11,1... | collective-permute-start | bytes 1572872 | tf_op jit(solution)/shard_map/ppermute | solution.py:349
  11.8 17.4 %collective-permute-start.7 = (f32[2,256,256]{2,1,0:T(8,128)S(1)}, f32[2,256,256]{2,1,0:T(8,128)S(1)}, u32[]{:S(2)}, u32[]{:S(2)}) collective-permute-start(f32[2,256,256]{2,1,0:T(8,128)S(1)} %get-tuple-element.17.z_peer), channel_id=1, source_target_pairs={{0,28},{4,8},{8,4},{12,16},{16,12},{20,24},{24,20},{28,0},{1,29},{... | collective-permute-start | bytes 1572872 | tf_op jit(solution)/shard_map/ppermute | solution.py:345
  19.4 6.6 %collective-permute-start.4 = (f32[256,256]{1,0:T(8,128)S(1)}, f32[256,256]{1,0:T(8,128)S(1)}, u32[]{:S(2)}, u32[]{:S(2)}) collective-permute-start(f32[256,256]{1,0:T(8,128)S(1)} %get-tuple-element.23.factor_own), channel_id=1, source_target_pairs={{0,4},{4,0},{8,12},{12,8},{16,20},{20,16},{24,28},{28,24},{1,5},{5... | collective-permute-start | bytes 786440 | tf_op jit(solution)/shard_map/ppermute | solution.py:341
  19.5 12.2 %collective-permute-start.6 = (f32[256,256]{1,0:T(8,128)S(1)}, f32[256,256]{1,0:T(8,128)S(1)}, u32[]{:S(2)}, u32[]{:S(2)}) collective-permute-start(f32[256,256]{1,0:T(8,128)S(1)} %get-tuple-element.23.factor_own), channel_id=1, source_target_pairs={{1,0},{2,1},{3,2},{0,3},{5,4},{6,5},{7,6},{4,7},{9,8},{10,9},{11,1... | collective-permute-start | bytes 786440 | tf_op jit(solution)/shard_map/ppermute | solution.py:349
  24.0 10.0 %collective-permute-start.5 = (f32[256,256]{1,0:T(8,128)S(1)}, f32[256,256]{1,0:T(8,128)S(1)}, u32[]{:S(2)}, u32[]{:S(2)}) collective-permute-start(f32[256,256]{1,0:T(8,128)S(1)} %get-tuple-element.25), channel_id=1, source_target_pairs={{0,28},{4,8},{8,4},{12,16},{16,12},{20,24},{24,20},{28,0},{1,29},{... | collective-permute-start | bytes 786440 | tf_op jit(solution)/shard_map/ppermute | solution.py:345

commit v6 on v5

--- a/solution.py
+++ b/solution.py
@@ -10,10 +10,10 @@
 PEER, OWN, MATE, SIDE = range(4)
 ROWS = 2
 SLOTS = 8
-PIECES = 4
 SLOT_AT, KEPT_AT, KEPT_PEER_AT, KEPT_MATE_AT, TABLE = 0, 16, 32, 36, 40
 LARGEST = float(jnp.finfo(jnp.bfloat16).max)
 VMEM_LIMIT = 24 * 2**20
+PEAK = 1.153e9
 
 
 def split(value):
@@ -89,62 +89,88 @@
         look_up(starts[MATE] + i, own_labels, None, KEPT_MATE_AT + i * ROWS)
 
 
+def quarter(i, j, size):
+    return slice(i * size, (i + 1) * size), slice(j * size, (j + 1) * size)
+
+
 def gather(slot_of, source, places):
     size = source.shape[1]
-    for i in range(ROWS):
-        rows = slice(i * size, (i + 1) * size)
-        for region, region_places in places.items():
+    for region, region_places in places.items():
+        for i in range(ROWS):
             for j in range(ROWS):
-                cols = slice(j * size, (j + 1) * size)
                 start = pl.multiple_of(slot_of(i, region * ROWS + j) * size, size)
                 block = source[i, :, pl.ds(start, size)]
                 for place in region_places:
-                    place[rows, cols] = block
-
-
-def pack_first_kernel(
-    row_devices, col_devices, pattern, order, sqrt_iterate,
-    y_peer, pattern_here, order_here, sqrt_here, sems,
-):
-    pieces = [(order, order_here), (pattern, pattern_here)]
-    height = sqrt_iterate.shape[1] // PIECES
-    for i in range(ROWS):
-        for piece in range(PIECES):
-            rows = pl.ds(piece * height, height)
-            pieces.append((sqrt_iterate.at[i, rows], sqrt_here.at[i, rows]))
-    copies = [
-        pltpu.make_async_copy(source, here, sems.at[at])
-        for at, (source, here) in enumerate(pieces)
-    ]
+                    place(i, j, size, block)
+
+
+def into(out):
+    def place(i, j, size, block):
+        rows, cols = quarter(i, j, size)
+        out[rows, cols] = block
+
+    return place
+
+
+def strip_peer(out):
+    def place(i, j, size, block):
+        out[i, :, j * size:(j + 1) * size] = block
+
+    return place
+
+
+def strip_own(out):
+    def place(i, j, size, block):
+        if i != j:
+            out[ROWS, :, i * size:(i + 1) * size] = block
+
+    return place
+
+
+def peer_part(strips):
+    return jnp.concatenate([strips[i] for i in range(ROWS)], axis=0)
+
+
+def own_part(strips, spread):
+    size = strips.shape[1]
+    beside = strips[ROWS]
+    return jnp.concatenate(
+        [
+            jnp.concatenate([spread[:size, :size], beside[:, :size]], axis=1),
+            jnp.concatenate([beside[:, size:], spread[size:, size:]], axis=1),
+        ],
+        axis=0,
+    )
+
+
+def diagonal_kernel(sqrt_iterate, inverse_iterate, diagonal, sems):
+    size = sqrt_iterate.shape[1]
+    copies = []
+    for source in (sqrt_iterate, inverse_iterate):
+        for i in range(ROWS):
+            at = len(copies)
+            copies.append(
+                pltpu.make_async_copy(source.at[i, :, pl.ds(0, size)], diagonal.at[at], sems.at[at])
+            )
+            copies[at].start()
     for copy in copies:
-        copy.start()
-    copies[0].wait()
-    copies[1].wait()
-    starts, labels = neighbours(row_devices, col_devices, order_here)
-    wanted = labels[PEER * ROWS:(OWN + 1) * ROWS]
-    slots = [find_slots(pattern_here, starts[OWN] + i, wanted) for i in range(ROWS)]
-    for copy in copies[2:]:
         copy.wait()
-    places = {PEER: (y_peer.at[0],), OWN: (y_peer.at[1],)}
-    gather(lambda i, j: slots[i][j], sqrt_here, places)
-
-
-def pack_rest_kernel(
-    row_devices, col_devices, pattern, keep, order, sqrt_iterate, inverse_iterate, y_peer,
-    table, z_peer, y_mate, z_mate, y_side, z_side, to_side,
+
+
+def pack_kernel(
+    row_devices, col_devices, pattern, keep, order, sqrt_iterate, inverse_iterate, after,
+    table, y_strips, z_strips, y_mate, mate_rest, y_side, z_side, to_side, last_slots,
     pattern_here, keep_here, order_here, sqrt_here, inverse_here, sems,
 ):
     copies = [
         pltpu.make_async_copy(source, here, sems.at[at])
         for at, (source, here) in enumerate((
             (order, order_here), (pattern, pattern_here), (keep, keep_here),
-            (inverse_iterate, inverse_here), (sqrt_iterate, sqrt_here),
+            (sqrt_iterate, sqrt_here), (inverse_iterate, inverse_here),
         ))
     ]
     for copy in copies:
         copy.start()
-    y_mate[1] = y_peer[1]
-    to_side[0] = y_peer[1]
     for copy in copies[:3]:
         copy.wait()
     fill_table(row_devices, col_devices, pattern_here, keep_here, order_here, table)
@@ -152,29 +178,61 @@
     def slot_of(i, j):
         return table[SLOT_AT + i * SLOTS + j]
 
+    line = lax.broadcasted_iota(jnp.int32, last_slots.shape, 0)
+    tile = jnp.zeros(last_slots.shape, jnp.int32)
+    for at, region in enumerate((PEER, SIDE)):
+        for i in range(ROWS):
+            for j in range(ROWS):
+                here = line == (at * ROWS + i) * ROWS + j
+                tile = jnp.where(here, slot_of(i, region * ROWS + j), tile)
+    last_slots[...] = tile
     copies[3].wait()
     places = {
-        PEER: (z_peer.at[0],), OWN: (z_peer.at[1], z_mate.at[1], to_side.at[1]),
-        MATE: (z_mate.at[0],), SIDE: (z_side,),
+        PEER: (strip_peer(y_strips),),
+        OWN: (strip_own(y_strips), into(mate_rest.at[0]), into(to_side.at[0])),
+        MATE: (into(y_mate),),
+        SIDE: (into(y_side),),
+    }
+    gather(slot_of, sqrt_here, places)
+    copies[4].wait()
+    places = {
+        PEER: (strip_peer(z_strips),),
+        OWN: (strip_own(z_strips), into(mate_rest.at[2]), into(to_side.at[1])),
+        MATE: (into(mate_rest.at[1]),),
+        SIDE: (into(z_side),),
     }
     gather(slot_of, inverse_here, places)
-    copies[4].wait()
-    gather(slot_of, sqrt_here, {MATE: (y_mate.at[0],), SIDE: (y_side,)})
-
-
-def factor_part_kernel(y_peer, z_peer, peer_y, part):
-    part[...] = products(
-        (split(z_peer[0]), split(peer_y[0])), (split(z_peer[1]), split(y_peer[1]))
-    )
-
-
-def factor_own_kernel(table, part, z_mate, mate_y, peer_y, factor_own, peer_term):
-    total = part[...] + products((split(z_mate[0]), split(mate_y[0])))
+
+
+def spread_kernel(diagonal, spread):
+    size = diagonal.shape[1]
+    for at in range(2):
+        for i in range(ROWS):
+            for j in range(ROWS):
+                rows, cols = quarter(i, j, size)
+                block = diagonal[at * ROWS + i]
+                spread[at, rows, cols] = block if i == j else jnp.zeros_like(block)
+
+
+def factor_part_kernel(
+    y_strips, mate_rest, z_strips, peer_y, peer_spread, own_total, peer_total
+):
+    z_own, z_to_peer = split(mate_rest[2]), split(peer_part(z_strips))
+    own_total[...] = products(
+        (z_to_peer, split(peer_part(peer_y))), (z_own, split(mate_rest[0]))
+    )
+    peer_total[...] = products(
+        (z_own, split(peer_part(y_strips))), (z_to_peer, split(own_part(peer_y, peer_spread[0])))
+    )
+
+
+def factor_own_kernel(table, part, mate_rest, mate_y, peer_y, factor_own, peer_term):
+    total = part[...] + products((split(mate_rest[1]), split(mate_y[...])))
     rows = lax.broadcasted_iota(jnp.int32, total.shape, 0)
     cols = lax.broadcasted_iota(jnp.int32, total.shape, 1)
     factor = jnp.where(rows == cols, 1.5, 0.0) + filtered(table, total, OWN, -0.5)
     factor_own[...] = factor
-    term = products((split(peer_y[0]), split(factor)))
+    term = products((split(peer_part(peer_y)), split(factor)))
     peer_term[...] = filtered(table, term, 0, None, KEPT_PEER_AT, ROWS)
 
 
@@ -184,29 +242,28 @@
 
 
 def middle_kernel(
-    table, y_peer, z_peer, y_mate, z_mate, y_side, z_side, mate_y, mate_z, peer_y, from_side,
-    factor_own, mate_factor,
+    table, y_strips, z_strips, y_mate, mate_rest, y_side, z_side, mate_y, from_mate,
+    peer_y, peer_total, from_side, factor_own, mate_factor,
     finished, partial, ready,
 ):
     def keep(at, parts):
         ready[at, 0], ready[at, 1] = parts
 
-    y_own, z_own = split(y_peer[1]), split(z_peer[1])
-    y_to_peer, z_to_peer = split(y_peer[0]), split(z_peer[0])
-    y_to_mate, z_to_mate = split(y_mate[0]), split(z_mate[0])
+    y_own, z_own = split(mate_rest[0]), split(mate_rest[2])
+    y_to_peer, z_to_peer = split(peer_part(y_strips)), split(peer_part(z_strips))
+    y_to_mate, z_to_mate = split(y_mate[...]), split(mate_rest[1])
     y_to_side, z_to_side = split(y_side[...]), split(z_side[...])
-    mate_y_mate, mate_y_own = split(mate_y[0]), split(mate_y[1])
-    mate_z_mate, mate_z_own = split(mate_z[0]), split(mate_z[1])
+    mate_y_mate, mate_y_own = split(mate_y[...]), split(from_mate[0])
+    mate_z_mate, mate_z_own = split(from_mate[1]), split(from_mate[2])
     f_own = split(factor_own[...])
     keep(Y_OWN, y_own)
     keep(Y_SIDE, y_to_side)
     keep(Y_PEER, y_to_peer)
-    keep(PEER_Y, split(peer_y[0]))
+    keep(PEER_Y, split(peer_part(peer_y)))
 
     total = products((z_own, y_to_mate), (z_to_mate, mate_y_own))
     f_mate = split(filtered(table, total, MATE, -0.5))
-    total = products((z_own, y_to_peer), (z_to_peer, split(peer_y[1])))
-    f_peer = split(filtered(table, total, PEER, -0.5))
+    f_peer = split(filtered(table, peer_total[...], PEER, -0.5))
     keep(F_PEER, f_peer)
     total = products((z_own, y_to_side), (z_to_side, split(from_side[0])))
     f_side = split(filtered(table, total, SIDE, -0.5))
@@ -257,7 +314,8 @@
 
 
 def peer_kernel(
-    table, finished, partial, ready, peer_z, sqrt_next, inverse_next, result, sems
+    table, finished, partial, ready, peer_z, peer_spread,
+    sqrt_next, inverse_next, result, sems,
 ):
     def held(at):
         return ready[at, 0], ready[at, 1]
@@ -266,7 +324,8 @@
     writer.write(finished.at[Y_MATE], sqrt_next, MATE)
     writer.write(finished.at[Z_MATE], inverse_next, MATE)
     writer.write(finished.at[Z_SIDE], inverse_next, SIDE)
-    peer_z_peer, peer_z_own = split(peer_z[0]), split(peer_z[1])
+    peer_z_peer = split(peer_part(peer_z))
+    peer_z_own = split(own_part(peer_z, peer_spread[1]))
     f_peer = held(F_PEER)
     value = partial[Z_PEER_PART] + products((f_peer, peer_z_own))
     writer.finish(value, inverse_next, PEER)
@@ -292,26 +351,31 @@
     writer.wait()
 
 
-def last_kernel(table, partial, term, unfinished, sqrt_next, table_here, result, sems):
-    fetch = pltpu.make_async_copy(table, table_here, sems.at[4])
-    fetch.start()
-    result[0] = partial[Y_PEER_PART] + term[...]
-    fetch.wait()
-    writer = Writer(table_here, result, sems)
-    writer.write(result.at[0], sqrt_next, PEER)
-    writer.wait()
+def last_kernel(slots, partial, term, unfinished, sqrt_next, result, sems):
+    size = sqrt_next.shape[1]
+    copies = []
+    for i in range(ROWS):
+        for j in range(ROWS):
+            at = len(copies)
+            rows, cols = quarter(i, j, size)
+            result[at] = partial[Y_PEER_PART, rows, cols] + term[rows, cols]
+            start = pl.multiple_of(slots[at, 0] * size, size)
+            out = sqrt_next.at[i, :, pl.ds(start, size)]
+            copies.append(pltpu.make_async_copy(result.at[at], out, sems.at[at]))
+            copies[at].start()
+    for copy in copies:
+        copy.wait()
 
 
 def call(
-    kernel, outs, operands, terms, scratch=(), hbm_in=(), any_in=(), hbm_out=False, in_place=None
+    kernel, outs, operands, micros=0, scratch=(), hbm_in=(), any_in=(), hbm_out=False, in_place=None
 ):
     def spec(array, outside=False, anywhere=False):
         if outside or anywhere:
             return pl.BlockSpec(memory_space=pltpu.HBM if outside else pl.ANY)
-        small = array.dtype == jnp.int32
+        small = array.dtype == jnp.int32 and array.ndim == 1
         return pl.BlockSpec(memory_space=pltpu.SMEM if small else pltpu.VMEM)
 
-    moved = sum(array.size * array.dtype.itemsize for array in (*outs, *operands))
     operands = [
         pltpu.with_memory_space_constraint(array, pltpu.HBM) if at in hbm_in else array
         for at, array in enumerate(operands)
@@ -325,7 +389,7 @@
         input_output_aliases={} if in_place is None else {in_place: 0},
         compiler_params=pltpu.CompilerParams(vmem_limit_bytes=VMEM_LIMIT),
         cost_estimate=pl.CostEstimate(
-            flops=terms * 6 * 256**3, bytes_accessed=moved, transcendentals=0
+            flops=int(micros * PEAK), bytes_accessed=0, transcendentals=0
         ),
     )(*operands)
 
@@ -352,45 +416,48 @@
         return jax.ShapeDtypeStruct(dims, dtype)
 
     one, pair = shape(size, size), shape(2, size, size)
-    labels = [
-        pltpu.SMEM(pattern.T.shape, jnp.int32),
-        pltpu.SMEM(keep_mask.T.shape, jnp.int32),
-        pltpu.SMEM(row_order.shape, jnp.int32),
-    ]
-    (y_peer,) = call(
-        functools.partial(pack_first_kernel, row_devices, col_devices),
-        (pair,),
-        (pattern.T, row_order, sqrt_iterate),
-        0,
+    (diagonal,) = call(
+        diagonal_kernel,
+        (shape(2 * ROWS, block, block),),
+        (sqrt_iterate, inverse_iterate),
+        scratch=[pltpu.SemaphoreType.DMA((2 * ROWS,))],
+        hbm_in=range(2),
+    )
+    peer_diagonal = to_peer(diagonal)
+    strips = shape(ROWS + 1, block, size)
+    (
+        table, y_strips, z_strips, y_mate, mate_rest, y_side, z_side, own_pair, last_slots
+    ) = call(
+        functools.partial(pack_kernel, row_devices, col_devices),
+        (
+            shape(TABLE, dtype=jnp.int32), strips, strips, one, shape(3, size, size), one, one,
+            pair, shape(8, 128, dtype=jnp.int32),
+        ),
+        (pattern.T, keep_mask.T, row_order, sqrt_iterate, inverse_iterate, diagonal),
         scratch=[
-            labels[0],
-            labels[2],
-            pltpu.VMEM(sqrt_iterate.shape, jnp.float32),
-            pltpu.SemaphoreType.DMA((2 + ROWS * PIECES,)),
-        ],
-        hbm_in=range(3),
-    )
-    peer_y = to_peer(y_peer)
-    table, z_peer, y_mate, z_mate, y_side, z_side, own_pair = call(
-        functools.partial(pack_rest_kernel, row_devices, col_devices),
-        (shape(TABLE, dtype=jnp.int32), pair, pair, pair, one, one, pair),
-        (pattern.T, keep_mask.T, row_order, sqrt_iterate, inverse_iterate, y_peer),
-        0,
-        scratch=[
-            *labels,
+            pltpu.SMEM(pattern.T.shape, jnp.int32),
+            pltpu.SMEM(keep_mask.T.shape, jnp.int32),
+            pltpu.SMEM(row_order.shape, jnp.int32),
             pltpu.VMEM(sqrt_iterate.shape, jnp.float32),
             pltpu.VMEM(inverse_iterate.shape, jnp.float32),
             pltpu.SemaphoreType.DMA((5,)),
         ],
         hbm_in=range(5),
-    )
-    peer_z = to_peer(z_peer)
+        any_in=(5,),
+    )
+    peer_y = to_peer(y_strips)
+    peer_z = to_peer(z_strips)
     mate_y = to_mate(y_mate)
-    mate_z = to_mate(z_mate)
+    from_mate = to_mate(mate_rest)
     from_side = to_side(own_pair)
-    (part,) = call(factor_part_kernel, (one,), (y_peer, z_peer, peer_y), 2)
+    (peer_spread,) = call(spread_kernel, (pair,), (peer_diagonal,), micros=3)
+    part, peer_total = call(
+        factor_part_kernel,
+        (one, one),
+        (y_strips, mate_rest, z_strips, peer_y, peer_spread),
+    )
     factor_own, peer_term = call(
-        factor_own_kernel, (one, one), (table, part, z_mate, mate_y, peer_y), 2
+        factor_own_kernel, (one, one), (table, part, mate_rest, mate_y, peer_y), micros=5
     )
     mate_factor = to_mate(factor_own)
     term = to_peer(peer_term)
@@ -402,38 +469,44 @@
             shape(5, 2, size, size, dtype=jnp.bfloat16),
         ),
         (
-            table, y_peer, z_peer, y_mate, z_mate, y_side, z_side, mate_y, mate_z, peer_y, from_side,
-            factor_own, mate_factor,
+            table, y_strips, z_strips, y_mate, mate_rest, y_side, z_side, mate_y, from_mate,
+            peer_y, peer_total, from_side, factor_own, mate_factor,
         ),
-        22,
-    )
+    )
+    output = shape(rows_dev, block, width)
     sqrt_next, inverse_next = call(
         peer_kernel,
-        (shape(rows_dev, block, width), shape(rows_dev, block, width)),
-        (table, finished, partial, ready, peer_z),
-        5,
+        (output, output),
+        (table, finished, partial, ready, peer_z, peer_spread),
         scratch=[pltpu.VMEM((3, size, size), jnp.float32), pltpu.SemaphoreType.DMA((24,))],
         hbm_out=True,
     )
-    for kernel, operands in (
-        (side_kernel, (table, partial, ready, side_factor)),
-        (last_kernel, (table, partial, term)),
-    ):
-        (sqrt_next,) = call(
-            kernel,
-            (shape(rows_dev, block, width),),
-            (*operands, sqrt_next),
-            1,
-            scratch=[
-                pltpu.SMEM((TABLE,), jnp.int32),
-                pltpu.VMEM((1, size, size), jnp.float32),
-                pltpu.SemaphoreType.DMA((5,)),
-            ],
-            hbm_in=(len(operands),),
-            any_in=(0,),
-            hbm_out=True,
-            in_place=len(operands),
-        )
+    (sqrt_next,) = call(
+        side_kernel,
+        (output,),
+        (table, partial, ready, side_factor, sqrt_next),
+        scratch=[
+            pltpu.SMEM((TABLE,), jnp.int32),
+            pltpu.VMEM((1, size, size), jnp.float32),
+            pltpu.SemaphoreType.DMA((5,)),
+        ],
+        hbm_in=(4,),
+        any_in=(0,),
+        hbm_out=True,
+        in_place=4,
+    )
+    (sqrt_next,) = call(
+        last_kernel,
+        (output,),
+        (last_slots, partial, term, sqrt_next),
+        scratch=[
+            pltpu.VMEM((ROWS * ROWS, block, block), jnp.float32),
+            pltpu.SemaphoreType.DMA((ROWS * ROWS,)),
+        ],
+        hbm_in=(3,),
+        hbm_out=True,
+        in_place=3,
+    )
     return sqrt_next, inverse_next
 
 

time: 35.5 us -> 36.6 us (1.031)
  starting transfers between devices: 14.6 us -> 17.2 us
  Pallas kernels: 13.5 us -> 12.6 us
  waiting for transfers between devices: 6.41 us -> 5.82 us
    ppermute x3 -> x4, starting transfers between devices: 5.89 us -> 7.85 us  [to_peer(): return lax.ppermute(value, 'row', route)]
    pallas_call x8 -> x9, Pallas kernels: 13.5 us -> 12.6 us  [call(): pl.pallas_call(kernel, out_shape=outs, in_specs=[spec(array, at in hbm_in...]
    ppermute x2, starting transfers between devices: 8.08 us -> 8.76 us  [to_side(): return lax.ppermute(value, 'col', route)]
    ppermute x3 -> x4, waiting for transfers between devices: 6.4 us -> 5.81 us  [to_peer(): return lax.ppermute(value, 'row', route)]
  transfers between devices with their start and end apart: 8 -> 9, of which waited for: 2 -> 2; matrix products, arithmetic and copies ran while one was open for 0% -> 0% of each run, Pallas kernels for 31% -> 30%
where the time goes in v6:
time: 36.6 us; the launch traced here: 36.4 us
  starting transfers between devices  17.2 us (47%)
  Pallas kernels  12.6 us (34%)
  waiting for transfers between devices  5.82 us (16%)
  between operations  0.73 us (2%)
    pallas_call x9, Pallas kernels, call(): pl.pallas_call(kernel, out_shape=outs, in_specs=[spec(array, at in hbm_in...  12.6 us
    ppermute x2, starting transfers between devices, to_side(): return lax.ppermute(value, 'col', route)  8.76 us
    ppermute x4, starting transfers between devices, to_peer(): return lax.ppermute(value, 'row', route)  7.85 us
    ppermute x4, waiting for transfers between devices, to_peer(): return lax.ppermute(value, 'row', route)  5.81 us
  transfers between devices with their start and end apart: 9, of which 2 were waited for; matrix products, arithmetic and copies ran while one was open for 0% of the time, Pallas kernels for 30%

profile of v6, /device:TPU:0, one launch (start us, length us, event | category | flops | bytes accessed | tf_op | source)
XLA Modules:
  0.0 36.4 jit_solution(4387080948779537725)
XLA Ops:
  0.6 1.0 %shard_map.68.after = f32[4,128,128]{2,1,0:T(8,128)S(1)} custom-call(f32[2,128,1024]{2,1,0:T(8,128)} %sqrt_iterate.3, f32[2,128,1024]{2,1,0:T(8,128)} %inverse_iterate.3), custom_call_target="tpu_custom_call" | custom-call | tf_op jit(solution)/shard_map/pallas_call | solution.py:383
  1.6 3.4 %collective-permute-start.3 = (f32[4,128,128]{2,1,0:T(8,128)S(1)}, f32[4,128,128]{2,1,0:T(8,128)S(1)}, u32[]{:S(2)}, u32[]{:S(2)}) collective-permute-start(f32[4,128,128]{2,1,0:T(8,128)S(1)} %shard_map.68.after), channel_id=1, source_target_pairs={{0,28},{4,8},{8,4},{12,16},{16,12},{20,24},{24,20},{28,0},{1,29},{... | collective-permute-start | bytes 786440 | tf_op jit(solution)/shard_map/ppermute | solution.py:409
  5.0 2.2 %shard_map.69 = (s32[40]{0:T(128)S(1)}, f32[3,128,256]{2,1,0:T(8,128)S(1)}, f32[3,128,256]{2,1,0:T(8,128)S(1)}, f32[256,256]{1,0:T(8,128)S(1)}, f32[3,256,256]{2...) custom-call(s32[8,64]{1,0:T(8,128)} %bitcast.2, ...), custom_call_target="tpu_custom_call" | custom-call | tf_op jit(solution)/shard_map/pallas_call | solution.py:383
  7.2 0.1 collective-permute-start.2
  7.3 0.1 collective-permute-start
  7.4 0.5 %collective-permute-start.1 = (f32[3,256,256]{2,1,0:T(8,128)S(1)}, f32[3,256,256]{2,1,0:T(8,128)S(1)}, u32[]{:S(2)}, u32[]{:S(2)}) collective-permute-start(f32[3,256,256]{2,1,0:T(8,128)S(1)} %get-tuple-element.25.mate_rest), channel_id=1, source_target_pairs={{0,4},{4,0},{8,12},{12,8},{16,20},{20,16},{24,28},{28,24},{1,5},{5... | collective-permute-start | bytes 2359304 | tf_op jit(solution)/shard_map/ppermute | solution.py:405
  7.9 4.3 %collective-permute-start.4 = (f32[2,256,256]{2,1,0:T(8,128)S(1)}, f32[2,256,256]{2,1,0:T(8,128)S(1)}, u32[]{:S(2)}, u32[]{:S(2)}) collective-permute-start(f32[2,256,256]{2,1,0:T(8,128)S(1)} %get-tuple-element.29), channel_id=1, source_target_pairs={{1,0},{2,1},{3,2},{0,3},{5,4},{6,5},{7,6},{4,7},{9,8},{10,9},{11,1... | collective-permute-start | bytes 1572872 | tf_op jit(solution)/shard_map/ppermute | solution.py:413
  12.1 0.0 collective-permute-done.3.diagonal
  12.1 2.4 %collective-permute-start.8 = (f32[3,128,256]{2,1,0:T(8,128)S(1)}, f32[3,128,256]{2,1,0:T(8,128)S(1)}, u32[]{:S(2)}, u32[]{:S(2)}) collective-permute-start(f32[3,128,256]{2,1,0:T(8,128)S(1)} %get-tuple-element.23.z_strips), channel_id=1, source_target_pairs={{0,28},{4,8},{8,4},{12,16},{16,12},{20,24},{24,20},{28,0},{1,29},{... | collective-permute-start | bytes 1179656 | tf_op jit(solution)/shard_map/ppermute | solution.py:409
  14.5 5.6 %collective-permute-done.2.peer_y = f32[3,128,256]{2,1,0:T(8,128)S(1)} collective-permute-done((f32[3,128,256]{2,1,0:T(8,128)S(1)}, f32[3,128,256]{2,1,0:T(8,128)S(1)}, u32[]{:S(2)}, u32[]{:S(2)}) %collective-permute-start.2) | collective-permute-done | bytes 393248 | tf_op jit(solution)/shard_map/ppermute | solution.py:409
  20.1 0.6 %shard_map.71 = (f32[256,256]{1,0:T(8,128)S(1)}, f32[256,256]{1,0:T(8,128)S(1)}) custom-call(f32[3,128,256]{2,1,0:T(8,128)S(1)} %get-tuple-element.22.y_strips, f32[3,256,256]{2,1,0:T(8,128)S(1)} %get-tuple-element.25.mate_rest, f32[3,128,256]{2,1,0:T(8,128)S(1)} %get-tuple-element.23.z_strips, f32[3,128,256]{2,1,0:T(8,128)S(1)} %collective-permute-done.2.peer_y, ...), custom_call_target="tpu_custom_call" | custom-call | tf_op jit(solution)/shard_map/pallas_call | solution.py:383
  20.8 0.0 collective-permute-done.mate_y
  20.8 1.2 %shard_map.72 = (f32[256,256]{1,0:T(8,128)S(1)}, f32[256,256]{1,0:T(8,128)S(1)}) custom-call(s32[40]{0:T(128)S(1)} %get-tuple-element.21.table, f32[256,256]{1,0:T(8,128)S(1)} %get-tuple-element.30.part, f32[3,256,256]{2,1,0:T(8,128)S(1)} %get-tuple-element.25.mate_rest, f32[256,256]{1,0:T(8,128)S(1)} %collective-permute-done.mate_y, ...), custom_call_target="tpu_custom_call" | custom-call | flops 5765000192 | tf_op jit(solution)/shard_map/pallas_call | solution.py:383
  22.0 0.1 collective-permute-start.5
  22.1 4.5 %collective-permute-start.7 = (f32[256,256]{1,0:T(8,128)S(1)}, f32[256,256]{1,0:T(8,128)S(1)}, u32[]{:S(2)}, u32[]{:S(2)}) collective-permute-start(f32[256,256]{1,0:T(8,128)S(1)} %get-tuple-element.31.factor_own), channel_id=1, source_target_pairs={{1,0},{2,1},{3,2},{0,3},{5,4},{6,5},{7,6},{4,7},{9,8},{10,9},{11,1... | collective-permute-start | bytes 786440 | tf_op jit(solution)/shard_map/ppermute | solution.py:413
  26.6 2.0 %collective-permute-start.6 = (f32[256,256]{1,0:T(8,128)S(1)}, f32[256,256]{1,0:T(8,128)S(1)}, u32[]{:S(2)}, u32[]{:S(2)}) collective-permute-start(f32[256,256]{1,0:T(8,128)S(1)} %get-tuple-element.33), channel_id=1, source_target_pairs={{0,28},{4,8},{8,4},{12,16},{16,12},{20,24},{24,20},{28,0},{1,29},{... | collective-permute-start | bytes 786440 | tf_op jit(solution)/shard_map/ppermute | solution.py:409
  28.6 0.0 collective-permute-done.5.mate_factor
  28.6 0.0 collective-permute-done.1.from_mate
  28.6 3.0 %shard_map.73 = (f32[3,256,256]{2,1,0:T(8,128)S(1)}, f32[5,256,256]{2,1,0:T(8,128)S(1)}, bf16[5,2,256,256]{3,2,1,0:T(8,128)(2,1)S(1)}) custom-call(s32[40]{0:T(128)S(1)} %get-tuple-element.21.table, f32[3,128,256]{2,1,0:T(8,128)S(1)} %get-tuple-element.22.y_strips, f32[3,128,256]{2,1,0:T(8,128)S(1)} %get-tuple-element.23.z_strips, ...), custom_call_target="tpu_custom_call" | custom-call | tf_op jit(solution)/shard_map/pallas_call | solution.py:383
  31.6 2.5 %shard_map.74 = (f32[2,128,1024]{2,1,0:T(8,128)}, f32[2,128,1024]{2,1,0:T(8,128)}) custom-call(s32[40]{0:T(128)S(1)} %get-tuple-element.21.table, f32[3,256,256]{2,1,0:T(8,128)S(1)} %get-tuple-element.35.finished, f32[5,256,256]{2,1,0:T(8,128)S(1)} %get-tuple-element.32.partial, bf16[5,2,256,256]{3,2,1,0:T(8,128)(2,1)S(1)} %get-tuple-element.34.ready, ...), custom_call_target="tpu_custom_call" | custom-call | tf_op jit(solution)/shard_map/pallas_call | solution.py:383
  34.1 0.0 collective-permute-done.7.factor
  34.1 1.3 %shard_map.75.unfinished = f32[2,128,1024]{2,1,0:T(8,128)} custom-call(s32[40]{0:T(128)S(1)} %get-tuple-element.21.table, f32[5,256,256]{2,1,0:T(8,128)S(1)} %get-tuple-element.32.partial, bf16[5,2,256,256]{3,2,1,0:T(8,128)(2,1)S(1)} %get-tuple-element.34.ready, f32[256,256]{1,0:T(8,128)S(1)} %collective-permute-done.7.factor, ...), custom_call_target="tpu_custom_call", output_to_operand_aliasing={{}: (4, {})} | custom-call | tf_op jit(solution)/shard_map/pallas_call | solution.py:383
  35.4 0.2 collective-permute-done.6.term
  35.7 0.8 %shard_map.76 = f32[2,128,1024]{2,1,0:T(8,128)} custom-call(s32[8,128]{1,0:T(8,128)S(1)} %get-tuple-element.20.slots, f32[5,256,256]{2,1,0:T(8,128)S(1)} %get-tuple-element.32.partial, f32[256,256]{1,0:T(8,128)S(1)} %collective-permute-done.6.term, f32[2,128,1024]{2,1,0:T(8,128)} %shard_map.75.unfinished), custom_call_target="tpu_custom_call", output_to_operand_aliasing={{}: (3, {})} | custom-call | tf_op jit(solution)/shard_map/pallas_call | solution.py:383
  (3 shorter events, 0.0 us)
Async XLA Ops:
  1.6 10.5 %collective-permute-start.3 = (f32[4,128,128]{2,1,0:T(8,128)S(1)}, f32[4,128,128]{2,1,0:T(8,128)S(1)}, u32[]{:S(2)}, u32[]{:S(2)}) collective-permute-start(f32[4,128,128]{2,1,0:T(8,128)S(1)} %shard_map.68.after), channel_id=1, source_target_pairs={{0,28},{4,8},{8,4},{12,16},{16,12},{20,24},{24,20},{28,0},{1,29},{... | collective-permute-start | bytes 786440 | tf_op jit(solution)/shard_map/ppermute | solution.py:409
  7.2 12.9 %collective-permute-start.2 = (f32[3,128,256]{2,1,0:T(8,128)S(1)}, f32[3,128,256]{2,1,0:T(8,128)S(1)}, u32[]{:S(2)}, u32[]{:S(2)}) collective-permute-start(f32[3,128,256]{2,1,0:T(8,128)S(1)} %get-tuple-element.22.y_strips), channel_id=1, source_target_pairs={{0,28},{4,8},{8,4},{12,16},{16,12},{20,24},{24,20},{28,0},{1,29},{... | collective-permute-start | bytes 1179656 | tf_op jit(solution)/shard_map/ppermute | solution.py:409
  7.3 13.5 %collective-permute-start = (f32[256,256]{1,0:T(8,128)S(1)}, f32[256,256]{1,0:T(8,128)S(1)}, u32[]{:S(2)}, u32[]{:S(2)}) collective-permute-start(f32[256,256]{1,0:T(8,128)S(1)} %get-tuple-element.24.y_mate), channel_id=1, source_target_pairs={{0,4},{4,0},{8,12},{12,8},{16,20},{20,16},{24,28},{28,24},{1,5},{5... | collective-permute-start | bytes 786440 | tf_op jit(solution)/shard_map/ppermute | solution.py:405
  7.4 21.2 %collective-permute-start.1 = (f32[3,256,256]{2,1,0:T(8,128)S(1)}, f32[3,256,256]{2,1,0:T(8,128)S(1)}, u32[]{:S(2)}, u32[]{:S(2)}) collective-permute-start(f32[3,256,256]{2,1,0:T(8,128)S(1)} %get-tuple-element.25.mate_rest), channel_id=1, source_target_pairs={{0,4},{4,0},{8,12},{12,8},{16,20},{20,16},{24,28},{28,24},{1,5},{5... | collective-permute-start | bytes 2359304 | tf_op jit(solution)/shard_map/ppermute | solution.py:405
  7.9 18.7 %collective-permute-start.4 = (f32[2,256,256]{2,1,0:T(8,128)S(1)}, f32[2,256,256]{2,1,0:T(8,128)S(1)}, u32[]{:S(2)}, u32[]{:S(2)}) collective-permute-start(f32[2,256,256]{2,1,0:T(8,128)S(1)} %get-tuple-element.29), channel_id=1, source_target_pairs={{1,0},{2,1},{3,2},{0,3},{5,4},{6,5},{7,6},{4,7},{9,8},{10,9},{11,1... | collective-permute-start | bytes 1572872 | tf_op jit(solution)/shard_map/ppermute | solution.py:413
  12.1 19.5 %collective-permute-start.8 = (f32[3,128,256]{2,1,0:T(8,128)S(1)}, f32[3,128,256]{2,1,0:T(8,128)S(1)}, u32[]{:S(2)}, u32[]{:S(2)}) collective-permute-start(f32[3,128,256]{2,1,0:T(8,128)S(1)} %get-tuple-element.23.z_strips), channel_id=1, source_target_pairs={{0,28},{4,8},{8,4},{12,16},{16,12},{20,24},{24,20},{28,0},{1,29},{... | collective-permute-start | bytes 1179656 | tf_op jit(solution)/shard_map/ppermute | solution.py:409
  22.0 6.6 %collective-permute-start.5 = (f32[256,256]{1,0:T(8,128)S(1)}, f32[256,256]{1,0:T(8,128)S(1)}, u32[]{:S(2)}, u32[]{:S(2)}) collective-permute-start(f32[256,256]{1,0:T(8,128)S(1)} %get-tuple-element.31.factor_own), channel_id=1, source_target_pairs={{0,4},{4,0},{8,12},{12,8},{16,20},{20,16},{24,28},{28,24},{1,5},{5... | collective-permute-start | bytes 786440 | tf_op jit(solution)/shard_map/ppermute | solution.py:405
  22.1 12.0 %collective-permute-start.7 = (f32[256,256]{1,0:T(8,128)S(1)}, f32[256,256]{1,0:T(8,128)S(1)}, u32[]{:S(2)}, u32[]{:S(2)}) collective-permute-start(f32[256,256]{1,0:T(8,128)S(1)} %get-tuple-element.31.factor_own), channel_id=1, source_target_pairs={{1,0},{2,1},{3,2},{0,3},{5,4},{6,5},{7,6},{4,7},{9,8},{10,9},{11,1... | collective-permute-start | bytes 786440 | tf_op jit(solution)/shard_map/ppermute | solution.py:413
  26.6 9.1 %collective-permute-start.6 = (f32[256,256]{1,0:T(8,128)S(1)}, f32[256,256]{1,0:T(8,128)S(1)}, u32[]{:S(2)}, u32[]{:S(2)}) collective-permute-start(f32[256,256]{1,0:T(8,128)S(1)} %get-tuple-element.33), channel_id=1, source_target_pairs={{0,28},{4,8},{8,4},{12,16},{16,12},{20,24},{24,20},{28,0},{1,29},{... | collective-permute-start | bytes 786440 | tf_op jit(solution)/shard_map/ppermute | solution.py:409

commit v7 on v6

v7 whole, which is shorter than its diff:
```python
import functools

import jax
import jax.numpy as jnp
from jax import lax
from jax.experimental import pallas as pl
from jax.experimental.pallas import tpu as pltpu
from jax.sharding import PartitionSpec as P

PEER, OWN, MATE, SIDE = range(4)
ROWS = 2
SLOTS = 8
KEPT_PEER_AT, KEPT_MATE_AT, KEPT_LINES = 16, 20, 24
LARGEST = float(jnp.finfo(jnp.bfloat16).max)
VMEM_LIMIT = 24 * 2**20
PEAK = 1.153e9


def split(value):
    clipped = jnp.clip(value, -LARGEST, LARGEST)
    high = clipped.astype(jnp.bfloat16)
    low = (value - high.astype(jnp.float32)).astype(jnp.bfloat16)
    return high, low


def products(*pairs):
    left = [part for (high, low), _ in pairs for part in (high, low, high)]
    right = [part for _, (high, low) in pairs for part in (high, high, low)]
    return jnp.dot(
        jnp.concatenate(left, axis=1),
        jnp.concatenate(right, axis=0),
        preferred_element_type=jnp.float32,
    )


def filtered(kept, value, region, scale=None, base=0, width=SLOTS):
    size = value.shape[0] // ROWS
    rows = []
    for i in range(ROWS):
        row = []
        for j in range(ROWS):
            at = base + i * width + region * ROWS + j
            flag = kept[at:at + 1, :]
            if scale is not None:
                flag = flag * scale
            row.append(value[i * size:(i + 1) * size, j * size:(j + 1) * size] * flag)
        rows.append(jnp.concatenate(row, axis=1))
    return jnp.concatenate(rows, axis=0)


def neighbours(row_devices, col_devices, order):
    row = lax.axis_index("row")
    col = lax.axis_index("col")
    odd = lax.rem(row, 2)

    def first(row_of, col_of):
        return (lax.rem(row_of, row_devices) * col_devices + lax.rem(col_of, col_devices)) * ROWS

    starts = (
        first(row + row_devices - 1 + 2 * odd, col),
        first(row, col),
        first(row + 1 - 2 * odd, col),
        first(row, col + 1),
    )
    return starts, [order[start + j] for start in starts for j in range(ROWS)]


def find_slots(pattern, stored, wanted):
    slots = [jnp.int32(0)] * len(wanted)
    for k in range(SLOTS):
        label = pattern[k, stored]
        slots = [jnp.where(label == want, k, slot) for want, slot in zip(wanted, slots)]
    return slots


def look_up(row_devices, col_devices, pattern, keep, order, slots, kept):
    starts, labels = neighbours(row_devices, col_devices, order)
    own_labels = labels[OWN * ROWS:(OWN + 1) * ROWS]

    def write_flags(stored, found, line):
        for j, slot in enumerate(found):
            flag = ((slot == 0) | (keep[slot, stored] == 1)).astype(jnp.float32)
            kept[line + j:line + j + 1, :] = jnp.full((1, kept.shape[1]), flag)

    result = []
    for i in range(ROWS):
        found = find_slots(pattern, starts[OWN] + i, labels)
        result.append(found)
        for j, slot in enumerate(found):
            line = i * SLOTS + j
            slots[line:line + 1, :] = jnp.full((1, slots.shape[1]), slot)
        write_flags(starts[OWN] + i, found, i * SLOTS)
        for region, line in ((PEER, KEPT_PEER_AT), (MATE, KEPT_MATE_AT)):
            stored = starts[region] + i
            write_flags(stored, find_slots(pattern, stored, own_labels), line + i * ROWS)
    return result


def quarter(i, j, size):
    return slice(i * size, (i + 1) * size), slice(j * size, (j + 1) * size)


def gather(slot_of, source, places):
    size = source.shape[1]
    for region, region_places in places.items():
        for i in range(ROWS):
            for j in range(ROWS):
                start = pl.multiple_of(slot_of(i, region * ROWS + j) * size, size)
                block = source[i, :, pl.ds(start, size)]
                for place in region_places:
                    place(i, j, size, block)


def into(out):
    def place(i, j, size, block):
        rows, cols = quarter(i, j, size)
        out[rows, cols] = block

    return place


def strip_peer(out):
    def place(i, j, size, block):
        out[i, :, j * size:(j + 1) * size] = block

    return place


def strip_own(out):
    def place(i, j, size, block):
        if i != j:
            out[ROWS, :, i * size:(i + 1) * size] = block

    return place


def peer_part(strips):
    return jnp.concatenate([strips[i] for i in range(ROWS)], axis=0)


def own_part(strips, spread):
    size = strips.shape[1]
    beside = strips[ROWS]
    return jnp.concatenate(
        [
            jnp.concatenate([spread[:size, :size], beside[:, :size]], axis=1),
            jnp.concatenate([beside[:, size:], spread[size:, size:]], axis=1),
        ],
        axis=0,
    )


def diagonal_kernel(sqrt_iterate, inverse_iterate, diagonal, sems):
    size = sqrt_iterate.shape[1]
    copies = []
    for source in (sqrt_iterate, inverse_iterate):
        for i in range(ROWS):
            at = len(copies)
            copies.append(
                pltpu.make_async_copy(source.at[i, :, pl.ds(0, size)], diagonal.at[at], sems.at[at])
            )
            copies[at].start()
    for copy in copies:
        copy.wait()


def pack_kernel(
    row_devices, col_devices, pattern, keep, order, sqrt_iterate, inverse_iterate, after,
    slots, kept, y_strips, z_strips, y_mate, mate_rest, y_side, z_side, to_side,
    pattern_here, keep_here, order_here, sqrt_here, inverse_here, sems,
):
    copies = [
        pltpu.make_async_copy(source, here, sems.at[at])
        for at, (source, here) in enumerate((
            (order, order_here), (pattern, pattern_here), (keep, keep_here),
            (sqrt_iterate, sqrt_here), (inverse_iterate, inverse_here),
        ))
    ]
    for copy in copies:
        copy.start()
    for copy in copies[:3]:
        copy.wait()
    found = look_up(
        row_devices, col_devices, pattern_here, keep_here, order_here, slots, kept
    )

    def slot_of(i, j):
        return found[i][j]

    copies[3].wait()
    places = {
        PEER: (strip_peer(y_strips),),
        OWN: (strip_own(y_strips), into(mate_rest.at[0]), into(to_side.at[0])),
        MATE: (into(y_mate),),
        SIDE: (into(y_side),),
    }
    gather(slot_of, sqrt_here, places)
    copies[4].wait()
    places = {
        PEER: (strip_peer(z_strips),),
        OWN: (strip_own(z_strips), into(mate_rest.at[2]), into(to_side.at[1])),
        MATE: (into(mate_rest.at[1]),),
        SIDE: (into(z_side),),
    }
    gather(slot_of, inverse_here, places)


def spread_kernel(diagonal, spread):
    size = diagonal.shape[1]
    for at in range(2):
        for i in range(ROWS):
            for j in range(ROWS):
                rows, cols = quarter(i, j, size)
                block = diagonal[at * ROWS + i]
                spread[at, rows, cols] = block if i == j else jnp.zeros_like(block)


M_OWN, M_Y_OWN, M_Y_MATE, M_Z_OWN, M_Z_MATE = range(5)


def mate_kernel(
    kept, y_mate, mate_rest, mate_y, from_mate, after, mate_terms
):
    y_own, z_to_mate, z_own = (split(mate_rest[at]) for at in range(3))
    y_to_mate = split(y_mate[...])
    mate_y_mate, mate_y_own = split(mate_y[...]), split(from_mate[0])
    mate_z_mate, mate_z_own = split(from_mate[1]), split(from_mate[2])
    mate_terms[M_OWN] = products((z_own, y_own), (z_to_mate, mate_y_mate))
    total = products((z_own, y_to_mate), (z_to_mate, mate_y_own))
    f_mate = split(filtered(kept, total, MATE, -0.5))
    total = products((mate_z_own, mate_y_mate), (mate_z_mate, y_own))
    mate_f_mate = split(filtered(kept, total, 0, -0.5, KEPT_MATE_AT, ROWS))
    mate_terms[M_Y_OWN] = products((y_to_mate, mate_f_mate))
    mate_terms[M_Y_MATE] = products((y_own, f_mate))
    mate_terms[M_Z_OWN] = products((f_mate, mate_z_mate))
    mate_terms[M_Z_MATE] = products((f_mate, mate_z_own))


def factor_own_kernel(kept, mate_terms, z_strips, peer_y, factor_own, peer_term):
    peer_y_peer = split(peer_part(peer_y))
    total = mate_terms[M_OWN] + products((split(peer_part(z_strips)), peer_y_peer))
    rows = lax.broadcasted_iota(jnp.int32, total.shape, 0)
    cols = lax.broadcasted_iota(jnp.int32, total.shape, 1)
    factor = jnp.where(rows == cols, 1.5, 0.0) + filtered(kept, total, OWN, -0.5)
    factor_own[...] = factor
    term = products((peer_y_peer, split(factor)))
    peer_term[...] = filtered(kept, term, 0, None, KEPT_PEER_AT, ROWS)


Y_MATE, Z_MATE, Z_SIDE = range(3)
Y_OWN_PART, Y_PEER_PART, Y_SIDE_PART, Z_OWN_PART, Z_PEER_PART = range(5)
Y_PEER, Y_OWN, Y_SIDE, F_PEER, PEER_Y = range(5)


def middle_kernel(
    kept, y_strips, z_strips, y_mate, mate_rest, y_side, z_side, mate_terms,
    peer_y, peer_spread, from_side, factor_own, mate_factor,
    finished, partial, ready,
):
    def keep(at, parts):
        ready[at, 0], ready[at, 1] = parts

    y_own, z_to_mate, z_own = (split(mate_rest[at]) for at in range(3))
    y_to_peer, z_to_peer = split(peer_part(y_strips)), split(peer_part(z_strips))
    y_to_side, z_to_side = split(y_side[...]), split(z_side[...])
    f_own = split(factor_own[...])
    keep(Y_OWN, y_own)
    keep(Y_SIDE, y_to_side)
    keep(Y_PEER, y_to_peer)
    keep(PEER_Y, split(peer_part(peer_y)))

    peer_y_own = split(own_part(peer_y, peer_spread[0]))
    total = products((z_own, y_to_peer), (z_to_peer, peer_y_own))
    f_peer = split(filtered(kept, total, PEER, -0.5))
    keep(F_PEER, f_peer)
    total = products((z_own, y_to_side), (z_to_side, split(from_side[0])))
    f_side = split(filtered(kept, total, SIDE, -0.5))

    partial[Y_PEER_PART] = filtered(kept, products((y_own, f_peer)), PEER)
    partial[Y_SIDE_PART] = products((y_own, f_side))
    partial[Y_OWN_PART] = mate_terms[M_Y_OWN] + products((y_own, f_own))
    partial[Z_PEER_PART] = products((f_own, z_to_peer))
    partial[Z_OWN_PART] = mate_terms[M_Z_OWN] + products((f_own, z_own))
    value = mate_terms[M_Y_MATE] + products((split(y_mate[...]), split(mate_factor[...])))
    finished[Y_MATE] = filtered(kept, value, MATE)
    value = mate_terms[M_Z_MATE] + products((f_own, z_to_mate))
    finished[Z_MATE] = filtered(kept, value, MATE)
    value = products((f_own, z_to_side), (f_side, split(from_side[1])))
    finished[Z_SIDE] = filtered(kept, value, SIDE)


class Writer:
    def __init__(self, slots, kept, result, sems):
        self.slots, self.kept, self.result, self.sems = slots, kept, result, sems
        self.started = []
        self.held = 0

    def write(self, source, out, region):
        size = out.shape[1]
        for i in range(ROWS):
            for j in range(ROWS):
                rows, cols = quarter(i, j, size)
                slot = self.slots[i * SLOTS + region * ROWS + j, 0]
                copy = pltpu.make_async_copy(
                    source.at[rows, cols],
                    out.at[i, :, pl.ds(pl.multiple_of(slot * size, size), size)],
                    self.sems.at[len(self.started)],
                )
                copy.start()
                self.started.append(copy)

    def finish(self, value, out, region):
        place = self.result.at[self.held]
        self.held += 1
        place[...] = value if self.kept is None else filtered(self.kept, value, region)
        self.write(place, out, region)

    def wait(self):
        for copy in self.started:
            copy.wait()


def peer_kernel(
    slots, kept, finished, partial, ready, peer_z, peer_spread,
    sqrt_next, inverse_next, result, sems,
):
    def held(at):
        return ready[at, 0], ready[at, 1]

    writer = Writer(slots, kept, result, sems)
    writer.write(finished.at[Y_MATE], sqrt_next, MATE)
    writer.write(finished.at[Z_MATE], inverse_next, MATE)
    writer.write(finished.at[Z_SIDE], inverse_next, SIDE)
    peer_z_peer = split(peer_part(peer_z))
    peer_z_own = split(own_part(peer_z, peer_spread[1]))
    f_peer = held(F_PEER)
    value = partial[Z_PEER_PART] + products((f_peer, peer_z_own))
    writer.finish(value, inverse_next, PEER)
    value = partial[Z_OWN_PART] + products((f_peer, peer_z_peer))
    writer.finish(value, inverse_next, OWN)
    total = products((peer_z_own, held(PEER_Y)), (peer_z_peer, held(Y_OWN)))
    peer_f_peer = split(filtered(kept, total, 0, -0.5, KEPT_PEER_AT, ROWS))
    value = partial[Y_OWN_PART] + products((held(Y_PEER), peer_f_peer))
    writer.finish(value, sqrt_next, OWN)
    writer.wait()


def side_kernel(slots, kept, partial, ready, factor, unfinished, sqrt_next, result, sems):
    left = (ready[Y_SIDE, 0], ready[Y_SIDE, 1])
    value = partial[Y_SIDE_PART] + products((left, split(factor[...])))
    writer = Writer(slots, kept, result, sems)
    writer.finish(value, sqrt_next, SIDE)
    writer.wait()


def last_kernel(slots, partial, term, unfinished, sqrt_next, result, sems):
    writer = Writer(slots, None, result, sems)
    writer.finish(partial[Y_PEER_PART] + term[...], sqrt_next, PEER)
    writer.wait()


def call(
    kernel, outs, operands, micros=0, scratch=(), hbm_in=(), any_in=(), hbm_out=False, in_place=None
):
    def spec(space=pltpu.VMEM):
        return pl.BlockSpec(memory_space=space)

    operands = [
        pltpu.with_memory_space_constraint(array, pltpu.HBM) if at in hbm_in else array
        for at, array in enumerate(operands)
    ]
    return pl.pallas_call(
        kernel,
        out_shape=outs,
        in_specs=[
            spec(pltpu.HBM if at in hbm_in else pl.ANY if at in any_in else pltpu.VMEM)
            for at in range(len(operands))
        ],
        out_specs=tuple(spec(pltpu.HBM if hbm_out else pltpu.VMEM) for _ in outs),
        scratch_shapes=scratch,
        input_output_aliases={} if in_place is None else {in_place: 0},
        compiler_params=pltpu.CompilerParams(vmem_limit_bytes=VMEM_LIMIT),
        cost_estimate=pl.CostEstimate(
            flops=int(micros * PEAK), bytes_accessed=0, transcendentals=0
        ),
    )(*operands)


def local(sqrt_iterate, inverse_iterate, pattern, keep_mask, row_order):
    rows_dev, block, width = sqrt_iterate.shape
    row_devices, col_devices = lax.axis_size("row"), lax.axis_size("col")
    assert rows_dev == ROWS and width == SLOTS * block and pattern.shape[1] == SLOTS
    assert row_devices > 3 and row_devices % 2 == 0 and col_devices > 2
    size = ROWS * block

    def to_mate(value):
        return lax.ppermute(value, "row", [(i, i ^ 1) for i in range(row_devices)])

    def to_peer(value):
        route = [(i, (i + (1 if i % 2 else -1)) % row_devices) for i in range(row_devices)]
        return lax.ppermute(value, "row", route)

    def to_side(value):
        route = [((i + 1) % col_devices, i) for i in range(col_devices)]
        return lax.ppermute(value, "col", route)

    def shape(*dims, dtype=jnp.float32):
        return jax.ShapeDtypeStruct(dims, dtype)

    one, pair = shape(size, size), shape(2, size, size)
    (diagonal,) = call(
        diagonal_kernel,
        (shape(2 * ROWS, block, block),),
        (sqrt_iterate, inverse_iterate),
        scratch=[pltpu.SemaphoreType.DMA((2 * ROWS,))],
        hbm_in=range(2),
    )
    peer_diagonal = to_peer(diagonal)
    strips = shape(ROWS + 1, block, size)
    slots, kept, y_strips, z_strips, y_mate, mate_rest, y_side, z_side, own_pair = call(
        functools.partial(pack_kernel, row_devices, col_devices),
        (
            shape(ROWS * SLOTS, block, dtype=jnp.int32), shape(KEPT_LINES, block),
            strips, strips, one, shape(3, size, size), one, one, pair,
        ),
        (pattern.T, keep_mask.T, row_order, sqrt_iterate, inverse_iterate, diagonal),
        scratch=[
            pltpu.SMEM(pattern.T.shape, jnp.int32),
            pltpu.SMEM(keep_mask.T.shape, jnp.int32),
            pltpu.SMEM(row_order.shape, jnp.int32),
            pltpu.VMEM(sqrt_iterate.shape, jnp.float32),
            pltpu.VMEM(inverse_iterate.shape, jnp.float32),
            pltpu.SemaphoreType.DMA((5,)),
        ],
        hbm_in=range(5),
        any_in=(5,),
    )
    peer_y = to_peer(y_strips)
    peer_z = to_peer(z_strips)
    mate_y = to_mate(y_mate)
    from_mate = to_mate(mate_rest)
    from_side = to_side(own_pair)
    (peer_spread,) = call(spread_kernel, (pair,), (peer_diagonal,), micros=10)
    (mate_terms,) = call(
        mate_kernel,
        (shape(5, size, size),),
        (kept, y_mate, mate_rest, mate_y, from_mate, peer_spread),
        any_in=(5,),
    )
    factor_own, peer_term = call(
        factor_own_kernel, (one, one), (kept, mate_terms, z_strips, peer_y), micros=5
    )
    mate_factor = to_mate(factor_own)
    term = to_peer(peer_term)
    side_factor = to_side(factor_own)
    finished, partial, ready = call(
        middle_kernel,
        (
            shape(3, size, size), shape(5, size, size),
            shape(5, 2, size, size, dtype=jnp.bfloat16),
        ),
        (
            kept, y_strips, z_strips, y_mate, mate_rest, y_side, z_side, mate_terms,
            peer_y, peer_spread, from_side, factor_own, mate_factor,
        ),
    )
    output = shape(rows_dev, block, width)

    def writing(blocks):
        return [
            pltpu.VMEM((blocks, size, size), jnp.float32),
            pltpu.SemaphoreType.DMA((24,)),
        ]

    sqrt_next, inverse_next = call(
        peer_kernel,
        (output, output),
        (slots, kept, finished, partial, ready, peer_z, peer_spread),
        scratch=writing(3),
        hbm_out=True,
    )
    (sqrt_next,) = call(
        side_kernel,
        (output,),
        (slots, kept, partial, ready, side_factor, sqrt_next),
        scratch=writing(1),
        hbm_in=(5,),
        hbm_out=True,
        in_place=5,
    )
    (sqrt_next,) = call(
        last_kernel,
        (output,),
        (slots, partial, term, sqrt_next),
        scratch=writing(1),
        hbm_in=(3,),
        hbm_out=True,
        in_place=3,
    )
    return sqrt_next, inverse_next


def solution(mesh):
    rows = P(("row", "col"), None, None)
    return jax.shard_map(
        local,
        mesh=mesh,
        in_specs=(rows, rows, P(), P(), P()),
        out_specs=(rows, rows),
        check_vma=False,
    )
```

time: 36.6 us -> 35.6 us (0.973)
  Pallas kernels: 12.6 us -> 11.2 us
  starting transfers between devices: 17.2 us -> 17.7 us
    pallas_call x9, Pallas kernels: 12.6 us -> 11.2 us  [call(): pl.pallas_call(kernel, out_shape=outs, in_specs=[spec(pltpu.HBM if at in...]
    ppermute x4, starting transfers between devices: 7.85 us -> 8.47 us  [to_peer(): return lax.ppermute(value, 'row', route)]
  transfers between devices with their start and end apart: 9 -> 9, of which waited for: 2 -> 3; matrix products, arithmetic and copies ran while one was open for 0% -> 0% of each run, Pallas kernels for 30% -> 26%
where the time goes in v7:
time: 35.6 us; the launch traced here: 35.4 us
  starting transfers between devices  17.7 us (50%)
  Pallas kernels  11.2 us (31%)
  waiting for transfers between devices  5.8 us (16%)
  between operations  0.73 us (2%)
    pallas_call x9, Pallas kernels, call(): pl.pallas_call(kernel, out_shape=outs, in_specs=[spec(pltpu.HBM if at in...  11.2 us
    ppermute x2, starting transfers between devices, to_side(): return lax.ppermute(value, 'col', route)  8.57 us
    ppermute x4, starting transfers between devices, to_peer(): return lax.ppermute(value, 'row', route)  8.47 us
    ppermute x4, waiting for transfers between devices, to_peer(): return lax.ppermute(value, 'row', route)  5.57 us
  transfers between devices with their start and end apart: 9, of which 3 were waited for; matrix products, arithmetic and copies ran while one was open for 0% of the time, Pallas kernels for 26%

profile of v7, /device:TPU:0, one launch (start us, length us, event | category | flops | bytes accessed | tf_op | source)
XLA Modules:
  0.0 35.4 jit_solution(16784409063593919856)
XLA Ops:
  0.6 1.0 %shard_map.68.after = f32[4,128,128]{2,1,0:T(8,128)S(1)} custom-call(f32[2,128,1024]{2,1,0:T(8,128)} %sqrt_iterate.3, f32[2,128,1024]{2,1,0:T(8,128)} %inverse_iterate.3), custom_call_target="tpu_custom_call" | custom-call | tf_op jit(solution)/shard_map/pallas_call | solution.py:372
  1.6 3.4 %collective-permute-start.2 = (f32[4,128,128]{2,1,0:T(8,128)S(1)}, f32[4,128,128]{2,1,0:T(8,128)S(1)}, u32[]{:S(2)}, u32[]{:S(2)}) collective-permute-start(f32[4,128,128]{2,1,0:T(8,128)S(1)} %shard_map.68.after), channel_id=1, source_target_pairs={{0,28},{4,8},{8,4},{12,16},{16,12},{20,24},{24,20},{28,0},{1,29},{... | collective-permute-start | bytes 786440 | tf_op jit(solution)/shard_map/ppermute | solution.py:401
  5.0 1.7 %shard_map.69 = (s32[16,128]{1,0:T(8,128)S(1)}, f32[24,128]{1,0:T(8,128)S(1)}, f32[3,128,256]{2,1,0:T(8,128)S(1)}, f32[3,128,256]{2,1,0:T(8,128)S(1)}, f32[256,2...) custom-call(s32[8,64]{1,0:T(8,128)} %bitcast.2, ...), custom_call_target="tpu_custom_call" | custom-call | tf_op jit(solution)/shard_map/pallas_call | solution.py:372
  6.7 0.1 collective-permute-start
  6.8 0.5 %collective-permute-start.1 = (f32[3,256,256]{2,1,0:T(8,128)S(1)}, f32[3,256,256]{2,1,0:T(8,128)S(1)}, u32[]{:S(2)}, u32[]{:S(2)}) collective-permute-start(f32[3,256,256]{2,1,0:T(8,128)S(1)} %get-tuple-element.23.mate_rest), channel_id=1, source_target_pairs={{0,4},{4,0},{8,12},{12,8},{16,20},{20,16},{24,28},{28,24},{1,5},{5... | collective-permute-start | bytes 2359304 | tf_op jit(solution)/shard_map/ppermute | solution.py:397
  7.3 0.3 collective-permute-start.3
  7.6 4.1 %collective-permute-start.4 = (f32[2,256,256]{2,1,0:T(8,128)S(1)}, f32[2,256,256]{2,1,0:T(8,128)S(1)}, u32[]{:S(2)}, u32[]{:S(2)}) collective-permute-start(f32[2,256,256]{2,1,0:T(8,128)S(1)} %get-tuple-element.26), channel_id=1, source_target_pairs={{1,0},{2,1},{3,2},{0,3},{5,4},{6,5},{7,6},{4,7},{9,8},{10,9},{11,1... | collective-permute-start | bytes 1572872 | tf_op jit(solution)/shard_map/ppermute | solution.py:405
  11.7 0.0 collective-permute-done.2.diagonal
  11.7 2.8 %collective-permute-start.8 = (f32[3,128,256]{2,1,0:T(8,128)S(1)}, f32[3,128,256]{2,1,0:T(8,128)S(1)}, u32[]{:S(2)}, u32[]{:S(2)}) collective-permute-start(f32[3,128,256]{2,1,0:T(8,128)S(1)} %get-tuple-element.21.z_strips), channel_id=1, source_target_pairs={{0,28},{4,8},{8,4},{12,16},{16,12},{20,24},{24,20},{28,0},{1,29},{... | collective-permute-start | bytes 1179656 | tf_op jit(solution)/shard_map/ppermute | solution.py:401
  14.6 1.7 %shard_map.71.mate_terms = f32[5,256,256]{2,1,0:T(8,128)S(1)} custom-call(f32[24,128]{1,0:T(8,128)S(1)} %get-tuple-element.19.kept, f32[256,256]{1,0:T(8,128)S(1)} %get-tuple-element.22.y_mate, f32[3,256,256]{2,1,0:T(8,128)S(1)} %get-tuple-element.23.mate_rest, f32[256,256]{1,0:T(8,128)S(1)} %collective-permute-done.mate_y, ...), custom_call_target="tpu_custom_call" | custom-call | tf_op jit(solution)/shard_map/pallas_call | solution.py:372
  16.3 3.8 %collective-permute-done.3.peer_y = f32[3,128,256]{2,1,0:T(8,128)S(1)} collective-permute-done((f32[3,128,256]{2,1,0:T(8,128)S(1)}, f32[3,128,256]{2,1,0:T(8,128)S(1)}, u32[]{:S(2)}, u32[]{:S(2)}) %collective-permute-start.3) | collective-permute-done | bytes 393248 | tf_op jit(solution)/shard_map/ppermute | solution.py:401
  20.1 0.7 %shard_map.72 = (f32[256,256]{1,0:T(8,128)S(1)}, f32[256,256]{1,0:T(8,128)S(1)}) custom-call(f32[24,128]{1,0:T(8,128)S(1)} %get-tuple-element.19.kept, f32[5,256,256]{2,1,0:T(8,128)S(1)} %shard_map.71.mate_terms, f32[3,128,256]{2,1,0:T(8,128)S(1)} %get-tuple-element.21.z_strips, f32[3,128,256]{2,1,0:T(8,128)S(1)} %collective-permute-done.3.peer_y), custom_call_target="tpu_custom_call" | custom-call | flops 5765000192 | tf_op jit(solution)/shard_map/pallas_call | solution.py:372
  20.8 0.1 collective-permute-start.5
  20.9 4.5 %collective-permute-start.7 = (f32[256,256]{1,0:T(8,128)S(1)}, f32[256,256]{1,0:T(8,128)S(1)}, u32[]{:S(2)}, u32[]{:S(2)}) collective-permute-start(f32[256,256]{1,0:T(8,128)S(1)} %get-tuple-element.27.factor_own), channel_id=1, source_target_pairs={{1,0},{2,1},{3,2},{0,3},{5,4},{6,5},{7,6},{4,7},{9,8},{10,9},{11,1... | collective-permute-start | bytes 786440 | tf_op jit(solution)/shard_map/ppermute | solution.py:405
  25.4 2.0 %collective-permute-start.6 = (f32[256,256]{1,0:T(8,128)S(1)}, f32[256,256]{1,0:T(8,128)S(1)}, u32[]{:S(2)}, u32[]{:S(2)}) collective-permute-start(f32[256,256]{1,0:T(8,128)S(1)} %get-tuple-element.29), channel_id=1, source_target_pairs={{0,28},{4,8},{8,4},{12,16},{16,12},{20,24},{24,20},{28,0},{1,29},{... | collective-permute-start | bytes 786440 | tf_op jit(solution)/shard_map/ppermute | solution.py:401
  27.4 0.0 collective-permute-done.4.from_side
  27.4 0.0 collective-permute-done.5.mate_factor
  27.4 2.0 %shard_map.73 = (f32[3,256,256]{2,1,0:T(8,128)S(1)}, f32[5,256,256]{2,1,0:T(8,128)S(1)}, bf16[5,2,256,256]{3,2,1,0:T(8,128)(2,1)S(1)}) custom-call(f32[24,128]{1,0:T(8,128)S(1)} %get-tuple-element.19.kept, f32[3,128,256]{2,1,0:T(8,128)S(1)} %get-tuple-element.20.y_strips, f32[3,128,256]{2,1,0:T(8,128)S(1)} %get-tuple-element.21.z_strips, ...), custom_call_target="tpu_custom_call" | custom-call | tf_op jit(solution)/shard_map/pallas_call | solution.py:372
  29.3 0.0 collective-permute-done.8.peer_z
  29.4 2.0 %shard_map.74 = (f32[2,128,1024]{2,1,0:T(8,128)}, f32[2,128,1024]{2,1,0:T(8,128)}) custom-call(s32[16,128]{1,0:T(8,128)S(1)} %get-tuple-element.18.slots, f32[24,128]{1,0:T(8,128)S(1)} %get-tuple-element.19.kept, f32[3,256,256]{2,1,0:T(8,128)S(1)} %get-tuple-element.31.finished, f32[5,256,256]{2,1,0:T(8,128)S(1)} %get-tuple-element.28.partial, ...), custom_call_target="tpu_custom_call" | custom-call | tf_op jit(solution)/shard_map/pallas_call | solution.py:372
  31.3 0.2 collective-permute-done.7.factor
  31.5 1.2 %shard_map.75.unfinished = f32[2,128,1024]{2,1,0:T(8,128)} custom-call(s32[16,128]{1,0:T(8,128)S(1)} %get-tuple-element.18.slots, f32[24,128]{1,0:T(8,128)S(1)} %get-tuple-element.19.kept, f32[5,256,256]{2,1,0:T(8,128)S(1)} %get-tuple-element.28.partial, bf16[5,2,256,256]{3,2,1,0:T(8,128)(2,1)S(1)} %get-tuple-element.30.ready, ...), custom_call_target="tpu_custom_call", output_to_operand_aliasing={{}: (5, {})} | custom-call | tf_op jit(solution)/shard_map/pallas_call | solution.py:372
  32.7 1.7 %collective-permute-done.6.term = f32[256,256]{1,0:T(8,128)S(1)} collective-permute-done((f32[256,256]{1,0:T(8,128)S(1)}, f32[256,256]{1,0:T(8,128)S(1)}, u32[]{:S(2)}, u32[]{:S(2)}) %collective-permute-start.6) | collective-permute-done | bytes 262176 | tf_op jit(solution)/shard_map/ppermute | solution.py:401
  34.5 0.9 %shard_map.76 = f32[2,128,1024]{2,1,0:T(8,128)} custom-call(s32[16,128]{1,0:T(8,128)S(1)} %get-tuple-element.18.slots, f32[5,256,256]{2,1,0:T(8,128)S(1)} %get-tuple-element.28.partial, f32[256,256]{1,0:T(8,128)S(1)} %collective-permute-done.6.term, f32[2,128,1024]{2,1,0:T(8,128)} %shard_map.75.unfinished), custom_call_target="tpu_custom_call", output_to_operand_aliasing={{}: (3, {})} | custom-call | tf_op jit(solution)/shard_map/pallas_call | solution.py:372
  (3 shorter events, 0.0 us)
Async XLA Ops:
  1.6 10.1 %collective-permute-start.2 = (f32[4,128,128]{2,1,0:T(8,128)S(1)}, f32[4,128,128]{2,1,0:T(8,128)S(1)}, u32[]{:S(2)}, u32[]{:S(2)}) collective-permute-start(f32[4,128,128]{2,1,0:T(8,128)S(1)} %shard_map.68.after), channel_id=1, source_target_pairs={{0,28},{4,8},{8,4},{12,16},{16,12},{20,24},{24,20},{28,0},{1,29},{... | collective-permute-start | bytes 786440 | tf_op jit(solution)/shard_map/ppermute | solution.py:401
  6.7 7.8 %collective-permute-start = (f32[256,256]{1,0:T(8,128)S(1)}, f32[256,256]{1,0:T(8,128)S(1)}, u32[]{:S(2)}, u32[]{:S(2)}) collective-permute-start(f32[256,256]{1,0:T(8,128)S(1)} %get-tuple-element.22.y_mate), channel_id=1, source_target_pairs={{0,4},{4,0},{8,12},{12,8},{16,20},{20,16},{24,28},{28,24},{1,5},{5... | collective-permute-start | bytes 786440 | tf_op jit(solution)/shard_map/ppermute | solution.py:397
  6.8 7.7 %collective-permute-start.1 = (f32[3,256,256]{2,1,0:T(8,128)S(1)}, f32[3,256,256]{2,1,0:T(8,128)S(1)}, u32[]{:S(2)}, u32[]{:S(2)}) collective-permute-start(f32[3,256,256]{2,1,0:T(8,128)S(1)} %get-tuple-element.23.mate_rest), channel_id=1, source_target_pairs={{0,4},{4,0},{8,12},{12,8},{16,20},{20,16},{24,28},{28,24},{1,5},{5... | collective-permute-start | bytes 2359304 | tf_op jit(solution)/shard_map/ppermute | solution.py:397
  7.3 12.8 %collective-permute-start.3 = (f32[3,128,256]{2,1,0:T(8,128)S(1)}, f32[3,128,256]{2,1,0:T(8,128)S(1)}, u32[]{:S(2)}, u32[]{:S(2)}) collective-permute-start(f32[3,128,256]{2,1,0:T(8,128)S(1)} %get-tuple-element.20.y_strips), channel_id=1, source_target_pairs={{0,28},{4,8},{8,4},{12,16},{16,12},{20,24},{24,20},{28,0},{1,29},{... | collective-permute-start | bytes 1179656 | tf_op jit(solution)/shard_map/ppermute | solution.py:401
  7.6 19.8 %collective-permute-start.4 = (f32[2,256,256]{2,1,0:T(8,128)S(1)}, f32[2,256,256]{2,1,0:T(8,128)S(1)}, u32[]{:S(2)}, u32[]{:S(2)}) collective-permute-start(f32[2,256,256]{2,1,0:T(8,128)S(1)} %get-tuple-element.26), channel_id=1, source_target_pairs={{1,0},{2,1},{3,2},{0,3},{5,4},{6,5},{7,6},{4,7},{9,8},{10,9},{11,1... | collective-permute-start | bytes 1572872 | tf_op jit(solution)/shard_map/ppermute | solution.py:405
  11.7 17.6 %collective-permute-start.8 = (f32[3,128,256]{2,1,0:T(8,128)S(1)}, f32[3,128,256]{2,1,0:T(8,128)S(1)}, u32[]{:S(2)}, u32[]{:S(2)}) collective-permute-start(f32[3,128,256]{2,1,0:T(8,128)S(1)} %get-tuple-element.21.z_strips), channel_id=1, source_target_pairs={{0,28},{4,8},{8,4},{12,16},{16,12},{20,24},{24,20},{28,0},{1,29},{... | collective-permute-start | bytes 1179656 | tf_op jit(solution)/shard_map/ppermute | solution.py:401
  20.8 6.6 %collective-permute-start.5 = (f32[256,256]{1,0:T(8,128)S(1)}, f32[256,256]{1,0:T(8,128)S(1)}, u32[]{:S(2)}, u32[]{:S(2)}) collective-permute-start(f32[256,256]{1,0:T(8,128)S(1)} %get-tuple-element.27.factor_own), channel_id=1, source_target_pairs={{0,4},{4,0},{8,12},{12,8},{16,20},{20,16},{24,28},{28,24},{1,5},{5... | collective-permute-start | bytes 786440 | tf_op jit(solution)/shard_map/ppermute | solution.py:397
  20.9 10.7 %collective-permute-start.7 = (f32[256,256]{1,0:T(8,128)S(1)}, f32[256,256]{1,0:T(8,128)S(1)}, u32[]{:S(2)}, u32[]{:S(2)}) collective-permute-start(f32[256,256]{1,0:T(8,128)S(1)} %get-tuple-element.27.factor_own), channel_id=1, source_target_pairs={{1,0},{2,1},{3,2},{0,3},{5,4},{6,5},{7,6},{4,7},{9,8},{10,9},{11,1... | collective-permute-start | bytes 786440 | tf_op jit(solution)/shard_map/ppermute | solution.py:405
  25.4 9.1 %collective-permute-start.6 = (f32[256,256]{1,0:T(8,128)S(1)}, f32[256,256]{1,0:T(8,128)S(1)}, u32[]{:S(2)}, u32[]{:S(2)}) collective-permute-start(f32[256,256]{1,0:T(8,128)S(1)} %get-tuple-element.29), channel_id=1, source_target_pairs={{0,28},{4,8},{8,4},{12,16},{16,12},{20,24},{24,20},{28,0},{1,29},{... | collective-permute-start | bytes 786440 | tf_op jit(solution)/shard_map/ppermute | solution.py:401

commit v8 on v7

--- a/solution.py
+++ b/solution.py
@@ -126,21 +126,23 @@
     return place
 
 
-def strip_own(out):
+def strip_own(out, at):
     def place(i, j, size, block):
         if i != j:
-            out[ROWS, :, i * size:(i + 1) * size] = block
+            out[at, :, i * size:(i + 1) * size] = block
 
     return place
+
+
+Y_BESIDE, Z_BESIDE = ROWS, ROWS + 1
 
 
 def peer_part(strips):
     return jnp.concatenate([strips[i] for i in range(ROWS)], axis=0)
 
 
-def own_part(strips, spread):
-    size = strips.shape[1]
-    beside = strips[ROWS]
+def own_part(beside, spread):
+    size = beside.shape[0]
     return jnp.concatenate(
         [
             jnp.concatenate([spread[:size, :size], beside[:, :size]], axis=1),
@@ -166,7 +168,7 @@
 
 def pack_kernel(
     row_devices, col_devices, pattern, keep, order, sqrt_iterate, inverse_iterate, after,
-    slots, kept, y_strips, z_strips, y_mate, mate_rest, y_side, z_side, to_side,
+    slots, kept, y_peer, strips, y_mate, mate_rest, y_side, z_side, to_side,
     pattern_here, keep_here, order_here, sqrt_here, inverse_here, sems,
 ):
     copies = [
@@ -189,16 +191,16 @@
 
     copies[3].wait()
     places = {
-        PEER: (strip_peer(y_strips),),
-        OWN: (strip_own(y_strips), into(mate_rest.at[0]), into(to_side.at[0])),
+        PEER: (into(y_peer),),
+        OWN: (strip_own(strips, Y_BESIDE), into(mate_rest.at[0]), into(to_side.at[0])),
         MATE: (into(y_mate),),
         SIDE: (into(y_side),),
     }
     gather(slot_of, sqrt_here, places)
     copies[4].wait()
     places = {
-        PEER: (strip_peer(z_strips),),
-        OWN: (strip_own(z_strips), into(mate_rest.at[2]), into(to_side.at[1])),
+        PEER: (strip_peer(strips),),
+        OWN: (strip_own(strips, Z_BESIDE), into(mate_rest.at[2]), into(to_side.at[1])),
         MATE: (into(mate_rest.at[1]),),
         SIDE: (into(z_side),),
     }
@@ -236,9 +238,9 @@
     mate_terms[M_Z_MATE] = products((f_mate, mate_z_own))
 
 
-def factor_own_kernel(kept, mate_terms, z_strips, peer_y, factor_own, peer_term):
-    peer_y_peer = split(peer_part(peer_y))
-    total = mate_terms[M_OWN] + products((split(peer_part(z_strips)), peer_y_peer))
+def factor_own_kernel(kept, mate_terms, strips, peer_y, factor_own, peer_term):
+    peer_y_peer = split(peer_y[...])
+    total = mate_terms[M_OWN] + products((split(peer_part(strips)), peer_y_peer))
     rows = lax.broadcasted_iota(jnp.int32, total.shape, 0)
     cols = lax.broadcasted_iota(jnp.int32, total.shape, 1)
     factor = jnp.where(rows == cols, 1.5, 0.0) + filtered(kept, total, OWN, -0.5)
@@ -248,35 +250,31 @@
 
 
 Y_MATE, Z_MATE, Z_SIDE = range(3)
-Y_OWN_PART, Y_PEER_PART, Y_SIDE_PART, Z_OWN_PART, Z_PEER_PART = range(5)
-Y_PEER, Y_OWN, Y_SIDE, F_PEER, PEER_Y = range(5)
+Y_OWN_PART, Y_SIDE_PART, Z_OWN_PART, Z_PEER_PART, PEER_PART = range(5)
+Y_PEER, Y_OWN, Y_SIDE, PEER_Y, Z_PEER = range(5)
 
 
 def middle_kernel(
-    kept, y_strips, z_strips, y_mate, mate_rest, y_side, z_side, mate_terms,
-    peer_y, peer_spread, from_side, factor_own, mate_factor,
+    kept, y_peer, strips, y_mate, mate_rest, y_side, z_side, mate_terms,
+    peer_y, from_side, factor_own, mate_factor,
     finished, partial, ready,
 ):
     def keep(at, parts):
         ready[at, 0], ready[at, 1] = parts
 
     y_own, z_to_mate, z_own = (split(mate_rest[at]) for at in range(3))
-    y_to_peer, z_to_peer = split(peer_part(y_strips)), split(peer_part(z_strips))
+    y_to_peer, z_to_peer = split(y_peer[...]), split(peer_part(strips))
     y_to_side, z_to_side = split(y_side[...]), split(z_side[...])
     f_own = split(factor_own[...])
     keep(Y_OWN, y_own)
     keep(Y_SIDE, y_to_side)
     keep(Y_PEER, y_to_peer)
-    keep(PEER_Y, split(peer_part(peer_y)))
-
-    peer_y_own = split(own_part(peer_y, peer_spread[0]))
-    total = products((z_own, y_to_peer), (z_to_peer, peer_y_own))
-    f_peer = split(filtered(kept, total, PEER, -0.5))
-    keep(F_PEER, f_peer)
+    keep(Z_PEER, z_to_peer)
+    keep(PEER_Y, split(peer_y[...]))
+
     total = products((z_own, y_to_side), (z_to_side, split(from_side[0])))
     f_side = split(filtered(kept, total, SIDE, -0.5))
-
-    partial[Y_PEER_PART] = filtered(kept, products((y_own, f_peer)), PEER)
+    partial[PEER_PART] = products((z_own, y_to_peer))
     partial[Y_SIDE_PART] = products((y_own, f_side))
     partial[Y_OWN_PART] = mate_terms[M_Y_OWN] + products((y_own, f_own))
     partial[Z_PEER_PART] = products((f_own, z_to_peer))
@@ -312,7 +310,7 @@
     def finish(self, value, out, region):
         place = self.result.at[self.held]
         self.held += 1
-        place[...] = value if self.kept is None else filtered(self.kept, value, region)
+        place[...] = filtered(self.kept, value, region)
         self.write(place, out, region)
 
     def wait(self):
@@ -321,8 +319,8 @@
 
 
 def peer_kernel(
-    slots, kept, finished, partial, ready, peer_z, peer_spread,
-    sqrt_next, inverse_next, result, sems,
+    slots, kept, finished, partial, ready, from_peer, peer_spread,
+    sqrt_next, inverse_next, y_peer_part, result, sems,
 ):
     def held(at):
         return ready[at, 0], ready[at, 1]
@@ -331,17 +329,20 @@
     writer.write(finished.at[Y_MATE], sqrt_next, MATE)
     writer.write(finished.at[Z_MATE], inverse_next, MATE)
     writer.write(finished.at[Z_SIDE], inverse_next, SIDE)
-    peer_z_peer = split(peer_part(peer_z))
-    peer_z_own = split(own_part(peer_z, peer_spread[1]))
-    f_peer = held(F_PEER)
+    peer_y_own = split(own_part(from_peer[Y_BESIDE], peer_spread[0]))
+    peer_z_own = split(own_part(from_peer[Z_BESIDE], peer_spread[1]))
+    peer_z_peer = split(peer_part(from_peer))
+    total = partial[PEER_PART] + products((held(Z_PEER), peer_y_own))
+    f_peer = split(filtered(kept, total, PEER, -0.5))
+    total = products((peer_z_own, held(PEER_Y)), (peer_z_peer, held(Y_OWN)))
+    peer_f_peer = split(filtered(kept, total, 0, -0.5, KEPT_PEER_AT, ROWS))
     value = partial[Z_PEER_PART] + products((f_peer, peer_z_own))
     writer.finish(value, inverse_next, PEER)
     value = partial[Z_OWN_PART] + products((f_peer, peer_z_peer))
     writer.finish(value, inverse_next, OWN)
-    total = products((peer_z_own, held(PEER_Y)), (peer_z_peer, held(Y_OWN)))
-    peer_f_peer = split(filtered(kept, total, 0, -0.5, KEPT_PEER_AT, ROWS))
     value = partial[Y_OWN_PART] + products((held(Y_PEER), peer_f_peer))
     writer.finish(value, sqrt_next, OWN)
+    y_peer_part[...] = filtered(kept, products((held(Y_OWN), f_peer)), PEER)
     writer.wait()
 
 
@@ -353,14 +354,24 @@
     writer.wait()
 
 
-def last_kernel(slots, partial, term, unfinished, sqrt_next, result, sems):
-    writer = Writer(slots, None, result, sems)
-    writer.finish(partial[Y_PEER_PART] + term[...], sqrt_next, PEER)
-    writer.wait()
+def last_kernel(slots, part, term, unfinished, sqrt_next, result, sems):
+    size = sqrt_next.shape[1]
+    copies = []
+    for i in range(ROWS):
+        for j in range(ROWS):
+            at = len(copies)
+            rows, cols = quarter(i, j, size)
+            result[at] = part[rows, cols] + term[rows, cols]
+            slot = slots[i * SLOTS + PEER * ROWS + j, 0]
+            out = sqrt_next.at[i, :, pl.ds(pl.multiple_of(slot * size, size), size)]
+            copies.append(pltpu.make_async_copy(result.at[at], out, sems.at[at]))
+            copies[at].start()
+    for copy in copies:
+        copy.wait()
 
 
 def call(
-    kernel, outs, operands, micros=0, scratch=(), hbm_in=(), any_in=(), hbm_out=False, in_place=None
+    kernel, outs, operands, micros=0, scratch=(), hbm_in=(), any_in=(), hbm_out=(), in_place=None
 ):
     def spec(space=pltpu.VMEM):
         return pl.BlockSpec(memory_space=space)
@@ -376,7 +387,9 @@
             spec(pltpu.HBM if at in hbm_in else pl.ANY if at in any_in else pltpu.VMEM)
             for at in range(len(operands))
         ],
-        out_specs=tuple(spec(pltpu.HBM if hbm_out else pltpu.VMEM) for _ in outs),
+        out_specs=tuple(
+            spec(pltpu.HBM if at in hbm_out else pltpu.VMEM) for at in range(len(outs))
+        ),
         scratch_shapes=scratch,
         input_output_aliases={} if in_place is None else {in_place: 0},
         compiler_params=pltpu.CompilerParams(vmem_limit_bytes=VMEM_LIMIT),
@@ -416,12 +429,11 @@
         hbm_in=range(2),
     )
     peer_diagonal = to_peer(diagonal)
-    strips = shape(ROWS + 1, block, size)
-    slots, kept, y_strips, z_strips, y_mate, mate_rest, y_side, z_side, own_pair = call(
+    slots, kept, y_peer, strips, y_mate, mate_rest, y_side, z_side, own_pair = call(
         functools.partial(pack_kernel, row_devices, col_devices),
         (
             shape(ROWS * SLOTS, block, dtype=jnp.int32), shape(KEPT_LINES, block),
-            strips, strips, one, shape(3, size, size), one, one, pair,
+            one, shape(ROWS + 2, block, size), one, shape(3, size, size), one, one, pair,
         ),
         (pattern.T, keep_mask.T, row_order, sqrt_iterate, inverse_iterate, diagonal),
         scratch=[
@@ -435,8 +447,8 @@
         hbm_in=range(5),
         any_in=(5,),
     )
-    peer_y = to_peer(y_strips)
-    peer_z = to_peer(z_strips)
+    peer_y = to_peer(y_peer)
+    from_peer = to_peer(strips)
     mate_y = to_mate(y_mate)
     from_mate = to_mate(mate_rest)
     from_side = to_side(own_pair)
@@ -448,7 +460,7 @@
         any_in=(5,),
     )
     factor_own, peer_term = call(
-        factor_own_kernel, (one, one), (kept, mate_terms, z_strips, peer_y), micros=5
+        factor_own_kernel, (one, one), (kept, mate_terms, strips, peer_y), micros=5
     )
     mate_factor = to_mate(factor_own)
     term = to_peer(peer_term)
@@ -460,8 +472,8 @@
             shape(5, 2, size, size, dtype=jnp.bfloat16),
         ),
         (
-            kept, y_strips, z_strips, y_mate, mate_rest, y_side, z_side, mate_terms,
-            peer_y, peer_spread, from_side, factor_own, mate_factor,
+            kept, y_peer, strips, y_mate, mate_rest, y_side, z_side, mate_terms,
+            peer_y, from_side, factor_own, mate_factor,
         ),
     )
     output = shape(rows_dev, block, width)
@@ -472,12 +484,12 @@
             pltpu.SemaphoreType.DMA((24,)),
         ]
 
-    sqrt_next, inverse_next = call(
+    sqrt_next, inverse_next, y_peer_part = call(
         peer_kernel,
-        (output, output),
-        (slots, kept, finished, partial, ready, peer_z, peer_spread),
+        (output, output, one),
+        (slots, kept, finished, partial, ready, from_peer, peer_spread),
         scratch=writing(3),
-        hbm_out=True,
+        hbm_out=(0, 1),
     )
     (sqrt_next,) = call(
         side_kernel,
@@ -485,16 +497,19 @@
         (slots, kept, partial, ready, side_factor, sqrt_next),
         scratch=writing(1),
         hbm_in=(5,),
-        hbm_out=True,
+        hbm_out=(0,),
         in_place=5,
     )
     (sqrt_next,) = call(
         last_kernel,
         (output,),
-        (slots, partial, term, sqrt_next),
-        scratch=writing(1),
+        (slots, y_peer_part, term, sqrt_next),
+        scratch=[
+            pltpu.VMEM((ROWS * ROWS, block, block), jnp.float32),
+            pltpu.SemaphoreType.DMA((ROWS * ROWS,)),
+        ],
         hbm_in=(3,),
-        hbm_out=True,
+        hbm_out=(0,),
         in_place=3,
     )
     return sqrt_next, inverse_next

time: 35.6 us -> 34.7 us (0.975)
  waiting for transfers between devices: 5.8 us -> 5.2 us
    ppermute x4, waiting for transfers between devices: 5.57 us -> 5.18 us  [to_peer(): return lax.ppermute(value, 'row', route)]
  transfers between devices with their start and end apart: 9 -> 9, of which waited for: 3 -> 3; matrix products, arithmetic and copies ran while one was open for 0% -> 0% of each run, Pallas kernels for 26% -> 27%
where the time goes in v8:
time: 34.7 us; the launch traced here: 34.5 us
  starting transfers between devices  17.7 us (51%)
  Pallas kernels  10.9 us (31%)
  waiting for transfers between devices  5.2 us (15%)
  between operations  0.73 us (2%)
    pallas_call x9, Pallas kernels, call(): pl.pallas_call(kernel, out_shape=outs, in_specs=[spec(pltpu.HBM if at in...  10.9 us
    ppermute x2, starting transfers between devices, to_side(): return lax.ppermute(value, 'col', route)  8.57 us
    ppermute x4, starting transfers between devices, to_peer(): return lax.ppermute(value, 'row', route)  8.47 us
    ppermute x4, waiting for transfers between devices, to_peer(): return lax.ppermute(value, 'row', route)  5.18 us
  transfers between devices with their start and end apart: 9, of which 3 were waited for; matrix products, arithmetic and copies ran while one was open for 0% of the time, Pallas kernels for 27%

profile of v8, /device:TPU:0, one launch (start us, length us, event | category | flops | bytes accessed | tf_op | source)
XLA Modules:
  0.0 34.5 jit_solution(1666166456986581889)
XLA Ops:
  0.6 1.0 %shard_map.68.after = f32[4,128,128]{2,1,0:T(8,128)S(1)} custom-call(f32[2,128,1024]{2,1,0:T(8,128)} %sqrt_iterate.3, f32[2,128,1024]{2,1,0:T(8,128)} %inverse_iterate.3), custom_call_target="tpu_custom_call" | custom-call | tf_op jit(solution)/shard_map/pallas_call | solution.py:383
  1.6 3.4 %collective-permute-start.2 = (f32[4,128,128]{2,1,0:T(8,128)S(1)}, f32[4,128,128]{2,1,0:T(8,128)S(1)}, u32[]{:S(2)}, u32[]{:S(2)}) collective-permute-start(f32[4,128,128]{2,1,0:T(8,128)S(1)} %shard_map.68.after), channel_id=1, source_target_pairs={{0,28},{4,8},{8,4},{12,16},{16,12},{20,24},{24,20},{28,0},{1,29},{... | collective-permute-start | bytes 786440 | tf_op jit(solution)/shard_map/ppermute | solution.py:414
  5.0 1.7 %shard_map.69 = (s32[16,128]{1,0:T(8,128)S(1)}, f32[24,128]{1,0:T(8,128)S(1)}, f32[256,256]{1,0:T(8,128)S(1)}, f32[4,128,256]{2,1,0:T(8,128)S(1)}, f32[256,256]{...) custom-call(s32[8,64]{1,0:T(8,128)} %bitcast.2, ...), custom_call_target="tpu_custom_call" | custom-call | tf_op jit(solution)/shard_map/pallas_call | solution.py:383
  6.7 0.1 collective-permute-start
  6.8 0.5 %collective-permute-start.1 = (f32[3,256,256]{2,1,0:T(8,128)S(1)}, f32[3,256,256]{2,1,0:T(8,128)S(1)}, u32[]{:S(2)}, u32[]{:S(2)}) collective-permute-start(f32[3,256,256]{2,1,0:T(8,128)S(1)} %get-tuple-element.24.mate_rest), channel_id=1, source_target_pairs={{0,4},{4,0},{8,12},{12,8},{16,20},{20,16},{24,28},{28,24},{1,5},{5... | collective-permute-start | bytes 2359304 | tf_op jit(solution)/shard_map/ppermute | solution.py:410
  7.3 0.3 collective-permute-start.3
  7.6 4.1 %collective-permute-start.4 = (f32[2,256,256]{2,1,0:T(8,128)S(1)}, f32[2,256,256]{2,1,0:T(8,128)S(1)}, u32[]{:S(2)}, u32[]{:S(2)}) collective-permute-start(f32[2,256,256]{2,1,0:T(8,128)S(1)} %get-tuple-element.27), channel_id=1, source_target_pairs={{1,0},{2,1},{3,2},{0,3},{5,4},{6,5},{7,6},{4,7},{9,8},{10,9},{11,1... | collective-permute-start | bytes 1572872 | tf_op jit(solution)/shard_map/ppermute | solution.py:418
  11.7 0.0 collective-permute-done.2.diagonal
  11.7 2.8 %collective-permute-start.6 = (f32[4,128,256]{2,1,0:T(8,128)S(1)}, f32[4,128,256]{2,1,0:T(8,128)S(1)}, u32[]{:S(2)}, u32[]{:S(2)}) collective-permute-start(f32[4,128,256]{2,1,0:T(8,128)S(1)} %get-tuple-element.22.strips), channel_id=1, source_target_pairs={{0,28},{4,8},{8,4},{12,16},{16,12},{20,24},{24,20},{28,0},{1,29},{... | collective-permute-start | bytes 1572872 | tf_op jit(solution)/shard_map/ppermute | solution.py:414
  14.5 0.0 collective-permute-done.mate_y
  14.6 0.0 collective-permute-done.1.from_mate
  14.6 1.7 %shard_map.71.mate_terms = f32[5,256,256]{2,1,0:T(8,128)S(1)} custom-call(f32[24,128]{1,0:T(8,128)S(1)} %get-tuple-element.20.kept, f32[256,256]{1,0:T(8,128)S(1)} %get-tuple-element.23.y_mate, f32[3,256,256]{2,1,0:T(8,128)S(1)} %get-tuple-element.24.mate_rest, f32[256,256]{1,0:T(8,128)S(1)} %collective-permute-done.mate_y, ...), custom_call_target="tpu_custom_call" | custom-call | tf_op jit(solution)/shard_map/pallas_call | solution.py:383
  16.3 1.0 %collective-permute-done.3.peer_y = f32[256,256]{1,0:T(8,128)S(1)} collective-permute-done((f32[256,256]{1,0:T(8,128)S(1)}, f32[256,256]{1,0:T(8,128)S(1)}, u32[]{:S(2)}, u32[]{:S(2)}) %collective-permute-start.3) | collective-permute-done | bytes 262176 | tf_op jit(solution)/shard_map/ppermute | solution.py:414
  17.3 0.7 %shard_map.72 = (f32[256,256]{1,0:T(8,128)S(1)}, f32[256,256]{1,0:T(8,128)S(1)}) custom-call(f32[24,128]{1,0:T(8,128)S(1)} %get-tuple-element.20.kept, f32[5,256,256]{2,1,0:T(8,128)S(1)} %shard_map.71.mate_terms, f32[4,128,256]{2,1,0:T(8,128)S(1)} %get-tuple-element.22.strips, f32[256,256]{1,0:T(8,128)S(1)} %collective-permute-done.3.peer_y), custom_call_target="tpu_custom_call" | custom-call | flops 5765000192 | tf_op jit(solution)/shard_map/pallas_call | solution.py:383
  18.0 0.1 collective-permute-start.5
  18.1 4.5 %collective-permute-start.8 = (f32[256,256]{1,0:T(8,128)S(1)}, f32[256,256]{1,0:T(8,128)S(1)}, u32[]{:S(2)}, u32[]{:S(2)}) collective-permute-start(f32[256,256]{1,0:T(8,128)S(1)} %get-tuple-element.28.factor_own), channel_id=1, source_target_pairs={{1,0},{2,1},{3,2},{0,3},{5,4},{6,5},{7,6},{4,7},{9,8},{10,9},{11,1... | collective-permute-start | bytes 786440 | tf_op jit(solution)/shard_map/ppermute | solution.py:418
  22.6 2.0 %collective-permute-start.7 = (f32[256,256]{1,0:T(8,128)S(1)}, f32[256,256]{1,0:T(8,128)S(1)}, u32[]{:S(2)}, u32[]{:S(2)}) collective-permute-start(f32[256,256]{1,0:T(8,128)S(1)} %get-tuple-element.33), channel_id=1, source_target_pairs={{0,28},{4,8},{8,4},{12,16},{16,12},{20,24},{24,20},{28,0},{1,29},{... | collective-permute-start | bytes 786440 | tf_op jit(solution)/shard_map/ppermute | solution.py:414
  24.6 0.0 collective-permute-done.4.from_side
  24.6 1.8 %shard_map.73 = (f32[3,256,256]{2,1,0:T(8,128)S(1)}, f32[5,256,256]{2,1,0:T(8,128)S(1)}, bf16[5,2,256,256]{3,2,1,0:T(8,128)(2,1)S(1)}) custom-call(f32[24,128]{1,0:T(8,128)S(1)} %get-tuple-element.20.kept, f32[256,256]{1,0:T(8,128)S(1)} %get-tuple-element.21.y_peer, f32[4,128,256]{2,1,0:T(8,128)S(1)} %get-tuple-element.22.strips, ...), custom_call_target="tpu_custom_call" | custom-call | tf_op jit(solution)/shard_map/pallas_call | solution.py:383
  26.4 2.1 %collective-permute-done.6.from_peer = f32[4,128,256]{2,1,0:T(8,128)S(1)} collective-permute-done((f32[4,128,256]{2,1,0:T(8,128)S(1)}, f32[4,128,256]{2,1,0:T(8,128)S(1)}, u32[]{:S(2)}, u32[]{:S(2)}) %collective-permute-start.6) | collective-permute-done | bytes 524320 | tf_op jit(solution)/shard_map/ppermute | solution.py:414
  28.6 2.0 %shard_map.74 = (f32[2,128,1024]{2,1,0:T(8,128)}, f32[2,128,1024]{2,1,0:T(8,128)}, f32[256,256]{1,0:T(8,128)S(1)}) custom-call(s32[16,128]{1,0:T(8,128)S(1)} %get-tuple-element.19.slots, f32[24,128]{1,0:T(8,128)S(1)} %get-tuple-element.20.kept, f32[3,256,256]{2,1,0:T(8,128)S(1)} %get-tuple-element.29.finished, f32[5,256,256]{2,1,0:T(8,128)S(1)} %get-tuple-element.30.partial, ...), custom_call_target="tpu_custom_call" | custom-call | tf_op jit(solution)/shard_map/pallas_call | solution.py:383
  30.5 1.2 %shard_map.75.unfinished = f32[2,128,1024]{2,1,0:T(8,128)} custom-call(s32[16,128]{1,0:T(8,128)S(1)} %get-tuple-element.19.slots, f32[24,128]{1,0:T(8,128)S(1)} %get-tuple-element.20.kept, f32[5,256,256]{2,1,0:T(8,128)S(1)} %get-tuple-element.30.partial, bf16[5,2,256,256]{3,2,1,0:T(8,128)(2,1)S(1)} %get-tuple-element.31.ready, ...), custom_call_target="tpu_custom_call", output_to_operand_aliasing={{}: (5, {})} | custom-call | tf_op jit(solution)/shard_map/pallas_call | solution.py:383
  31.7 2.0 %collective-permute-done.7.term = f32[256,256]{1,0:T(8,128)S(1)} collective-permute-done((f32[256,256]{1,0:T(8,128)S(1)}, f32[256,256]{1,0:T(8,128)S(1)}, u32[]{:S(2)}, u32[]{:S(2)}) %collective-permute-start.7) | collective-permute-done | bytes 262176 | tf_op jit(solution)/shard_map/ppermute | solution.py:414
  33.7 0.8 %shard_map.76 = f32[2,128,1024]{2,1,0:T(8,128)} custom-call(s32[16,128]{1,0:T(8,128)S(1)} %get-tuple-element.19.slots, f32[256,256]{1,0:T(8,128)S(1)} %get-tuple-element.32.part, f32[256,256]{1,0:T(8,128)S(1)} %collective-permute-done.7.term, f32[2,128,1024]{2,1,0:T(8,128)} %shard_map.75.unfinished), custom_call_target="tpu_custom_call", output_to_operand_aliasing={{}: (3, {})} | custom-call | tf_op jit(solution)/shard_map/pallas_call | solution.py:383
  (3 shorter events, 0.0 us)
Async XLA Ops:
  1.6 10.1 %collective-permute-start.2 = (f32[4,128,128]{2,1,0:T(8,128)S(1)}, f32[4,128,128]{2,1,0:T(8,128)S(1)}, u32[]{:S(2)}, u32[]{:S(2)}) collective-permute-start(f32[4,128,128]{2,1,0:T(8,128)S(1)} %shard_map.68.after), channel_id=1, source_target_pairs={{0,28},{4,8},{8,4},{12,16},{16,12},{20,24},{24,20},{28,0},{1,29},{... | collective-permute-start | bytes 786440 | tf_op jit(solution)/shard_map/ppermute | solution.py:414
  6.7 7.8 %collective-permute-start = (f32[256,256]{1,0:T(8,128)S(1)}, f32[256,256]{1,0:T(8,128)S(1)}, u32[]{:S(2)}, u32[]{:S(2)}) collective-permute-start(f32[256,256]{1,0:T(8,128)S(1)} %get-tuple-element.23.y_mate), channel_id=1, source_target_pairs={{0,4},{4,0},{8,12},{12,8},{16,20},{20,16},{24,28},{28,24},{1,5},{5... | collective-permute-start | bytes 786440 | tf_op jit(solution)/shard_map/ppermute | solution.py:410
  6.8 7.7 %collective-permute-start.1 = (f32[3,256,256]{2,1,0:T(8,128)S(1)}, f32[3,256,256]{2,1,0:T(8,128)S(1)}, u32[]{:S(2)}, u32[]{:S(2)}) collective-permute-start(f32[3,256,256]{2,1,0:T(8,128)S(1)} %get-tuple-element.24.mate_rest), channel_id=1, source_target_pairs={{0,4},{4,0},{8,12},{12,8},{16,20},{20,16},{24,28},{28,24},{1,5},{5... | collective-permute-start | bytes 2359304 | tf_op jit(solution)/shard_map/ppermute | solution.py:410
  7.3 10.0 %collective-permute-start.3 = (f32[256,256]{1,0:T(8,128)S(1)}, f32[256,256]{1,0:T(8,128)S(1)}, u32[]{:S(2)}, u32[]{:S(2)}) collective-permute-start(f32[256,256]{1,0:T(8,128)S(1)} %get-tuple-element.21.y_peer), channel_id=1, source_target_pairs={{0,28},{4,8},{8,4},{12,16},{16,12},{20,24},{24,20},{28,0},{1,29},{... | collective-permute-start | bytes 786440 | tf_op jit(solution)/shard_map/ppermute | solution.py:414
  7.6 17.0 %collective-permute-start.4 = (f32[2,256,256]{2,1,0:T(8,128)S(1)}, f32[2,256,256]{2,1,0:T(8,128)S(1)}, u32[]{:S(2)}, u32[]{:S(2)}) collective-permute-start(f32[2,256,256]{2,1,0:T(8,128)S(1)} %get-tuple-element.27), channel_id=1, source_target_pairs={{1,0},{2,1},{3,2},{0,3},{5,4},{6,5},{7,6},{4,7},{9,8},{10,9},{11,1... | collective-permute-start | bytes 1572872 | tf_op jit(solution)/shard_map/ppermute | solution.py:418
  11.7 16.9 %collective-permute-start.6 = (f32[4,128,256]{2,1,0:T(8,128)S(1)}, f32[4,128,256]{2,1,0:T(8,128)S(1)}, u32[]{:S(2)}, u32[]{:S(2)}) collective-permute-start(f32[4,128,256]{2,1,0:T(8,128)S(1)} %get-tuple-element.22.strips), channel_id=1, source_target_pairs={{0,28},{4,8},{8,4},{12,16},{16,12},{20,24},{24,20},{28,0},{1,29},{... | collective-permute-start | bytes 1572872 | tf_op jit(solution)/shard_map/ppermute | solution.py:414
  18.0 6.6 %collective-permute-start.5 = (f32[256,256]{1,0:T(8,128)S(1)}, f32[256,256]{1,0:T(8,128)S(1)}, u32[]{:S(2)}, u32[]{:S(2)}) collective-permute-start(f32[256,256]{1,0:T(8,128)S(1)} %get-tuple-element.28.factor_own), channel_id=1, source_target_pairs={{0,4},{4,0},{8,12},{12,8},{16,20},{20,16},{24,28},{28,24},{1,5},{5... | collective-permute-start | bytes 786440 | tf_op jit(solution)/shard_map/ppermute | solution.py:410
  18.1 12.4 %collective-permute-start.8 = (f32[256,256]{1,0:T(8,128)S(1)}, f32[256,256]{1,0:T(8,128)S(1)}, u32[]{:S(2)}, u32[]{:S(2)}) collective-permute-start(f32[256,256]{1,0:T(8,128)S(1)} %get-tuple-element.28.factor_own), channel_id=1, source_target_pairs={{1,0},{2,1},{3,2},{0,3},{5,4},{6,5},{7,6},{4,7},{9,8},{10,9},{11,1... | collective-permute-start | bytes 786440 | tf_op jit(solution)/shard_map/ppermute | solution.py:418
  22.6 11.2 %collective-permute-start.7 = (f32[256,256]{1,0:T(8,128)S(1)}, f32[256,256]{1,0:T(8,128)S(1)}, u32[]{:S(2)}, u32[]{:S(2)}) collective-permute-start(f32[256,256]{1,0:T(8,128)S(1)} %get-tuple-element.33), channel_id=1, source_target_pairs={{0,28},{4,8},{8,4},{12,16},{16,12},{20,24},{24,20},{28,0},{1,29},{... | collective-permute-start | bytes 786440 | tf_op jit(solution)/shard_map/ppermute | solution.py:414

commit v9 on v8

--- a/solution.py
+++ b/solution.py
@@ -154,21 +154,21 @@
 
 def diagonal_kernel(sqrt_iterate, inverse_iterate, diagonal, sems):
     size = sqrt_iterate.shape[1]
-    copies = []
-    for source in (sqrt_iterate, inverse_iterate):
-        for i in range(ROWS):
-            at = len(copies)
-            copies.append(
-                pltpu.make_async_copy(source.at[i, :, pl.ds(0, size)], diagonal.at[at], sems.at[at])
-            )
-            copies[at].start()
+    copies = [
+        pltpu.make_async_copy(
+            source.at[:, :, pl.ds(0, size)], diagonal.at[pl.ds(at * ROWS, ROWS)], sems.at[at]
+        )
+        for at, source in enumerate((sqrt_iterate, inverse_iterate))
+    ]
+    for copy in copies:
+        copy.start()
     for copy in copies:
         copy.wait()
 
 
 def pack_kernel(
     row_devices, col_devices, pattern, keep, order, sqrt_iterate, inverse_iterate, after,
-    slots, kept, y_peer, strips, y_mate, mate_rest, y_side, z_side, to_side,
+    slots, kept, y_peer, strips, mate, y_side, z_side, to_side,
     pattern_here, keep_here, order_here, sqrt_here, inverse_here, sems,
 ):
     copies = [
@@ -192,16 +192,16 @@
     copies[3].wait()
     places = {
         PEER: (into(y_peer),),
-        OWN: (strip_own(strips, Y_BESIDE), into(mate_rest.at[0]), into(to_side.at[0])),
-        MATE: (into(y_mate),),
+        OWN: (strip_own(strips, Y_BESIDE), into(mate.at[1]), into(to_side.at[0])),
+        MATE: (into(mate.at[0]),),
         SIDE: (into(y_side),),
     }
     gather(slot_of, sqrt_here, places)
     copies[4].wait()
     places = {
         PEER: (strip_peer(strips),),
-        OWN: (strip_own(strips, Z_BESIDE), into(mate_rest.at[2]), into(to_side.at[1])),
-        MATE: (into(mate_rest.at[1]),),
+        OWN: (strip_own(strips, Z_BESIDE), into(mate.at[3]), into(to_side.at[1])),
+        MATE: (into(mate.at[2]),),
         SIDE: (into(z_side),),
     }
     gather(slot_of, inverse_here, places)
@@ -220,13 +220,9 @@
 M_OWN, M_Y_OWN, M_Y_MATE, M_Z_OWN, M_Z_MATE = range(5)
 
 
-def mate_kernel(
-    kept, y_mate, mate_rest, mate_y, from_mate, after, mate_terms
-):
-    y_own, z_to_mate, z_own = (split(mate_rest[at]) for at in range(3))
-    y_to_mate = split(y_mate[...])
-    mate_y_mate, mate_y_own = split(mate_y[...]), split(from_mate[0])
-    mate_z_mate, mate_z_own = split(from_mate[1]), split(from_mate[2])
+def mate_kernel(kept, mate, from_mate, after, mate_terms):
+    y_to_mate, y_own, z_to_mate, z_own = (split(mate[at]) for at in range(4))
+    mate_y_mate, mate_y_own, mate_z_mate, mate_z_own = (split(from_mate[at]) for at in range(4))
     mate_terms[M_OWN] = products((z_own, y_own), (z_to_mate, mate_y_mate))
     total = products((z_own, y_to_mate), (z_to_mate, mate_y_own))
     f_mate = split(filtered(kept, total, MATE, -0.5))
@@ -255,14 +251,14 @@
 
 
 def middle_kernel(
-    kept, y_peer, strips, y_mate, mate_rest, y_side, z_side, mate_terms,
+    kept, y_peer, strips, mate, y_side, z_side, mate_terms,
     peer_y, from_side, factor_own, mate_factor,
     finished, partial, ready,
 ):
     def keep(at, parts):
         ready[at, 0], ready[at, 1] = parts
 
-    y_own, z_to_mate, z_own = (split(mate_rest[at]) for at in range(3))
+    y_to_mate, y_own, z_to_mate, z_own = (split(mate[at]) for at in range(4))
     y_to_peer, z_to_peer = split(y_peer[...]), split(peer_part(strips))
     y_to_side, z_to_side = split(y_side[...]), split(z_side[...])
     f_own = split(factor_own[...])
@@ -279,7 +275,7 @@
     partial[Y_OWN_PART] = mate_terms[M_Y_OWN] + products((y_own, f_own))
     partial[Z_PEER_PART] = products((f_own, z_to_peer))
     partial[Z_OWN_PART] = mate_terms[M_Z_OWN] + products((f_own, z_own))
-    value = mate_terms[M_Y_MATE] + products((split(y_mate[...]), split(mate_factor[...])))
+    value = mate_terms[M_Y_MATE] + products((y_to_mate, split(mate_factor[...])))
     finished[Y_MATE] = filtered(kept, value, MATE)
     value = mate_terms[M_Z_MATE] + products((f_own, z_to_mate))
     finished[Z_MATE] = filtered(kept, value, MATE)
@@ -357,15 +353,14 @@
 def last_kernel(slots, part, term, unfinished, sqrt_next, result, sems):
     size = sqrt_next.shape[1]
     copies = []
-    for i in range(ROWS):
-        for j in range(ROWS):
-            at = len(copies)
-            rows, cols = quarter(i, j, size)
-            result[at] = part[rows, cols] + term[rows, cols]
-            slot = slots[i * SLOTS + PEER * ROWS + j, 0]
-            out = sqrt_next.at[i, :, pl.ds(pl.multiple_of(slot * size, size), size)]
-            copies.append(pltpu.make_async_copy(result.at[at], out, sems.at[at]))
-            copies[at].start()
+    blocks = [(i, j) for i in range(ROWS) for j in range(ROWS)]
+    starts = [slots[i * SLOTS + PEER * ROWS + j, 0] * size for i, j in blocks]
+    for at, (i, j) in enumerate(blocks):
+        rows, cols = quarter(i, j, size)
+        result[at] = part[rows, cols] + term[rows, cols]
+        out = sqrt_next.at[i, :, pl.ds(pl.multiple_of(starts[at], size), size)]
+        copies.append(pltpu.make_async_copy(result.at[at], out, sems.at[at]))
+        copies[at].start()
     for copy in copies:
         copy.wait()
 
@@ -425,15 +420,15 @@
         diagonal_kernel,
         (shape(2 * ROWS, block, block),),
         (sqrt_iterate, inverse_iterate),
-        scratch=[pltpu.SemaphoreType.DMA((2 * ROWS,))],
+        scratch=[pltpu.SemaphoreType.DMA((2,))],
         hbm_in=range(2),
     )
     peer_diagonal = to_peer(diagonal)
-    slots, kept, y_peer, strips, y_mate, mate_rest, y_side, z_side, own_pair = call(
+    slots, kept, y_peer, strips, mate, y_side, z_side, own_pair = call(
         functools.partial(pack_kernel, row_devices, col_devices),
         (
             shape(ROWS * SLOTS, block, dtype=jnp.int32), shape(KEPT_LINES, block),
-            one, shape(ROWS + 2, block, size), one, shape(3, size, size), one, one, pair,
+            one, shape(ROWS + 2, block, size), shape(4, size, size), one, one, pair,
         ),
         (pattern.T, keep_mask.T, row_order, sqrt_iterate, inverse_iterate, diagonal),
         scratch=[
@@ -449,15 +444,14 @@
     )
     peer_y = to_peer(y_peer)
     from_peer = to_peer(strips)
-    mate_y = to_mate(y_mate)
-    from_mate = to_mate(mate_rest)
+    from_mate = to_mate(mate)
     from_side = to_side(own_pair)
     (peer_spread,) = call(spread_kernel, (pair,), (peer_diagonal,), micros=10)
     (mate_terms,) = call(
         mate_kernel,
         (shape(5, size, size),),
-        (kept, y_mate, mate_rest, mate_y, from_mate, peer_spread),
-        any_in=(5,),
+        (kept, mate, from_mate, peer_spread),
+        any_in=(3,),
     )
     factor_own, peer_term = call(
         factor_own_kernel, (one, one), (kept, mate_terms, strips, peer_y), micros=5
@@ -472,7 +466,7 @@
             shape(5, 2, size, size, dtype=jnp.bfloat16),
         ),
         (
-            kept, y_peer, strips, y_mate, mate_rest, y_side, z_side, mate_terms,
+            kept, y_peer, strips, mate, y_side, z_side, mate_terms,
             peer_y, from_side, factor_own, mate_factor,
         ),
     )

time: 34.7 us -> 34.6 us (level)
  starting transfers between devices: 17.7 us -> 16 us
  waiting for transfers between devices: 5.2 us -> 6.62 us
    ppermute x4, waiting for transfers between devices: 5.18 us -> 6.61 us  [to_peer(): return lax.ppermute(value, 'row', route)]
    ppermute x4, starting transfers between devices: 8.47 us -> 7.68 us  [to_peer(): return lax.ppermute(value, 'row', route)]
    ppermute x3 -> x2, starting transfers between devices: 0.64 us -> 0.14 us  [to_mate(): return lax.ppermute(value, 'row', [(i, i ^ 1) for i in range(row_devices)])]
    ppermute x2, starting transfers between devices: 8.57 us -> 8.22 us  [to_side(): return lax.ppermute(value, 'col', route)]
  transfers between devices with their start and end apart: 9 -> 8, of which waited for: 3 -> 3; matrix products, arithmetic and copies ran while one was open for 0% -> 0% of each run, Pallas kernels for 27% -> 27%
where the time goes in v9:
time: 34.6 us; the launch traced here: 34.3 us
  starting transfers between devices  16 us (46%)
  Pallas kernels  10.9 us (32%)
  waiting for transfers between devices  6.62 us (19%)
  between operations  0.72 us (2%)
    pallas_call x9, Pallas kernels, call(): pl.pallas_call(kernel, out_shape=outs, in_specs=[spec(pltpu.HBM if at in...  10.9 us
    ppermute x2, starting transfers between devices, to_side(): return lax.ppermute(value, 'col', route)  8.22 us
    ppermute x4, starting transfers between devices, to_peer(): return lax.ppermute(value, 'row', route)  7.68 us
    ppermute x4, waiting for transfers between devices, to_peer(): return lax.ppermute(value, 'row', route)  6.61 us
  transfers between devices with their start and end apart: 8, of which 3 were waited for; matrix products, arithmetic and copies ran while one was open for 0% of the time, Pallas kernels for 27%

profile of v9, /device:TPU:0, one launch (start us, length us, event | category | flops | bytes accessed | tf_op | source)
XLA Modules:
  0.0 34.3 jit_solution(16907495991922779939)
XLA Ops:
  0.6 1.0 %shard_map.68.after = f32[4,128,128]{2,1,0:T(8,128)S(1)} custom-call(f32[2,128,1024]{2,1,0:T(8,128)} %sqrt_iterate.3, f32[2,128,1024]{2,1,0:T(8,128)} %inverse_iterate.3), custom_call_target="tpu_custom_call" | custom-call | tf_op jit(solution)/shard_map/pallas_call | solution.py:378
  1.6 3.4 %collective-permute-start.1 = (f32[4,128,128]{2,1,0:T(8,128)S(1)}, f32[4,128,128]{2,1,0:T(8,128)S(1)}, u32[]{:S(2)}, u32[]{:S(2)}) collective-permute-start(f32[4,128,128]{2,1,0:T(8,128)S(1)} %shard_map.68.after), channel_id=1, source_target_pairs={{0,28},{4,8},{8,4},{12,16},{16,12},{20,24},{24,20},{28,0},{1,29},{... | collective-permute-start | bytes 786440 | tf_op jit(solution)/shard_map/ppermute | solution.py:409
  5.0 1.7 %shard_map.69 = (s32[16,128]{1,0:T(8,128)S(1)}, f32[24,128]{1,0:T(8,128)S(1)}, f32[256,256]{1,0:T(8,128)S(1)}, f32[4,128,256]{2,1,0:T(8,128)S(1)}, f32[4,256,256...) custom-call(s32[8,64]{1,0:T(8,128)} %bitcast.2, ...), custom_call_target="tpu_custom_call" | custom-call | tf_op jit(solution)/shard_map/pallas_call | solution.py:378
  6.8 0.1 collective-permute-start
  6.8 0.7 %collective-permute-start.2 = (f32[256,256]{1,0:T(8,128)S(1)}, f32[256,256]{1,0:T(8,128)S(1)}, u32[]{:S(2)}, u32[]{:S(2)}) collective-permute-start(f32[256,256]{1,0:T(8,128)S(1)} %get-tuple-element.20.y_peer), channel_id=1, source_target_pairs={{0,28},{4,8},{8,4},{12,16},{16,12},{20,24},{24,20},{28,0},{1,29},{... | collective-permute-start | bytes 786440 | tf_op jit(solution)/shard_map/ppermute | solution.py:409
  7.5 3.7 %collective-permute-start.3 = (f32[2,256,256]{2,1,0:T(8,128)S(1)}, f32[2,256,256]{2,1,0:T(8,128)S(1)}, u32[]{:S(2)}, u32[]{:S(2)}) collective-permute-start(f32[2,256,256]{2,1,0:T(8,128)S(1)} %get-tuple-element.25), channel_id=1, source_target_pairs={{1,0},{2,1},{3,2},{0,3},{5,4},{6,5},{7,6},{4,7},{9,8},{10,9},{11,1... | collective-permute-start | bytes 1572872 | tf_op jit(solution)/shard_map/ppermute | solution.py:413
  11.3 1.6 %collective-permute-start.5 = (f32[4,128,256]{2,1,0:T(8,128)S(1)}, f32[4,128,256]{2,1,0:T(8,128)S(1)}, u32[]{:S(2)}, u32[]{:S(2)}) collective-permute-start(f32[4,128,256]{2,1,0:T(8,128)S(1)} %get-tuple-element.21.strips), channel_id=1, source_target_pairs={{0,28},{4,8},{8,4},{12,16},{16,12},{20,24},{24,20},{28,0},{1,29},{... | collective-permute-start | bytes 1572872 | tf_op jit(solution)/shard_map/ppermute | solution.py:409
  12.9 0.0 collective-permute-done.1.diagonal
  12.9 0.0 collective-permute-done.from_mate
  12.9 1.7 %shard_map.71.mate_terms = f32[5,256,256]{2,1,0:T(8,128)S(1)} custom-call(f32[24,128]{1,0:T(8,128)S(1)} %get-tuple-element.19.kept, f32[4,256,256]{2,1,0:T(8,128)S(1)} %get-tuple-element.22.mate, f32[4,256,256]{2,1,0:T(8,128)S(1)} %collective-permute-done.from_mate, f32[2,256,256]{2,1,0:T(8,128)S(1)} %shard_map.70.after.peer_spread), custom_call_target="tpu_custom_call" | custom-call | tf_op jit(solution)/shard_map/pallas_call | solution.py:378
  14.7 2.7 %collective-permute-done.2.peer_y = f32[256,256]{1,0:T(8,128)S(1)} collective-permute-done((f32[256,256]{1,0:T(8,128)S(1)}, f32[256,256]{1,0:T(8,128)S(1)}, u32[]{:S(2)}, u32[]{:S(2)}) %collective-permute-start.2) | collective-permute-done | bytes 262176 | tf_op jit(solution)/shard_map/ppermute | solution.py:409
  17.3 0.7 %shard_map.72 = (f32[256,256]{1,0:T(8,128)S(1)}, f32[256,256]{1,0:T(8,128)S(1)}) custom-call(f32[24,128]{1,0:T(8,128)S(1)} %get-tuple-element.19.kept, f32[5,256,256]{2,1,0:T(8,128)S(1)} %shard_map.71.mate_terms, f32[4,128,256]{2,1,0:T(8,128)S(1)} %get-tuple-element.21.strips, f32[256,256]{1,0:T(8,128)S(1)} %collective-permute-done.2.peer_y), custom_call_target="tpu_custom_call" | custom-call | flops 5765000192 | tf_op jit(solution)/shard_map/pallas_call | solution.py:378
  18.0 0.1 collective-permute-start.4
  18.1 4.5 %collective-permute-start.7 = (f32[256,256]{1,0:T(8,128)S(1)}, f32[256,256]{1,0:T(8,128)S(1)}, u32[]{:S(2)}, u32[]{:S(2)}) collective-permute-start(f32[256,256]{1,0:T(8,128)S(1)} %get-tuple-element.26.factor_own), channel_id=1, source_target_pairs={{1,0},{2,1},{3,2},{0,3},{5,4},{6,5},{7,6},{4,7},{9,8},{10,9},{11,1... | collective-permute-start | bytes 786440 | tf_op jit(solution)/shard_map/ppermute | solution.py:413
  22.6 2.0 %collective-permute-start.6 = (f32[256,256]{1,0:T(8,128)S(1)}, f32[256,256]{1,0:T(8,128)S(1)}, u32[]{:S(2)}, u32[]{:S(2)}) collective-permute-start(f32[256,256]{1,0:T(8,128)S(1)} %get-tuple-element.31), channel_id=1, source_target_pairs={{0,28},{4,8},{8,4},{12,16},{16,12},{20,24},{24,20},{28,0},{1,29},{... | collective-permute-start | bytes 786440 | tf_op jit(solution)/shard_map/ppermute | solution.py:409
  24.6 0.0 collective-permute-done.3.from_side
  24.6 0.0 collective-permute-done.4.mate_factor
  24.6 1.8 %shard_map.73 = (f32[3,256,256]{2,1,0:T(8,128)S(1)}, f32[5,256,256]{2,1,0:T(8,128)S(1)}, bf16[5,2,256,256]{3,2,1,0:T(8,128)(2,1)S(1)}) custom-call(f32[24,128]{1,0:T(8,128)S(1)} %get-tuple-element.19.kept, f32[256,256]{1,0:T(8,128)S(1)} %get-tuple-element.20.y_peer, f32[4,128,256]{2,1,0:T(8,128)S(1)} %get-tuple-element.21.strips, ...), custom_call_target="tpu_custom_call" | custom-call | tf_op jit(solution)/shard_map/pallas_call | solution.py:378
  26.4 2.2 %collective-permute-done.5.from_peer = f32[4,128,256]{2,1,0:T(8,128)S(1)} collective-permute-done((f32[4,128,256]{2,1,0:T(8,128)S(1)}, f32[4,128,256]{2,1,0:T(8,128)S(1)}, u32[]{:S(2)}, u32[]{:S(2)}) %collective-permute-start.5) | collective-permute-done | bytes 524320 | tf_op jit(solution)/shard_map/ppermute | solution.py:409
  28.6 2.0 %shard_map.74 = (f32[2,128,1024]{2,1,0:T(8,128)}, f32[2,128,1024]{2,1,0:T(8,128)}, f32[256,256]{1,0:T(8,128)S(1)}) custom-call(s32[16,128]{1,0:T(8,128)S(1)} %get-tuple-element.18.slots, f32[24,128]{1,0:T(8,128)S(1)} %get-tuple-element.19.kept, f32[3,256,256]{2,1,0:T(8,128)S(1)} %get-tuple-element.27.finished, f32[5,256,256]{2,1,0:T(8,128)S(1)} %get-tuple-element.28.partial, ...), custom_call_target="tpu_custom_call" | custom-call | tf_op jit(solution)/shard_map/pallas_call | solution.py:378
  30.5 0.0 collective-permute-done.7.factor
  30.6 1.2 %shard_map.75.unfinished = f32[2,128,1024]{2,1,0:T(8,128)} custom-call(s32[16,128]{1,0:T(8,128)S(1)} %get-tuple-element.18.slots, f32[24,128]{1,0:T(8,128)S(1)} %get-tuple-element.19.kept, f32[5,256,256]{2,1,0:T(8,128)S(1)} %get-tuple-element.28.partial, bf16[5,2,256,256]{3,2,1,0:T(8,128)(2,1)S(1)} %get-tuple-element.29.ready, ...), custom_call_target="tpu_custom_call", output_to_operand_aliasing={{}: (5, {})} | custom-call | tf_op jit(solution)/shard_map/pallas_call | solution.py:378
  31.8 1.8 %collective-permute-done.6.term = f32[256,256]{1,0:T(8,128)S(1)} collective-permute-done((f32[256,256]{1,0:T(8,128)S(1)}, f32[256,256]{1,0:T(8,128)S(1)}, u32[]{:S(2)}, u32[]{:S(2)}) %collective-permute-start.6) | collective-permute-done | bytes 262176 | tf_op jit(solution)/shard_map/ppermute | solution.py:409
  33.5 0.8 %shard_map.76 = f32[2,128,1024]{2,1,0:T(8,128)} custom-call(s32[16,128]{1,0:T(8,128)S(1)} %get-tuple-element.18.slots, f32[256,256]{1,0:T(8,128)S(1)} %get-tuple-element.30.part, f32[256,256]{1,0:T(8,128)S(1)} %collective-permute-done.6.term, f32[2,128,1024]{2,1,0:T(8,128)} %shard_map.75.unfinished), custom_call_target="tpu_custom_call", output_to_operand_aliasing={{}: (3, {})} | custom-call | tf_op jit(solution)/shard_map/pallas_call | solution.py:378
  (1 shorter events, 0.0 us)
Async XLA Ops:
  1.6 11.2 %collective-permute-start.1 = (f32[4,128,128]{2,1,0:T(8,128)S(1)}, f32[4,128,128]{2,1,0:T(8,128)S(1)}, u32[]{:S(2)}, u32[]{:S(2)}) collective-permute-start(f32[4,128,128]{2,1,0:T(8,128)S(1)} %shard_map.68.after), channel_id=1, source_target_pairs={{0,28},{4,8},{8,4},{12,16},{16,12},{20,24},{24,20},{28,0},{1,29},{... | collective-permute-start | bytes 786440 | tf_op jit(solution)/shard_map/ppermute | solution.py:409
  6.8 6.2 %collective-permute-start = (f32[4,256,256]{2,1,0:T(8,128)S(1)}, f32[4,256,256]{2,1,0:T(8,128)S(1)}, u32[]{:S(2)}, u32[]{:S(2)}) collective-permute-start(f32[4,256,256]{2,1,0:T(8,128)S(1)} %get-tuple-element.22.mate), channel_id=1, source_target_pairs={{0,4},{4,0},{8,12},{12,8},{16,20},{20,16},{24,28},{28,24},{1,5},{5... | collective-permute-start | bytes 3145736 | tf_op jit(solution)/shard_map/ppermute | solution.py:405
  6.8 10.5 %collective-permute-start.2 = (f32[256,256]{1,0:T(8,128)S(1)}, f32[256,256]{1,0:T(8,128)S(1)}, u32[]{:S(2)}, u32[]{:S(2)}) collective-permute-start(f32[256,256]{1,0:T(8,128)S(1)} %get-tuple-element.20.y_peer), channel_id=1, source_target_pairs={{0,28},{4,8},{8,4},{12,16},{16,12},{20,24},{24,20},{28,0},{1,29},{... | collective-permute-start | bytes 786440 | tf_op jit(solution)/shard_map/ppermute | solution.py:409
  7.5 17.0 %collective-permute-start.3 = (f32[2,256,256]{2,1,0:T(8,128)S(1)}, f32[2,256,256]{2,1,0:T(8,128)S(1)}, u32[]{:S(2)}, u32[]{:S(2)}) collective-permute-start(f32[2,256,256]{2,1,0:T(8,128)S(1)} %get-tuple-element.25), channel_id=1, source_target_pairs={{1,0},{2,1},{3,2},{0,3},{5,4},{6,5},{7,6},{4,7},{9,8},{10,9},{11,1... | collective-permute-start | bytes 1572872 | tf_op jit(solution)/shard_map/ppermute | solution.py:413
  11.3 17.3 %collective-permute-start.5 = (f32[4,128,256]{2,1,0:T(8,128)S(1)}, f32[4,128,256]{2,1,0:T(8,128)S(1)}, u32[]{:S(2)}, u32[]{:S(2)}) collective-permute-start(f32[4,128,256]{2,1,0:T(8,128)S(1)} %get-tuple-element.21.strips), channel_id=1, source_target_pairs={{0,28},{4,8},{8,4},{12,16},{16,12},{20,24},{24,20},{28,0},{1,29},{... | collective-permute-start | bytes 1572872 | tf_op jit(solution)/shard_map/ppermute | solution.py:409
  18.0 6.6 %collective-permute-start.4 = (f32[256,256]{1,0:T(8,128)S(1)}, f32[256,256]{1,0:T(8,128)S(1)}, u32[]{:S(2)}, u32[]{:S(2)}) collective-permute-start(f32[256,256]{1,0:T(8,128)S(1)} %get-tuple-element.26.factor_own), channel_id=1, source_target_pairs={{0,4},{4,0},{8,12},{12,8},{16,20},{20,16},{24,28},{28,24},{1,5},{5... | collective-permute-start | bytes 786440 | tf_op jit(solution)/shard_map/ppermute | solution.py:405
  18.1 12.5 %collective-permute-start.7 = (f32[256,256]{1,0:T(8,128)S(1)}, f32[256,256]{1,0:T(8,128)S(1)}, u32[]{:S(2)}, u32[]{:S(2)}) collective-permute-start(f32[256,256]{1,0:T(8,128)S(1)} %get-tuple-element.26.factor_own), channel_id=1, source_target_pairs={{1,0},{2,1},{3,2},{0,3},{5,4},{6,5},{7,6},{4,7},{9,8},{10,9},{11,1... | collective-permute-start | bytes 786440 | tf_op jit(solution)/shard_map/ppermute | solution.py:413
  22.6 11.0 %collective-permute-start.6 = (f32[256,256]{1,0:T(8,128)S(1)}, f32[256,256]{1,0:T(8,128)S(1)}, u32[]{:S(2)}, u32[]{:S(2)}) collective-permute-start(f32[256,256]{1,0:T(8,128)S(1)} %get-tuple-element.31), channel_id=1, source_target_pairs={{0,28},{4,8},{8,4},{12,16},{16,12},{20,24},{24,20},{28,0},{1,29},{... | collective-permute-start | bytes 786440 | tf_op jit(solution)/shard_map/ppermute | solution.py:409

commit v10 on v9

--- a/solution.py
+++ b/solution.py
@@ -11,6 +11,7 @@
 ROWS = 2
 SLOTS = 8
 KEPT_PEER_AT, KEPT_MATE_AT, KEPT_LINES = 16, 20, 24
+MATE_SLOT_AT, SLOT_LINES = 16, 24
 LARGEST = float(jnp.finfo(jnp.bfloat16).max)
 VMEM_LIMIT = 24 * 2**20
 PEAK = 1.153e9
@@ -76,6 +77,7 @@
 def look_up(row_devices, col_devices, pattern, keep, order, slots, kept):
     starts, labels = neighbours(row_devices, col_devices, order)
     own_labels = labels[OWN * ROWS:(OWN + 1) * ROWS]
+    mate_labels = labels[MATE * ROWS:(MATE + 1) * ROWS]
 
     def write_flags(stored, found, line):
         for j, slot in enumerate(found):
@@ -86,8 +88,10 @@
     for i in range(ROWS):
         found = find_slots(pattern, starts[OWN] + i, labels)
         result.append(found)
-        for j, slot in enumerate(found):
-            line = i * SLOTS + j
+        there = find_slots(pattern, starts[MATE] + i, own_labels + mate_labels)
+        for line, slot in (
+            *enumerate(found, i * SLOTS), *enumerate(there, MATE_SLOT_AT + i * 2 * ROWS)
+        ):
             slots[line:line + 1, :] = jnp.full((1, slots.shape[1]), slot)
         write_flags(starts[OWN] + i, found, i * SLOTS)
         for region, line in ((PEER, KEPT_PEER_AT), (MATE, KEPT_MATE_AT)):
@@ -168,7 +172,7 @@
 
 def pack_kernel(
     row_devices, col_devices, pattern, keep, order, sqrt_iterate, inverse_iterate, after,
-    slots, kept, y_peer, strips, mate, y_side, z_side, to_side,
+    slots, kept, y_peer, strips, y_mate, z_mate, y_side, z_side, to_side,
     pattern_here, keep_here, order_here, sqrt_here, inverse_here, sems,
 ):
     copies = [
@@ -192,22 +196,33 @@
     copies[3].wait()
     places = {
         PEER: (into(y_peer),),
-        OWN: (strip_own(strips, Y_BESIDE), into(mate.at[1]), into(to_side.at[0])),
-        MATE: (into(mate.at[0]),),
+        OWN: (strip_own(strips, Y_BESIDE), into(y_mate.at[1]), into(to_side.at[0])),
+        MATE: (into(y_mate.at[0]),),
         SIDE: (into(y_side),),
     }
     gather(slot_of, sqrt_here, places)
     copies[4].wait()
     places = {
         PEER: (strip_peer(strips),),
-        OWN: (strip_own(strips, Z_BESIDE), into(mate.at[3]), into(to_side.at[1])),
-        MATE: (into(mate.at[2]),),
+        OWN: (strip_own(strips, Z_BESIDE), into(z_mate.at[1]), into(to_side.at[1])),
+        MATE: (into(z_mate.at[0]),),
         SIDE: (into(z_side),),
     }
     gather(slot_of, inverse_here, places)
 
 
-def spread_kernel(diagonal, spread):
+def unpack_kernel(slots, whole, mate_y):
+    size = whole.shape[1]
+    for at in range(2):
+        for i in range(ROWS):
+            for j in range(ROWS):
+                slot = slots[MATE_SLOT_AT + (i * 2 + at) * ROWS + j, 0]
+                rows, cols = quarter(i, j, size)
+                start = pl.multiple_of(slot * size, size)
+                mate_y[at, rows, cols] = whole[i, :, pl.ds(start, size)]
+
+
+def spread_kernel(diagonal, after, spread):
     size = diagonal.shape[1]
     for at in range(2):
         for i in range(ROWS):
@@ -220,9 +235,11 @@
 M_OWN, M_Y_OWN, M_Y_MATE, M_Z_OWN, M_Z_MATE = range(5)
 
 
-def mate_kernel(kept, mate, from_mate, after, mate_terms):
-    y_to_mate, y_own, z_to_mate, z_own = (split(mate[at]) for at in range(4))
-    mate_y_mate, mate_y_own, mate_z_mate, mate_z_own = (split(from_mate[at]) for at in range(4))
+def mate_kernel(kept, y_mate, z_mate, mate_y, mate_z, after, mate_terms):
+    y_to_mate, y_own = split(y_mate[0]), split(y_mate[1])
+    z_to_mate, z_own = split(z_mate[0]), split(z_mate[1])
+    mate_y_mate, mate_y_own = split(mate_y[0]), split(mate_y[1])
+    mate_z_mate, mate_z_own = split(mate_z[0]), split(mate_z[1])
     mate_terms[M_OWN] = products((z_own, y_own), (z_to_mate, mate_y_mate))
     total = products((z_own, y_to_mate), (z_to_mate, mate_y_own))
     f_mate = split(filtered(kept, total, MATE, -0.5))
@@ -251,14 +268,15 @@
 
 
 def middle_kernel(
-    kept, y_peer, strips, mate, y_side, z_side, mate_terms,
+    kept, y_peer, strips, y_mate, z_mate, y_side, z_side, mate_terms,
     peer_y, from_side, factor_own, mate_factor,
     finished, partial, ready,
 ):
     def keep(at, parts):
         ready[at, 0], ready[at, 1] = parts
 
-    y_to_mate, y_own, z_to_mate, z_own = (split(mate[at]) for at in range(4))
+    y_to_mate, y_own = split(y_mate[0]), split(y_mate[1])
+    z_to_mate, z_own = split(z_mate[0]), split(z_mate[1])
     y_to_peer, z_to_peer = split(y_peer[...]), split(peer_part(strips))
     y_to_side, z_to_side = split(y_side[...]), split(z_side[...])
     f_own = split(factor_own[...])
@@ -416,6 +434,7 @@
         return jax.ShapeDtypeStruct(dims, dtype)
 
     one, pair = shape(size, size), shape(2, size, size)
+    whole = to_mate(sqrt_iterate)
     (diagonal,) = call(
         diagonal_kernel,
         (shape(2 * ROWS, block, block),),
@@ -424,11 +443,11 @@
         hbm_in=range(2),
     )
     peer_diagonal = to_peer(diagonal)
-    slots, kept, y_peer, strips, mate, y_side, z_side, own_pair = call(
+    slots, kept, y_peer, strips, y_mate, z_mate, y_side, z_side, own_pair = call(
         functools.partial(pack_kernel, row_devices, col_devices),
         (
-            shape(ROWS * SLOTS, block, dtype=jnp.int32), shape(KEPT_LINES, block),
-            one, shape(ROWS + 2, block, size), shape(4, size, size), one, one, pair,
+            shape(SLOT_LINES, block, dtype=jnp.int32), shape(KEPT_LINES, block),
+            one, shape(ROWS + 2, block, size), pair, pair, one, one, pair,
         ),
         (pattern.T, keep_mask.T, row_order, sqrt_iterate, inverse_iterate, diagonal),
         scratch=[
@@ -444,14 +463,17 @@
     )
     peer_y = to_peer(y_peer)
     from_peer = to_peer(strips)
-    from_mate = to_mate(mate)
+    mate_z = to_mate(z_mate)
     from_side = to_side(own_pair)
-    (peer_spread,) = call(spread_kernel, (pair,), (peer_diagonal,), micros=10)
+    (mate_y,) = call(unpack_kernel, (pair,), (slots, whole), micros=5)
+    (peer_spread,) = call(
+        spread_kernel, (pair,), (peer_diagonal, mate_y), any_in=(1,), micros=10
+    )
     (mate_terms,) = call(
         mate_kernel,
         (shape(5, size, size),),
-        (kept, mate, from_mate, peer_spread),
-        any_in=(3,),
+        (kept, y_mate, z_mate, mate_y, mate_z, peer_spread),
+        any_in=(5,),
     )
     factor_own, peer_term = call(
         factor_own_kernel, (one, one), (kept, mate_terms, strips, peer_y), micros=5
@@ -466,7 +488,7 @@
             shape(5, 2, size, size, dtype=jnp.bfloat16),
         ),
         (
-            kept, y_peer, strips, mate, y_side, z_side, mate_terms,
+            kept, y_peer, strips, y_mate, z_mate, y_side, z_side, mate_terms,
             peer_y, from_side, factor_own, mate_factor,
         ),
     )

time: 34.6 us -> 35.2 us (1.017)
  starting transfers between devices: 16 us -> 16.8 us
    ppermute x4, starting transfers between devices: 7.68 us -> 8.87 us  [to_peer(): return lax.ppermute(value, 'row', route)]
    ppermute x2, starting transfers between devices: 8.22 us -> 7.26 us  [to_side(): return lax.ppermute(value, 'col', route)]
    ppermute x2 -> x3, starting transfers between devices: 0.14 us -> 0.66 us  [to_mate(): return lax.ppermute(value, 'row', [(i, i ^ 1) for i in range(row_devices)])]
    pallas_call x9 -> x10, Pallas kernels: 10.9 us -> 11 us  [call(): pl.pallas_call(kernel, out_shape=outs, in_specs=[spec(pltpu.HBM if at in...]
  transfers between devices with their start and end apart: 8 -> 9, of which waited for: 3 -> 3; matrix products, arithmetic and copies ran while one was open for 0% -> 0% of each run, Pallas kernels for 27% -> 29%
where the time goes in v10:
time: 35.2 us; the launch traced here: 35.1 us
  starting transfers between devices  16.8 us (48%)
  Pallas kernels  11 us (31%)
  waiting for transfers between devices  6.51 us (18%)
  between operations  0.74 us (2%)
    pallas_call x10, Pallas kernels, call(): pl.pallas_call(kernel, out_shape=outs, in_specs=[spec(pltpu.HBM if at in...  11 us
    ppermute x4, starting transfers between devices, to_peer(): return lax.ppermute(value, 'row', route)  8.87 us
    ppermute x2, starting transfers between devices, to_side(): return lax.ppermute(value, 'col', route)  7.26 us
    ppermute x4, waiting for transfers between devices, to_peer(): return lax.ppermute(value, 'row', route)  6.49 us
  transfers between devices with their start and end apart: 9, of which 3 were waited for; matrix products, arithmetic and copies ran while one was open for 0% of the time, Pallas kernels for 29%

profile of v10, /device:TPU:0, one launch (start us, length us, event | category | flops | bytes accessed | tf_op | source)
XLA Modules:
  0.0 35.1 jit_solution(9578585686317139426)
XLA Ops:
  0.6 0.5 %collective-permute-start = (f32[2,128,1024]{2,1,0:T(8,128)}, f32[2,128,1024]{2,1,0:T(8,128)S(1)}, u32[]{:S(2)}, u32[]{:S(2)}) collective-permute-start(f32[2,128,1024]{2,1,0:T(8,128)} %sqrt_iterate.3), channel_id=1, source_target_pairs={{0,4},{4,0},{8,12},{12,8},{16,20},{20,16},{24,28},{28,24},{1,5},{5... | collective-permute-start | bytes 3145736 | tf_op jit(solution)/shard_map/ppermute | solution.py:423
  1.1 1.0 %shard_map.68.after = f32[4,128,128]{2,1,0:T(8,128)S(1)} custom-call(f32[2,128,1024]{2,1,0:T(8,128)} %sqrt_iterate.3, f32[2,128,1024]{2,1,0:T(8,128)} %inverse_iterate.3), custom_call_target="tpu_custom_call" | custom-call | tf_op jit(solution)/shard_map/pallas_call | solution.py:396
  2.1 3.6 %collective-permute-start.2 = (f32[4,128,128]{2,1,0:T(8,128)S(1)}, f32[4,128,128]{2,1,0:T(8,128)S(1)}, u32[]{:S(2)}, u32[]{:S(2)}) collective-permute-start(f32[4,128,128]{2,1,0:T(8,128)S(1)} %shard_map.68.after), channel_id=1, source_target_pairs={{0,28},{4,8},{8,4},{12,16},{16,12},{20,24},{24,20},{28,0},{1,29},{... | collective-permute-start | bytes 786440 | tf_op jit(solution)/shard_map/ppermute | solution.py:427
  5.8 1.7 %shard_map.69 = (s32[24,128]{1,0:T(8,128)S(1)}, f32[24,128]{1,0:T(8,128)S(1)}, f32[256,256]{1,0:T(8,128)S(1)}, f32[4,128,256]{2,1,0:T(8,128)S(1)}, f32[2,256,256...) custom-call(s32[8,64]{1,0:T(8,128)} %bitcast.2, ...), custom_call_target="tpu_custom_call" | custom-call | tf_op jit(solution)/shard_map/pallas_call | solution.py:396
  7.5 0.1 collective-permute-start.1
  7.6 0.6 %collective-permute-start.3 = (f32[256,256]{1,0:T(8,128)S(1)}, f32[256,256]{1,0:T(8,128)S(1)}, u32[]{:S(2)}, u32[]{:S(2)}) collective-permute-start(f32[256,256]{1,0:T(8,128)S(1)} %get-tuple-element.21.y_peer), channel_id=1, source_target_pairs={{0,28},{4,8},{8,4},{12,16},{16,12},{20,24},{24,20},{28,0},{1,29},{... | collective-permute-start | bytes 786440 | tf_op jit(solution)/shard_map/ppermute | solution.py:427
  8.2 3.6 %collective-permute-start.4 = (f32[2,256,256]{2,1,0:T(8,128)S(1)}, f32[2,256,256]{2,1,0:T(8,128)S(1)}, u32[]{:S(2)}, u32[]{:S(2)}) collective-permute-start(f32[2,256,256]{2,1,0:T(8,128)S(1)} %get-tuple-element.27), channel_id=1, source_target_pairs={{1,0},{2,1},{3,2},{0,3},{5,4},{6,5},{7,6},{4,7},{9,8},{10,9},{11,1... | collective-permute-start | bytes 1572872 | tf_op jit(solution)/shard_map/ppermute | solution.py:431
  11.8 0.0 collective-permute-done.whole
  11.8 1.8 %collective-permute-start.6 = (f32[4,128,256]{2,1,0:T(8,128)S(1)}, f32[4,128,256]{2,1,0:T(8,128)S(1)}, u32[]{:S(2)}, u32[]{:S(2)}) collective-permute-start(f32[4,128,256]{2,1,0:T(8,128)S(1)} %get-tuple-element.22.strips), channel_id=1, source_target_pairs={{0,28},{4,8},{8,4},{12,16},{16,12},{20,24},{24,20},{28,0},{1,29},{... | collective-permute-start | bytes 1572872 | tf_op jit(solution)/shard_map/ppermute | solution.py:427
  13.6 0.1 shard_map.70.after.mate_y
  13.7 0.0 collective-permute-done.2.diagonal
  13.8 0.0 collective-permute-done.1.mate_z
  13.8 1.7 %shard_map.72.mate_terms = f32[5,256,256]{2,1,0:T(8,128)S(1)} custom-call(f32[24,128]{1,0:T(8,128)S(1)} %get-tuple-element.20.kept, f32[2,256,256]{2,1,0:T(8,128)S(1)} %get-tuple-element.23.y_mate, f32[2,256,256]{2,1,0:T(8,128)S(1)} %get-tuple-element.24.z_mate, f32[2,256,256]{2,1,0:T(8,128)S(1)} %shard_map.70.after.mate_y, ...), custom_call_target="tpu_custom_call" | custom-call | tf_op jit(solution)/shard_map/pallas_call | solution.py:396
  15.5 2.6 %collective-permute-done.3.peer_y = f32[256,256]{1,0:T(8,128)S(1)} collective-permute-done((f32[256,256]{1,0:T(8,128)S(1)}, f32[256,256]{1,0:T(8,128)S(1)}, u32[]{:S(2)}, u32[]{:S(2)}) %collective-permute-start.3) | collective-permute-done | bytes 262176 | tf_op jit(solution)/shard_map/ppermute | solution.py:427
  18.1 0.7 %shard_map.73 = (f32[256,256]{1,0:T(8,128)S(1)}, f32[256,256]{1,0:T(8,128)S(1)}) custom-call(f32[24,128]{1,0:T(8,128)S(1)} %get-tuple-element.20.kept, f32[5,256,256]{2,1,0:T(8,128)S(1)} %shard_map.72.mate_terms, f32[4,128,256]{2,1,0:T(8,128)S(1)} %get-tuple-element.22.strips, f32[256,256]{1,0:T(8,128)S(1)} %collective-permute-done.3.peer_y), custom_call_target="tpu_custom_call" | custom-call | flops 5765000192 | tf_op jit(solution)/shard_map/pallas_call | solution.py:396
  18.8 0.1 collective-permute-start.5
  18.9 3.7 %collective-permute-start.8 = (f32[256,256]{1,0:T(8,128)S(1)}, f32[256,256]{1,0:T(8,128)S(1)}, u32[]{:S(2)}, u32[]{:S(2)}) collective-permute-start(f32[256,256]{1,0:T(8,128)S(1)} %get-tuple-element.28.factor_own), channel_id=1, source_target_pairs={{1,0},{2,1},{3,2},{0,3},{5,4},{6,5},{7,6},{4,7},{9,8},{10,9},{11,1... | collective-permute-start | bytes 786440 | tf_op jit(solution)/shard_map/ppermute | solution.py:431
  22.6 2.8 %collective-permute-start.7 = (f32[256,256]{1,0:T(8,128)S(1)}, f32[256,256]{1,0:T(8,128)S(1)}, u32[]{:S(2)}, u32[]{:S(2)}) collective-permute-start(f32[256,256]{1,0:T(8,128)S(1)} %get-tuple-element.33), channel_id=1, source_target_pairs={{0,28},{4,8},{8,4},{12,16},{16,12},{20,24},{24,20},{28,0},{1,29},{... | collective-permute-start | bytes 786440 | tf_op jit(solution)/shard_map/ppermute | solution.py:427
  25.4 1.8 %shard_map.74 = (f32[3,256,256]{2,1,0:T(8,128)S(1)}, f32[5,256,256]{2,1,0:T(8,128)S(1)}, bf16[5,2,256,256]{3,2,1,0:T(8,128)(2,1)S(1)}) custom-call(f32[24,128]{1,0:T(8,128)S(1)} %get-tuple-element.20.kept, f32[256,256]{1,0:T(8,128)S(1)} %get-tuple-element.21.y_peer, f32[4,128,256]{2,1,0:T(8,128)S(1)} %get-tuple-element.22.strips, ...), custom_call_target="tpu_custom_call" | custom-call | tf_op jit(solution)/shard_map/pallas_call | solution.py:396
  27.2 2.1 %collective-permute-done.6.from_peer = f32[4,128,256]{2,1,0:T(8,128)S(1)} collective-permute-done((f32[4,128,256]{2,1,0:T(8,128)S(1)}, f32[4,128,256]{2,1,0:T(8,128)S(1)}, u32[]{:S(2)}, u32[]{:S(2)}) %collective-permute-start.6) | collective-permute-done | bytes 524320 | tf_op jit(solution)/shard_map/ppermute | solution.py:427
  29.4 2.0 %shard_map.75 = (f32[2,128,1024]{2,1,0:T(8,128)}, f32[2,128,1024]{2,1,0:T(8,128)}, f32[256,256]{1,0:T(8,128)S(1)}) custom-call(s32[24,128]{1,0:T(8,128)S(1)} %get-tuple-element.19.slots, f32[24,128]{1,0:T(8,128)S(1)} %get-tuple-element.20.kept, f32[3,256,256]{2,1,0:T(8,128)S(1)} %get-tuple-element.29.finished, f32[5,256,256]{2,1,0:T(8,128)S(1)} %get-tuple-element.30.partial, ...), custom_call_target="tpu_custom_call" | custom-call | tf_op jit(solution)/shard_map/pallas_call | solution.py:396
  31.4 1.2 %shard_map.76.unfinished = f32[2,128,1024]{2,1,0:T(8,128)} custom-call(s32[24,128]{1,0:T(8,128)S(1)} %get-tuple-element.19.slots, f32[24,128]{1,0:T(8,128)S(1)} %get-tuple-element.20.kept, f32[5,256,256]{2,1,0:T(8,128)S(1)} %get-tuple-element.30.partial, bf16[5,2,256,256]{3,2,1,0:T(8,128)(2,1)S(1)} %get-tuple-element.31.ready, ...), custom_call_target="tpu_custom_call", output_to_operand_aliasing={{}: (5, {})} | custom-call | tf_op jit(solution)/shard_map/pallas_call | solution.py:396
  32.6 1.7 %collective-permute-done.7.term = f32[256,256]{1,0:T(8,128)S(1)} collective-permute-done((f32[256,256]{1,0:T(8,128)S(1)}, f32[256,256]{1,0:T(8,128)S(1)}, u32[]{:S(2)}, u32[]{:S(2)}) %collective-permute-start.7) | collective-permute-done | bytes 262176 | tf_op jit(solution)/shard_map/ppermute | solution.py:427
  34.3 0.8 %shard_map.77 = f32[2,128,1024]{2,1,0:T(8,128)} custom-call(s32[24,128]{1,0:T(8,128)S(1)} %get-tuple-element.19.slots, f32[256,256]{1,0:T(8,128)S(1)} %get-tuple-element.32.part, f32[256,256]{1,0:T(8,128)S(1)} %collective-permute-done.7.term, f32[2,128,1024]{2,1,0:T(8,128)} %shard_map.76.unfinished), custom_call_target="tpu_custom_call", output_to_operand_aliasing={{}: (3, {})} | custom-call | tf_op jit(solution)/shard_map/pallas_call | solution.py:396
  (4 shorter events, 0.0 us)
Async XLA Ops:
  0.6 11.2 %collective-permute-start = (f32[2,128,1024]{2,1,0:T(8,128)}, f32[2,128,1024]{2,1,0:T(8,128)S(1)}, u32[]{:S(2)}, u32[]{:S(2)}) collective-permute-start(f32[2,128,1024]{2,1,0:T(8,128)} %sqrt_iterate.3), channel_id=1, source_target_pairs={{0,4},{4,0},{8,12},{12,8},{16,20},{20,16},{24,28},{28,24},{1,5},{5... | collective-permute-start | bytes 3145736 | tf_op jit(solution)/shard_map/ppermute | solution.py:423
  2.1 11.6 %collective-permute-start.2 = (f32[4,128,128]{2,1,0:T(8,128)S(1)}, f32[4,128,128]{2,1,0:T(8,128)S(1)}, u32[]{:S(2)}, u32[]{:S(2)}) collective-permute-start(f32[4,128,128]{2,1,0:T(8,128)S(1)} %shard_map.68.after), channel_id=1, source_target_pairs={{0,28},{4,8},{8,4},{12,16},{16,12},{20,24},{24,20},{28,0},{1,29},{... | collective-permute-start | bytes 786440 | tf_op jit(solution)/shard_map/ppermute | solution.py:427
  7.5 6.3 %collective-permute-start.1 = (f32[2,256,256]{2,1,0:T(8,128)S(1)}, f32[2,256,256]{2,1,0:T(8,128)S(1)}, u32[]{:S(2)}, u32[]{:S(2)}) collective-permute-start(f32[2,256,256]{2,1,0:T(8,128)S(1)} %get-tuple-element.24.z_mate), channel_id=1, source_target_pairs={{0,4},{4,0},{8,12},{12,8},{16,20},{20,16},{24,28},{28,24},{1,5},{5... | collective-permute-start | bytes 1572872 | tf_op jit(solution)/shard_map/ppermute | solution.py:423
  7.6 10.6 %collective-permute-start.3 = (f32[256,256]{1,0:T(8,128)S(1)}, f32[256,256]{1,0:T(8,128)S(1)}, u32[]{:S(2)}, u32[]{:S(2)}) collective-permute-start(f32[256,256]{1,0:T(8,128)S(1)} %get-tuple-element.21.y_peer), channel_id=1, source_target_pairs={{0,28},{4,8},{8,4},{12,16},{16,12},{20,24},{24,20},{28,0},{1,29},{... | collective-permute-start | bytes 786440 | tf_op jit(solution)/shard_map/ppermute | solution.py:427
  8.2 17.2 %collective-permute-start.4 = (f32[2,256,256]{2,1,0:T(8,128)S(1)}, f32[2,256,256]{2,1,0:T(8,128)S(1)}, u32[]{:S(2)}, u32[]{:S(2)}) collective-permute-start(f32[2,256,256]{2,1,0:T(8,128)S(1)} %get-tuple-element.27), channel_id=1, source_target_pairs={{1,0},{2,1},{3,2},{0,3},{5,4},{6,5},{7,6},{4,7},{9,8},{10,9},{11,1... | collective-permute-start | bytes 1572872 | tf_op jit(solution)/shard_map/ppermute | solution.py:431
  11.8 17.6 %collective-permute-start.6 = (f32[4,128,256]{2,1,0:T(8,128)S(1)}, f32[4,128,256]{2,1,0:T(8,128)S(1)}, u32[]{:S(2)}, u32[]{:S(2)}) collective-permute-start(f32[4,128,256]{2,1,0:T(8,128)S(1)} %get-tuple-element.22.strips), channel_id=1, source_target_pairs={{0,28},{4,8},{8,4},{12,16},{16,12},{20,24},{24,20},{28,0},{1,29},{... | collective-permute-start | bytes 1572872 | tf_op jit(solution)/shard_map/ppermute | solution.py:427
  18.8 6.6 %collective-permute-start.5 = (f32[256,256]{1,0:T(8,128)S(1)}, f32[256,256]{1,0:T(8,128)S(1)}, u32[]{:S(2)}, u32[]{:S(2)}) collective-permute-start(f32[256,256]{1,0:T(8,128)S(1)} %get-tuple-element.28.factor_own), channel_id=1, source_target_pairs={{0,4},{4,0},{8,12},{12,8},{16,20},{20,16},{24,28},{28,24},{1,5},{5... | collective-permute-start | bytes 786440 | tf_op jit(solution)/shard_map/ppermute | solution.py:423
  18.9 12.5 %collective-permute-start.8 = (f32[256,256]{1,0:T(8,128)S(1)}, f32[256,256]{1,0:T(8,128)S(1)}, u32[]{:S(2)}, u32[]{:S(2)}) collective-permute-start(f32[256,256]{1,0:T(8,128)S(1)} %get-tuple-element.28.factor_own), channel_id=1, source_target_pairs={{1,0},{2,1},{3,2},{0,3},{5,4},{6,5},{7,6},{4,7},{9,8},{10,9},{11,1... | collective-permute-start | bytes 786440 | tf_op jit(solution)/shard_map/ppermute | solution.py:431
  22.6 11.7 %collective-permute-start.7 = (f32[256,256]{1,0:T(8,128)S(1)}, f32[256,256]{1,0:T(8,128)S(1)}, u32[]{:S(2)}, u32[]{:S(2)}) collective-permute-start(f32[256,256]{1,0:T(8,128)S(1)} %get-tuple-element.33), channel_id=1, source_target_pairs={{0,28},{4,8},{8,4},{12,16},{16,12},{20,24},{24,20},{28,0},{1,29},{... | collective-permute-start | bytes 786440 | tf_op jit(solution)/shard_map/ppermute | solution.py:427

commit v11 on v9

--- a/solution.py
+++ b/solution.py
@@ -169,18 +169,17 @@
 def pack_kernel(
     row_devices, col_devices, pattern, keep, order, sqrt_iterate, inverse_iterate, after,
     slots, kept, y_peer, strips, mate, y_side, z_side, to_side,
-    pattern_here, keep_here, order_here, sqrt_here, inverse_here, sems,
+    pattern_here, keep_here, order_here, sems,
 ):
     copies = [
         pltpu.make_async_copy(source, here, sems.at[at])
         for at, (source, here) in enumerate((
             (order, order_here), (pattern, pattern_here), (keep, keep_here),
-            (sqrt_iterate, sqrt_here), (inverse_iterate, inverse_here),
         ))
     ]
     for copy in copies:
         copy.start()
-    for copy in copies[:3]:
+    for copy in copies:
         copy.wait()
     found = look_up(
         row_devices, col_devices, pattern_here, keep_here, order_here, slots, kept
@@ -189,22 +188,20 @@
     def slot_of(i, j):
         return found[i][j]
 
-    copies[3].wait()
     places = {
         PEER: (into(y_peer),),
         OWN: (strip_own(strips, Y_BESIDE), into(mate.at[1]), into(to_side.at[0])),
         MATE: (into(mate.at[0]),),
         SIDE: (into(y_side),),
     }
-    gather(slot_of, sqrt_here, places)
-    copies[4].wait()
+    gather(slot_of, sqrt_iterate, places)
     places = {
         PEER: (strip_peer(strips),),
         OWN: (strip_own(strips, Z_BESIDE), into(mate.at[3]), into(to_side.at[1])),
         MATE: (into(mate.at[2]),),
         SIDE: (into(z_side),),
     }
-    gather(slot_of, inverse_here, places)
+    gather(slot_of, inverse_iterate, places)
 
 
 def spread_kernel(diagonal, spread):
@@ -435,11 +432,9 @@
             pltpu.SMEM(pattern.T.shape, jnp.int32),
             pltpu.SMEM(keep_mask.T.shape, jnp.int32),
             pltpu.SMEM(row_order.shape, jnp.int32),
-            pltpu.VMEM(sqrt_iterate.shape, jnp.float32),
-            pltpu.VMEM(inverse_iterate.shape, jnp.float32),
-            pltpu.SemaphoreType.DMA((5,)),
+            pltpu.SemaphoreType.DMA((3,)),
         ],
-        hbm_in=range(5),
+        hbm_in=range(3),
         any_in=(5,),
     )
     peer_y = to_peer(y_peer)

time: 34.6 us -> 34.7 us (level)
  waiting for transfers between devices: 6.62 us -> 7.07 us
    ppermute x4, waiting for transfers between devices: 6.61 us -> 7.05 us  [to_peer(): return lax.ppermute(value, 'row', route)]
  transfers between devices with their start and end apart: 8 -> 8, of which waited for: 3 -> 3; matrix products, arithmetic and copies ran while one was open for 0% -> 0% of each run, Pallas kernels for 27% -> 25%
where the time goes in v11:
time: 34.7 us; the launch traced here: 34.5 us
  starting transfers between devices  16 us (46%)
  Pallas kernels  10.6 us (31%)
  waiting for transfers between devices  7.07 us (20%)
  between operations  0.74 us (2%)
    pallas_call x9, Pallas kernels, call(): pl.pallas_call(kernel, out_shape=outs, in_specs=[spec(pltpu.HBM if at in...  10.6 us
    ppermute x2, starting transfers between devices, to_side(): return lax.ppermute(value, 'col', route)  8.08 us
    ppermute x4, starting transfers between devices, to_peer(): return lax.ppermute(value, 'row', route)  7.83 us
    ppermute x4, waiting for transfers between devices, to_peer(): return lax.ppermute(value, 'row', route)  7.05 us
  transfers between devices with their start and end apart: 8, of which 3 were waited for; matrix products, arithmetic and copies ran while one was open for 0% of the time, Pallas kernels for 25%

profile of v11, /device:TPU:0, one launch (start us, length us, event | category | flops | bytes accessed | tf_op | source)
XLA Modules:
  0.0 34.5 jit_solution(13866625830831680601)
XLA Ops:
  0.6 1.1 %shard_map.68.after = f32[4,128,128]{2,1,0:T(8,128)S(1)} custom-call(f32[2,128,1024]{2,1,0:T(8,128)} %sqrt_iterate.3, f32[2,128,1024]{2,1,0:T(8,128)} %inverse_iterate.3), custom_call_target="tpu_custom_call" | custom-call | tf_op jit(solution)/shard_map/pallas_call | solution.py:375
  1.8 3.4 %collective-permute-start.1 = (f32[4,128,128]{2,1,0:T(8,128)S(1)}, f32[4,128,128]{2,1,0:T(8,128)S(1)}, u32[]{:S(2)}, u32[]{:S(2)}) collective-permute-start(f32[4,128,128]{2,1,0:T(8,128)S(1)} %shard_map.68.after), channel_id=1, source_target_pairs={{0,28},{4,8},{8,4},{12,16},{16,12},{20,24},{24,20},{28,0},{1,29},{... | collective-permute-start | bytes 786440 | tf_op jit(solution)/shard_map/ppermute | solution.py:406
  5.2 1.3 %shard_map.69 = (s32[16,128]{1,0:T(8,128)S(1)}, f32[24,128]{1,0:T(8,128)S(1)}, f32[256,256]{1,0:T(8,128)S(1)}, f32[4,128,256]{2,1,0:T(8,128)S(1)}, f32[4,256,256...) custom-call(s32[8,64]{1,0:T(8,128)} %bitcast.2, ...), custom_call_target="tpu_custom_call" | custom-call | tf_op jit(solution)/shard_map/pallas_call | solution.py:375
  6.5 0.1 collective-permute-start
  6.6 1.1 %collective-permute-start.2 = (f32[256,256]{1,0:T(8,128)S(1)}, f32[256,256]{1,0:T(8,128)S(1)}, u32[]{:S(2)}, u32[]{:S(2)}) collective-permute-start(f32[256,256]{1,0:T(8,128)S(1)} %get-tuple-element.20.y_peer), channel_id=1, source_target_pairs={{0,28},{4,8},{8,4},{12,16},{16,12},{20,24},{24,20},{28,0},{1,29},{... | collective-permute-start | bytes 786440 | tf_op jit(solution)/shard_map/ppermute | solution.py:406
  7.7 3.6 %collective-permute-start.3 = (f32[2,256,256]{2,1,0:T(8,128)S(1)}, f32[2,256,256]{2,1,0:T(8,128)S(1)}, u32[]{:S(2)}, u32[]{:S(2)}) collective-permute-start(f32[2,256,256]{2,1,0:T(8,128)S(1)} %get-tuple-element.25), channel_id=1, source_target_pairs={{1,0},{2,1},{3,2},{0,3},{5,4},{6,5},{7,6},{4,7},{9,8},{10,9},{11,1... | collective-permute-start | bytes 1572872 | tf_op jit(solution)/shard_map/ppermute | solution.py:410
  11.3 1.3 %collective-permute-start.5 = (f32[4,128,256]{2,1,0:T(8,128)S(1)}, f32[4,128,256]{2,1,0:T(8,128)S(1)}, u32[]{:S(2)}, u32[]{:S(2)}) collective-permute-start(f32[4,128,256]{2,1,0:T(8,128)S(1)} %get-tuple-element.21.strips), channel_id=1, source_target_pairs={{0,28},{4,8},{8,4},{12,16},{16,12},{20,24},{24,20},{28,0},{1,29},{... | collective-permute-start | bytes 1572872 | tf_op jit(solution)/shard_map/ppermute | solution.py:406
  12.6 0.0 collective-permute-done.1.diagonal
  12.6 0.0 collective-permute-done.from_mate
  12.7 1.7 %shard_map.71.mate_terms = f32[5,256,256]{2,1,0:T(8,128)S(1)} custom-call(f32[24,128]{1,0:T(8,128)S(1)} %get-tuple-element.19.kept, f32[4,256,256]{2,1,0:T(8,128)S(1)} %get-tuple-element.22.mate, f32[4,256,256]{2,1,0:T(8,128)S(1)} %collective-permute-done.from_mate, f32[2,256,256]{2,1,0:T(8,128)S(1)} %shard_map.70.after.peer_spread), custom_call_target="tpu_custom_call" | custom-call | tf_op jit(solution)/shard_map/pallas_call | solution.py:375
  14.4 3.1 %collective-permute-done.2.peer_y = f32[256,256]{1,0:T(8,128)S(1)} collective-permute-done((f32[256,256]{1,0:T(8,128)S(1)}, f32[256,256]{1,0:T(8,128)S(1)}, u32[]{:S(2)}, u32[]{:S(2)}) %collective-permute-start.2) | collective-permute-done | bytes 262176 | tf_op jit(solution)/shard_map/ppermute | solution.py:406
  17.5 0.7 %shard_map.72 = (f32[256,256]{1,0:T(8,128)S(1)}, f32[256,256]{1,0:T(8,128)S(1)}) custom-call(f32[24,128]{1,0:T(8,128)S(1)} %get-tuple-element.19.kept, f32[5,256,256]{2,1,0:T(8,128)S(1)} %shard_map.71.mate_terms, f32[4,128,256]{2,1,0:T(8,128)S(1)} %get-tuple-element.21.strips, f32[256,256]{1,0:T(8,128)S(1)} %collective-permute-done.2.peer_y), custom_call_target="tpu_custom_call" | custom-call | flops 5765000192 | tf_op jit(solution)/shard_map/pallas_call | solution.py:375
  18.2 0.1 collective-permute-start.4
  18.3 4.5 %collective-permute-start.7 = (f32[256,256]{1,0:T(8,128)S(1)}, f32[256,256]{1,0:T(8,128)S(1)}, u32[]{:S(2)}, u32[]{:S(2)}) collective-permute-start(f32[256,256]{1,0:T(8,128)S(1)} %get-tuple-element.26.factor_own), channel_id=1, source_target_pairs={{1,0},{2,1},{3,2},{0,3},{5,4},{6,5},{7,6},{4,7},{9,8},{10,9},{11,1... | collective-permute-start | bytes 786440 | tf_op jit(solution)/shard_map/ppermute | solution.py:410
  22.7 2.0 %collective-permute-start.6 = (f32[256,256]{1,0:T(8,128)S(1)}, f32[256,256]{1,0:T(8,128)S(1)}, u32[]{:S(2)}, u32[]{:S(2)}) collective-permute-start(f32[256,256]{1,0:T(8,128)S(1)} %get-tuple-element.31), channel_id=1, source_target_pairs={{0,28},{4,8},{8,4},{12,16},{16,12},{20,24},{24,20},{28,0},{1,29},{... | collective-permute-start | bytes 786440 | tf_op jit(solution)/shard_map/ppermute | solution.py:406
  24.7 0.0 collective-permute-done.3.from_side
  24.7 0.0 collective-permute-done.4.mate_factor
  24.7 1.8 %shard_map.73 = (f32[3,256,256]{2,1,0:T(8,128)S(1)}, f32[5,256,256]{2,1,0:T(8,128)S(1)}, bf16[5,2,256,256]{3,2,1,0:T(8,128)(2,1)S(1)}) custom-call(f32[24,128]{1,0:T(8,128)S(1)} %get-tuple-element.19.kept, f32[256,256]{1,0:T(8,128)S(1)} %get-tuple-element.20.y_peer, f32[4,128,256]{2,1,0:T(8,128)S(1)} %get-tuple-element.21.strips, ...), custom_call_target="tpu_custom_call" | custom-call | tf_op jit(solution)/shard_map/pallas_call | solution.py:375
  26.6 2.2 %collective-permute-done.5.from_peer = f32[4,128,256]{2,1,0:T(8,128)S(1)} collective-permute-done((f32[4,128,256]{2,1,0:T(8,128)S(1)}, f32[4,128,256]{2,1,0:T(8,128)S(1)}, u32[]{:S(2)}, u32[]{:S(2)}) %collective-permute-start.5) | collective-permute-done | bytes 524320 | tf_op jit(solution)/shard_map/ppermute | solution.py:406
  28.7 2.0 %shard_map.74 = (f32[2,128,1024]{2,1,0:T(8,128)}, f32[2,128,1024]{2,1,0:T(8,128)}, f32[256,256]{1,0:T(8,128)S(1)}) custom-call(s32[16,128]{1,0:T(8,128)S(1)} %get-tuple-element.18.slots, f32[24,128]{1,0:T(8,128)S(1)} %get-tuple-element.19.kept, f32[3,256,256]{2,1,0:T(8,128)S(1)} %get-tuple-element.27.finished, f32[5,256,256]{2,1,0:T(8,128)S(1)} %get-tuple-element.28.partial, ...), custom_call_target="tpu_custom_call" | custom-call | tf_op jit(solution)/shard_map/pallas_call | solution.py:375
  30.7 0.0 collective-permute-done.7.factor
  30.7 1.2 %shard_map.75.unfinished = f32[2,128,1024]{2,1,0:T(8,128)} custom-call(s32[16,128]{1,0:T(8,128)S(1)} %get-tuple-element.18.slots, f32[24,128]{1,0:T(8,128)S(1)} %get-tuple-element.19.kept, f32[5,256,256]{2,1,0:T(8,128)S(1)} %get-tuple-element.28.partial, bf16[5,2,256,256]{3,2,1,0:T(8,128)(2,1)S(1)} %get-tuple-element.29.ready, ...), custom_call_target="tpu_custom_call", output_to_operand_aliasing={{}: (5, {})} | custom-call | tf_op jit(solution)/shard_map/pallas_call | solution.py:375
  31.9 1.8 %collective-permute-done.6.term = f32[256,256]{1,0:T(8,128)S(1)} collective-permute-done((f32[256,256]{1,0:T(8,128)S(1)}, f32[256,256]{1,0:T(8,128)S(1)}, u32[]{:S(2)}, u32[]{:S(2)}) %collective-permute-start.6) | collective-permute-done | bytes 262176 | tf_op jit(solution)/shard_map/ppermute | solution.py:406
  33.7 0.8 %shard_map.76 = f32[2,128,1024]{2,1,0:T(8,128)} custom-call(s32[16,128]{1,0:T(8,128)S(1)} %get-tuple-element.18.slots, f32[256,256]{1,0:T(8,128)S(1)} %get-tuple-element.30.part, f32[256,256]{1,0:T(8,128)S(1)} %collective-permute-done.6.term, f32[2,128,1024]{2,1,0:T(8,128)} %shard_map.75.unfinished), custom_call_target="tpu_custom_call", output_to_operand_aliasing={{}: (3, {})} | custom-call | tf_op jit(solution)/shard_map/pallas_call | solution.py:375
  (5 shorter events, 0.0 us)
Async XLA Ops:
  0.6 4.6 %copy-start = (f32[2,128,1024]{2,1,0:T(8,128)S(1)}, f32[2,128,1024]{2,1,0:T(8,128)}, u32[]{:S(2)}) copy-start(f32[2,128,1024]{2,1,0:T(8,128)} %sqrt_iterate.3) | copy-start | bytes 3145732
  0.6 4.6 %copy-start.1 = (f32[2,128,1024]{2,1,0:T(8,128)S(1)}, f32[2,128,1024]{2,1,0:T(8,128)}, u32[]{:S(2)}) copy-start(f32[2,128,1024]{2,1,0:T(8,128)} %inverse_iterate.3) | copy-start | bytes 3145732
  1.8 10.8 %collective-permute-start.1 = (f32[4,128,128]{2,1,0:T(8,128)S(1)}, f32[4,128,128]{2,1,0:T(8,128)S(1)}, u32[]{:S(2)}, u32[]{:S(2)}) collective-permute-start(f32[4,128,128]{2,1,0:T(8,128)S(1)} %shard_map.68.after), channel_id=1, source_target_pairs={{0,28},{4,8},{8,4},{12,16},{16,12},{20,24},{24,20},{28,0},{1,29},{... | collective-permute-start | bytes 786440 | tf_op jit(solution)/shard_map/ppermute | solution.py:406
  6.5 6.2 %collective-permute-start = (f32[4,256,256]{2,1,0:T(8,128)S(1)}, f32[4,256,256]{2,1,0:T(8,128)S(1)}, u32[]{:S(2)}, u32[]{:S(2)}) collective-permute-start(f32[4,256,256]{2,1,0:T(8,128)S(1)} %get-tuple-element.22.mate), channel_id=1, source_target_pairs={{0,4},{4,0},{8,12},{12,8},{16,20},{20,16},{24,28},{28,24},{1,5},{5... | collective-permute-start | bytes 3145736 | tf_op jit(solution)/shard_map/ppermute | solution.py:402
  6.6 10.9 %collective-permute-start.2 = (f32[256,256]{1,0:T(8,128)S(1)}, f32[256,256]{1,0:T(8,128)S(1)}, u32[]{:S(2)}, u32[]{:S(2)}) collective-permute-start(f32[256,256]{1,0:T(8,128)S(1)} %get-tuple-element.20.y_peer), channel_id=1, source_target_pairs={{0,28},{4,8},{8,4},{12,16},{16,12},{20,24},{24,20},{28,0},{1,29},{... | collective-permute-start | bytes 786440 | tf_op jit(solution)/shard_map/ppermute | solution.py:406
  7.7 17.1 %collective-permute-start.3 = (f32[2,256,256]{2,1,0:T(8,128)S(1)}, f32[2,256,256]{2,1,0:T(8,128)S(1)}, u32[]{:S(2)}, u32[]{:S(2)}) collective-permute-start(f32[2,256,256]{2,1,0:T(8,128)S(1)} %get-tuple-element.25), channel_id=1, source_target_pairs={{1,0},{2,1},{3,2},{0,3},{5,4},{6,5},{7,6},{4,7},{9,8},{10,9},{11,1... | collective-permute-start | bytes 1572872 | tf_op jit(solution)/shard_map/ppermute | solution.py:410
  11.3 17.5 %collective-permute-start.5 = (f32[4,128,256]{2,1,0:T(8,128)S(1)}, f32[4,128,256]{2,1,0:T(8,128)S(1)}, u32[]{:S(2)}, u32[]{:S(2)}) collective-permute-start(f32[4,128,256]{2,1,0:T(8,128)S(1)} %get-tuple-element.21.strips), channel_id=1, source_target_pairs={{0,28},{4,8},{8,4},{12,16},{16,12},{20,24},{24,20},{28,0},{1,29},{... | collective-permute-start | bytes 1572872 | tf_op jit(solution)/shard_map/ppermute | solution.py:406
  18.2 6.6 %collective-permute-start.4 = (f32[256,256]{1,0:T(8,128)S(1)}, f32[256,256]{1,0:T(8,128)S(1)}, u32[]{:S(2)}, u32[]{:S(2)}) collective-permute-start(f32[256,256]{1,0:T(8,128)S(1)} %get-tuple-element.26.factor_own), channel_id=1, source_target_pairs={{0,4},{4,0},{8,12},{12,8},{16,20},{20,16},{24,28},{28,24},{1,5},{5... | collective-permute-start | bytes 786440 | tf_op jit(solution)/shard_map/ppermute | solution.py:402
  18.3 12.4 %collective-permute-start.7 = (f32[256,256]{1,0:T(8,128)S(1)}, f32[256,256]{1,0:T(8,128)S(1)}, u32[]{:S(2)}, u32[]{:S(2)}) collective-permute-start(f32[256,256]{1,0:T(8,128)S(1)} %get-tuple-element.26.factor_own), channel_id=1, source_target_pairs={{1,0},{2,1},{3,2},{0,3},{5,4},{6,5},{7,6},{4,7},{9,8},{10,9},{11,1... | collective-permute-start | bytes 786440 | tf_op jit(solution)/shard_map/ppermute | solution.py:410
  22.7 11.0 %collective-permute-start.6 = (f32[256,256]{1,0:T(8,128)S(1)}, f32[256,256]{1,0:T(8,128)S(1)}, u32[]{:S(2)}, u32[]{:S(2)}) collective-permute-start(f32[256,256]{1,0:T(8,128)S(1)} %get-tuple-element.31), channel_id=1, source_target_pairs={{0,28},{4,8},{8,4},{12,16},{16,12},{20,24},{24,20},{28,0},{1,29},{... | collective-permute-start | bytes 786440 | tf_op jit(solution)/shard_map/ppermute | solution.py:406

commit v12 on v9

--- a/solution.py
+++ b/solution.py
@@ -207,7 +207,15 @@
     gather(slot_of, inverse_here, places)
 
 
-def spread_kernel(diagonal, spread):
+def greet_kernel(greeting):
+    greeting[...] = jnp.zeros_like(greeting)
+
+
+def heard_kernel(greeting, heard):
+    heard[...] = greeting[...]
+
+
+def spread_kernel(diagonal, after, spread):
     size = diagonal.shape[1]
     for at in range(2):
         for i in range(ROWS):
@@ -416,6 +424,8 @@
         return jax.ShapeDtypeStruct(dims, dtype)
 
     one, pair = shape(size, size), shape(2, size, size)
+    (greeting,) = call(greet_kernel, (shape(8, block),), ())
+    peer_greeting = to_peer(greeting)
     (diagonal,) = call(
         diagonal_kernel,
         (shape(2 * ROWS, block, block),),
@@ -446,7 +456,10 @@
     from_peer = to_peer(strips)
     from_mate = to_mate(mate)
     from_side = to_side(own_pair)
-    (peer_spread,) = call(spread_kernel, (pair,), (peer_diagonal,), micros=10)
+    (heard,) = call(heard_kernel, (shape(8, block),), (peer_greeting,), micros=5)
+    (peer_spread,) = call(
+        spread_kernel, (pair,), (peer_diagonal, heard), any_in=(1,), micros=10
+    )
     (mate_terms,) = call(
         mate_kernel,
         (shape(5, size, size),),

time: 34.6 us -> 38 us (1.098)
  waiting for transfers between devices: 6.62 us -> 11.7 us
  starting transfers between devices: 16 us -> 14.4 us
    ppermute x4 -> x5, waiting for transfers between devices: 6.61 us -> 11.7 us  [to_peer(): return lax.ppermute(value, 'row', route)]
    ppermute x2, starting transfers between devices: 8.22 us -> 7.25 us  [to_side(): return lax.ppermute(value, 'col', route)]
    ppermute x4 -> x5, starting transfers between devices: 7.68 us -> 7.01 us  [to_peer(): return lax.ppermute(value, 'row', route)]
    pallas_call x9 -> x11, Pallas kernels: 10.9 us -> 10.9 us  [call(): pl.pallas_call(kernel, out_shape=outs, in_specs=[spec(pltpu.HBM if at in...]
  transfers between devices with their start and end apart: 8 -> 9, of which waited for: 3 -> 4; matrix products, arithmetic and copies ran while one was open for 0% -> 0% of each run, Pallas kernels for 27% -> 27%
where the time goes in v12:
time: 38 us; the launch traced here: 37.8 us
  starting transfers between devices  14.4 us (38%)
  waiting for transfers between devices  11.7 us (31%)
  Pallas kernels  10.9 us (29%)
  between operations  0.73 us (2%)
    ppermute x5, waiting for transfers between devices, to_peer(): return lax.ppermute(value, 'row', route)  11.7 us
    pallas_call x11, Pallas kernels, call(): pl.pallas_call(kernel, out_shape=outs, in_specs=[spec(pltpu.HBM if at in...  10.9 us
    ppermute x2, starting transfers between devices, to_side(): return lax.ppermute(value, 'col', route)  7.25 us
    ppermute x5, starting transfers between devices, to_peer(): return lax.ppermute(value, 'row', route)  7.01 us
  transfers between devices with their start and end apart: 9, of which 4 were waited for; matrix products, arithmetic and copies ran while one was open for 0% of the time, Pallas kernels for 27%

profile of v12, /device:TPU:0, one launch (start us, length us, event | category | flops | bytes accessed | tf_op | source)
XLA Modules:
  0.0 37.8 jit_solution(14651667565530815229)
XLA Ops:
  0.6 3.4 %collective-permute-start.2 = (f32[8,128]{1,0:T(8,128)S(1)}, f32[8,128]{1,0:T(8,128)S(1)}, u32[]{:S(2)}, u32[]{:S(2)}) collective-permute-start(f32[8,128]{1,0:T(8,128)S(1)} %shard_map.70), channel_id=1, source_target_pairs={{0,28},{4,8},{8,4},{12,16},{16,12},{20,24},{24,20},{28,0},{1,29},{... | collective-permute-start | bytes 12296 | tf_op jit(solution)/shard_map/ppermute | solution.py:417
  4.0 1.0 %shard_map.68.after = f32[4,128,128]{2,1,0:T(8,128)S(1)} custom-call(f32[2,128,1024]{2,1,0:T(8,128)} %sqrt_iterate.3, f32[2,128,1024]{2,1,0:T(8,128)} %inverse_iterate.3), custom_call_target="tpu_custom_call" | custom-call | tf_op jit(solution)/shard_map/pallas_call | solution.py:386
  5.0 0.1 collective-permute-start.1
  5.1 1.7 %shard_map.69 = (s32[16,128]{1,0:T(8,128)S(1)}, f32[24,128]{1,0:T(8,128)S(1)}, f32[256,256]{1,0:T(8,128)S(1)}, f32[4,128,256]{2,1,0:T(8,128)S(1)}, f32[4,256,256...) custom-call(s32[8,64]{1,0:T(8,128)} %bitcast.2, ...), custom_call_target="tpu_custom_call" | custom-call | tf_op jit(solution)/shard_map/pallas_call | solution.py:386
  6.9 0.1 collective-permute-start
  6.9 2.7 %collective-permute-start.3 = (f32[256,256]{1,0:T(8,128)S(1)}, f32[256,256]{1,0:T(8,128)S(1)}, u32[]{:S(2)}, u32[]{:S(2)}) collective-permute-start(f32[256,256]{1,0:T(8,128)S(1)} %get-tuple-element.20.y_peer), channel_id=1, source_target_pairs={{0,28},{4,8},{8,4},{12,16},{16,12},{20,24},{24,20},{28,0},{1,29},{... | collective-permute-start | bytes 786440 | tf_op jit(solution)/shard_map/ppermute | solution.py:417
  9.6 3.6 %collective-permute-start.4 = (f32[2,256,256]{2,1,0:T(8,128)S(1)}, f32[2,256,256]{2,1,0:T(8,128)S(1)}, u32[]{:S(2)}, u32[]{:S(2)}) collective-permute-start(f32[2,256,256]{2,1,0:T(8,128)S(1)} %get-tuple-element.25), channel_id=1, source_target_pairs={{1,0},{2,1},{3,2},{0,3},{5,4},{6,5},{7,6},{4,7},{9,8},{10,9},{11,1... | collective-permute-start | bytes 1572872 | tf_op jit(solution)/shard_map/ppermute | solution.py:421
  13.2 0.0 collective-permute-done.2.greeting
  13.2 0.5 %collective-permute-start.6 = (f32[4,128,256]{2,1,0:T(8,128)S(1)}, f32[4,128,256]{2,1,0:T(8,128)S(1)}, u32[]{:S(2)}, u32[]{:S(2)}) collective-permute-start(f32[4,128,256]{2,1,0:T(8,128)S(1)} %get-tuple-element.21.strips), channel_id=1, source_target_pairs={{0,28},{4,8},{8,4},{12,16},{16,12},{20,24},{24,20},{28,0},{1,29},{... | collective-permute-start | bytes 1572872 | tf_op jit(solution)/shard_map/ppermute | solution.py:417
  13.7 0.9 %collective-permute-done.1.diagonal = f32[4,128,128]{2,1,0:T(8,128)S(1)} collective-permute-done((f32[4,128,128]{2,1,0:T(8,128)S(1)}, f32[4,128,128]{2,1,0:T(8,128)S(1)}, u32[]{:S(2)}, u32[]{:S(2)}) %collective-permute-start.1) | collective-permute-done | bytes 262176 | tf_op jit(solution)/shard_map/ppermute | solution.py:417
  14.6 0.0 collective-permute-done.from_mate
  14.6 1.7 %shard_map.73.mate_terms = f32[5,256,256]{2,1,0:T(8,128)S(1)} custom-call(f32[24,128]{1,0:T(8,128)S(1)} %get-tuple-element.19.kept, f32[4,256,256]{2,1,0:T(8,128)S(1)} %get-tuple-element.22.mate, f32[4,256,256]{2,1,0:T(8,128)S(1)} %collective-permute-done.from_mate, f32[2,256,256]{2,1,0:T(8,128)S(1)} %shard_map.72.after.peer_spread), custom_call_target="tpu_custom_call" | custom-call | tf_op jit(solution)/shard_map/pallas_call | solution.py:386
  16.4 3.8 %collective-permute-done.3.peer_y = f32[256,256]{1,0:T(8,128)S(1)} collective-permute-done((f32[256,256]{1,0:T(8,128)S(1)}, f32[256,256]{1,0:T(8,128)S(1)}, u32[]{:S(2)}, u32[]{:S(2)}) %collective-permute-start.3) | collective-permute-done | bytes 262176 | tf_op jit(solution)/shard_map/ppermute | solution.py:417
  20.2 0.7 %shard_map.74 = (f32[256,256]{1,0:T(8,128)S(1)}, f32[256,256]{1,0:T(8,128)S(1)}) custom-call(f32[24,128]{1,0:T(8,128)S(1)} %get-tuple-element.19.kept, f32[5,256,256]{2,1,0:T(8,128)S(1)} %shard_map.73.mate_terms, f32[4,128,256]{2,1,0:T(8,128)S(1)} %get-tuple-element.21.strips, f32[256,256]{1,0:T(8,128)S(1)} %collective-permute-done.3.peer_y), custom_call_target="tpu_custom_call" | custom-call | flops 5765000192 | tf_op jit(solution)/shard_map/pallas_call | solution.py:386
  20.9 0.1 collective-permute-start.5
  21.0 3.7 %collective-permute-start.8 = (f32[256,256]{1,0:T(8,128)S(1)}, f32[256,256]{1,0:T(8,128)S(1)}, u32[]{:S(2)}, u32[]{:S(2)}) collective-permute-start(f32[256,256]{1,0:T(8,128)S(1)} %get-tuple-element.26.factor_own), channel_id=1, source_target_pairs={{1,0},{2,1},{3,2},{0,3},{5,4},{6,5},{7,6},{4,7},{9,8},{10,9},{11,1... | collective-permute-start | bytes 786440 | tf_op jit(solution)/shard_map/ppermute | solution.py:421
  24.6 0.4 collective-permute-start.7
  25.0 0.0 collective-permute-done.4.from_side
  25.0 1.8 %shard_map.75 = (f32[3,256,256]{2,1,0:T(8,128)S(1)}, f32[5,256,256]{2,1,0:T(8,128)S(1)}, bf16[5,2,256,256]{3,2,1,0:T(8,128)(2,1)S(1)}) custom-call(f32[24,128]{1,0:T(8,128)S(1)} %get-tuple-element.19.kept, f32[256,256]{1,0:T(8,128)S(1)} %get-tuple-element.20.y_peer, f32[4,128,256]{2,1,0:T(8,128)S(1)} %get-tuple-element.21.strips, ...), custom_call_target="tpu_custom_call" | custom-call | tf_op jit(solution)/shard_map/pallas_call | solution.py:386
  26.8 4.6 %collective-permute-done.6.from_peer = f32[4,128,256]{2,1,0:T(8,128)S(1)} collective-permute-done((f32[4,128,256]{2,1,0:T(8,128)S(1)}, f32[4,128,256]{2,1,0:T(8,128)S(1)}, u32[]{:S(2)}, u32[]{:S(2)}) %collective-permute-start.6) | collective-permute-done | bytes 524320 | tf_op jit(solution)/shard_map/ppermute | solution.py:417
  31.4 2.0 %shard_map.76 = (f32[2,128,1024]{2,1,0:T(8,128)}, f32[2,128,1024]{2,1,0:T(8,128)}, f32[256,256]{1,0:T(8,128)S(1)}) custom-call(s32[16,128]{1,0:T(8,128)S(1)} %get-tuple-element.18.slots, f32[24,128]{1,0:T(8,128)S(1)} %get-tuple-element.19.kept, f32[3,256,256]{2,1,0:T(8,128)S(1)} %get-tuple-element.27.finished, f32[5,256,256]{2,1,0:T(8,128)S(1)} %get-tuple-element.28.partial, ...), custom_call_target="tpu_custom_call" | custom-call | tf_op jit(solution)/shard_map/pallas_call | solution.py:386
  33.4 1.2 %shard_map.77.unfinished = f32[2,128,1024]{2,1,0:T(8,128)} custom-call(s32[16,128]{1,0:T(8,128)S(1)} %get-tuple-element.18.slots, f32[24,128]{1,0:T(8,128)S(1)} %get-tuple-element.19.kept, f32[5,256,256]{2,1,0:T(8,128)S(1)} %get-tuple-element.28.partial, bf16[5,2,256,256]{3,2,1,0:T(8,128)(2,1)S(1)} %get-tuple-element.29.ready, ...), custom_call_target="tpu_custom_call", output_to_operand_aliasing={{}: (5, {})} | custom-call | tf_op jit(solution)/shard_map/pallas_call | solution.py:386
  34.6 2.4 %collective-permute-done.7.term = f32[256,256]{1,0:T(8,128)S(1)} collective-permute-done((f32[256,256]{1,0:T(8,128)S(1)}, f32[256,256]{1,0:T(8,128)S(1)}, u32[]{:S(2)}, u32[]{:S(2)}) %collective-permute-start.7) | collective-permute-done | bytes 262176 | tf_op jit(solution)/shard_map/ppermute | solution.py:417
  37.0 0.8 %shard_map.78 = f32[2,128,1024]{2,1,0:T(8,128)} custom-call(s32[16,128]{1,0:T(8,128)S(1)} %get-tuple-element.18.slots, f32[256,256]{1,0:T(8,128)S(1)} %get-tuple-element.30.part, f32[256,256]{1,0:T(8,128)S(1)} %collective-permute-done.7.term, f32[2,128,1024]{2,1,0:T(8,128)} %shard_map.77.unfinished), custom_call_target="tpu_custom_call", output_to_operand_aliasing={{}: (3, {})} | custom-call | tf_op jit(solution)/shard_map/pallas_call | solution.py:386
  (5 shorter events, 0.0 us)
Async XLA Ops:
  0.6 12.6 %collective-permute-start.2 = (f32[8,128]{1,0:T(8,128)S(1)}, f32[8,128]{1,0:T(8,128)S(1)}, u32[]{:S(2)}, u32[]{:S(2)}) collective-permute-start(f32[8,128]{1,0:T(8,128)S(1)} %shard_map.70), channel_id=1, source_target_pairs={{0,28},{4,8},{8,4},{12,16},{16,12},{20,24},{24,20},{28,0},{1,29},{... | collective-permute-start | bytes 12296 | tf_op jit(solution)/shard_map/ppermute | solution.py:417
  5.0 9.6 %collective-permute-start.1 = (f32[4,128,128]{2,1,0:T(8,128)S(1)}, f32[4,128,128]{2,1,0:T(8,128)S(1)}, u32[]{:S(2)}, u32[]{:S(2)}) collective-permute-start(f32[4,128,128]{2,1,0:T(8,128)S(1)} %shard_map.68.after), channel_id=1, source_target_pairs={{0,28},{4,8},{8,4},{12,16},{16,12},{20,24},{24,20},{28,0},{1,29},{... | collective-permute-start | bytes 786440 | tf_op jit(solution)/shard_map/ppermute | solution.py:417
  6.9 7.8 %collective-permute-start = (f32[4,256,256]{2,1,0:T(8,128)S(1)}, f32[4,256,256]{2,1,0:T(8,128)S(1)}, u32[]{:S(2)}, u32[]{:S(2)}) collective-permute-start(f32[4,256,256]{2,1,0:T(8,128)S(1)} %get-tuple-element.22.mate), channel_id=1, source_target_pairs={{0,4},{4,0},{8,12},{12,8},{16,20},{20,16},{24,28},{28,24},{1,5},{5... | collective-permute-start | bytes 3145736 | tf_op jit(solution)/shard_map/ppermute | solution.py:413
  6.9 13.3 %collective-permute-start.3 = (f32[256,256]{1,0:T(8,128)S(1)}, f32[256,256]{1,0:T(8,128)S(1)}, u32[]{:S(2)}, u32[]{:S(2)}) collective-permute-start(f32[256,256]{1,0:T(8,128)S(1)} %get-tuple-element.20.y_peer), channel_id=1, source_target_pairs={{0,28},{4,8},{8,4},{12,16},{16,12},{20,24},{24,20},{28,0},{1,29},{... | collective-permute-start | bytes 786440 | tf_op jit(solution)/shard_map/ppermute | solution.py:417
  9.6 15.4 %collective-permute-start.4 = (f32[2,256,256]{2,1,0:T(8,128)S(1)}, f32[2,256,256]{2,1,0:T(8,128)S(1)}, u32[]{:S(2)}, u32[]{:S(2)}) collective-permute-start(f32[2,256,256]{2,1,0:T(8,128)S(1)} %get-tuple-element.25), channel_id=1, source_target_pairs={{1,0},{2,1},{3,2},{0,3},{5,4},{6,5},{7,6},{4,7},{9,8},{10,9},{11,1... | collective-permute-start | bytes 1572872 | tf_op jit(solution)/shard_map/ppermute | solution.py:421
  13.2 18.2 %collective-permute-start.6 = (f32[4,128,256]{2,1,0:T(8,128)S(1)}, f32[4,128,256]{2,1,0:T(8,128)S(1)}, u32[]{:S(2)}, u32[]{:S(2)}) collective-permute-start(f32[4,128,256]{2,1,0:T(8,128)S(1)} %get-tuple-element.21.strips), channel_id=1, source_target_pairs={{0,28},{4,8},{8,4},{12,16},{16,12},{20,24},{24,20},{28,0},{1,29},{... | collective-permute-start | bytes 1572872 | tf_op jit(solution)/shard_map/ppermute | solution.py:417
  20.9 4.1 %collective-permute-start.5 = (f32[256,256]{1,0:T(8,128)S(1)}, f32[256,256]{1,0:T(8,128)S(1)}, u32[]{:S(2)}, u32[]{:S(2)}) collective-permute-start(f32[256,256]{1,0:T(8,128)S(1)} %get-tuple-element.26.factor_own), channel_id=1, source_target_pairs={{0,4},{4,0},{8,12},{12,8},{16,20},{20,16},{24,28},{28,24},{1,5},{5... | collective-permute-start | bytes 786440 | tf_op jit(solution)/shard_map/ppermute | solution.py:413
  21.0 12.5 %collective-permute-start.8 = (f32[256,256]{1,0:T(8,128)S(1)}, f32[256,256]{1,0:T(8,128)S(1)}, u32[]{:S(2)}, u32[]{:S(2)}) collective-permute-start(f32[256,256]{1,0:T(8,128)S(1)} %get-tuple-element.26.factor_own), channel_id=1, source_target_pairs={{1,0},{2,1},{3,2},{0,3},{5,4},{6,5},{7,6},{4,7},{9,8},{10,9},{11,1... | collective-permute-start | bytes 786440 | tf_op jit(solution)/shard_map/ppermute | solution.py:421
  24.6 12.4 %collective-permute-start.7 = (f32[256,256]{1,0:T(8,128)S(1)}, f32[256,256]{1,0:T(8,128)S(1)}, u32[]{:S(2)}, u32[]{:S(2)}) collective-permute-start(f32[256,256]{1,0:T(8,128)S(1)} %get-tuple-element.31), channel_id=1, source_target_pairs={{0,28},{4,8},{8,4},{12,16},{16,12},{20,24},{24,20},{28,0},{1,29},{... | collective-permute-start | bytes 786440 | tf_op jit(solution)/shard_map/ppermute | solution.py:417

commit v13 on v9

--- a/solution.py
+++ b/solution.py
@@ -154,14 +154,20 @@
 
 def diagonal_kernel(sqrt_iterate, inverse_iterate, diagonal, sems):
     size = sqrt_iterate.shape[1]
-    copies = [
-        pltpu.make_async_copy(
-            source.at[:, :, pl.ds(0, size)], diagonal.at[pl.ds(at * ROWS, ROWS)], sems.at[at]
-        )
-        for at, source in enumerate((sqrt_iterate, inverse_iterate))
-    ]
-    for copy in copies:
-        copy.start()
+    half = size // 2
+    copies = []
+    for source in (sqrt_iterate, inverse_iterate):
+        for i in range(ROWS):
+            block = len(copies) // 2
+            for rows in (pl.ds(0, half), pl.ds(half, half)):
+                copies.append(
+                    pltpu.make_async_copy(
+                        source.at[i, rows, pl.ds(0, size)],
+                        diagonal.at[block, rows],
+                        sems.at[len(copies)],
+                    )
+                )
+                copies[-1].start()
     for copy in copies:
         copy.wait()
 
@@ -358,9 +364,12 @@
     for at, (i, j) in enumerate(blocks):
         rows, cols = quarter(i, j, size)
         result[at] = part[rows, cols] + term[rows, cols]
-        out = sqrt_next.at[i, :, pl.ds(pl.multiple_of(starts[at], size), size)]
-        copies.append(pltpu.make_async_copy(result.at[at], out, sems.at[at]))
-        copies[at].start()
+        for half in (pl.ds(0, size // 2), pl.ds(size // 2, size // 2)):
+            out = sqrt_next.at[i, half, pl.ds(pl.multiple_of(starts[at], size), size)]
+            copies.append(
+                pltpu.make_async_copy(result.at[at, half], out, sems.at[len(copies)])
+            )
+            copies[-1].start()
     for copy in copies:
         copy.wait()
 
@@ -420,7 +429,7 @@
         diagonal_kernel,
         (shape(2 * ROWS, block, block),),
         (sqrt_iterate, inverse_iterate),
-        scratch=[pltpu.SemaphoreType.DMA((2,))],
+        scratch=[pltpu.SemaphoreType.DMA((4 * ROWS,))],
         hbm_in=range(2),
     )
     peer_diagonal = to_peer(diagonal)
@@ -500,7 +509,7 @@
         (slots, y_peer_part, term, sqrt_next),
         scratch=[
             pltpu.VMEM((ROWS * ROWS, block, block), jnp.float32),
-            pltpu.SemaphoreType.DMA((ROWS * ROWS,)),
+            pltpu.SemaphoreType.DMA((2 * ROWS * ROWS,)),
         ],
         hbm_in=(3,),
         hbm_out=(0,),

time: 34.6 us -> 34.6 us (level)
  no operation moved by 1% of the time
where the time goes in v13:
time: 34.6 us; the launch traced here: 34.3 us
  starting transfers between devices  16 us (46%)
  Pallas kernels  10.9 us (32%)
  waiting for transfers between devices  6.63 us (19%)
  between operations  0.72 us (2%)
    pallas_call x9, Pallas kernels, call(): pl.pallas_call(kernel, out_shape=outs, in_specs=[spec(pltpu.HBM if at in...  10.9 us
    ppermute x2, starting transfers between devices, to_side(): return lax.ppermute(value, 'col', route)  8.23 us
    ppermute x4, starting transfers between devices, to_peer(): return lax.ppermute(value, 'row', route)  7.68 us
    ppermute x4, waiting for transfers between devices, to_peer(): return lax.ppermute(value, 'row', route)  6.62 us
  transfers between devices with their start and end apart: 8, of which 3 were waited for; matrix products, arithmetic and copies ran while one was open for 0% of the time, Pallas kernels for 27%

profile of v13, /device:TPU:0, one launch (start us, length us, event | category | flops | bytes accessed | tf_op | source)
XLA Modules:
  0.0 34.3 jit_solution(17665910275408433433)
XLA Ops:
  0.6 0.9 %shard_map.68.after = f32[4,128,128]{2,1,0:T(8,128)S(1)} custom-call(f32[2,128,1024]{2,1,0:T(8,128)} %sqrt_iterate.3, f32[2,128,1024]{2,1,0:T(8,128)} %inverse_iterate.3), custom_call_target="tpu_custom_call" | custom-call | tf_op jit(solution)/shard_map/pallas_call | solution.py:387
  1.6 3.4 %collective-permute-start.1 = (f32[4,128,128]{2,1,0:T(8,128)S(1)}, f32[4,128,128]{2,1,0:T(8,128)S(1)}, u32[]{:S(2)}, u32[]{:S(2)}) collective-permute-start(f32[4,128,128]{2,1,0:T(8,128)S(1)} %shard_map.68.after), channel_id=1, source_target_pairs={{0,28},{4,8},{8,4},{12,16},{16,12},{20,24},{24,20},{28,0},{1,29},{... | collective-permute-start | bytes 786440 | tf_op jit(solution)/shard_map/ppermute | solution.py:418
  5.0 1.7 %shard_map.69 = (s32[16,128]{1,0:T(8,128)S(1)}, f32[24,128]{1,0:T(8,128)S(1)}, f32[256,256]{1,0:T(8,128)S(1)}, f32[4,128,256]{2,1,0:T(8,128)S(1)}, f32[4,256,256...) custom-call(s32[8,64]{1,0:T(8,128)} %bitcast.2, ...), custom_call_target="tpu_custom_call" | custom-call | tf_op jit(solution)/shard_map/pallas_call | solution.py:387
  6.7 0.1 collective-permute-start
  6.8 0.7 %collective-permute-start.2 = (f32[256,256]{1,0:T(8,128)S(1)}, f32[256,256]{1,0:T(8,128)S(1)}, u32[]{:S(2)}, u32[]{:S(2)}) collective-permute-start(f32[256,256]{1,0:T(8,128)S(1)} %get-tuple-element.20.y_peer), channel_id=1, source_target_pairs={{0,28},{4,8},{8,4},{12,16},{16,12},{20,24},{24,20},{28,0},{1,29},{... | collective-permute-start | bytes 786440 | tf_op jit(solution)/shard_map/ppermute | solution.py:418
  7.5 3.7 %collective-permute-start.3 = (f32[2,256,256]{2,1,0:T(8,128)S(1)}, f32[2,256,256]{2,1,0:T(8,128)S(1)}, u32[]{:S(2)}, u32[]{:S(2)}) collective-permute-start(f32[2,256,256]{2,1,0:T(8,128)S(1)} %get-tuple-element.25), channel_id=1, source_target_pairs={{1,0},{2,1},{3,2},{0,3},{5,4},{6,5},{7,6},{4,7},{9,8},{10,9},{11,1... | collective-permute-start | bytes 1572872 | tf_op jit(solution)/shard_map/ppermute | solution.py:422
  11.2 1.6 %collective-permute-start.5 = (f32[4,128,256]{2,1,0:T(8,128)S(1)}, f32[4,128,256]{2,1,0:T(8,128)S(1)}, u32[]{:S(2)}, u32[]{:S(2)}) collective-permute-start(f32[4,128,256]{2,1,0:T(8,128)S(1)} %get-tuple-element.21.strips), channel_id=1, source_target_pairs={{0,28},{4,8},{8,4},{12,16},{16,12},{20,24},{24,20},{28,0},{1,29},{... | collective-permute-start | bytes 1572872 | tf_op jit(solution)/shard_map/ppermute | solution.py:418
  12.8 0.0 collective-permute-done.1.diagonal
  12.9 0.0 collective-permute-done.from_mate
  12.9 1.7 %shard_map.71.mate_terms = f32[5,256,256]{2,1,0:T(8,128)S(1)} custom-call(f32[24,128]{1,0:T(8,128)S(1)} %get-tuple-element.19.kept, f32[4,256,256]{2,1,0:T(8,128)S(1)} %get-tuple-element.22.mate, f32[4,256,256]{2,1,0:T(8,128)S(1)} %collective-permute-done.from_mate, f32[2,256,256]{2,1,0:T(8,128)S(1)} %shard_map.70.after.peer_spread), custom_call_target="tpu_custom_call" | custom-call | tf_op jit(solution)/shard_map/pallas_call | solution.py:387
  14.6 2.7 %collective-permute-done.2.peer_y = f32[256,256]{1,0:T(8,128)S(1)} collective-permute-done((f32[256,256]{1,0:T(8,128)S(1)}, f32[256,256]{1,0:T(8,128)S(1)}, u32[]{:S(2)}, u32[]{:S(2)}) %collective-permute-start.2) | collective-permute-done | bytes 262176 | tf_op jit(solution)/shard_map/ppermute | solution.py:418
  17.3 0.7 %shard_map.72 = (f32[256,256]{1,0:T(8,128)S(1)}, f32[256,256]{1,0:T(8,128)S(1)}) custom-call(f32[24,128]{1,0:T(8,128)S(1)} %get-tuple-element.19.kept, f32[5,256,256]{2,1,0:T(8,128)S(1)} %shard_map.71.mate_terms, f32[4,128,256]{2,1,0:T(8,128)S(1)} %get-tuple-element.21.strips, f32[256,256]{1,0:T(8,128)S(1)} %collective-permute-done.2.peer_y), custom_call_target="tpu_custom_call" | custom-call | flops 5765000192 | tf_op jit(solution)/shard_map/pallas_call | solution.py:387
  18.0 0.1 collective-permute-start.4
  18.0 4.5 %collective-permute-start.7 = (f32[256,256]{1,0:T(8,128)S(1)}, f32[256,256]{1,0:T(8,128)S(1)}, u32[]{:S(2)}, u32[]{:S(2)}) collective-permute-start(f32[256,256]{1,0:T(8,128)S(1)} %get-tuple-element.26.factor_own), channel_id=1, source_target_pairs={{1,0},{2,1},{3,2},{0,3},{5,4},{6,5},{7,6},{4,7},{9,8},{10,9},{11,1... | collective-permute-start | bytes 786440 | tf_op jit(solution)/shard_map/ppermute | solution.py:422
  22.5 2.0 %collective-permute-start.6 = (f32[256,256]{1,0:T(8,128)S(1)}, f32[256,256]{1,0:T(8,128)S(1)}, u32[]{:S(2)}, u32[]{:S(2)}) collective-permute-start(f32[256,256]{1,0:T(8,128)S(1)} %get-tuple-element.31), channel_id=1, source_target_pairs={{0,28},{4,8},{8,4},{12,16},{16,12},{20,24},{24,20},{28,0},{1,29},{... | collective-permute-start | bytes 786440 | tf_op jit(solution)/shard_map/ppermute | solution.py:418
  24.5 0.0 collective-permute-done.3.from_side
  24.5 0.0 collective-permute-done.4.mate_factor
  24.5 1.8 %shard_map.73 = (f32[3,256,256]{2,1,0:T(8,128)S(1)}, f32[5,256,256]{2,1,0:T(8,128)S(1)}, bf16[5,2,256,256]{3,2,1,0:T(8,128)(2,1)S(1)}) custom-call(f32[24,128]{1,0:T(8,128)S(1)} %get-tuple-element.19.kept, f32[256,256]{1,0:T(8,128)S(1)} %get-tuple-element.20.y_peer, f32[4,128,256]{2,1,0:T(8,128)S(1)} %get-tuple-element.21.strips, ...), custom_call_target="tpu_custom_call" | custom-call | tf_op jit(solution)/shard_map/pallas_call | solution.py:387
  26.4 2.2 %collective-permute-done.5.from_peer = f32[4,128,256]{2,1,0:T(8,128)S(1)} collective-permute-done((f32[4,128,256]{2,1,0:T(8,128)S(1)}, f32[4,128,256]{2,1,0:T(8,128)S(1)}, u32[]{:S(2)}, u32[]{:S(2)}) %collective-permute-start.5) | collective-permute-done | bytes 524320 | tf_op jit(solution)/shard_map/ppermute | solution.py:418
  28.5 2.0 %shard_map.74 = (f32[2,128,1024]{2,1,0:T(8,128)}, f32[2,128,1024]{2,1,0:T(8,128)}, f32[256,256]{1,0:T(8,128)S(1)}) custom-call(s32[16,128]{1,0:T(8,128)S(1)} %get-tuple-element.18.slots, f32[24,128]{1,0:T(8,128)S(1)} %get-tuple-element.19.kept, f32[3,256,256]{2,1,0:T(8,128)S(1)} %get-tuple-element.27.finished, f32[5,256,256]{2,1,0:T(8,128)S(1)} %get-tuple-element.28.partial, ...), custom_call_target="tpu_custom_call" | custom-call | tf_op jit(solution)/shard_map/pallas_call | solution.py:387
  30.5 0.0 collective-permute-done.7.factor
  30.5 1.2 %shard_map.75.unfinished = f32[2,128,1024]{2,1,0:T(8,128)} custom-call(s32[16,128]{1,0:T(8,128)S(1)} %get-tuple-element.18.slots, f32[24,128]{1,0:T(8,128)S(1)} %get-tuple-element.19.kept, f32[5,256,256]{2,1,0:T(8,128)S(1)} %get-tuple-element.28.partial, bf16[5,2,256,256]{3,2,1,0:T(8,128)(2,1)S(1)} %get-tuple-element.29.ready, ...), custom_call_target="tpu_custom_call", output_to_operand_aliasing={{}: (5, {})} | custom-call | tf_op jit(solution)/shard_map/pallas_call | solution.py:387
  31.7 1.8 %collective-permute-done.6.term = f32[256,256]{1,0:T(8,128)S(1)} collective-permute-done((f32[256,256]{1,0:T(8,128)S(1)}, f32[256,256]{1,0:T(8,128)S(1)}, u32[]{:S(2)}, u32[]{:S(2)}) %collective-permute-start.6) | collective-permute-done | bytes 262176 | tf_op jit(solution)/shard_map/ppermute | solution.py:418
  33.5 0.8 %shard_map.76 = f32[2,128,1024]{2,1,0:T(8,128)} custom-call(s32[16,128]{1,0:T(8,128)S(1)} %get-tuple-element.18.slots, f32[256,256]{1,0:T(8,128)S(1)} %get-tuple-element.30.part, f32[256,256]{1,0:T(8,128)S(1)} %collective-permute-done.6.term, f32[2,128,1024]{2,1,0:T(8,128)} %shard_map.75.unfinished), custom_call_target="tpu_custom_call", output_to_operand_aliasing={{}: (3, {})} | custom-call | tf_op jit(solution)/shard_map/pallas_call | solution.py:387
  (1 shorter events, 0.0 us)
Async XLA Ops:
  1.6 11.2 %collective-permute-start.1 = (f32[4,128,128]{2,1,0:T(8,128)S(1)}, f32[4,128,128]{2,1,0:T(8,128)S(1)}, u32[]{:S(2)}, u32[]{:S(2)}) collective-permute-start(f32[4,128,128]{2,1,0:T(8,128)S(1)} %shard_map.68.after), channel_id=1, source_target_pairs={{0,28},{4,8},{8,4},{12,16},{16,12},{20,24},{24,20},{28,0},{1,29},{... | collective-permute-start | bytes 786440 | tf_op jit(solution)/shard_map/ppermute | solution.py:418
  6.7 6.2 %collective-permute-start = (f32[4,256,256]{2,1,0:T(8,128)S(1)}, f32[4,256,256]{2,1,0:T(8,128)S(1)}, u32[]{:S(2)}, u32[]{:S(2)}) collective-permute-start(f32[4,256,256]{2,1,0:T(8,128)S(1)} %get-tuple-element.22.mate), channel_id=1, source_target_pairs={{0,4},{4,0},{8,12},{12,8},{16,20},{20,16},{24,28},{28,24},{1,5},{5... | collective-permute-start | bytes 3145736 | tf_op jit(solution)/shard_map/ppermute | solution.py:414
  6.8 10.5 %collective-permute-start.2 = (f32[256,256]{1,0:T(8,128)S(1)}, f32[256,256]{1,0:T(8,128)S(1)}, u32[]{:S(2)}, u32[]{:S(2)}) collective-permute-start(f32[256,256]{1,0:T(8,128)S(1)} %get-tuple-element.20.y_peer), channel_id=1, source_target_pairs={{0,28},{4,8},{8,4},{12,16},{16,12},{20,24},{24,20},{28,0},{1,29},{... | collective-permute-start | bytes 786440 | tf_op jit(solution)/shard_map/ppermute | solution.py:418
  7.5 17.1 %collective-permute-start.3 = (f32[2,256,256]{2,1,0:T(8,128)S(1)}, f32[2,256,256]{2,1,0:T(8,128)S(1)}, u32[]{:S(2)}, u32[]{:S(2)}) collective-permute-start(f32[2,256,256]{2,1,0:T(8,128)S(1)} %get-tuple-element.25), channel_id=1, source_target_pairs={{1,0},{2,1},{3,2},{0,3},{5,4},{6,5},{7,6},{4,7},{9,8},{10,9},{11,1... | collective-permute-start | bytes 1572872 | tf_op jit(solution)/shard_map/ppermute | solution.py:422
  11.2 17.3 %collective-permute-start.5 = (f32[4,128,256]{2,1,0:T(8,128)S(1)}, f32[4,128,256]{2,1,0:T(8,128)S(1)}, u32[]{:S(2)}, u32[]{:S(2)}) collective-permute-start(f32[4,128,256]{2,1,0:T(8,128)S(1)} %get-tuple-element.21.strips), channel_id=1, source_target_pairs={{0,28},{4,8},{8,4},{12,16},{16,12},{20,24},{24,20},{28,0},{1,29},{... | collective-permute-start | bytes 1572872 | tf_op jit(solution)/shard_map/ppermute | solution.py:418
  18.0 6.6 %collective-permute-start.4 = (f32[256,256]{1,0:T(8,128)S(1)}, f32[256,256]{1,0:T(8,128)S(1)}, u32[]{:S(2)}, u32[]{:S(2)}) collective-permute-start(f32[256,256]{1,0:T(8,128)S(1)} %get-tuple-element.26.factor_own), channel_id=1, source_target_pairs={{0,4},{4,0},{8,12},{12,8},{16,20},{20,16},{24,28},{28,24},{1,5},{5... | collective-permute-start | bytes 786440 | tf_op jit(solution)/shard_map/ppermute | solution.py:414
  18.0 12.4 %collective-permute-start.7 = (f32[256,256]{1,0:T(8,128)S(1)}, f32[256,256]{1,0:T(8,128)S(1)}, u32[]{:S(2)}, u32[]{:S(2)}) collective-permute-start(f32[256,256]{1,0:T(8,128)S(1)} %get-tuple-element.26.factor_own), channel_id=1, source_target_pairs={{1,0},{2,1},{3,2},{0,3},{5,4},{6,5},{7,6},{4,7},{9,8},{10,9},{11,1... | collective-permute-start | bytes 786440 | tf_op jit(solution)/shard_map/ppermute | solution.py:422
  22.5 11.0 %collective-permute-start.6 = (f32[256,256]{1,0:T(8,128)S(1)}, f32[256,256]{1,0:T(8,128)S(1)}, u32[]{:S(2)}, u32[]{:S(2)}) collective-permute-start(f32[256,256]{1,0:T(8,128)S(1)} %get-tuple-element.31), channel_id=1, source_target_pairs={{0,28},{4,8},{8,4},{12,16},{16,12},{20,24},{24,20},{28,0},{1,29},{... | collective-permute-start | bytes 786440 | tf_op jit(solution)/shard_map/ppermute | solution.py:418

commit v14 on v13

--- a/solution.py
+++ b/solution.py
@@ -240,7 +240,7 @@
     mate_terms[M_Z_MATE] = products((f_mate, mate_z_own))
 
 
-def factor_own_kernel(kept, mate_terms, strips, peer_y, factor_own, peer_term):
+def factor_own_kernel(kept, mate_terms, strips, peer_y, factor_own, *peer_term):
     peer_y_peer = split(peer_y[...])
     total = mate_terms[M_OWN] + products((split(peer_part(strips)), peer_y_peer))
     rows = lax.broadcasted_iota(jnp.int32, total.shape, 0)
@@ -248,7 +248,10 @@
     factor = jnp.where(rows == cols, 1.5, 0.0) + filtered(kept, total, OWN, -0.5)
     factor_own[...] = factor
     term = products((peer_y_peer, split(factor)))
-    peer_term[...] = filtered(kept, term, 0, None, KEPT_PEER_AT, ROWS)
+    term = filtered(kept, term, 0, None, KEPT_PEER_AT, ROWS)
+    size = term.shape[0] // ROWS
+    for i, place in enumerate(peer_term):
+        place[...] = term[i * size:(i + 1) * size]
 
 
 Y_MATE, Z_MATE, Z_SIDE = range(3)
@@ -356,20 +359,16 @@
     writer.wait()
 
 
-def last_kernel(slots, part, term, unfinished, sqrt_next, result, sems):
+def last_kernel(i, slots, part, term, unfinished, sqrt_next, result, sems):
     size = sqrt_next.shape[1]
     copies = []
-    blocks = [(i, j) for i in range(ROWS) for j in range(ROWS)]
-    starts = [slots[i * SLOTS + PEER * ROWS + j, 0] * size for i, j in blocks]
-    for at, (i, j) in enumerate(blocks):
+    starts = [slots[i * SLOTS + PEER * ROWS + j, 0] * size for j in range(ROWS)]
+    for j in range(ROWS):
         rows, cols = quarter(i, j, size)
-        result[at] = part[rows, cols] + term[rows, cols]
-        for half in (pl.ds(0, size // 2), pl.ds(size // 2, size // 2)):
-            out = sqrt_next.at[i, half, pl.ds(pl.multiple_of(starts[at], size), size)]
-            copies.append(
-                pltpu.make_async_copy(result.at[at, half], out, sems.at[len(copies)])
-            )
-            copies[-1].start()
+        result[j] = part[rows, cols] + term[:, cols]
+        out = sqrt_next.at[i, :, pl.ds(pl.multiple_of(starts[j], size), size)]
+        copies.append(pltpu.make_async_copy(result.at[j], out, sems.at[j]))
+        copies[j].start()
     for copy in copies:
         copy.wait()
 
@@ -462,11 +461,11 @@
         (kept, mate, from_mate, peer_spread),
         any_in=(3,),
     )
-    factor_own, peer_term = call(
-        factor_own_kernel, (one, one), (kept, mate_terms, strips, peer_y), micros=5
+    factor_own, *peer_term = call(
+        factor_own_kernel, (one, *[shape(block, size)] * ROWS), (kept, mate_terms, strips, peer_y), micros=5
     )
     mate_factor = to_mate(factor_own)
-    term = to_peer(peer_term)
+    term = [to_peer(value) for value in peer_term]
     side_factor = to_side(factor_own)
     finished, partial, ready = call(
         middle_kernel,
@@ -503,18 +502,19 @@
         hbm_out=(0,),
         in_place=5,
     )
-    (sqrt_next,) = call(
-        last_kernel,
-        (output,),
-        (slots, y_peer_part, term, sqrt_next),
-        scratch=[
-            pltpu.VMEM((ROWS * ROWS, block, block), jnp.float32),
-            pltpu.SemaphoreType.DMA((2 * ROWS * ROWS,)),
-        ],
-        hbm_in=(3,),
-        hbm_out=(0,),
-        in_place=3,
-    )
+    for i in range(ROWS):
+        (sqrt_next,) = call(
+            functools.partial(last_kernel, i),
+            (output,),
+            (slots, y_peer_part, term[i], sqrt_next),
+            scratch=[
+                pltpu.VMEM((ROWS, block, block), jnp.float32),
+                pltpu.SemaphoreType.DMA((ROWS,)),
+            ],
+            hbm_in=(3,),
+            hbm_out=(0,),
+            in_place=3,
+        )
     return sqrt_next, inverse_next
 
 

time: 34.6 us -> 34.5 us (level)
  waiting for transfers between devices: 6.63 us -> 5.25 us
  starting transfers between devices: 16 us -> 16.7 us
  Pallas kernels: 10.9 us -> 11.5 us
    ppermute x4 -> x5, waiting for transfers between devices: 6.62 us -> 5.24 us  [to_peer(): return lax.ppermute(value, 'row', route)]
    ppermute x4 -> x5, starting transfers between devices: 7.68 us -> 8.34 us  [to_peer(): return lax.ppermute(value, 'row', route)]
    pallas_call x9 -> x10, Pallas kernels: 10.9 us -> 11.5 us  [call(): pl.pallas_call(kernel, out_shape=outs, in_specs=[spec(pltpu.HBM if at in...]
  transfers between devices with their start and end apart: 8 -> 9, of which waited for: 3 -> 3; matrix products, arithmetic and copies ran while one was open for 0% -> 0% of each run, Pallas kernels for 27% -> 29%
where the time goes in v14:
time: 34.5 us; the launch traced here: 34.2 us
  starting transfers between devices  16.7 us (48%)
  Pallas kernels  11.5 us (33%)
  waiting for transfers between devices  5.25 us (15%)
  between operations  0.74 us (2%)
    pallas_call x10, Pallas kernels, call(): pl.pallas_call(kernel, out_shape=outs, in_specs=[spec(pltpu.HBM if at in...  11.5 us
    ppermute x5, starting transfers between devices, to_peer(): return lax.ppermute(value, 'row', route)  8.34 us
    ppermute x2, starting transfers between devices, to_side(): return lax.ppermute(value, 'col', route)  8.22 us
    ppermute x5, waiting for transfers between devices, to_peer(): return lax.ppermute(value, 'row', route)  5.24 us
  transfers between devices with their start and end apart: 9, of which 3 were waited for; matrix products, arithmetic and copies ran while one was open for 0% of the time, Pallas kernels for 29%

profile of v14, /device:TPU:0, one launch (start us, length us, event | category | flops | bytes accessed | tf_op | source)
XLA Modules:
  0.0 34.2 jit_solution(9581551231870371436)
XLA Ops:
  0.6 0.9 %shard_map.68.after = f32[4,128,128]{2,1,0:T(8,128)S(1)} custom-call(f32[2,128,1024]{2,1,0:T(8,128)} %sqrt_iterate.3, f32[2,128,1024]{2,1,0:T(8,128)} %inverse_iterate.3), custom_call_target="tpu_custom_call" | custom-call | tf_op jit(solution)/shard_map/pallas_call | solution.py:386
  1.6 3.4 %collective-permute-start.1 = (f32[4,128,128]{2,1,0:T(8,128)S(1)}, f32[4,128,128]{2,1,0:T(8,128)S(1)}, u32[]{:S(2)}, u32[]{:S(2)}) collective-permute-start(f32[4,128,128]{2,1,0:T(8,128)S(1)} %shard_map.68.after), channel_id=1, source_target_pairs={{0,28},{4,8},{8,4},{12,16},{16,12},{20,24},{24,20},{28,0},{1,29},{... | collective-permute-start | bytes 786440 | tf_op jit(solution)/shard_map/ppermute | solution.py:417
  5.0 1.7 %shard_map.69 = (s32[16,128]{1,0:T(8,128)S(1)}, f32[24,128]{1,0:T(8,128)S(1)}, f32[256,256]{1,0:T(8,128)S(1)}, f32[4,128,256]{2,1,0:T(8,128)S(1)}, f32[4,256,256...) custom-call(s32[8,64]{1,0:T(8,128)} %bitcast.2, ...), custom_call_target="tpu_custom_call" | custom-call | tf_op jit(solution)/shard_map/pallas_call | solution.py:386
  6.7 0.1 collective-permute-start
  6.8 0.7 %collective-permute-start.2 = (f32[256,256]{1,0:T(8,128)S(1)}, f32[256,256]{1,0:T(8,128)S(1)}, u32[]{:S(2)}, u32[]{:S(2)}) collective-permute-start(f32[256,256]{1,0:T(8,128)S(1)} %get-tuple-element.21.y_peer), channel_id=1, source_target_pairs={{0,28},{4,8},{8,4},{12,16},{16,12},{20,24},{24,20},{28,0},{1,29},{... | collective-permute-start | bytes 786440 | tf_op jit(solution)/shard_map/ppermute | solution.py:417
  7.5 3.7 %collective-permute-start.3 = (f32[2,256,256]{2,1,0:T(8,128)S(1)}, f32[2,256,256]{2,1,0:T(8,128)S(1)}, u32[]{:S(2)}, u32[]{:S(2)}) collective-permute-start(f32[2,256,256]{2,1,0:T(8,128)S(1)} %get-tuple-element.26), channel_id=1, source_target_pairs={{1,0},{2,1},{3,2},{0,3},{5,4},{6,5},{7,6},{4,7},{9,8},{10,9},{11,1... | collective-permute-start | bytes 1572872 | tf_op jit(solution)/shard_map/ppermute | solution.py:421
  11.2 1.6 %collective-permute-start.5 = (f32[4,128,256]{2,1,0:T(8,128)S(1)}, f32[4,128,256]{2,1,0:T(8,128)S(1)}, u32[]{:S(2)}, u32[]{:S(2)}) collective-permute-start(f32[4,128,256]{2,1,0:T(8,128)S(1)} %get-tuple-element.22.strips), channel_id=1, source_target_pairs={{0,28},{4,8},{8,4},{12,16},{16,12},{20,24},{24,20},{28,0},{1,29},{... | collective-permute-start | bytes 1572872 | tf_op jit(solution)/shard_map/ppermute | solution.py:417
  12.9 0.0 collective-permute-done.from_mate
  12.9 1.7 %shard_map.71.mate_terms = f32[5,256,256]{2,1,0:T(8,128)S(1)} custom-call(f32[24,128]{1,0:T(8,128)S(1)} %get-tuple-element.20.kept, f32[4,256,256]{2,1,0:T(8,128)S(1)} %get-tuple-element.23.mate, f32[4,256,256]{2,1,0:T(8,128)S(1)} %collective-permute-done.from_mate, f32[2,256,256]{2,1,0:T(8,128)S(1)} %shard_map.70.after.peer_spread), custom_call_target="tpu_custom_call" | custom-call | tf_op jit(solution)/shard_map/pallas_call | solution.py:386
  14.6 2.7 %collective-permute-done.2.peer_y = f32[256,256]{1,0:T(8,128)S(1)} collective-permute-done((f32[256,256]{1,0:T(8,128)S(1)}, f32[256,256]{1,0:T(8,128)S(1)}, u32[]{:S(2)}, u32[]{:S(2)}) %collective-permute-start.2) | collective-permute-done | bytes 262176 | tf_op jit(solution)/shard_map/ppermute | solution.py:417
  17.3 0.7 %shard_map.72 = (f32[256,256]{1,0:T(8,128)S(1)}, f32[128,256]{1,0:T(8,128)S(1)}, f32[128,256]{1,0:T(8,128)S(1)}) custom-call(f32[24,128]{1,0:T(8,128)S(1)} %get-tuple-element.20.kept, f32[5,256,256]{2,1,0:T(8,128)S(1)} %shard_map.71.mate_terms, f32[4,128,256]{2,1,0:T(8,128)S(1)} %get-tuple-element.22.strips, f32[256,256]{1,0:T(8,128)S(1)} %collective-permute-done.2.peer_y), custom_call_target="tpu_custom_call" | custom-call | flops 5765000192 | tf_op jit(solution)/shard_map/pallas_call | solution.py:386
  18.0 0.1 collective-permute-start.4
  18.0 4.5 %collective-permute-start.8 = (f32[256,256]{1,0:T(8,128)S(1)}, f32[256,256]{1,0:T(8,128)S(1)}, u32[]{:S(2)}, u32[]{:S(2)}) collective-permute-start(f32[256,256]{1,0:T(8,128)S(1)} %get-tuple-element.27.factor_own), channel_id=1, source_target_pairs={{1,0},{2,1},{3,2},{0,3},{5,4},{6,5},{7,6},{4,7},{9,8},{10,9},{11,1... | collective-permute-start | bytes 786440 | tf_op jit(solution)/shard_map/ppermute | solution.py:421
  22.5 2.0 %collective-permute-start.7 = (f32[128,256]{1,0:T(8,128)S(1)}, f32[128,256]{1,0:T(8,128)S(1)}, u32[]{:S(2)}, u32[]{:S(2)}) collective-permute-start(f32[128,256]{1,0:T(8,128)S(1)} %get-tuple-element.33), channel_id=1, source_target_pairs={{0,28},{4,8},{8,4},{12,16},{16,12},{20,24},{24,20},{28,0},{1,29},{... | collective-permute-start | bytes 393224 | tf_op jit(solution)/shard_map/ppermute | solution.py:417
  24.5 0.7 %collective-permute-start.6 = (f32[128,256]{1,0:T(8,128)S(1)}, f32[128,256]{1,0:T(8,128)S(1)}, u32[]{:S(2)}, u32[]{:S(2)}) collective-permute-start(f32[128,256]{1,0:T(8,128)S(1)} %get-tuple-element.32), channel_id=1, source_target_pairs={{0,28},{4,8},{8,4},{12,16},{16,12},{20,24},{24,20},{28,0},{1,29},{... | collective-permute-start | bytes 393224 | tf_op jit(solution)/shard_map/ppermute | solution.py:417
  25.2 0.0 collective-permute-done.4.mate_factor
  25.2 1.8 %shard_map.73 = (f32[3,256,256]{2,1,0:T(8,128)S(1)}, f32[5,256,256]{2,1,0:T(8,128)S(1)}, bf16[5,2,256,256]{3,2,1,0:T(8,128)(2,1)S(1)}) custom-call(f32[24,128]{1,0:T(8,128)S(1)} %get-tuple-element.20.kept, f32[256,256]{1,0:T(8,128)S(1)} %get-tuple-element.21.y_peer, f32[4,128,256]{2,1,0:T(8,128)S(1)} %get-tuple-element.22.strips, ...), custom_call_target="tpu_custom_call" | custom-call | tf_op jit(solution)/shard_map/pallas_call | solution.py:386
  27.0 1.5 %collective-permute-done.5.from_peer = f32[4,128,256]{2,1,0:T(8,128)S(1)} collective-permute-done((f32[4,128,256]{2,1,0:T(8,128)S(1)}, f32[4,128,256]{2,1,0:T(8,128)S(1)}, u32[]{:S(2)}, u32[]{:S(2)}) %collective-permute-start.5) | collective-permute-done | bytes 524320 | tf_op jit(solution)/shard_map/ppermute | solution.py:417
  28.5 2.0 %shard_map.74 = (f32[2,128,1024]{2,1,0:T(8,128)}, f32[2,128,1024]{2,1,0:T(8,128)}, f32[256,256]{1,0:T(8,128)S(1)}) custom-call(s32[16,128]{1,0:T(8,128)S(1)} %get-tuple-element.19.slots, f32[24,128]{1,0:T(8,128)S(1)} %get-tuple-element.20.kept, f32[3,256,256]{2,1,0:T(8,128)S(1)} %get-tuple-element.28.finished, f32[5,256,256]{2,1,0:T(8,128)S(1)} %get-tuple-element.29.partial, ...), custom_call_target="tpu_custom_call" | custom-call | tf_op jit(solution)/shard_map/pallas_call | solution.py:386
  30.5 0.0 collective-permute-done.8.factor
  30.5 1.2 %shard_map.75.unfinished = f32[2,128,1024]{2,1,0:T(8,128)} custom-call(s32[16,128]{1,0:T(8,128)S(1)} %get-tuple-element.19.slots, f32[24,128]{1,0:T(8,128)S(1)} %get-tuple-element.20.kept, f32[5,256,256]{2,1,0:T(8,128)S(1)} %get-tuple-element.29.partial, bf16[5,2,256,256]{3,2,1,0:T(8,128)(2,1)S(1)} %get-tuple-element.30.ready, ...), custom_call_target="tpu_custom_call", output_to_operand_aliasing={{}: (5, {})} | custom-call | tf_op jit(solution)/shard_map/pallas_call | solution.py:386
  31.7 0.7 %shard_map.76.unfinished = f32[2,128,1024]{2,1,0:T(8,128)} custom-call(s32[16,128]{1,0:T(8,128)S(1)} %get-tuple-element.19.slots, f32[256,256]{1,0:T(8,128)S(1)} %get-tuple-element.31.part, f32[128,256]{1,0:T(8,128)S(1)} %collective-permute-done.7.term, f32[2,128,1024]{2,1,0:T(8,128)} %shard_map.75.unfinished), custom_call_target="tpu_custom_call", output_to_operand_aliasing={{}: (3, {})} | custom-call | tf_op jit(solution)/shard_map/pallas_call | solution.py:386
  32.4 1.0 %collective-permute-done.6.term = f32[128,256]{1,0:T(8,128)S(1)} collective-permute-done((f32[128,256]{1,0:T(8,128)S(1)}, f32[128,256]{1,0:T(8,128)S(1)}, u32[]{:S(2)}, u32[]{:S(2)}) %collective-permute-start.6) | collective-permute-done | bytes 131104 | tf_op jit(solution)/shard_map/ppermute | solution.py:417
  33.5 0.7 %shard_map.77 = f32[2,128,1024]{2,1,0:T(8,128)} custom-call(s32[16,128]{1,0:T(8,128)S(1)} %get-tuple-element.19.slots, f32[256,256]{1,0:T(8,128)S(1)} %get-tuple-element.31.part, f32[128,256]{1,0:T(8,128)S(1)} %collective-permute-done.6.term, f32[2,128,1024]{2,1,0:T(8,128)} %shard_map.76.unfinished), custom_call_target="tpu_custom_call", output_to_operand_aliasing={{}: (3, {})} | custom-call | tf_op jit(solution)/shard_map/pallas_call | solution.py:386
  (4 shorter events, 0.0 us)
Async XLA Ops:
  1.6 11.2 %collective-permute-start.1 = (f32[4,128,128]{2,1,0:T(8,128)S(1)}, f32[4,128,128]{2,1,0:T(8,128)S(1)}, u32[]{:S(2)}, u32[]{:S(2)}) collective-permute-start(f32[4,128,128]{2,1,0:T(8,128)S(1)} %shard_map.68.after), channel_id=1, source_target_pairs={{0,28},{4,8},{8,4},{12,16},{16,12},{20,24},{24,20},{28,0},{1,29},{... | collective-permute-start | bytes 786440 | tf_op jit(solution)/shard_map/ppermute | solution.py:417
  6.7 6.2 %collective-permute-start = (f32[4,256,256]{2,1,0:T(8,128)S(1)}, f32[4,256,256]{2,1,0:T(8,128)S(1)}, u32[]{:S(2)}, u32[]{:S(2)}) collective-permute-start(f32[4,256,256]{2,1,0:T(8,128)S(1)} %get-tuple-element.23.mate), channel_id=1, source_target_pairs={{0,4},{4,0},{8,12},{12,8},{16,20},{20,16},{24,28},{28,24},{1,5},{5... | collective-permute-start | bytes 3145736 | tf_op jit(solution)/shard_map/ppermute | solution.py:413
  6.8 10.5 %collective-permute-start.2 = (f32[256,256]{1,0:T(8,128)S(1)}, f32[256,256]{1,0:T(8,128)S(1)}, u32[]{:S(2)}, u32[]{:S(2)}) collective-permute-start(f32[256,256]{1,0:T(8,128)S(1)} %get-tuple-element.21.y_peer), channel_id=1, source_target_pairs={{0,28},{4,8},{8,4},{12,16},{16,12},{20,24},{24,20},{28,0},{1,29},{... | collective-permute-start | bytes 786440 | tf_op jit(solution)/shard_map/ppermute | solution.py:417
  7.5 17.0 %collective-permute-start.3 = (f32[2,256,256]{2,1,0:T(8,128)S(1)}, f32[2,256,256]{2,1,0:T(8,128)S(1)}, u32[]{:S(2)}, u32[]{:S(2)}) collective-permute-start(f32[2,256,256]{2,1,0:T(8,128)S(1)} %get-tuple-element.26), channel_id=1, source_target_pairs={{1,0},{2,1},{3,2},{0,3},{5,4},{6,5},{7,6},{4,7},{9,8},{10,9},{11,1... | collective-permute-start | bytes 1572872 | tf_op jit(solution)/shard_map/ppermute | solution.py:421
  11.2 17.3 %collective-permute-start.5 = (f32[4,128,256]{2,1,0:T(8,128)S(1)}, f32[4,128,256]{2,1,0:T(8,128)S(1)}, u32[]{:S(2)}, u32[]{:S(2)}) collective-permute-start(f32[4,128,256]{2,1,0:T(8,128)S(1)} %get-tuple-element.22.strips), channel_id=1, source_target_pairs={{0,28},{4,8},{8,4},{12,16},{16,12},{20,24},{24,20},{28,0},{1,29},{... | collective-permute-start | bytes 1572872 | tf_op jit(solution)/shard_map/ppermute | solution.py:417
  18.0 7.2 %collective-permute-start.4 = (f32[256,256]{1,0:T(8,128)S(1)}, f32[256,256]{1,0:T(8,128)S(1)}, u32[]{:S(2)}, u32[]{:S(2)}) collective-permute-start(f32[256,256]{1,0:T(8,128)S(1)} %get-tuple-element.27.factor_own), channel_id=1, source_target_pairs={{0,4},{4,0},{8,12},{12,8},{16,20},{20,16},{24,28},{28,24},{1,5},{5... | collective-permute-start | bytes 786440 | tf_op jit(solution)/shard_map/ppermute | solution.py:413
  18.0 12.4 %collective-permute-start.8 = (f32[256,256]{1,0:T(8,128)S(1)}, f32[256,256]{1,0:T(8,128)S(1)}, u32[]{:S(2)}, u32[]{:S(2)}) collective-permute-start(f32[256,256]{1,0:T(8,128)S(1)} %get-tuple-element.27.factor_own), channel_id=1, source_target_pairs={{1,0},{2,1},{3,2},{0,3},{5,4},{6,5},{7,6},{4,7},{9,8},{10,9},{11,1... | collective-permute-start | bytes 786440 | tf_op jit(solution)/shard_map/ppermute | solution.py:421
  22.5 9.2 %collective-permute-start.7 = (f32[128,256]{1,0:T(8,128)S(1)}, f32[128,256]{1,0:T(8,128)S(1)}, u32[]{:S(2)}, u32[]{:S(2)}) collective-permute-start(f32[128,256]{1,0:T(8,128)S(1)} %get-tuple-element.33), channel_id=1, source_target_pairs={{0,28},{4,8},{8,4},{12,16},{16,12},{20,24},{24,20},{28,0},{1,29},{... | collective-permute-start | bytes 393224 | tf_op jit(solution)/shard_map/ppermute | solution.py:417
  24.5 9.0 %collective-permute-start.6 = (f32[128,256]{1,0:T(8,128)S(1)}, f32[128,256]{1,0:T(8,128)S(1)}, u32[]{:S(2)}, u32[]{:S(2)}) collective-permute-start(f32[128,256]{1,0:T(8,128)S(1)} %get-tuple-element.32), channel_id=1, source_target_pairs={{0,28},{4,8},{8,4},{12,16},{16,12},{20,24},{24,20},{28,0},{1,29},{... | collective-permute-start | bytes 393224 | tf_op jit(solution)/shard_map/ppermute | solution.py:417

commit v15 on v14

--- a/solution.py
+++ b/solution.py
@@ -119,9 +119,9 @@
     return place
 
 
-def strip_peer(out):
+def strip_whole(out, at):
     def place(i, j, size, block):
-        out[i, :, j * size:(j + 1) * size] = block
+        out[at + i, :, j * size:(j + 1) * size] = block
 
     return place
 
@@ -134,11 +134,11 @@
     return place
 
 
-Y_BESIDE, Z_BESIDE = ROWS, ROWS + 1
-
-
-def peer_part(strips):
-    return jnp.concatenate([strips[i] for i in range(ROWS)], axis=0)
+Y_BESIDE, Z_OWN, STRIPS = ROWS, ROWS + 1, 2 * ROWS + 1
+
+
+def whole_part(strips, at=0):
+    return jnp.concatenate([strips[at + i] for i in range(ROWS)], axis=0)
 
 
 def own_part(beside, spread):
@@ -152,22 +152,20 @@
     )
 
 
-def diagonal_kernel(sqrt_iterate, inverse_iterate, diagonal, sems):
+def diagonal_kernel(sqrt_iterate, diagonal, sems):
     size = sqrt_iterate.shape[1]
     half = size // 2
     copies = []
-    for source in (sqrt_iterate, inverse_iterate):
-        for i in range(ROWS):
-            block = len(copies) // 2
-            for rows in (pl.ds(0, half), pl.ds(half, half)):
-                copies.append(
-                    pltpu.make_async_copy(
-                        source.at[i, rows, pl.ds(0, size)],
-                        diagonal.at[block, rows],
-                        sems.at[len(copies)],
-                    )
+    for i in range(ROWS):
+        for rows in (pl.ds(0, half), pl.ds(half, half)):
+            copies.append(
+                pltpu.make_async_copy(
+                    sqrt_iterate.at[i, rows, pl.ds(0, size)],
+                    diagonal.at[i, rows],
+                    sems.at[len(copies)],
                 )
-                copies[-1].start()
+            )
+            copies[-1].start()
     for copy in copies:
         copy.wait()
 
@@ -205,8 +203,8 @@
     gather(slot_of, sqrt_here, places)
     copies[4].wait()
     places = {
-        PEER: (strip_peer(strips),),
-        OWN: (strip_own(strips, Z_BESIDE), into(mate.at[3]), into(to_side.at[1])),
+        PEER: (strip_whole(strips, 0),),
+        OWN: (strip_whole(strips, Z_OWN), into(mate.at[3]), into(to_side.at[1])),
         MATE: (into(mate.at[2]),),
         SIDE: (into(z_side),),
     }
@@ -215,12 +213,10 @@
 
 def spread_kernel(diagonal, spread):
     size = diagonal.shape[1]
-    for at in range(2):
-        for i in range(ROWS):
-            for j in range(ROWS):
-                rows, cols = quarter(i, j, size)
-                block = diagonal[at * ROWS + i]
-                spread[at, rows, cols] = block if i == j else jnp.zeros_like(block)
+    for i in range(ROWS):
+        for j in range(ROWS):
+            rows, cols = quarter(i, j, size)
+            spread[rows, cols] = diagonal[i] if i == j else jnp.zeros_like(diagonal[i])
 
 
 M_OWN, M_Y_OWN, M_Y_MATE, M_Z_OWN, M_Z_MATE = range(5)
@@ -242,7 +238,7 @@
 
 def factor_own_kernel(kept, mate_terms, strips, peer_y, factor_own, *peer_term):
     peer_y_peer = split(peer_y[...])
-    total = mate_terms[M_OWN] + products((split(peer_part(strips)), peer_y_peer))
+    total = mate_terms[M_OWN] + products((split(whole_part(strips)), peer_y_peer))
     rows = lax.broadcasted_iota(jnp.int32, total.shape, 0)
     cols = lax.broadcasted_iota(jnp.int32, total.shape, 1)
     factor = jnp.where(rows == cols, 1.5, 0.0) + filtered(kept, total, OWN, -0.5)
@@ -268,7 +264,7 @@
         ready[at, 0], ready[at, 1] = parts
 
     y_to_mate, y_own, z_to_mate, z_own = (split(mate[at]) for at in range(4))
-    y_to_peer, z_to_peer = split(y_peer[...]), split(peer_part(strips))
+    y_to_peer, z_to_peer = split(y_peer[...]), split(whole_part(strips))
     y_to_side, z_to_side = split(y_side[...]), split(z_side[...])
     f_own = split(factor_own[...])
     keep(Y_OWN, y_own)
@@ -334,9 +330,9 @@
     writer.write(finished.at[Y_MATE], sqrt_next, MATE)
     writer.write(finished.at[Z_MATE], inverse_next, MATE)
     writer.write(finished.at[Z_SIDE], inverse_next, SIDE)
-    peer_y_own = split(own_part(from_peer[Y_BESIDE], peer_spread[0]))
-    peer_z_own = split(own_part(from_peer[Z_BESIDE], peer_spread[1]))
-    peer_z_peer = split(peer_part(from_peer))
+    peer_y_own = split(own_part(from_peer[Y_BESIDE], peer_spread))
+    peer_z_own = split(whole_part(from_peer, Z_OWN))
+    peer_z_peer = split(whole_part(from_peer))
     total = partial[PEER_PART] + products((held(Z_PEER), peer_y_own))
     f_peer = split(filtered(kept, total, PEER, -0.5))
     total = products((peer_z_own, held(PEER_Y)), (peer_z_peer, held(Y_OWN)))
@@ -426,17 +422,17 @@
     one, pair = shape(size, size), shape(2, size, size)
     (diagonal,) = call(
         diagonal_kernel,
-        (shape(2 * ROWS, block, block),),
-        (sqrt_iterate, inverse_iterate),
-        scratch=[pltpu.SemaphoreType.DMA((4 * ROWS,))],
-        hbm_in=range(2),
+        (shape(ROWS, block, block),),
+        (sqrt_iterate,),
+        scratch=[pltpu.SemaphoreType.DMA((2 * ROWS,))],
+        hbm_in=(0,),
     )
     peer_diagonal = to_peer(diagonal)
     slots, kept, y_peer, strips, mate, y_side, z_side, own_pair = call(
         functools.partial(pack_kernel, row_devices, col_devices),
         (
             shape(ROWS * SLOTS, block, dtype=jnp.int32), shape(KEPT_LINES, block),
-            one, shape(ROWS + 2, block, size), shape(4, size, size), one, one, pair,
+            one, shape(STRIPS, block, size), shape(4, size, size), one, one, pair,
         ),
         (pattern.T, keep_mask.T, row_order, sqrt_iterate, inverse_iterate, diagonal),
         scratch=[
@@ -454,7 +450,7 @@
     from_peer = to_peer(strips)
     from_mate = to_mate(mate)
     from_side = to_side(own_pair)
-    (peer_spread,) = call(spread_kernel, (pair,), (peer_diagonal,), micros=10)
+    (peer_spread,) = call(spread_kernel, (one,), (peer_diagonal,), micros=10)
     (mate_terms,) = call(
         mate_kernel,
         (shape(5, size, size),),

time: 34.5 us -> 36.8 us (1.067)
  waiting for transfers between devices: 5.25 us -> 9.58 us
  starting transfers between devices: 16.7 us -> 14.9 us
    ppermute x5, waiting for transfers between devices: 5.24 us -> 7.67 us  [to_peer(): return lax.ppermute(value, 'row', route)]
    ppermute x2, waiting for transfers between devices: 0.01 us -> 1.91 us  [to_side(): return lax.ppermute(value, 'col', route)]
    ppermute x5, starting transfers between devices: 8.34 us -> 7.33 us  [to_peer(): return lax.ppermute(value, 'row', route)]
    ppermute x2, starting transfers between devices: 8.22 us -> 7.39 us  [to_side(): return lax.ppermute(value, 'col', route)]
  transfers between devices with their start and end apart: 9 -> 9, of which waited for: 3 -> 4; matrix products, arithmetic and copies ran while one was open for 0% -> 0% of each run, Pallas kernels for 29% -> 27%
where the time goes in v15:
time: 36.8 us; the launch traced here: 36.6 us
  starting transfers between devices  14.9 us (40%)
  Pallas kernels  11.4 us (31%)
  waiting for transfers between devices  9.58 us (26%)
  between operations  0.74 us (2%)
    pallas_call x10, Pallas kernels, call(): pl.pallas_call(kernel, out_shape=outs, in_specs=[spec(pltpu.HBM if at in...  11.4 us
    ppermute x5, waiting for transfers between devices, to_peer(): return lax.ppermute(value, 'row', route)  7.67 us
    ppermute x2, starting transfers between devices, to_side(): return lax.ppermute(value, 'col', route)  7.39 us
    ppermute x5, starting transfers between devices, to_peer(): return lax.ppermute(value, 'row', route)  7.33 us
    ppermute x2, waiting for transfers between devices, to_side(): return lax.ppermute(value, 'col', route)  1.91 us
  transfers between devices with their start and end apart: 9, of which 4 were waited for; matrix products, arithmetic and copies ran while one was open for 0% of the time, Pallas kernels for 27%

profile of v15, /device:TPU:0, one launch (start us, length us, event | category | flops | bytes accessed | tf_op | source)
XLA Modules:
  0.0 36.6 jit_solution(11473153590828877479)
XLA Ops:
  0.6 0.8 %shard_map.68.after = f32[2,128,128]{2,1,0:T(8,128)S(1)} custom-call(f32[2,128,1024]{2,1,0:T(8,128)} %sqrt_iterate.3), custom_call_target="tpu_custom_call" | custom-call | tf_op jit(solution)/shard_map/pallas_call | solution.py:382
  1.5 3.4 %collective-permute-start.1 = (f32[2,128,128]{2,1,0:T(8,128)S(1)}, f32[2,128,128]{2,1,0:T(8,128)S(1)}, u32[]{:S(2)}, u32[]{:S(2)}) collective-permute-start(f32[2,128,128]{2,1,0:T(8,128)S(1)} %shard_map.68.after), channel_id=1, source_target_pairs={{0,28},{4,8},{8,4},{12,16},{16,12},{20,24},{24,20},{28,0},{1,29},{... | collective-permute-start | bytes 393224 | tf_op jit(solution)/shard_map/ppermute | solution.py:413
  4.9 1.7 %shard_map.69 = (s32[16,128]{1,0:T(8,128)S(1)}, f32[24,128]{1,0:T(8,128)S(1)}, f32[256,256]{1,0:T(8,128)S(1)}, f32[5,128,256]{2,1,0:T(8,128)S(1)}, f32[4,256,256...) custom-call(s32[8,64]{1,0:T(8,128)} %bitcast.2, ...), custom_call_target="tpu_custom_call" | custom-call | tf_op jit(solution)/shard_map/pallas_call | solution.py:382
  6.6 0.1 collective-permute-start
  6.7 0.7 %collective-permute-start.2 = (f32[256,256]{1,0:T(8,128)S(1)}, f32[256,256]{1,0:T(8,128)S(1)}, u32[]{:S(2)}, u32[]{:S(2)}) collective-permute-start(f32[256,256]{1,0:T(8,128)S(1)} %get-tuple-element.21.y_peer), channel_id=1, source_target_pairs={{0,28},{4,8},{8,4},{12,16},{16,12},{20,24},{24,20},{28,0},{1,29},{... | collective-permute-start | bytes 786440 | tf_op jit(solution)/shard_map/ppermute | solution.py:413
  7.4 3.7 %collective-permute-start.3 = (f32[2,256,256]{2,1,0:T(8,128)S(1)}, f32[2,256,256]{2,1,0:T(8,128)S(1)}, u32[]{:S(2)}, u32[]{:S(2)}) collective-permute-start(f32[2,256,256]{2,1,0:T(8,128)S(1)} %get-tuple-element.26), channel_id=1, source_target_pairs={{1,0},{2,1},{3,2},{0,3},{5,4},{6,5},{7,6},{4,7},{9,8},{10,9},{11,1... | collective-permute-start | bytes 1572872 | tf_op jit(solution)/shard_map/ppermute | solution.py:417
  11.1 1.6 %collective-permute-start.5 = (f32[5,128,256]{2,1,0:T(8,128)S(1)}, f32[5,128,256]{2,1,0:T(8,128)S(1)}, u32[]{:S(2)}, u32[]{:S(2)}) collective-permute-start(f32[5,128,256]{2,1,0:T(8,128)S(1)} %get-tuple-element.22.strips), channel_id=1, source_target_pairs={{0,28},{4,8},{8,4},{12,16},{16,12},{20,24},{24,20},{28,0},{1,29},{... | collective-permute-start | bytes 1966088 | tf_op jit(solution)/shard_map/ppermute | solution.py:413
  12.7 0.0 collective-permute-done.1.diagonal
  12.7 0.0 collective-permute-done.from_mate
  12.8 1.7 %shard_map.71.mate_terms = f32[5,256,256]{2,1,0:T(8,128)S(1)} custom-call(f32[24,128]{1,0:T(8,128)S(1)} %get-tuple-element.20.kept, f32[4,256,256]{2,1,0:T(8,128)S(1)} %get-tuple-element.23.mate, f32[4,256,256]{2,1,0:T(8,128)S(1)} %collective-permute-done.from_mate, f32[256,256]{1,0:T(8,128)S(1)} %shard_map.70.after.peer_spread), custom_call_target="tpu_custom_call" | custom-call | tf_op jit(solution)/shard_map/pallas_call | solution.py:382
  14.5 1.8 %collective-permute-done.2.peer_y = f32[256,256]{1,0:T(8,128)S(1)} collective-permute-done((f32[256,256]{1,0:T(8,128)S(1)}, f32[256,256]{1,0:T(8,128)S(1)}, u32[]{:S(2)}, u32[]{:S(2)}) %collective-permute-start.2) | collective-permute-done | bytes 262176 | tf_op jit(solution)/shard_map/ppermute | solution.py:413
  16.3 0.7 %shard_map.72 = (f32[256,256]{1,0:T(8,128)S(1)}, f32[128,256]{1,0:T(8,128)S(1)}, f32[128,256]{1,0:T(8,128)S(1)}) custom-call(f32[24,128]{1,0:T(8,128)S(1)} %get-tuple-element.20.kept, f32[5,256,256]{2,1,0:T(8,128)S(1)} %shard_map.71.mate_terms, f32[5,128,256]{2,1,0:T(8,128)S(1)} %get-tuple-element.22.strips, f32[256,256]{1,0:T(8,128)S(1)} %collective-permute-done.2.peer_y), custom_call_target="tpu_custom_call" | custom-call | flops 5765000192 | tf_op jit(solution)/shard_map/pallas_call | solution.py:382
  16.9 0.1 collective-permute-start.4
  17.0 3.7 %collective-permute-start.8 = (f32[256,256]{1,0:T(8,128)S(1)}, f32[256,256]{1,0:T(8,128)S(1)}, u32[]{:S(2)}, u32[]{:S(2)}) collective-permute-start(f32[256,256]{1,0:T(8,128)S(1)} %get-tuple-element.27.factor_own), channel_id=1, source_target_pairs={{1,0},{2,1},{3,2},{0,3},{5,4},{6,5},{7,6},{4,7},{9,8},{10,9},{11,1... | collective-permute-start | bytes 786440 | tf_op jit(solution)/shard_map/ppermute | solution.py:417
  20.7 0.8 %collective-permute-start.7 = (f32[128,256]{1,0:T(8,128)S(1)}, f32[128,256]{1,0:T(8,128)S(1)}, u32[]{:S(2)}, u32[]{:S(2)}) collective-permute-start(f32[128,256]{1,0:T(8,128)S(1)} %get-tuple-element.33), channel_id=1, source_target_pairs={{0,28},{4,8},{8,4},{12,16},{16,12},{20,24},{24,20},{28,0},{1,29},{... | collective-permute-start | bytes 393224 | tf_op jit(solution)/shard_map/ppermute | solution.py:413
  21.4 1.9 %collective-permute-done.3.from_side = f32[2,256,256]{2,1,0:T(8,128)S(1)} collective-permute-done((f32[2,256,256]{2,1,0:T(8,128)S(1)}, f32[2,256,256]{2,1,0:T(8,128)S(1)}, u32[]{:S(2)}, u32[]{:S(2)}) %collective-permute-start.3) | collective-permute-done | bytes 524320 | tf_op jit(solution)/shard_map/ppermute | solution.py:417
  23.4 0.9 %collective-permute-start.6 = (f32[128,256]{1,0:T(8,128)S(1)}, f32[128,256]{1,0:T(8,128)S(1)}, u32[]{:S(2)}, u32[]{:S(2)}) collective-permute-start(f32[128,256]{1,0:T(8,128)S(1)} %get-tuple-element.32), channel_id=1, source_target_pairs={{0,28},{4,8},{8,4},{12,16},{16,12},{20,24},{24,20},{28,0},{1,29},{... | collective-permute-start | bytes 393224 | tf_op jit(solution)/shard_map/ppermute | solution.py:413
  24.2 1.8 %shard_map.73 = (f32[3,256,256]{2,1,0:T(8,128)S(1)}, f32[5,256,256]{2,1,0:T(8,128)S(1)}, bf16[5,2,256,256]{3,2,1,0:T(8,128)(2,1)S(1)}) custom-call(f32[24,128]{1,0:T(8,128)S(1)} %get-tuple-element.20.kept, f32[256,256]{1,0:T(8,128)S(1)} %get-tuple-element.21.y_peer, f32[5,128,256]{2,1,0:T(8,128)S(1)} %get-tuple-element.22.strips, ...), custom_call_target="tpu_custom_call" | custom-call | tf_op jit(solution)/shard_map/pallas_call | solution.py:382
  26.1 4.2 %collective-permute-done.5.from_peer = f32[5,128,256]{2,1,0:T(8,128)S(1)} collective-permute-done((f32[5,128,256]{2,1,0:T(8,128)S(1)}, f32[5,128,256]{2,1,0:T(8,128)S(1)}, u32[]{:S(2)}, u32[]{:S(2)}) %collective-permute-start.5) | collective-permute-done | bytes 655392 | tf_op jit(solution)/shard_map/ppermute | solution.py:413
  30.3 2.0 %shard_map.74 = (f32[2,128,1024]{2,1,0:T(8,128)}, f32[2,128,1024]{2,1,0:T(8,128)}, f32[256,256]{1,0:T(8,128)S(1)}) custom-call(s32[16,128]{1,0:T(8,128)S(1)} %get-tuple-element.19.slots, f32[24,128]{1,0:T(8,128)S(1)} %get-tuple-element.20.kept, f32[3,256,256]{2,1,0:T(8,128)S(1)} %get-tuple-element.28.finished, f32[5,256,256]{2,1,0:T(8,128)S(1)} %get-tuple-element.29.partial, ...), custom_call_target="tpu_custom_call" | custom-call | tf_op jit(solution)/shard_map/pallas_call | solution.py:382
  32.3 1.2 %shard_map.75.unfinished = f32[2,128,1024]{2,1,0:T(8,128)} custom-call(s32[16,128]{1,0:T(8,128)S(1)} %get-tuple-element.19.slots, f32[24,128]{1,0:T(8,128)S(1)} %get-tuple-element.20.kept, f32[5,256,256]{2,1,0:T(8,128)S(1)} %get-tuple-element.29.partial, bf16[5,2,256,256]{3,2,1,0:T(8,128)(2,1)S(1)} %get-tuple-element.30.ready, ...), custom_call_target="tpu_custom_call", output_to_operand_aliasing={{}: (5, {})} | custom-call | tf_op jit(solution)/shard_map/pallas_call | solution.py:382
  33.5 0.7 %shard_map.76.unfinished = f32[2,128,1024]{2,1,0:T(8,128)} custom-call(s32[16,128]{1,0:T(8,128)S(1)} %get-tuple-element.19.slots, f32[256,256]{1,0:T(8,128)S(1)} %get-tuple-element.31.part, f32[128,256]{1,0:T(8,128)S(1)} %collective-permute-done.7.term, f32[2,128,1024]{2,1,0:T(8,128)} %shard_map.75.unfinished), custom_call_target="tpu_custom_call", output_to_operand_aliasing={{}: (3, {})} | custom-call | tf_op jit(solution)/shard_map/pallas_call | solution.py:382
  34.2 1.7 %collective-permute-done.6.term = f32[128,256]{1,0:T(8,128)S(1)} collective-permute-done((f32[128,256]{1,0:T(8,128)S(1)}, f32[128,256]{1,0:T(8,128)S(1)}, u32[]{:S(2)}, u32[]{:S(2)}) %collective-permute-start.6) | collective-permute-done | bytes 131104 | tf_op jit(solution)/shard_map/ppermute | solution.py:413
  35.9 0.7 %shard_map.77 = f32[2,128,1024]{2,1,0:T(8,128)} custom-call(s32[16,128]{1,0:T(8,128)S(1)} %get-tuple-element.19.slots, f32[256,256]{1,0:T(8,128)S(1)} %get-tuple-element.31.part, f32[128,256]{1,0:T(8,128)S(1)} %collective-permute-done.6.term, f32[2,128,1024]{2,1,0:T(8,128)} %shard_map.76.unfinished), custom_call_target="tpu_custom_call", output_to_operand_aliasing={{}: (3, {})} | custom-call | tf_op jit(solution)/shard_map/pallas_call | solution.py:382
  (4 shorter events, 0.0 us)
Async XLA Ops:
  1.5 11.2 %collective-permute-start.1 = (f32[2,128,128]{2,1,0:T(8,128)S(1)}, f32[2,128,128]{2,1,0:T(8,128)S(1)}, u32[]{:S(2)}, u32[]{:S(2)}) collective-permute-start(f32[2,128,128]{2,1,0:T(8,128)S(1)} %shard_map.68.after), channel_id=1, source_target_pairs={{0,28},{4,8},{8,4},{12,16},{16,12},{20,24},{24,20},{28,0},{1,29},{... | collective-permute-start | bytes 393224 | tf_op jit(solution)/shard_map/ppermute | solution.py:413
  6.6 6.1 %collective-permute-start = (f32[4,256,256]{2,1,0:T(8,128)S(1)}, f32[4,256,256]{2,1,0:T(8,128)S(1)}, u32[]{:S(2)}, u32[]{:S(2)}) collective-permute-start(f32[4,256,256]{2,1,0:T(8,128)S(1)} %get-tuple-element.23.mate), channel_id=1, source_target_pairs={{0,4},{4,0},{8,12},{12,8},{16,20},{20,16},{24,28},{28,24},{1,5},{5... | collective-permute-start | bytes 3145736 | tf_op jit(solution)/shard_map/ppermute | solution.py:409
  6.7 9.6 %collective-permute-start.2 = (f32[256,256]{1,0:T(8,128)S(1)}, f32[256,256]{1,0:T(8,128)S(1)}, u32[]{:S(2)}, u32[]{:S(2)}) collective-permute-start(f32[256,256]{1,0:T(8,128)S(1)} %get-tuple-element.21.y_peer), channel_id=1, source_target_pairs={{0,28},{4,8},{8,4},{12,16},{16,12},{20,24},{24,20},{28,0},{1,29},{... | collective-permute-start | bytes 786440 | tf_op jit(solution)/shard_map/ppermute | solution.py:413
  7.4 16.0 %collective-permute-start.3 = (f32[2,256,256]{2,1,0:T(8,128)S(1)}, f32[2,256,256]{2,1,0:T(8,128)S(1)}, u32[]{:S(2)}, u32[]{:S(2)}) collective-permute-start(f32[2,256,256]{2,1,0:T(8,128)S(1)} %get-tuple-element.26), channel_id=1, source_target_pairs={{1,0},{2,1},{3,2},{0,3},{5,4},{6,5},{7,6},{4,7},{9,8},{10,9},{11,1... | collective-permute-start | bytes 1572872 | tf_op jit(solution)/shard_map/ppermute | solution.py:417
  11.1 19.2 %collective-permute-start.5 = (f32[5,128,256]{2,1,0:T(8,128)S(1)}, f32[5,128,256]{2,1,0:T(8,128)S(1)}, u32[]{:S(2)}, u32[]{:S(2)}) collective-permute-start(f32[5,128,256]{2,1,0:T(8,128)S(1)} %get-tuple-element.22.strips), channel_id=1, source_target_pairs={{0,28},{4,8},{8,4},{12,16},{16,12},{20,24},{24,20},{28,0},{1,29},{... | collective-permute-start | bytes 1966088 | tf_op jit(solution)/shard_map/ppermute | solution.py:413
  16.9 7.3 %collective-permute-start.4 = (f32[256,256]{1,0:T(8,128)S(1)}, f32[256,256]{1,0:T(8,128)S(1)}, u32[]{:S(2)}, u32[]{:S(2)}) collective-permute-start(f32[256,256]{1,0:T(8,128)S(1)} %get-tuple-element.27.factor_own), channel_id=1, source_target_pairs={{0,4},{4,0},{8,12},{12,8},{16,20},{20,16},{24,28},{28,24},{1,5},{5... | collective-permute-start | bytes 786440 | tf_op jit(solution)/shard_map/ppermute | solution.py:409
  17.0 15.3 %collective-permute-start.8 = (f32[256,256]{1,0:T(8,128)S(1)}, f32[256,256]{1,0:T(8,128)S(1)}, u32[]{:S(2)}, u32[]{:S(2)}) collective-permute-start(f32[256,256]{1,0:T(8,128)S(1)} %get-tuple-element.27.factor_own), channel_id=1, source_target_pairs={{1,0},{2,1},{3,2},{0,3},{5,4},{6,5},{7,6},{4,7},{9,8},{10,9},{11,1... | collective-permute-start | bytes 786440 | tf_op jit(solution)/shard_map/ppermute | solution.py:417
  20.7 12.8 %collective-permute-start.7 = (f32[128,256]{1,0:T(8,128)S(1)}, f32[128,256]{1,0:T(8,128)S(1)}, u32[]{:S(2)}, u32[]{:S(2)}) collective-permute-start(f32[128,256]{1,0:T(8,128)S(1)} %get-tuple-element.33), channel_id=1, source_target_pairs={{0,28},{4,8},{8,4},{12,16},{16,12},{20,24},{24,20},{28,0},{1,29},{... | collective-permute-start | bytes 393224 | tf_op jit(solution)/shard_map/ppermute | solution.py:413
  23.4 12.5 %collective-permute-start.6 = (f32[128,256]{1,0:T(8,128)S(1)}, f32[128,256]{1,0:T(8,128)S(1)}, u32[]{:S(2)}, u32[]{:S(2)}) collective-permute-start(f32[128,256]{1,0:T(8,128)S(1)} %get-tuple-element.32), channel_id=1, source_target_pairs={{0,28},{4,8},{8,4},{12,16},{16,12},{20,24},{24,20},{28,0},{1,29},{... | collective-permute-start | bytes 393224 | tf_op jit(solution)/shard_map/ppermute | solution.py:413

commit v16 on v14

--- a/solution.py
+++ b/solution.py
@@ -426,10 +426,11 @@
     one, pair = shape(size, size), shape(2, size, size)
     (diagonal,) = call(
         diagonal_kernel,
-        (shape(2 * ROWS, block, block),),
+        (pltpu.HBM((2 * ROWS, block, block), jnp.float32),),
         (sqrt_iterate, inverse_iterate),
         scratch=[pltpu.SemaphoreType.DMA((4 * ROWS,))],
         hbm_in=range(2),
+        hbm_out=(0,),
     )
     peer_diagonal = to_peer(diagonal)
     slots, kept, y_peer, strips, mate, y_side, z_side, own_pair = call(
@@ -447,8 +448,7 @@
             pltpu.VMEM(inverse_iterate.shape, jnp.float32),
             pltpu.SemaphoreType.DMA((5,)),
         ],
-        hbm_in=range(5),
-        any_in=(5,),
+        hbm_in=range(6),
     )
     peer_y = to_peer(y_peer)
     from_peer = to_peer(strips)

time: 34.5 us -> 42.8 us (1.24)
  Pallas kernels: 11.5 us -> 19.7 us
    pallas_call x10, Pallas kernels: 11.5 us -> 19.7 us  [call(): pl.pallas_call(kernel, out_shape=outs, in_specs=[spec(pltpu.HBM if at in...]
  transfers between devices with their start and end apart: 9 -> 9, of which waited for: 3 -> 3; matrix products, arithmetic and copies ran while one was open for 0% -> 0% of each run, Pallas kernels for 29% -> 23%
where the time goes in v16:
time: 42.8 us; the launch traced here: 42.6 us
  Pallas kernels  19.7 us (46%)
  starting transfers between devices  16.7 us (39%)
  waiting for transfers between devices  5.43 us (13%)
  between operations  0.74 us (2%)
    pallas_call x10, Pallas kernels, call(): pl.pallas_call(kernel, out_shape=outs, in_specs=[spec(pltpu.HBM if at in...  19.7 us
    ppermute x5, starting transfers between devices, to_peer(): return lax.ppermute(value, 'row', route)  8.33 us
    ppermute x2, starting transfers between devices, to_side(): return lax.ppermute(value, 'col', route)  8.22 us
    ppermute x5, waiting for transfers between devices, to_peer(): return lax.ppermute(value, 'row', route)  5.42 us
  transfers between devices with their start and end apart: 9, of which 3 were waited for; matrix products, arithmetic and copies ran while one was open for 0% of the time, Pallas kernels for 23%

profile of v16, /device:TPU:0, one launch (start us, length us, event | category | flops | bytes accessed | tf_op | source)
XLA Modules:
  0.0 42.6 jit_solution(9715670988954644329)
XLA Ops:
  0.6 9.1 %shard_map.68.after = f32[4,128,128]{2,1,0:T(8,128)} custom-call(f32[2,128,1024]{2,1,0:T(8,128)} %sqrt_iterate.3, f32[2,128,1024]{2,1,0:T(8,128)} %inverse_iterate.3), custom_call_target="tpu_custom_call" | custom-call | tf_op jit(solution)/shard_map/pallas_call | solution.py:386
  9.8 3.4 %collective-permute-start.1 = (f32[4,128,128]{2,1,0:T(8,128)}, f32[4,128,128]{2,1,0:T(8,128)S(1)}, u32[]{:S(2)}, u32[]{:S(2)}) collective-permute-start(f32[4,128,128]{2,1,0:T(8,128)} %shard_map.68.after), channel_id=1, source_target_pairs={{0,28},{4,8},{8,4},{12,16},{16,12},{20,24},{24,20},{28,0},{1,29},{... | collective-permute-start | bytes 786440 | tf_op jit(solution)/shard_map/ppermute | solution.py:417
  13.2 1.7 %shard_map.69 = (s32[16,128]{1,0:T(8,128)S(1)}, f32[24,128]{1,0:T(8,128)S(1)}, f32[256,256]{1,0:T(8,128)S(1)}, f32[4,128,256]{2,1,0:T(8,128)S(1)}, f32[4,256,256...) custom-call(s32[8,64]{1,0:T(8,128)} %bitcast.2, ...), custom_call_target="tpu_custom_call" | custom-call | tf_op jit(solution)/shard_map/pallas_call | solution.py:386
  14.9 0.1 collective-permute-start
  15.0 0.7 %collective-permute-start.2 = (f32[256,256]{1,0:T(8,128)S(1)}, f32[256,256]{1,0:T(8,128)S(1)}, u32[]{:S(2)}, u32[]{:S(2)}) collective-permute-start(f32[256,256]{1,0:T(8,128)S(1)} %get-tuple-element.21.y_peer), channel_id=1, source_target_pairs={{0,28},{4,8},{8,4},{12,16},{16,12},{20,24},{24,20},{28,0},{1,29},{... | collective-permute-start | bytes 786440 | tf_op jit(solution)/shard_map/ppermute | solution.py:417
  15.6 3.7 %collective-permute-start.3 = (f32[2,256,256]{2,1,0:T(8,128)S(1)}, f32[2,256,256]{2,1,0:T(8,128)S(1)}, u32[]{:S(2)}, u32[]{:S(2)}) collective-permute-start(f32[2,256,256]{2,1,0:T(8,128)S(1)} %get-tuple-element.26), channel_id=1, source_target_pairs={{1,0},{2,1},{3,2},{0,3},{5,4},{6,5},{7,6},{4,7},{9,8},{10,9},{11,1... | collective-permute-start | bytes 1572872 | tf_op jit(solution)/shard_map/ppermute | solution.py:421
  19.4 1.6 %collective-permute-start.5 = (f32[4,128,256]{2,1,0:T(8,128)S(1)}, f32[4,128,256]{2,1,0:T(8,128)S(1)}, u32[]{:S(2)}, u32[]{:S(2)}) collective-permute-start(f32[4,128,256]{2,1,0:T(8,128)S(1)} %get-tuple-element.22.strips), channel_id=1, source_target_pairs={{0,28},{4,8},{8,4},{12,16},{16,12},{20,24},{24,20},{28,0},{1,29},{... | collective-permute-start | bytes 1572872 | tf_op jit(solution)/shard_map/ppermute | solution.py:417
  21.0 0.0 collective-permute-done.1.diagonal
  21.1 1.7 %shard_map.71.mate_terms = f32[5,256,256]{2,1,0:T(8,128)S(1)} custom-call(f32[24,128]{1,0:T(8,128)S(1)} %get-tuple-element.20.kept, f32[4,256,256]{2,1,0:T(8,128)S(1)} %get-tuple-element.23.mate, f32[4,256,256]{2,1,0:T(8,128)S(1)} %collective-permute-done.from_mate, f32[2,256,256]{2,1,0:T(8,128)S(1)} %shard_map.70.after.peer_spread), custom_call_target="tpu_custom_call" | custom-call | tf_op jit(solution)/shard_map/pallas_call | solution.py:386
  22.8 2.9 %collective-permute-done.2.peer_y = f32[256,256]{1,0:T(8,128)S(1)} collective-permute-done((f32[256,256]{1,0:T(8,128)S(1)}, f32[256,256]{1,0:T(8,128)S(1)}, u32[]{:S(2)}, u32[]{:S(2)}) %collective-permute-start.2) | collective-permute-done | bytes 262176 | tf_op jit(solution)/shard_map/ppermute | solution.py:417
  25.7 0.7 %shard_map.72 = (f32[256,256]{1,0:T(8,128)S(1)}, f32[128,256]{1,0:T(8,128)S(1)}, f32[128,256]{1,0:T(8,128)S(1)}) custom-call(f32[24,128]{1,0:T(8,128)S(1)} %get-tuple-element.20.kept, f32[5,256,256]{2,1,0:T(8,128)S(1)} %shard_map.71.mate_terms, f32[4,128,256]{2,1,0:T(8,128)S(1)} %get-tuple-element.22.strips, f32[256,256]{1,0:T(8,128)S(1)} %collective-permute-done.2.peer_y), custom_call_target="tpu_custom_call" | custom-call | flops 5765000192 | tf_op jit(solution)/shard_map/pallas_call | solution.py:386
  26.4 0.1 collective-permute-start.4
  26.4 4.5 %collective-permute-start.8 = (f32[256,256]{1,0:T(8,128)S(1)}, f32[256,256]{1,0:T(8,128)S(1)}, u32[]{:S(2)}, u32[]{:S(2)}) collective-permute-start(f32[256,256]{1,0:T(8,128)S(1)} %get-tuple-element.27.factor_own), channel_id=1, source_target_pairs={{1,0},{2,1},{3,2},{0,3},{5,4},{6,5},{7,6},{4,7},{9,8},{10,9},{11,1... | collective-permute-start | bytes 786440 | tf_op jit(solution)/shard_map/ppermute | solution.py:421
  30.9 2.0 %collective-permute-start.7 = (f32[128,256]{1,0:T(8,128)S(1)}, f32[128,256]{1,0:T(8,128)S(1)}, u32[]{:S(2)}, u32[]{:S(2)}) collective-permute-start(f32[128,256]{1,0:T(8,128)S(1)} %get-tuple-element.33), channel_id=1, source_target_pairs={{0,28},{4,8},{8,4},{12,16},{16,12},{20,24},{24,20},{28,0},{1,29},{... | collective-permute-start | bytes 393224 | tf_op jit(solution)/shard_map/ppermute | solution.py:417
  32.9 0.0 collective-permute-done.3.from_side
  32.9 0.7 %collective-permute-start.6 = (f32[128,256]{1,0:T(8,128)S(1)}, f32[128,256]{1,0:T(8,128)S(1)}, u32[]{:S(2)}, u32[]{:S(2)}) collective-permute-start(f32[128,256]{1,0:T(8,128)S(1)} %get-tuple-element.32), channel_id=1, source_target_pairs={{0,28},{4,8},{8,4},{12,16},{16,12},{20,24},{24,20},{28,0},{1,29},{... | collective-permute-start | bytes 393224 | tf_op jit(solution)/shard_map/ppermute | solution.py:417
  33.6 0.0 collective-permute-done.4.mate_factor
  33.6 1.8 %shard_map.73 = (f32[3,256,256]{2,1,0:T(8,128)S(1)}, f32[5,256,256]{2,1,0:T(8,128)S(1)}, bf16[5,2,256,256]{3,2,1,0:T(8,128)(2,1)S(1)}) custom-call(f32[24,128]{1,0:T(8,128)S(1)} %get-tuple-element.20.kept, f32[256,256]{1,0:T(8,128)S(1)} %get-tuple-element.21.y_peer, f32[4,128,256]{2,1,0:T(8,128)S(1)} %get-tuple-element.22.strips, ...), custom_call_target="tpu_custom_call" | custom-call | tf_op jit(solution)/shard_map/pallas_call | solution.py:386
  35.4 1.5 %collective-permute-done.5.from_peer = f32[4,128,256]{2,1,0:T(8,128)S(1)} collective-permute-done((f32[4,128,256]{2,1,0:T(8,128)S(1)}, f32[4,128,256]{2,1,0:T(8,128)S(1)}, u32[]{:S(2)}, u32[]{:S(2)}) %collective-permute-start.5) | collective-permute-done | bytes 524320 | tf_op jit(solution)/shard_map/ppermute | solution.py:417
  36.9 2.0 %shard_map.74 = (f32[2,128,1024]{2,1,0:T(8,128)}, f32[2,128,1024]{2,1,0:T(8,128)}, f32[256,256]{1,0:T(8,128)S(1)}) custom-call(s32[16,128]{1,0:T(8,128)S(1)} %get-tuple-element.19.slots, f32[24,128]{1,0:T(8,128)S(1)} %get-tuple-element.20.kept, f32[3,256,256]{2,1,0:T(8,128)S(1)} %get-tuple-element.28.finished, f32[5,256,256]{2,1,0:T(8,128)S(1)} %get-tuple-element.29.partial, ...), custom_call_target="tpu_custom_call" | custom-call | tf_op jit(solution)/shard_map/pallas_call | solution.py:386
  38.9 1.2 %shard_map.75.unfinished = f32[2,128,1024]{2,1,0:T(8,128)} custom-call(s32[16,128]{1,0:T(8,128)S(1)} %get-tuple-element.19.slots, f32[24,128]{1,0:T(8,128)S(1)} %get-tuple-element.20.kept, f32[5,256,256]{2,1,0:T(8,128)S(1)} %get-tuple-element.29.partial, bf16[5,2,256,256]{3,2,1,0:T(8,128)(2,1)S(1)} %get-tuple-element.30.ready, ...), custom_call_target="tpu_custom_call", output_to_operand_aliasing={{}: (5, {})} | custom-call | tf_op jit(solution)/shard_map/pallas_call | solution.py:386
  40.1 0.7 %shard_map.76.unfinished = f32[2,128,1024]{2,1,0:T(8,128)} custom-call(s32[16,128]{1,0:T(8,128)S(1)} %get-tuple-element.19.slots, f32[256,256]{1,0:T(8,128)S(1)} %get-tuple-element.31.part, f32[128,256]{1,0:T(8,128)S(1)} %collective-permute-done.7.term, f32[2,128,1024]{2,1,0:T(8,128)} %shard_map.75.unfinished), custom_call_target="tpu_custom_call", output_to_operand_aliasing={{}: (3, {})} | custom-call | tf_op jit(solution)/shard_map/pallas_call | solution.py:386
  40.8 1.0 %collective-permute-done.6.term = f32[128,256]{1,0:T(8,128)S(1)} collective-permute-done((f32[128,256]{1,0:T(8,128)S(1)}, f32[128,256]{1,0:T(8,128)S(1)}, u32[]{:S(2)}, u32[]{:S(2)}) %collective-permute-start.6) | collective-permute-done | bytes 131104 | tf_op jit(solution)/shard_map/ppermute | solution.py:417
  41.9 0.7 %shard_map.77 = f32[2,128,1024]{2,1,0:T(8,128)} custom-call(s32[16,128]{1,0:T(8,128)S(1)} %get-tuple-element.19.slots, f32[256,256]{1,0:T(8,128)S(1)} %get-tuple-element.31.part, f32[128,256]{1,0:T(8,128)S(1)} %collective-permute-done.6.term, f32[2,128,1024]{2,1,0:T(8,128)} %shard_map.76.unfinished), custom_call_target="tpu_custom_call", output_to_operand_aliasing={{}: (3, {})} | custom-call | tf_op jit(solution)/shard_map/pallas_call | solution.py:386
  (4 shorter events, 0.0 us)
Async XLA Ops:
  9.8 11.2 %collective-permute-start.1 = (f32[4,128,128]{2,1,0:T(8,128)}, f32[4,128,128]{2,1,0:T(8,128)S(1)}, u32[]{:S(2)}, u32[]{:S(2)}) collective-permute-start(f32[4,128,128]{2,1,0:T(8,128)} %shard_map.68.after), channel_id=1, source_target_pairs={{0,28},{4,8},{8,4},{12,16},{16,12},{20,24},{24,20},{28,0},{1,29},{... | collective-permute-start | bytes 786440 | tf_op jit(solution)/shard_map/ppermute | solution.py:417
  14.9 6.2 %collective-permute-start = (f32[4,256,256]{2,1,0:T(8,128)S(1)}, f32[4,256,256]{2,1,0:T(8,128)S(1)}, u32[]{:S(2)}, u32[]{:S(2)}) collective-permute-start(f32[4,256,256]{2,1,0:T(8,128)S(1)} %get-tuple-element.23.mate), channel_id=1, source_target_pairs={{0,4},{4,0},{8,12},{12,8},{16,20},{20,16},{24,28},{28,24},{1,5},{5... | collective-permute-start | bytes 3145736 | tf_op jit(solution)/shard_map/ppermute | solution.py:413
  15.0 10.7 %collective-permute-start.2 = (f32[256,256]{1,0:T(8,128)S(1)}, f32[256,256]{1,0:T(8,128)S(1)}, u32[]{:S(2)}, u32[]{:S(2)}) collective-permute-start(f32[256,256]{1,0:T(8,128)S(1)} %get-tuple-element.21.y_peer), channel_id=1, source_target_pairs={{0,28},{4,8},{8,4},{12,16},{16,12},{20,24},{24,20},{28,0},{1,29},{... | collective-permute-start | bytes 786440 | tf_op jit(solution)/shard_map/ppermute | solution.py:417
  15.6 17.3 %collective-permute-start.3 = (f32[2,256,256]{2,1,0:T(8,128)S(1)}, f32[2,256,256]{2,1,0:T(8,128)S(1)}, u32[]{:S(2)}, u32[]{:S(2)}) collective-permute-start(f32[2,256,256]{2,1,0:T(8,128)S(1)} %get-tuple-element.26), channel_id=1, source_target_pairs={{1,0},{2,1},{3,2},{0,3},{5,4},{6,5},{7,6},{4,7},{9,8},{10,9},{11,1... | collective-permute-start | bytes 1572872 | tf_op jit(solution)/shard_map/ppermute | solution.py:421
  19.4 17.5 %collective-permute-start.5 = (f32[4,128,256]{2,1,0:T(8,128)S(1)}, f32[4,128,256]{2,1,0:T(8,128)S(1)}, u32[]{:S(2)}, u32[]{:S(2)}) collective-permute-start(f32[4,128,256]{2,1,0:T(8,128)S(1)} %get-tuple-element.22.strips), channel_id=1, source_target_pairs={{0,28},{4,8},{8,4},{12,16},{16,12},{20,24},{24,20},{28,0},{1,29},{... | collective-permute-start | bytes 1572872 | tf_op jit(solution)/shard_map/ppermute | solution.py:417
  26.4 7.2 %collective-permute-start.4 = (f32[256,256]{1,0:T(8,128)S(1)}, f32[256,256]{1,0:T(8,128)S(1)}, u32[]{:S(2)}, u32[]{:S(2)}) collective-permute-start(f32[256,256]{1,0:T(8,128)S(1)} %get-tuple-element.27.factor_own), channel_id=1, source_target_pairs={{0,4},{4,0},{8,12},{12,8},{16,20},{20,16},{24,28},{28,24},{1,5},{5... | collective-permute-start | bytes 786440 | tf_op jit(solution)/shard_map/ppermute | solution.py:413
  26.4 12.5 %collective-permute-start.8 = (f32[256,256]{1,0:T(8,128)S(1)}, f32[256,256]{1,0:T(8,128)S(1)}, u32[]{:S(2)}, u32[]{:S(2)}) collective-permute-start(f32[256,256]{1,0:T(8,128)S(1)} %get-tuple-element.27.factor_own), channel_id=1, source_target_pairs={{1,0},{2,1},{3,2},{0,3},{5,4},{6,5},{7,6},{4,7},{9,8},{10,9},{11,1... | collective-permute-start | bytes 786440 | tf_op jit(solution)/shard_map/ppermute | solution.py:421
  30.9 9.2 %collective-permute-start.7 = (f32[128,256]{1,0:T(8,128)S(1)}, f32[128,256]{1,0:T(8,128)S(1)}, u32[]{:S(2)}, u32[]{:S(2)}) collective-permute-start(f32[128,256]{1,0:T(8,128)S(1)} %get-tuple-element.33), channel_id=1, source_target_pairs={{0,28},{4,8},{8,4},{12,16},{16,12},{20,24},{24,20},{28,0},{1,29},{... | collective-permute-start | bytes 393224 | tf_op jit(solution)/shard_map/ppermute | solution.py:417
  32.9 9.0 %collective-permute-start.6 = (f32[128,256]{1,0:T(8,128)S(1)}, f32[128,256]{1,0:T(8,128)S(1)}, u32[]{:S(2)}, u32[]{:S(2)}) collective-permute-start(f32[128,256]{1,0:T(8,128)S(1)} %get-tuple-element.32), channel_id=1, source_target_pairs={{0,28},{4,8},{8,4},{12,16},{16,12},{20,24},{24,20},{28,0},{1,29},{... | collective-permute-start | bytes 393224 | tf_op jit(solution)/shard_map/ppermute | solution.py:417

commit v17 on v14

--- a/solution.py
+++ b/solution.py
@@ -10,6 +10,7 @@
 PEER, OWN, MATE, SIDE = range(4)
 ROWS = 2
 SLOTS = 8
+PIECES = 4
 KEPT_PEER_AT, KEPT_MATE_AT, KEPT_LINES = 16, 20, 24
 LARGEST = float(jnp.finfo(jnp.bfloat16).max)
 VMEM_LIMIT = 24 * 2**20
@@ -154,12 +155,13 @@
 
 def diagonal_kernel(sqrt_iterate, inverse_iterate, diagonal, sems):
     size = sqrt_iterate.shape[1]
-    half = size // 2
+    height = size // PIECES
     copies = []
     for source in (sqrt_iterate, inverse_iterate):
         for i in range(ROWS):
-            block = len(copies) // 2
-            for rows in (pl.ds(0, half), pl.ds(half, half)):
+            block = len(copies) // PIECES
+            for piece in range(PIECES):
+                rows = pl.ds(piece * height, height)
                 copies.append(
                     pltpu.make_async_copy(
                         source.at[i, rows, pl.ds(0, size)],
@@ -428,7 +430,7 @@
         diagonal_kernel,
         (shape(2 * ROWS, block, block),),
         (sqrt_iterate, inverse_iterate),
-        scratch=[pltpu.SemaphoreType.DMA((4 * ROWS,))],
+        scratch=[pltpu.SemaphoreType.DMA((2 * ROWS * PIECES,))],
         hbm_in=range(2),
     )
     peer_diagonal = to_peer(diagonal)

time: 34.5 us -> 34.6 us (level)
  no operation moved by 1% of the time
where the time goes in v17:
time: 34.6 us; the launch traced here: 34.3 us
  starting transfers between devices  16.7 us (48%)
  Pallas kernels  11.6 us (34%)
  waiting for transfers between devices  5.24 us (15%)
  between operations  0.74 us (2%)
    pallas_call x10, Pallas kernels, call(): pl.pallas_call(kernel, out_shape=outs, in_specs=[spec(pltpu.HBM if at in...  11.6 us
    ppermute x5, starting transfers between devices, to_peer(): return lax.ppermute(value, 'row', route)  8.33 us
    ppermute x2, starting transfers between devices, to_side(): return lax.ppermute(value, 'col', route)  8.22 us
    ppermute x5, waiting for transfers between devices, to_peer(): return lax.ppermute(value, 'row', route)  5.23 us
  transfers between devices with their start and end apart: 9, of which 3 were waited for; matrix products, arithmetic and copies ran while one was open for 0% of the time, Pallas kernels for 29%

profile of v17, /device:TPU:0, one launch (start us, length us, event | category | flops | bytes accessed | tf_op | source)
XLA Modules:
  0.0 34.3 jit_solution(1263325284879180300)
XLA Ops:
  0.6 1.0 %shard_map.68.after = f32[4,128,128]{2,1,0:T(8,128)S(1)} custom-call(f32[2,128,1024]{2,1,0:T(8,128)} %sqrt_iterate.3, f32[2,128,1024]{2,1,0:T(8,128)} %inverse_iterate.3), custom_call_target="tpu_custom_call" | custom-call | tf_op jit(solution)/shard_map/pallas_call | solution.py:388
  1.7 3.4 %collective-permute-start.1 = (f32[4,128,128]{2,1,0:T(8,128)S(1)}, f32[4,128,128]{2,1,0:T(8,128)S(1)}, u32[]{:S(2)}, u32[]{:S(2)}) collective-permute-start(f32[4,128,128]{2,1,0:T(8,128)S(1)} %shard_map.68.after), channel_id=1, source_target_pairs={{0,28},{4,8},{8,4},{12,16},{16,12},{20,24},{24,20},{28,0},{1,29},{... | collective-permute-start | bytes 786440 | tf_op jit(solution)/shard_map/ppermute | solution.py:419
  5.1 1.7 %shard_map.69 = (s32[16,128]{1,0:T(8,128)S(1)}, f32[24,128]{1,0:T(8,128)S(1)}, f32[256,256]{1,0:T(8,128)S(1)}, f32[4,128,256]{2,1,0:T(8,128)S(1)}, f32[4,256,256...) custom-call(s32[8,64]{1,0:T(8,128)} %bitcast.2, ...), custom_call_target="tpu_custom_call" | custom-call | tf_op jit(solution)/shard_map/pallas_call | solution.py:388
  6.8 0.1 collective-permute-start
  6.9 0.7 %collective-permute-start.2 = (f32[256,256]{1,0:T(8,128)S(1)}, f32[256,256]{1,0:T(8,128)S(1)}, u32[]{:S(2)}, u32[]{:S(2)}) collective-permute-start(f32[256,256]{1,0:T(8,128)S(1)} %get-tuple-element.21.y_peer), channel_id=1, source_target_pairs={{0,28},{4,8},{8,4},{12,16},{16,12},{20,24},{24,20},{28,0},{1,29},{... | collective-permute-start | bytes 786440 | tf_op jit(solution)/shard_map/ppermute | solution.py:419
  7.6 3.7 %collective-permute-start.3 = (f32[2,256,256]{2,1,0:T(8,128)S(1)}, f32[2,256,256]{2,1,0:T(8,128)S(1)}, u32[]{:S(2)}, u32[]{:S(2)}) collective-permute-start(f32[2,256,256]{2,1,0:T(8,128)S(1)} %get-tuple-element.26), channel_id=1, source_target_pairs={{1,0},{2,1},{3,2},{0,3},{5,4},{6,5},{7,6},{4,7},{9,8},{10,9},{11,1... | collective-permute-start | bytes 1572872 | tf_op jit(solution)/shard_map/ppermute | solution.py:423
  11.3 1.6 %collective-permute-start.5 = (f32[4,128,256]{2,1,0:T(8,128)S(1)}, f32[4,128,256]{2,1,0:T(8,128)S(1)}, u32[]{:S(2)}, u32[]{:S(2)}) collective-permute-start(f32[4,128,256]{2,1,0:T(8,128)S(1)} %get-tuple-element.22.strips), channel_id=1, source_target_pairs={{0,28},{4,8},{8,4},{12,16},{16,12},{20,24},{24,20},{28,0},{1,29},{... | collective-permute-start | bytes 1572872 | tf_op jit(solution)/shard_map/ppermute | solution.py:419
  12.9 0.0 collective-permute-done.1.diagonal
  13.0 0.0 collective-permute-done.from_mate
  13.0 1.7 %shard_map.71.mate_terms = f32[5,256,256]{2,1,0:T(8,128)S(1)} custom-call(f32[24,128]{1,0:T(8,128)S(1)} %get-tuple-element.20.kept, f32[4,256,256]{2,1,0:T(8,128)S(1)} %get-tuple-element.23.mate, f32[4,256,256]{2,1,0:T(8,128)S(1)} %collective-permute-done.from_mate, f32[2,256,256]{2,1,0:T(8,128)S(1)} %shard_map.70.after.peer_spread), custom_call_target="tpu_custom_call" | custom-call | tf_op jit(solution)/shard_map/pallas_call | solution.py:388
  14.7 2.7 %collective-permute-done.2.peer_y = f32[256,256]{1,0:T(8,128)S(1)} collective-permute-done((f32[256,256]{1,0:T(8,128)S(1)}, f32[256,256]{1,0:T(8,128)S(1)}, u32[]{:S(2)}, u32[]{:S(2)}) %collective-permute-start.2) | collective-permute-done | bytes 262176 | tf_op jit(solution)/shard_map/ppermute | solution.py:419
  17.4 0.7 %shard_map.72 = (f32[256,256]{1,0:T(8,128)S(1)}, f32[128,256]{1,0:T(8,128)S(1)}, f32[128,256]{1,0:T(8,128)S(1)}) custom-call(f32[24,128]{1,0:T(8,128)S(1)} %get-tuple-element.20.kept, f32[5,256,256]{2,1,0:T(8,128)S(1)} %shard_map.71.mate_terms, f32[4,128,256]{2,1,0:T(8,128)S(1)} %get-tuple-element.22.strips, f32[256,256]{1,0:T(8,128)S(1)} %collective-permute-done.2.peer_y), custom_call_target="tpu_custom_call" | custom-call | flops 5765000192 | tf_op jit(solution)/shard_map/pallas_call | solution.py:388
  18.1 0.1 collective-permute-start.4
  18.1 4.5 %collective-permute-start.8 = (f32[256,256]{1,0:T(8,128)S(1)}, f32[256,256]{1,0:T(8,128)S(1)}, u32[]{:S(2)}, u32[]{:S(2)}) collective-permute-start(f32[256,256]{1,0:T(8,128)S(1)} %get-tuple-element.27.factor_own), channel_id=1, source_target_pairs={{1,0},{2,1},{3,2},{0,3},{5,4},{6,5},{7,6},{4,7},{9,8},{10,9},{11,1... | collective-permute-start | bytes 786440 | tf_op jit(solution)/shard_map/ppermute | solution.py:423
  22.6 2.0 %collective-permute-start.7 = (f32[128,256]{1,0:T(8,128)S(1)}, f32[128,256]{1,0:T(8,128)S(1)}, u32[]{:S(2)}, u32[]{:S(2)}) collective-permute-start(f32[128,256]{1,0:T(8,128)S(1)} %get-tuple-element.33), channel_id=1, source_target_pairs={{0,28},{4,8},{8,4},{12,16},{16,12},{20,24},{24,20},{28,0},{1,29},{... | collective-permute-start | bytes 393224 | tf_op jit(solution)/shard_map/ppermute | solution.py:419
  24.6 0.7 %collective-permute-start.6 = (f32[128,256]{1,0:T(8,128)S(1)}, f32[128,256]{1,0:T(8,128)S(1)}, u32[]{:S(2)}, u32[]{:S(2)}) collective-permute-start(f32[128,256]{1,0:T(8,128)S(1)} %get-tuple-element.32), channel_id=1, source_target_pairs={{0,28},{4,8},{8,4},{12,16},{16,12},{20,24},{24,20},{28,0},{1,29},{... | collective-permute-start | bytes 393224 | tf_op jit(solution)/shard_map/ppermute | solution.py:419
  25.3 0.0 collective-permute-done.4.mate_factor
  25.3 1.8 %shard_map.73 = (f32[3,256,256]{2,1,0:T(8,128)S(1)}, f32[5,256,256]{2,1,0:T(8,128)S(1)}, bf16[5,2,256,256]{3,2,1,0:T(8,128)(2,1)S(1)}) custom-call(f32[24,128]{1,0:T(8,128)S(1)} %get-tuple-element.20.kept, f32[256,256]{1,0:T(8,128)S(1)} %get-tuple-element.21.y_peer, f32[4,128,256]{2,1,0:T(8,128)S(1)} %get-tuple-element.22.strips, ...), custom_call_target="tpu_custom_call" | custom-call | tf_op jit(solution)/shard_map/pallas_call | solution.py:388
  27.1 1.5 %collective-permute-done.5.from_peer = f32[4,128,256]{2,1,0:T(8,128)S(1)} collective-permute-done((f32[4,128,256]{2,1,0:T(8,128)S(1)}, f32[4,128,256]{2,1,0:T(8,128)S(1)}, u32[]{:S(2)}, u32[]{:S(2)}) %collective-permute-start.5) | collective-permute-done | bytes 524320 | tf_op jit(solution)/shard_map/ppermute | solution.py:419
  28.6 2.0 %shard_map.74 = (f32[2,128,1024]{2,1,0:T(8,128)}, f32[2,128,1024]{2,1,0:T(8,128)}, f32[256,256]{1,0:T(8,128)S(1)}) custom-call(s32[16,128]{1,0:T(8,128)S(1)} %get-tuple-element.19.slots, f32[24,128]{1,0:T(8,128)S(1)} %get-tuple-element.20.kept, f32[3,256,256]{2,1,0:T(8,128)S(1)} %get-tuple-element.28.finished, f32[5,256,256]{2,1,0:T(8,128)S(1)} %get-tuple-element.29.partial, ...), custom_call_target="tpu_custom_call" | custom-call | tf_op jit(solution)/shard_map/pallas_call | solution.py:388
  30.6 1.2 %shard_map.75.unfinished = f32[2,128,1024]{2,1,0:T(8,128)} custom-call(s32[16,128]{1,0:T(8,128)S(1)} %get-tuple-element.19.slots, f32[24,128]{1,0:T(8,128)S(1)} %get-tuple-element.20.kept, f32[5,256,256]{2,1,0:T(8,128)S(1)} %get-tuple-element.29.partial, bf16[5,2,256,256]{3,2,1,0:T(8,128)(2,1)S(1)} %get-tuple-element.30.ready, ...), custom_call_target="tpu_custom_call", output_to_operand_aliasing={{}: (5, {})} | custom-call | tf_op jit(solution)/shard_map/pallas_call | solution.py:388
  31.8 0.7 %shard_map.76.unfinished = f32[2,128,1024]{2,1,0:T(8,128)} custom-call(s32[16,128]{1,0:T(8,128)S(1)} %get-tuple-element.19.slots, f32[256,256]{1,0:T(8,128)S(1)} %get-tuple-element.31.part, f32[128,256]{1,0:T(8,128)S(1)} %collective-permute-done.7.term, f32[2,128,1024]{2,1,0:T(8,128)} %shard_map.75.unfinished), custom_call_target="tpu_custom_call", output_to_operand_aliasing={{}: (3, {})} | custom-call | tf_op jit(solution)/shard_map/pallas_call | solution.py:388
  32.5 1.0 %collective-permute-done.6.term = f32[128,256]{1,0:T(8,128)S(1)} collective-permute-done((f32[128,256]{1,0:T(8,128)S(1)}, f32[128,256]{1,0:T(8,128)S(1)}, u32[]{:S(2)}, u32[]{:S(2)}) %collective-permute-start.6) | collective-permute-done | bytes 131104 | tf_op jit(solution)/shard_map/ppermute | solution.py:419
  33.6 0.7 %shard_map.77 = f32[2,128,1024]{2,1,0:T(8,128)} custom-call(s32[16,128]{1,0:T(8,128)S(1)} %get-tuple-element.19.slots, f32[256,256]{1,0:T(8,128)S(1)} %get-tuple-element.31.part, f32[128,256]{1,0:T(8,128)S(1)} %collective-permute-done.6.term, f32[2,128,1024]{2,1,0:T(8,128)} %shard_map.76.unfinished), custom_call_target="tpu_custom_call", output_to_operand_aliasing={{}: (3, {})} | custom-call | tf_op jit(solution)/shard_map/pallas_call | solution.py:388
  (4 shorter events, 0.0 us)
Async XLA Ops:
  1.7 11.2 %collective-permute-start.1 = (f32[4,128,128]{2,1,0:T(8,128)S(1)}, f32[4,128,128]{2,1,0:T(8,128)S(1)}, u32[]{:S(2)}, u32[]{:S(2)}) collective-permute-start(f32[4,128,128]{2,1,0:T(8,128)S(1)} %shard_map.68.after), channel_id=1, source_target_pairs={{0,28},{4,8},{8,4},{12,16},{16,12},{20,24},{24,20},{28,0},{1,29},{... | collective-permute-start | bytes 786440 | tf_op jit(solution)/shard_map/ppermute | solution.py:419
  6.8 6.2 %collective-permute-start = (f32[4,256,256]{2,1,0:T(8,128)S(1)}, f32[4,256,256]{2,1,0:T(8,128)S(1)}, u32[]{:S(2)}, u32[]{:S(2)}) collective-permute-start(f32[4,256,256]{2,1,0:T(8,128)S(1)} %get-tuple-element.23.mate), channel_id=1, source_target_pairs={{0,4},{4,0},{8,12},{12,8},{16,20},{20,16},{24,28},{28,24},{1,5},{5... | collective-permute-start | bytes 3145736 | tf_op jit(solution)/shard_map/ppermute | solution.py:415
  6.9 10.5 %collective-permute-start.2 = (f32[256,256]{1,0:T(8,128)S(1)}, f32[256,256]{1,0:T(8,128)S(1)}, u32[]{:S(2)}, u32[]{:S(2)}) collective-permute-start(f32[256,256]{1,0:T(8,128)S(1)} %get-tuple-element.21.y_peer), channel_id=1, source_target_pairs={{0,28},{4,8},{8,4},{12,16},{16,12},{20,24},{24,20},{28,0},{1,29},{... | collective-permute-start | bytes 786440 | tf_op jit(solution)/shard_map/ppermute | solution.py:419
  7.6 17.0 %collective-permute-start.3 = (f32[2,256,256]{2,1,0:T(8,128)S(1)}, f32[2,256,256]{2,1,0:T(8,128)S(1)}, u32[]{:S(2)}, u32[]{:S(2)}) collective-permute-start(f32[2,256,256]{2,1,0:T(8,128)S(1)} %get-tuple-element.26), channel_id=1, source_target_pairs={{1,0},{2,1},{3,2},{0,3},{5,4},{6,5},{7,6},{4,7},{9,8},{10,9},{11,1... | collective-permute-start | bytes 1572872 | tf_op jit(solution)/shard_map/ppermute | solution.py:423
  11.3 17.3 %collective-permute-start.5 = (f32[4,128,256]{2,1,0:T(8,128)S(1)}, f32[4,128,256]{2,1,0:T(8,128)S(1)}, u32[]{:S(2)}, u32[]{:S(2)}) collective-permute-start(f32[4,128,256]{2,1,0:T(8,128)S(1)} %get-tuple-element.22.strips), channel_id=1, source_target_pairs={{0,28},{4,8},{8,4},{12,16},{16,12},{20,24},{24,20},{28,0},{1,29},{... | collective-permute-start | bytes 1572872 | tf_op jit(solution)/shard_map/ppermute | solution.py:419
  18.1 7.2 %collective-permute-start.4 = (f32[256,256]{1,0:T(8,128)S(1)}, f32[256,256]{1,0:T(8,128)S(1)}, u32[]{:S(2)}, u32[]{:S(2)}) collective-permute-start(f32[256,256]{1,0:T(8,128)S(1)} %get-tuple-element.27.factor_own), channel_id=1, source_target_pairs={{0,4},{4,0},{8,12},{12,8},{16,20},{20,16},{24,28},{28,24},{1,5},{5... | collective-permute-start | bytes 786440 | tf_op jit(solution)/shard_map/ppermute | solution.py:415
  18.1 12.5 %collective-permute-start.8 = (f32[256,256]{1,0:T(8,128)S(1)}, f32[256,256]{1,0:T(8,128)S(1)}, u32[]{:S(2)}, u32[]{:S(2)}) collective-permute-start(f32[256,256]{1,0:T(8,128)S(1)} %get-tuple-element.27.factor_own), channel_id=1, source_target_pairs={{1,0},{2,1},{3,2},{0,3},{5,4},{6,5},{7,6},{4,7},{9,8},{10,9},{11,1... | collective-permute-start | bytes 786440 | tf_op jit(solution)/shard_map/ppermute | solution.py:423
  22.6 9.2 %collective-permute-start.7 = (f32[128,256]{1,0:T(8,128)S(1)}, f32[128,256]{1,0:T(8,128)S(1)}, u32[]{:S(2)}, u32[]{:S(2)}) collective-permute-start(f32[128,256]{1,0:T(8,128)S(1)} %get-tuple-element.33), channel_id=1, source_target_pairs={{0,28},{4,8},{8,4},{12,16},{16,12},{20,24},{24,20},{28,0},{1,29},{... | collective-permute-start | bytes 393224 | tf_op jit(solution)/shard_map/ppermute | solution.py:419
  24.6 9.0 %collective-permute-start.6 = (f32[128,256]{1,0:T(8,128)S(1)}, f32[128,256]{1,0:T(8,128)S(1)}, u32[]{:S(2)}, u32[]{:S(2)}) collective-permute-start(f32[128,256]{1,0:T(8,128)S(1)} %get-tuple-element.32), channel_id=1, source_target_pairs={{0,28},{4,8},{8,4},{12,16},{16,12},{20,24},{24,20},{28,0},{1,29},{... | collective-permute-start | bytes 393224 | tf_op jit(solution)/shard_map/ppermute | solution.py:419

commit v18 on v14

--- a/solution.py
+++ b/solution.py
@@ -156,9 +156,9 @@
     size = sqrt_iterate.shape[1]
     half = size // 2
     copies = []
-    for source in (sqrt_iterate, inverse_iterate):
-        for i in range(ROWS):
-            block = len(copies) // 2
+    for i in range(ROWS):
+        for at, source in enumerate((sqrt_iterate, inverse_iterate)):
+            block = at * ROWS + i
             for rows in (pl.ds(0, half), pl.ds(half, half)):
                 copies.append(
                     pltpu.make_async_copy(

time: 34.5 us -> 34.5 us (level)
  no operation moved by 1% of the time
where the time goes in v18:
time: 34.5 us; the launch traced here: 34.2 us
  starting transfers between devices  16.7 us (48%)
  Pallas kernels  11.5 us (33%)
  waiting for transfers between devices  5.24 us (15%)
  between operations  0.74 us (2%)
    pallas_call x10, Pallas kernels, call(): pl.pallas_call(kernel, out_shape=outs, in_specs=[spec(pltpu.HBM if at in...  11.5 us
    ppermute x5, starting transfers between devices, to_peer(): return lax.ppermute(value, 'row', route)  8.34 us
    ppermute x2, starting transfers between devices, to_side(): return lax.ppermute(value, 'col', route)  8.22 us
    ppermute x5, waiting for transfers between devices, to_peer(): return lax.ppermute(value, 'row', route)  5.23 us
  transfers between devices with their start and end apart: 9, of which 3 were waited for; matrix products, arithmetic and copies ran while one was open for 0% of the time, Pallas kernels for 29%

profile of v18, /device:TPU:0, one launch (start us, length us, event | category | flops | bytes accessed | tf_op | source)
XLA Modules:
  0.0 34.2 jit_solution(8526004964581966342)
XLA Ops:
  0.6 0.9 %shard_map.68.after = f32[4,128,128]{2,1,0:T(8,128)S(1)} custom-call(f32[2,128,1024]{2,1,0:T(8,128)} %sqrt_iterate.3, f32[2,128,1024]{2,1,0:T(8,128)} %inverse_iterate.3), custom_call_target="tpu_custom_call" | custom-call | tf_op jit(solution)/shard_map/pallas_call | solution.py:386
  1.6 3.4 %collective-permute-start.1 = (f32[4,128,128]{2,1,0:T(8,128)S(1)}, f32[4,128,128]{2,1,0:T(8,128)S(1)}, u32[]{:S(2)}, u32[]{:S(2)}) collective-permute-start(f32[4,128,128]{2,1,0:T(8,128)S(1)} %shard_map.68.after), channel_id=1, source_target_pairs={{0,28},{4,8},{8,4},{12,16},{16,12},{20,24},{24,20},{28,0},{1,29},{... | collective-permute-start | bytes 786440 | tf_op jit(solution)/shard_map/ppermute | solution.py:417
  5.0 1.7 %shard_map.69 = (s32[16,128]{1,0:T(8,128)S(1)}, f32[24,128]{1,0:T(8,128)S(1)}, f32[256,256]{1,0:T(8,128)S(1)}, f32[4,128,256]{2,1,0:T(8,128)S(1)}, f32[4,256,256...) custom-call(s32[8,64]{1,0:T(8,128)} %bitcast.2, ...), custom_call_target="tpu_custom_call" | custom-call | tf_op jit(solution)/shard_map/pallas_call | solution.py:386
  6.7 0.1 collective-permute-start
  6.8 0.7 %collective-permute-start.2 = (f32[256,256]{1,0:T(8,128)S(1)}, f32[256,256]{1,0:T(8,128)S(1)}, u32[]{:S(2)}, u32[]{:S(2)}) collective-permute-start(f32[256,256]{1,0:T(8,128)S(1)} %get-tuple-element.21.y_peer), channel_id=1, source_target_pairs={{0,28},{4,8},{8,4},{12,16},{16,12},{20,24},{24,20},{28,0},{1,29},{... | collective-permute-start | bytes 786440 | tf_op jit(solution)/shard_map/ppermute | solution.py:417
  7.5 3.7 %collective-permute-start.3 = (f32[2,256,256]{2,1,0:T(8,128)S(1)}, f32[2,256,256]{2,1,0:T(8,128)S(1)}, u32[]{:S(2)}, u32[]{:S(2)}) collective-permute-start(f32[2,256,256]{2,1,0:T(8,128)S(1)} %get-tuple-element.26), channel_id=1, source_target_pairs={{1,0},{2,1},{3,2},{0,3},{5,4},{6,5},{7,6},{4,7},{9,8},{10,9},{11,1... | collective-permute-start | bytes 1572872 | tf_op jit(solution)/shard_map/ppermute | solution.py:421
  11.2 1.6 %collective-permute-start.5 = (f32[4,128,256]{2,1,0:T(8,128)S(1)}, f32[4,128,256]{2,1,0:T(8,128)S(1)}, u32[]{:S(2)}, u32[]{:S(2)}) collective-permute-start(f32[4,128,256]{2,1,0:T(8,128)S(1)} %get-tuple-element.22.strips), channel_id=1, source_target_pairs={{0,28},{4,8},{8,4},{12,16},{16,12},{20,24},{24,20},{28,0},{1,29},{... | collective-permute-start | bytes 1572872 | tf_op jit(solution)/shard_map/ppermute | solution.py:417
  12.8 0.0 collective-permute-done.1.diagonal
  12.9 1.7 %shard_map.71.mate_terms = f32[5,256,256]{2,1,0:T(8,128)S(1)} custom-call(f32[24,128]{1,0:T(8,128)S(1)} %get-tuple-element.20.kept, f32[4,256,256]{2,1,0:T(8,128)S(1)} %get-tuple-element.23.mate, f32[4,256,256]{2,1,0:T(8,128)S(1)} %collective-permute-done.from_mate, f32[2,256,256]{2,1,0:T(8,128)S(1)} %shard_map.70.after.peer_spread), custom_call_target="tpu_custom_call" | custom-call | tf_op jit(solution)/shard_map/pallas_call | solution.py:386
  14.6 2.7 %collective-permute-done.2.peer_y = f32[256,256]{1,0:T(8,128)S(1)} collective-permute-done((f32[256,256]{1,0:T(8,128)S(1)}, f32[256,256]{1,0:T(8,128)S(1)}, u32[]{:S(2)}, u32[]{:S(2)}) %collective-permute-start.2) | collective-permute-done | bytes 262176 | tf_op jit(solution)/shard_map/ppermute | solution.py:417
  17.3 0.7 %shard_map.72 = (f32[256,256]{1,0:T(8,128)S(1)}, f32[128,256]{1,0:T(8,128)S(1)}, f32[128,256]{1,0:T(8,128)S(1)}) custom-call(f32[24,128]{1,0:T(8,128)S(1)} %get-tuple-element.20.kept, f32[5,256,256]{2,1,0:T(8,128)S(1)} %shard_map.71.mate_terms, f32[4,128,256]{2,1,0:T(8,128)S(1)} %get-tuple-element.22.strips, f32[256,256]{1,0:T(8,128)S(1)} %collective-permute-done.2.peer_y), custom_call_target="tpu_custom_call" | custom-call | flops 5765000192 | tf_op jit(solution)/shard_map/pallas_call | solution.py:386
  18.0 0.1 collective-permute-start.4
  18.0 4.5 %collective-permute-start.8 = (f32[256,256]{1,0:T(8,128)S(1)}, f32[256,256]{1,0:T(8,128)S(1)}, u32[]{:S(2)}, u32[]{:S(2)}) collective-permute-start(f32[256,256]{1,0:T(8,128)S(1)} %get-tuple-element.27.factor_own), channel_id=1, source_target_pairs={{1,0},{2,1},{3,2},{0,3},{5,4},{6,5},{7,6},{4,7},{9,8},{10,9},{11,1... | collective-permute-start | bytes 786440 | tf_op jit(solution)/shard_map/ppermute | solution.py:421
  22.5 2.0 %collective-permute-start.7 = (f32[128,256]{1,0:T(8,128)S(1)}, f32[128,256]{1,0:T(8,128)S(1)}, u32[]{:S(2)}, u32[]{:S(2)}) collective-permute-start(f32[128,256]{1,0:T(8,128)S(1)} %get-tuple-element.33), channel_id=1, source_target_pairs={{0,28},{4,8},{8,4},{12,16},{16,12},{20,24},{24,20},{28,0},{1,29},{... | collective-permute-start | bytes 393224 | tf_op jit(solution)/shard_map/ppermute | solution.py:417
  24.5 0.7 %collective-permute-start.6 = (f32[128,256]{1,0:T(8,128)S(1)}, f32[128,256]{1,0:T(8,128)S(1)}, u32[]{:S(2)}, u32[]{:S(2)}) collective-permute-start(f32[128,256]{1,0:T(8,128)S(1)} %get-tuple-element.32), channel_id=1, source_target_pairs={{0,28},{4,8},{8,4},{12,16},{16,12},{20,24},{24,20},{28,0},{1,29},{... | collective-permute-start | bytes 393224 | tf_op jit(solution)/shard_map/ppermute | solution.py:417
  25.2 0.0 collective-permute-done.4.mate_factor
  25.2 1.8 %shard_map.73 = (f32[3,256,256]{2,1,0:T(8,128)S(1)}, f32[5,256,256]{2,1,0:T(8,128)S(1)}, bf16[5,2,256,256]{3,2,1,0:T(8,128)(2,1)S(1)}) custom-call(f32[24,128]{1,0:T(8,128)S(1)} %get-tuple-element.20.kept, f32[256,256]{1,0:T(8,128)S(1)} %get-tuple-element.21.y_peer, f32[4,128,256]{2,1,0:T(8,128)S(1)} %get-tuple-element.22.strips, ...), custom_call_target="tpu_custom_call" | custom-call | tf_op jit(solution)/shard_map/pallas_call | solution.py:386
  27.0 1.5 %collective-permute-done.5.from_peer = f32[4,128,256]{2,1,0:T(8,128)S(1)} collective-permute-done((f32[4,128,256]{2,1,0:T(8,128)S(1)}, f32[4,128,256]{2,1,0:T(8,128)S(1)}, u32[]{:S(2)}, u32[]{:S(2)}) %collective-permute-start.5) | collective-permute-done | bytes 524320 | tf_op jit(solution)/shard_map/ppermute | solution.py:417
  28.5 2.0 %shard_map.74 = (f32[2,128,1024]{2,1,0:T(8,128)}, f32[2,128,1024]{2,1,0:T(8,128)}, f32[256,256]{1,0:T(8,128)S(1)}) custom-call(s32[16,128]{1,0:T(8,128)S(1)} %get-tuple-element.19.slots, f32[24,128]{1,0:T(8,128)S(1)} %get-tuple-element.20.kept, f32[3,256,256]{2,1,0:T(8,128)S(1)} %get-tuple-element.28.finished, f32[5,256,256]{2,1,0:T(8,128)S(1)} %get-tuple-element.29.partial, ...), custom_call_target="tpu_custom_call" | custom-call | tf_op jit(solution)/shard_map/pallas_call | solution.py:386
  30.5 0.0 collective-permute-done.8.factor
  30.5 1.2 %shard_map.75.unfinished = f32[2,128,1024]{2,1,0:T(8,128)} custom-call(s32[16,128]{1,0:T(8,128)S(1)} %get-tuple-element.19.slots, f32[24,128]{1,0:T(8,128)S(1)} %get-tuple-element.20.kept, f32[5,256,256]{2,1,0:T(8,128)S(1)} %get-tuple-element.29.partial, bf16[5,2,256,256]{3,2,1,0:T(8,128)(2,1)S(1)} %get-tuple-element.30.ready, ...), custom_call_target="tpu_custom_call", output_to_operand_aliasing={{}: (5, {})} | custom-call | tf_op jit(solution)/shard_map/pallas_call | solution.py:386
  31.7 0.7 %shard_map.76.unfinished = f32[2,128,1024]{2,1,0:T(8,128)} custom-call(s32[16,128]{1,0:T(8,128)S(1)} %get-tuple-element.19.slots, f32[256,256]{1,0:T(8,128)S(1)} %get-tuple-element.31.part, f32[128,256]{1,0:T(8,128)S(1)} %collective-permute-done.7.term, f32[2,128,1024]{2,1,0:T(8,128)} %shard_map.75.unfinished), custom_call_target="tpu_custom_call", output_to_operand_aliasing={{}: (3, {})} | custom-call | tf_op jit(solution)/shard_map/pallas_call | solution.py:386
  32.4 1.0 %collective-permute-done.6.term = f32[128,256]{1,0:T(8,128)S(1)} collective-permute-done((f32[128,256]{1,0:T(8,128)S(1)}, f32[128,256]{1,0:T(8,128)S(1)}, u32[]{:S(2)}, u32[]{:S(2)}) %collective-permute-start.6) | collective-permute-done | bytes 131104 | tf_op jit(solution)/shard_map/ppermute | solution.py:417
  33.5 0.7 %shard_map.77 = f32[2,128,1024]{2,1,0:T(8,128)} custom-call(s32[16,128]{1,0:T(8,128)S(1)} %get-tuple-element.19.slots, f32[256,256]{1,0:T(8,128)S(1)} %get-tuple-element.31.part, f32[128,256]{1,0:T(8,128)S(1)} %collective-permute-done.6.term, f32[2,128,1024]{2,1,0:T(8,128)} %shard_map.76.unfinished), custom_call_target="tpu_custom_call", output_to_operand_aliasing={{}: (3, {})} | custom-call | tf_op jit(solution)/shard_map/pallas_call | solution.py:386
  (4 shorter events, 0.0 us)
Async XLA Ops:
  1.6 11.3 %collective-permute-start.1 = (f32[4,128,128]{2,1,0:T(8,128)S(1)}, f32[4,128,128]{2,1,0:T(8,128)S(1)}, u32[]{:S(2)}, u32[]{:S(2)}) collective-permute-start(f32[4,128,128]{2,1,0:T(8,128)S(1)} %shard_map.68.after), channel_id=1, source_target_pairs={{0,28},{4,8},{8,4},{12,16},{16,12},{20,24},{24,20},{28,0},{1,29},{... | collective-permute-start | bytes 786440 | tf_op jit(solution)/shard_map/ppermute | solution.py:417
  6.7 6.2 %collective-permute-start = (f32[4,256,256]{2,1,0:T(8,128)S(1)}, f32[4,256,256]{2,1,0:T(8,128)S(1)}, u32[]{:S(2)}, u32[]{:S(2)}) collective-permute-start(f32[4,256,256]{2,1,0:T(8,128)S(1)} %get-tuple-element.23.mate), channel_id=1, source_target_pairs={{0,4},{4,0},{8,12},{12,8},{16,20},{20,16},{24,28},{28,24},{1,5},{5... | collective-permute-start | bytes 3145736 | tf_op jit(solution)/shard_map/ppermute | solution.py:413
  6.8 10.5 %collective-permute-start.2 = (f32[256,256]{1,0:T(8,128)S(1)}, f32[256,256]{1,0:T(8,128)S(1)}, u32[]{:S(2)}, u32[]{:S(2)}) collective-permute-start(f32[256,256]{1,0:T(8,128)S(1)} %get-tuple-element.21.y_peer), channel_id=1, source_target_pairs={{0,28},{4,8},{8,4},{12,16},{16,12},{20,24},{24,20},{28,0},{1,29},{... | collective-permute-start | bytes 786440 | tf_op jit(solution)/shard_map/ppermute | solution.py:417
  7.5 17.0 %collective-permute-start.3 = (f32[2,256,256]{2,1,0:T(8,128)S(1)}, f32[2,256,256]{2,1,0:T(8,128)S(1)}, u32[]{:S(2)}, u32[]{:S(2)}) collective-permute-start(f32[2,256,256]{2,1,0:T(8,128)S(1)} %get-tuple-element.26), channel_id=1, source_target_pairs={{1,0},{2,1},{3,2},{0,3},{5,4},{6,5},{7,6},{4,7},{9,8},{10,9},{11,1... | collective-permute-start | bytes 1572872 | tf_op jit(solution)/shard_map/ppermute | solution.py:421
  11.2 17.3 %collective-permute-start.5 = (f32[4,128,256]{2,1,0:T(8,128)S(1)}, f32[4,128,256]{2,1,0:T(8,128)S(1)}, u32[]{:S(2)}, u32[]{:S(2)}) collective-permute-start(f32[4,128,256]{2,1,0:T(8,128)S(1)} %get-tuple-element.22.strips), channel_id=1, source_target_pairs={{0,28},{4,8},{8,4},{12,16},{16,12},{20,24},{24,20},{28,0},{1,29},{... | collective-permute-start | bytes 1572872 | tf_op jit(solution)/shard_map/ppermute | solution.py:417
  18.0 7.2 %collective-permute-start.4 = (f32[256,256]{1,0:T(8,128)S(1)}, f32[256,256]{1,0:T(8,128)S(1)}, u32[]{:S(2)}, u32[]{:S(2)}) collective-permute-start(f32[256,256]{1,0:T(8,128)S(1)} %get-tuple-element.27.factor_own), channel_id=1, source_target_pairs={{0,4},{4,0},{8,12},{12,8},{16,20},{20,16},{24,28},{28,24},{1,5},{5... | collective-permute-start | bytes 786440 | tf_op jit(solution)/shard_map/ppermute | solution.py:413
  18.0 12.4 %collective-permute-start.8 = (f32[256,256]{1,0:T(8,128)S(1)}, f32[256,256]{1,0:T(8,128)S(1)}, u32[]{:S(2)}, u32[]{:S(2)}) collective-permute-start(f32[256,256]{1,0:T(8,128)S(1)} %get-tuple-element.27.factor_own), channel_id=1, source_target_pairs={{1,0},{2,1},{3,2},{0,3},{5,4},{6,5},{7,6},{4,7},{9,8},{10,9},{11,1... | collective-permute-start | bytes 786440 | tf_op jit(solution)/shard_map/ppermute | solution.py:421
  22.5 9.2 %collective-permute-start.7 = (f32[128,256]{1,0:T(8,128)S(1)}, f32[128,256]{1,0:T(8,128)S(1)}, u32[]{:S(2)}, u32[]{:S(2)}) collective-permute-start(f32[128,256]{1,0:T(8,128)S(1)} %get-tuple-element.33), channel_id=1, source_target_pairs={{0,28},{4,8},{8,4},{12,16},{16,12},{20,24},{24,20},{28,0},{1,29},{... | collective-permute-start | bytes 393224 | tf_op jit(solution)/shard_map/ppermute | solution.py:417
  24.5 9.0 %collective-permute-start.6 = (f32[128,256]{1,0:T(8,128)S(1)}, f32[128,256]{1,0:T(8,128)S(1)}, u32[]{:S(2)}, u32[]{:S(2)}) collective-permute-start(f32[128,256]{1,0:T(8,128)S(1)} %get-tuple-element.32), channel_id=1, source_target_pairs={{0,28},{4,8},{8,4},{12,16},{16,12},{20,24},{24,20},{28,0},{1,29},{... | collective-permute-start | bytes 393224 | tf_op jit(solution)/shard_map/ppermute | solution.py:417
